TPU v7x, 32 devices: a whole 2x2x4 slice. The times are simulated.
32 devices in a mesh: parts: 2 (over y), lat: 8 (over z, x), tok: 2 (over core).
Axes of the slice: x: 2, y: 2, z: 4, core: 2. Of those that a mesh axis runs over, the one named last changes fastest.
Arguments:
- residual: bfloat16 [512, 3584], P(('parts', 'tok'), 'lat'), parts along dimension 0, may hold values from -6 to 6
- enc_weight: bfloat16 [3584, 4096], P(None, 'lat'), may hold values from -0.09375 to 0.09375
- enc_bias: float32 [4096], P('lat'), may hold values from -3 to 3
- threshold: float32 [4096], P('lat'), may hold values from 0.15 to 0.7
- partners: int32 [8, 4], replicated, may hold values from 0 to 8, as said below
Outputs:
- gram_tiles: bfloat16 [16, 4, 512, 512], P(('parts', 'lat'), None, 'tok'), parts along dimension 0
There are 2 independent parts, one for each index of `parts`. A program takes and returns all parts, laid end to end along the dimension named above; an argument that names none is the same for every part. Nothing has to cross between parts.
Inputs may be any that keep to these rules, and one draw needn't show every extreme that they name: `partners`: row d lists the partner blocks of latent block d in 4 slots: slot 0 is d itself, the live slots come first and hold distinct block numbers, the others hold the null value 8; every row has one live slot or more, and some row has all 4 slots live.
All inputs are finite; a program needn't handle non-finite values.
Results may differ from a plain program's by a relative error of at most 0.0023.
Values may be sent and summed in bfloat16 or wider, within the bound.
No kernel may reach another device: no remote copies, remote signals or barrier semaphores. Data moves between devices by JAX's collectives and lax.ppermute only.
A program may use at most 64 MiB of HBM per device.

v0:
```python
import jax
import jax.numpy as jnp
from jax import lax
from jax.sharding import PartitionSpec as P

ramp_width = 0.25


def body(residual, enc_weight, enc_bias, threshold, partners):
    tok_rows = residual.shape[0]
    lat_width = enc_weight.shape[1]
    tok_scale = 1.0 / (tok_rows * lax.axis_size("tok"))
    pre_acts = (
        jnp.dot(
            lax.all_gather(residual, "lat", axis=1, tiled=True),
            enc_weight,
            preferred_element_type=jnp.float32,
        )
        + enc_bias
    )
    activations = (pre_acts * jnp.clip((pre_acts - threshold) / ramp_width + 0.5, 0.0, 1.0)).astype(
        jnp.bfloat16
    )
    slices = lax.all_to_all(
        activations.reshape(1, tok_rows, lat_width), "lat", split_axis=1, concat_axis=0, tiled=True
    )
    padded = jnp.concatenate([slices, jnp.zeros((1,) + slices.shape[1:], jnp.bfloat16)], 0)
    outgoing = jnp.take(padded, partners, axis=0)
    partial_value = jnp.einsum(
        "tl,ktm->klm",
        activations,
        lax.all_to_all(outgoing, "lat", split_axis=0, concat_axis=2, tiled=True)[0],
        preferred_element_type=jnp.float32,
    )[None]
    gram_sums = lax.psum_scatter(partial_value, "tok", scatter_dimension=2, tiled=True)
    return (gram_sums * tok_scale).astype(jnp.bfloat16)


def solution(mesh):
    return jax.shard_map(
        body,
        mesh=mesh,
        in_specs=(P(("parts", "tok"), "lat"), P(None, "lat"), P("lat"), P("lat"), P()),
        out_specs=P(("parts", "lat"), None, "tok", None),
        check_vma=False,
    )
```

profile of v0, /device:TPU:0, one launch (start us, length us, event | category | flops | bytes accessed | tf_op | source)
XLA Modules:
  0.0 97.2 jit_solution(7200445196114425167)
XLA Ops:
  6.5 0.0 copy-start
  6.5 34.5 %all_gather.3 = bf16[128,3584]{0,1:T(8,128)(2,1)S(1)} all-gather(bf16[128,448]{0,1:T(8,128)(2,1)} %param.5), channel_id=1, replica_groups=mesh['parts'=2,'lat'=8,'tok'=2] {'lat'}, dimensions={1}, use_global_device_ids=true | all-gather | bytes 1032192 | tf_op jit(solution)/shard_map/all_gather | solution.py:15
  41.0 2.8 %multiply_convert_fusion.1 = bf16[128,512]{1,0:T(8,128)(2,1)S(1)} fusion(bf16[128,3584]{0,1:T(8,128)(2,1)S(1)} %all_gather.3, bf16[3584,512]{1,0:T(8,128)(2,1)} %param.6, f32[512]{0:T(512)} %param.8, f32[512]{0:T(512)} %param.7), kind=kOutput, calls=%fused_computation.5 | convolution fusion | flops 470220800 | bytes 4722688 | tf_op jit(solution)/shard_map/dot_general | solution.py:14
  43.8 0.2 copy.32
  44.0 0.5 broadcast.12
  44.5 1.4 %reduce = bf16[128,512]{1,0:T(8,128)(2,1)S(1)} reduce(bf16[128,1,512]{2,1,0:T(2,128)(2,1)S(1)} %bitcast.25, bf16[]{:T(256)} %broadcast.12), dimensions={1}, to_apply=%bitcast.20.reduce_sub_computation | reduce | bytes 262146
  45.9 0.7 reshape.26
  46.7 5.5 %all-to-all-start = ((bf16[8,2,4096]{2,1,0:T(2,128)(2,1)}), bf16[8,2,4096]{2,1,0:T(2,128)(2,1)S(1)}, u32[]{:S(2)}, u32[]{:S(2)}) async-start(bf16[8,2,4096]{2,1,0:T(2,128)(2,1)} %reshape.26), calls=%async_computation | async-start | bytes 262144 | tf_op jit(solution)/shard_map/all_to_all | solution.py:24
  52.2 0.0 reduce-scatter.2.cloned.1.call-start
  52.2 0.0 copy-done
  52.2 0.1 copy.23
  52.3 0.1 copy.25
  52.4 0.1 reshape.17
  52.5 7.1 %all-to-all-done = bf16[8,2,4096]{2,1,0:T(2,128)(2,1)S(1)} async-done(((bf16[8,2,4096]{2,1,0:T(2,128)(2,1)}), bf16[8,2,4096]{2,1,0:T(2,128)(2,1)S(1)}, u32[]{:S(2)}, u32[]{:S(2)}) %all-to-all-start) | async-done | bytes 131104 | tf_op jit(solution)/shard_map/all_to_all | solution.py:24
  59.6 0.1 reshape.27
  59.8 0.6 gather_fusion
  60.4 0.1 broadcast_select_fusion
  60.5 12.7 %all_to_all.27 = bf16[8,4,16,512]{3,2,1,0:T(8,128)(2,1)S(1)} all-to-all(bf16[8,4,16,512]{3,2,1,0:T(8,128)(2,1)S(1)} %broadcast_select_fusion), channel_id=1, replica_groups=mesh['parts'=2,'lat'=8,'tok'=2] {'lat'}, dimensions={0} | all-to-all | bytes 1048576 | tf_op jit(solution)/shard_map/all_to_all | solution.py:32
  73.3 2.7 %convolution_bitcast_fusion = f32[1,4,512,512]{2,3,1,0:T(8,128)} fusion(bf16[4,128,512]{2,1,0:T(8,128)(2,1)S(1)} %bitcast.21, bf16[128,512]{1,0:T(8,128)(2,1)S(1)} %multiply_convert_fusion.1), kind=kOutput, calls=%fused_computation.1 | convolution fusion | flops 268435456 | bytes 4849664 | tf_op jit(solution)/shard_map/tl,ktm->klm/dot_general | solution.py:29
  76.0 0.0 reduce-scatter.2.cloned.1.call-update
  76.0 11.2 %reduce-scatter.2.cloned.1.call-done = f32[1,4,256,512]{2,3,1,0:T(8,128)} async-done(((f32[1,4,512,512]{2,3,1,0:T(8,128)}), f32[1,4,256,512]{2,3,1,0:T(8,128)}) %reduce-scatter.2.cloned.1.call-update) | async-done | bytes 2097168 | tf_op jit(solution)/shard_map/reduce_scatter | solution.py:35
  87.2 1.8 %multiply_convert_fusion = bf16[1,4,256,512]{2,3,1,0:T(8,128)(2,1)S(1)} fusion(f32[1,4,256,512]{2,3,1,0:T(8,128)} %reduce-scatter.2.cloned.1.call-done), kind=kLoop, calls=%fused_computation.2 | loop fusion | flops 1048576 | bytes 3145728 | tf_op jit(solution)/shard_map/convert_element_type | solution.py:36
  89.0 1.3 %copy.28 = bf16[1,4,256,512]{3,2,1,0:T(8,128)(2,1)} copy(bf16[1,4,256,512]{2,3,1,0:T(8,128)(2,1)S(1)} %multiply_convert_fusion) | data formatting | bytes 2097152 | tf_op jit(solution)/shard_map/convert_element_type | solution.py:36
  (6 shorter events, 0.1 us)
Async XLA Ops:
  6.5 45.7 %copy-start = (s32[8,4]{0,1:T(4,128)S(1)}, s32[8,4]{0,1:T(4,128)}, u32[]{:S(2)}) copy-start(s32[8,4]{0,1:T(4,128)} %param.9) | copy-start | bytes 388
  46.7 13.0 %all-to-all-start = ((bf16[8,2,4096]{2,1,0:T(2,128)(2,1)}), bf16[8,2,4096]{2,1,0:T(2,128)(2,1)S(1)}, u32[]{:S(2)}, u32[]{:S(2)}) async-start(bf16[8,2,4096]{2,1,0:T(2,128)(2,1)} %reshape.26), calls=%async_computation | async-start | bytes 262144 | tf_op jit(solution)/shard_map/all_to_all | solution.py:24
  52.2 35.0 %reduce-scatter.2.cloned.1.call-start = ((), (), s32[]{:S(2)}) async-start(), calls=%async_computation.3 | async-start | bytes 6291456 | tf_op jit(solution)/shard_map/reduce_scatter | solution.py:35
Sparse Core Ops, SparseCore 0:
  76.1 11.0 reduce-scatter.1
where the time goes:
time: 97.5 us; the launch traced here: 97.2 us
  blocking collectives  47.2 us (48%)
  waiting for transfers between devices  18.3 us (19%)
  between operations  13.5 us (14%)
  starting transfers between devices  5.55 us (6%)
  matrix products  5.44 us (6%)
  local copies, waits for them, and re-layouts  3.81 us (4%)
  other arithmetic  3.31 us (3%)
    all_gather x1, blocking collectives, body(): lax.all_gather(residual, 'lat', axis=1, tiled=True)  34.5 us
    all_to_all x1, blocking collectives, body(): lax.all_to_all(outgoing, 'lat', split_axis=0, concat_axis=2, tiled=True)[0]  12.7 us
    reduce_scatter x1, waiting for transfers between devices, body(): lax.psum_scatter(partial_value, 'tok', scatter_dimension=2, tiled=True)  11.2 us
    all_to_all x1, waiting for transfers between devices, body(): lax.all_to_all(activations.reshape(1, tok_rows, lat_width), 'lat', split_...  7.1 us
    all_to_all x1, starting transfers between devices, body(): lax.all_to_all(activations.reshape(1, tok_rows, lat_width), 'lat', split_...  5.51 us
    dot_general x1, matrix products, body(): jnp.dot(lax.all_gather(residual, 'lat', axis=1, tiled=True), enc_weight,...  2.77 us
    dot_general x1, matrix products, body(): jnp.einsum('tl,ktm->klm', activations, lax.all_to_all(outgoing, 'lat', sp...  2.67 us
  transfers between devices with their start and end apart: 2, of which 2 were waited for; matrix products, arithmetic and copies ran while one was open for 0% of the time, Pallas kernels for 0%

commit v1 on v0

v1 whole, which is shorter than its diff:
```python
import functools

import jax
import jax.numpy as jnp
import numpy as np
from jax import lax
from jax.experimental import pallas as pl
from jax.experimental.pallas import tpu as pltpu
from jax.sharding import PartitionSpec as P

ramp_width = 0.25
ring_limit = 16
vmem_limit = 32 * 1024 * 1024

rows_by_rows = (((0,), (0,)), ((), ()))


def ring_order(n):
    return list(range(0, n, 2)) + list(range(1, n, 2))[::-1]


def activate(pre_acts, threshold):
    gate = jnp.clip((pre_acts - threshold) / ramp_width + 0.5, 0.0, 1.0)
    return (pre_acts * gate).astype(jnp.bfloat16)


def project(x, w):
    return lax.dot_general(x, w, rows_by_rows, preferred_element_type=jnp.float32)


def first_step(_, x, w, total):
    total[...] = project(x[...], w[0])


def middle_step(_, x_f, x_b, w_f, w_b, before, total):
    total[...] = before[...] + project(x_f[...], w_f[0]) + project(x_b[...], w_b[0])


def last_step(_, x_f, x_b, w, before, bias, threshold, acts):
    half = x_f.shape[0]
    pre_acts = (
        before[...] + project(x_f[...], w[0, :half]) + project(x_b[...], w[0, half:]) + bias[...]
    )
    acts[...] = activate(pre_acts, threshold[...])


def whole(shape):
    return pl.BlockSpec(shape, lambda i, ids: (0,) * len(shape))


def step_call(kernel, ids, places, xs, weights, others, out):
    depth, width = weights.shape[1:]
    picks = [
        pl.BlockSpec((1, depth, width), functools.partial(lambda k, i, ids: (ids[k], 0, 0), k))
        for k in places
    ]
    rows = sum(x.shape[0] for x in xs)
    return pl.pallas_call(
        kernel,
        out_shape=out,
        grid_spec=pltpu.PrefetchScalarGridSpec(
            num_scalar_prefetch=1,
            grid=(1,),
            in_specs=[whole(x.shape) for x in xs] + picks + [whole(o.shape) for o in others],
            out_specs=whole(out.shape),
        ),
        compiler_params=pltpu.CompilerParams(vmem_limit_bytes=vmem_limit),
        cost_estimate=pl.CostEstimate(
            flops=2 * rows * xs[0].shape[1] * width,
            bytes_accessed=2 * rows * width + 8 * xs[0].shape[1] * width,
            transcendentals=0,
        ),
    )(ids, *xs, *([weights] * len(places)), *others)


def encode_on_ring(residual, enc_weight, enc_bias, threshold, n):
    tok_rows, depth = residual.shape
    width = enc_weight.shape[1]
    order = ring_order(n)
    forward = [(order[i], order[(i + 1) % n]) for i in range(n)]
    backward = [(d, s) for s, d in forward]
    position = {b: i for i, b in enumerate(order)}
    origins = np.array(
        [[order[(position[b] - h) % n] for h in range(n)] for b in range(n)], np.int32
    )
    ids = jnp.asarray(origins)[lax.axis_index("lat")]
    x = residual.T
    weights = enc_weight.reshape(n, depth, width)
    total_shape = jax.ShapeDtypeStruct((tok_rows, width), jnp.float32)
    ahead = behind = x
    total = None
    for hop in range(1, n // 2):
        ahead = lax.ppermute(ahead, "lat", forward)
        behind = lax.ppermute(behind, "lat", backward)
        if hop == 1:
            total = step_call(first_step, ids, [0], [x], weights, [], total_shape)
        total = step_call(
            middle_step, ids, [hop, n - hop], [ahead, behind], weights, [total], total_shape
        )
    half = depth // 2
    ahead = lax.ppermute(ahead[:half], "lat", forward)
    behind = lax.ppermute(behind[half:], "lat", backward)
    return step_call(
        last_step,
        ids,
        [n // 2],
        [ahead, behind],
        weights,
        [total, enc_bias.reshape(1, width), threshold.reshape(1, width)],
        jax.ShapeDtypeStruct((tok_rows, width), jnp.bfloat16),
    )


def encode_gathered(residual, enc_weight, enc_bias, threshold):
    pre_acts = (
        jnp.dot(
            lax.all_gather(residual, "lat", axis=1, tiled=True),
            enc_weight,
            preferred_element_type=jnp.float32,
        )
        + enc_bias
    )
    return activate(pre_acts, threshold)


def select_kernel(partners, slices, outgoing):
    blocks, slots = partners.shape
    for d in range(blocks):
        for k in range(1, slots):
            outgoing[d, k - 1] = slices[jnp.minimum(partners[d, k], blocks - 1)]


def select(slices, partners):
    blocks, rows, width = slices.shape
    slots = partners.shape[1]
    out = (blocks, slots - 1, rows, width)
    if rows % 16:
        return jnp.take(slices, jnp.minimum(partners[:, 1:], blocks - 1), axis=0)
    return pl.pallas_call(
        select_kernel,
        out_shape=jax.ShapeDtypeStruct(out, slices.dtype),
        grid_spec=pltpu.PrefetchScalarGridSpec(
            num_scalar_prefetch=1,
            grid=(1,),
            in_specs=[whole(slices.shape)],
            out_specs=whole(out),
        ),
        compiler_params=pltpu.CompilerParams(vmem_limit_bytes=vmem_limit),
    )(partners, slices)


def gram_kernel(tok_scale, place, own, own_twin, got, got_twin, tiles):
    slots, rows, width = tiles.shape[1:]
    columns = pl.ds(pl.multiple_of(place[0] * rows, rows), rows)
    left, left_twin = own[:, columns], own_twin[:, columns]
    tiles[0, 0] = (
        (project(left, own[...]) + project(left_twin, own_twin[...])) * tok_scale
    ).astype(tiles.dtype)
    for k in range(1, slots):

        @pl.when(place[k] != 0)
        def _():
            tile = project(left, got[k - 1]) + project(left_twin, got_twin[k - 1])
            tiles[0, k] = (tile * tok_scale).astype(tiles.dtype)

        @pl.when(place[k] == 0)
        def _():
            tiles[0, k] = jnp.zeros((rows, width), tiles.dtype)


def gram(own, own_twin, got, got_twin, place, tok_scale, halves):
    tok_rows, width = own.shape
    slots = got.shape[0] + 1
    out = (1, slots, width // halves, width)
    return pl.pallas_call(
        functools.partial(gram_kernel, tok_scale),
        out_shape=jax.ShapeDtypeStruct(out, own.dtype),
        grid_spec=pltpu.PrefetchScalarGridSpec(
            num_scalar_prefetch=1,
            grid=(1,),
            in_specs=[whole(a.shape) for a in (own, own_twin, got, got_twin)],
            out_specs=whole(out),
        ),
        compiler_params=pltpu.CompilerParams(vmem_limit_bytes=vmem_limit),
    )(place, own, own_twin, got, got_twin)


def body(residual, enc_weight, enc_bias, threshold, partners):
    n = lax.axis_size("lat")
    halves = lax.axis_size("tok")
    tok_rows = residual.shape[0]
    width = enc_weight.shape[1]
    slots = partners.shape[1]
    tok_scale = 1.0 / (tok_rows * halves)
    swap = [(i, 1 - i) for i in range(2)]
    if n <= ring_limit:
        acts = encode_on_ring(residual, enc_weight, enc_bias, threshold, n)
    else:
        acts = encode_gathered(residual, enc_weight, enc_bias, threshold)
    acts_twin = lax.ppermute(acts, "tok", swap)
    slices = lax.all_to_all(acts.reshape(n, tok_rows // n, width), "lat", 0, 0)
    got = lax.all_to_all(select(slices, partners), "lat", 0, 0)
    got = got.transpose(1, 0, 2, 3).reshape(slots - 1, tok_rows, width)
    got_twin = lax.ppermute(got, "tok", swap)
    row = lax.dynamic_index_in_dim(partners, lax.axis_index("lat"), 0, keepdims=False)
    place = jnp.where(
        jnp.arange(slots) == 0, lax.axis_index("tok"), (row < n).astype(jnp.int32)
    ).astype(jnp.int32)
    return gram(acts, acts_twin, got, got_twin, place, tok_scale, halves)


def solution(mesh):
    return jax.shard_map(
        body,
        mesh=mesh,
        in_specs=(P(("parts", "tok"), "lat"), P(None, "lat"), P("lat"), P("lat"), P()),
        out_specs=P(("parts", "lat"), None, "tok", None),
        check_vma=False,
    )
```

time: 97.5 us -> 60.3 us (0.62)
  blocking collectives: 47.2 us -> 11.8 us
  between operations: 13.5 us -> 0.13 us
  starting transfers between devices: 5.55 us -> 15.9 us
  Pallas kernels: 0 us -> 8.57 us
  matrix products: 5.44 us -> 0 us
  other arithmetic: 3.31 us -> 0.19 us
  local copies, waits for them, and re-layouts: 3.81 us -> 5.01 us
    all_gather x1 -> x0, blocking collectives: 34.5 us -> none  [body(): lax.all_gather(residual, 'lat', axis=1, tiled=True)]
    reduce_scatter x1 -> x0, waiting for transfers between devices: 11.2 us -> none  [body(): lax.psum_scatter(partial_value, 'tok', scatter_dimension=2, tiled=True)]
    ppermute x0 -> x10, waiting for transfers between devices: none -> 10.8 us  [the longest x3 9.31 us: encode_on_ring(): behind = lax.ppermute(behind, 'lat', backward)]
    ppermute x0 -> x10, starting transfers between devices: none -> 9.82 us  [the longest x3 6.25 us: encode_on_ring(): behind = lax.ppermute(behind, 'lat', backward)]
    pallas_call x0 -> x7, Pallas kernels: none -> 8.57 us  [the longest x5 4.86 us: step_call(): pl.pallas_call(kernel, out_shape=out, grid_spec=pltpu.PrefetchScalarGridS...]
    dot_general x2 -> x0, matrix products: 5.44 us -> none  [the longest x1 2.77 us: body(): jnp.dot(lax.all_gather(residual, 'lat', axis=1, tiled=True), enc_weight,...]
    unnamed x6 -> x13, local copies, waits for them, and re-layouts: 1.39 us -> 4.29 us
    convert_element_type x1, other arithmetic: 1.77 us -> 0.19 us  [body(): (row < n).astype(jnp.int32)]
  transfers between devices with their start and end apart: 2 -> 11, of which waited for: 2 -> 6; matrix products, arithmetic and copies ran while one was open for 0% -> 2% of each run, Pallas kernels for 0% -> 6%
where the time goes in v1:
time: 60.3 us; the launch traced here: 59.6 us
  waiting for transfers between devices  18 us (30%)
  starting transfers between devices  15.9 us (26%)
  blocking collectives  11.8 us (20%)
  Pallas kernels  8.57 us (14%)
  local copies, waits for them, and re-layouts  5.01 us (8%)
    all_to_all x1, blocking collectives, body(): got = lax.all_to_all(select(slices, partners), 'lat', 0, 0)  11.8 us
    ppermute x3, waiting for transfers between devices, encode_on_ring(): behind = lax.ppermute(behind, 'lat', backward)  9.31 us
    all_to_all x1, waiting for transfers between devices, body(): slices = lax.all_to_all(acts.reshape(n, tok_rows // n, width), 'lat', 0, 0)  7.26 us
    ppermute x3, starting transfers between devices, encode_on_ring(): behind = lax.ppermute(behind, 'lat', backward)  6.25 us
    all_to_all x1, starting transfers between devices, body(): slices = lax.all_to_all(acts.reshape(n, tok_rows // n, width), 'lat', 0, 0)  6.03 us
    pallas_call x5, Pallas kernels, step_call(): pl.pallas_call(kernel, out_shape=out, grid_spec=pltpu.PrefetchScalarGridS...  4.86 us
    unnamed x13, local copies, waits for them, and re-layouts  4.29 us
    pallas_call x1, Pallas kernels, gram(): pl.pallas_call(functools.partial(gram_kernel, tok_scale), out_shape=jax.S...  3.08 us
  transfers between devices with their start and end apart: 11, of which 6 were waited for; matrix products, arithmetic and copies ran while one was open for 2% of the time, Pallas kernels for 6%

profile of v1, /device:TPU:0, one launch (start us, length us, event | category | flops | bytes accessed | tf_op | source)
XLA Modules:
  0.0 59.6 jit_solution(14901179587382326135)
XLA Ops:
  0.0 2.9 %collective-permute-start.4 = (bf16[448,128]{1,0:T(8,128)(2,1)}, bf16[448,128]{1,0:T(8,128)(2,1)S(1)}, u32[]{:S(2)}, u32[]{:S(2)}) collective-permute-start(bf16[448,128]{1,0:T(8,128)(2,1)} %bitcast.19), channel_id=1, source_target_pairs={{4,0},{8,4},{12,8},{14,12},{10,14},{6,10},{2,6},{0,2},{5,1},{9,5},... | collective-permute-start | bytes 344072 | tf_op jit(solution)/shard_map/ppermute | solution.py:94
  2.9 0.1 collective-permute-start
  3.0 3.3 %collective-permute-done.4.x_b = bf16[448,128]{1,0:T(8,128)(2,1)S(1)} collective-permute-done((bf16[448,128]{1,0:T(8,128)(2,1)}, bf16[448,128]{1,0:T(8,128)(2,1)S(1)}, u32[]{:S(2)}, u32[]{:S(2)}) %collective-permute-start.4) | collective-permute-done | bytes 114720 | tf_op jit(solution)/shard_map/ppermute | solution.py:94
  6.4 1.7 %collective-permute-start.5 = (bf16[448,128]{1,0:T(8,128)(2,1)S(1)}, bf16[448,128]{1,0:T(8,128)(2,1)S(1)}, u32[]{:S(2)}, u32[]{:S(2)}) collective-permute-start(bf16[448,128]{1,0:T(8,128)(2,1)S(1)} %collective-permute-done.4.x_b), channel_id=1, source_target_pairs={{4,0},{8,4},{12,8},{14,12},{10,14},{6,10},{2,6},{0,2},{5,1},{9,5},... | collective-permute-start | bytes 344072 | tf_op jit(solution)/shard_map/ppermute | solution.py:94
  8.0 0.0 collective-permute-done.x_f
  8.0 0.4 collective-permute-start.1
  8.4 2.8 %collective-permute-done.5.x_b = bf16[448,128]{1,0:T(8,128)(2,1)S(1)} collective-permute-done((bf16[448,128]{1,0:T(8,128)(2,1)S(1)}, bf16[448,128]{1,0:T(8,128)(2,1)S(1)}, u32[]{:S(2)}, u32[]{:S(2)}) %collective-permute-start.5) | collective-permute-done | bytes 114720 | tf_op jit(solution)/shard_map/ppermute | solution.py:94
  11.2 1.7 %collective-permute-start.6 = (bf16[448,128]{1,0:T(8,128)(2,1)S(1)}, bf16[448,128]{1,0:T(8,128)(2,1)S(1)}, u32[]{:S(2)}, u32[]{:S(2)}) collective-permute-start(bf16[448,128]{1,0:T(8,128)(2,1)S(1)} %collective-permute-done.5.x_b), channel_id=1, source_target_pairs={{4,0},{8,4},{12,8},{14,12},{10,14},{6,10},{2,6},{0,2},{5,1},{9,5},... | collective-permute-start | bytes 344072 | tf_op jit(solution)/shard_map/ppermute | solution.py:94
  12.8 0.0 collective-permute-done.1.x_f
  12.8 0.4 collective-permute-start.2
  13.2 3.2 %collective-permute-done.6.x_b = bf16[448,128]{1,0:T(8,128)(2,1)S(1)} collective-permute-done((bf16[448,128]{1,0:T(8,128)(2,1)S(1)}, bf16[448,128]{1,0:T(8,128)(2,1)S(1)}, u32[]{:S(2)}, u32[]{:S(2)}) %collective-permute-start.6) | collective-permute-done | bytes 114720 | tf_op jit(solution)/shard_map/ppermute | solution.py:94
  16.4 1.8 %collective-permute-start.7 = (bf16[224,128]{1,0:T(8,128)(2,1)S(1)}, bf16[224,128]{1,0:T(8,128)(2,1)S(1)}, u32[]{:S(2)}, u32[]{:S(2)}) collective-permute-start(bf16[224,128]{1,0:T(8,128)(2,1)S(1)} %slice.9), channel_id=1, source_target_pairs={{4,0},{8,4},{12,8},{14,12},{10,14},{6,10},{2,6},{0,2},{5,1},{9,5},... | collective-permute-start | bytes 172040 | tf_op jit(solution)/shard_map/ppermute | solution.py:102
  18.2 0.1 collective-permute-done.2.x_f
  18.2 0.4 collective-permute-start.3
  18.6 0.7 %dynamic-slice_bitcast_fusion._ = s32[8]{0:T(128)S(1)} fusion(s32[8,8]{1,0:T(8,128)} %constant.20.clone, s32[]{:T(128)S(6)} %select_n.9), kind=kLoop, calls=%fused_computation.3 | loop fusion | bytes 68 | tf_op jit(solution)/shard_map/squeeze | solution.py:86
  19.3 0.0 copy-start
  19.3 2.0 %copy-done = bf16[3584,512]{1,0:T(8,128)(2,1)S(1)} copy-done((bf16[3584,512]{1,0:T(8,128)(2,1)S(1)}, bf16[3584,512]{1,0:T(8,128)(2,1)}, u32[]{:S(2)}) %copy-start) | copy-done | bytes 3670040
  21.3 0.0 copy-start.2
  21.3 0.9 %copy-done.2 = bf16[128,448]{0,1:T(8,128)(2,1)S(1)} copy-done((bf16[128,448]{0,1:T(8,128)(2,1)S(1)}, bf16[128,448]{0,1:T(8,128)(2,1)}, u32[]{:S(2)}) %copy-start.2) | copy-done | bytes 114712
  22.2 0.0 copy-start.1
  22.2 0.8 %shard_map.64.before = f32[128,512]{1,0:T(8,128)S(1)} custom-call(s32[8]{0:T(128)S(1)} %dynamic-slice_bitcast_fusion._, bf16[448,128]{1,0:T(8,128)(2,1)S(1)} %bitcast.21, bf16[8,448,512]{2,1,0:T(8,128)(2,1)S(1)} %bitcast.9), custom_call_target="tpu_custom_call" | custom-call | flops 58720256 | bytes 983040 | tf_op jit(solution)/shard_map/pallas_call | solution.py:58
  23.0 1.2 %copy-done.1 = bf16[3584,512]{1,0:T(8,128)(2,1)S(1)} copy-done((bf16[3584,512]{1,0:T(8,128)(2,1)S(1)}, bf16[3584,512]{1,0:T(8,128)(2,1)}, u32[]{:S(2)}) %copy-start.1) | copy-done | bytes 3670040
  24.3 0.9 %shard_map.65.before = f32[128,512]{1,0:T(8,128)S(1)} custom-call(s32[8]{0:T(128)S(1)} %dynamic-slice_bitcast_fusion._, bf16[448,128]{1,0:T(8,128)(2,1)S(1)} %collective-permute-done.x_f, bf16[448,128]{1,0:T(8,128)(2,1)S(1)} %collective-permute-done.4.x_b, bf16[8,448,512]{2,1,0:T(8,128)(2,1)S(1)} %bitcast.10, bf16[8,448,512]{2,1,0:T(8,128)(2,1)S(1)} %bitcast.11, ...), custom_call_target="tpu_custom_call" | custom-call | flops 117440512 | bytes 1441792 | tf_op jit(solution)/shard_map/pallas_call | solution.py:58
  25.1 0.9 %shard_map.66.before = f32[128,512]{1,0:T(8,128)S(1)} custom-call(s32[8]{0:T(128)S(1)} %dynamic-slice_bitcast_fusion._, bf16[448,128]{1,0:T(8,128)(2,1)S(1)} %collective-permute-done.1.x_f, bf16[448,128]{1,0:T(8,128)(2,1)S(1)} %collective-permute-done.5.x_b, bf16[8,448,512]{2,1,0:T(8,128)(2,1)S(1)} %bitcast.12, bf16[8,448,512]{2,1,0:T(8,128)(2,1)S(1)} %bitcast.13, ...), custom_call_target="tpu_custom_call" | custom-call | flops 117440512 | bytes 1441792 | tf_op jit(solution)/shard_map/pallas_call | solution.py:58
  26.0 0.0 copy-start.3
  26.0 0.0 copy-start.4
  26.0 0.9 %shard_map.67.before = f32[128,512]{1,0:T(8,128)S(1)} custom-call(s32[8]{0:T(128)S(1)} %dynamic-slice_bitcast_fusion._, bf16[448,128]{1,0:T(8,128)(2,1)S(1)} %collective-permute-done.2.x_f, bf16[448,128]{1,0:T(8,128)(2,1)S(1)} %collective-permute-done.6.x_b, bf16[8,448,512]{2,1,0:T(8,128)(2,1)S(1)} %bitcast.14, bf16[8,448,512]{2,1,0:T(8,128)(2,1)S(1)} %bitcast.15, ...), custom_call_target="tpu_custom_call" | custom-call | flops 117440512 | bytes 1441792 | tf_op jit(solution)/shard_map/pallas_call | solution.py:58
  26.9 0.0 copy-start.5
  26.9 0.0 collective-permute-done.7.x_b
  26.9 0.0 collective-permute-done.3.x_f
  27.0 0.0 copy-done.3
  27.0 0.0 copy-done.4
  27.0 1.5 %shard_map.68.own = bf16[128,512]{1,0:T(8,128)(2,1)} custom-call(s32[8]{0:T(128)S(1)} %dynamic-slice_bitcast_fusion._, bf16[224,128]{1,0:T(8,128)(2,1)S(1)} %collective-permute-done.3.x_f, bf16[224,128]{1,0:T(8,128)(2,1)S(1)} %collective-permute-done.7.x_b, bf16[8,448,512]{2,1,0:T(8,128)(2,1)S(1)} %bitcast.16, f32[128,512]{1,0:T(8,128)S(1)} %shard_map.67.before, ...), custom_call_target="tpu_custom_call" | custom-call | flops 58720256 | bytes 983040 | tf_op jit(solution)/shard_map/pallas_call | solution.py:58
  28.5 6.0 %all-to-all-start = ((bf16[8,16,512]{2,1,0:T(8,128)(2,1)}), bf16[8,16,512]{2,1,0:T(8,128)(2,1)S(1)}, u32[]{:S(2)}, u32[]{:S(2)}) async-start(bf16[8,16,512]{2,1,0:T(8,128)(2,1)} %bitcast.5), calls=%async_computation | async-start | bytes 262144 | tf_op jit(solution)/shard_map/all_to_all | solution.py:201
  34.5 0.0 copy-done.5
  34.5 0.1 copy.7.partners
  34.6 7.3 %all-to-all-done.slices = bf16[8,16,512]{2,1,0:T(8,128)(2,1)S(1)} async-done(((bf16[8,16,512]{2,1,0:T(8,128)(2,1)}), bf16[8,16,512]{2,1,0:T(8,128)(2,1)S(1)}, u32[]{:S(2)}, u32[]{:S(2)}) %all-to-all-start) | async-done | bytes 131104 | tf_op jit(solution)/shard_map/all_to_all | solution.py:201
  41.8 0.6 %shard_map.69 = bf16[8,3,16,512]{3,2,1,0:T(8,128)(2,1)S(1)} custom-call(s32[8,4]{1,0:T(8,128)S(1)} %copy.7.partners, bf16[8,16,512]{2,1,0:T(8,128)(2,1)S(1)} %all-to-all-done.slices), custom_call_target="tpu_custom_call" | custom-call | tf_op jit(solution)/shard_map/pallas_call | solution.py:139
  42.5 11.8 %all_to_all.10 = bf16[8,3,16,512]{3,2,1,0:T(8,128)(2,1)S(1)} all-to-all(bf16[8,3,16,512]{3,2,1,0:T(8,128)(2,1)S(1)} %shard_map.69), channel_id=1, replica_groups=mesh['parts'=2,'lat'=8,'tok'=2] {'lat'}, dimensions={0} | all-to-all | bytes 786432 | tf_op jit(solution)/shard_map/all_to_all | solution.py:202
  54.4 0.1 collective-permute-start.9
  54.4 0.2 convert_reduce_fusion
  54.6 0.6 collective-permute-start.8
  55.2 1.4 %collective-permute-done.8.own_twin = bf16[128,512]{1,0:T(8,128)(2,1)S(1)} collective-permute-done((bf16[128,512]{1,0:T(8,128)(2,1)}, bf16[128,512]{1,0:T(8,128)(2,1)S(1)}, u32[]{:S(2)}, u32[]{:S(2)}) %collective-permute-start.8) | collective-permute-done | bytes 131104 | tf_op jit(solution)/shard_map/ppermute | solution.py:200
  56.6 0.0 collective-permute-done.9.got_twin
  56.6 3.1 %shard_map.70 = bf16[1,4,256,512]{3,2,1,0:T(8,128)(2,1)} custom-call(s32[4]{0:T(128)S(1)} %compare_select_fusion.place, bf16[128,512]{1,0:T(8,128)(2,1)} %shard_map.68.own, bf16[128,512]{1,0:T(8,128)(2,1)S(1)} %collective-permute-done.8.own_twin, bf16[3,128,512]{2,1,0:T(8,128)(2,1)S(1)} %bitcast.18, bf16[3,128,512]{2,1,0:T(8,128)(2,1)S(1)} %collective-permute-done.9.got_twin), custom_call_target="tpu_custom_call" | custom-call | tf_op jit(solution)/shard_map/pallas_call | solution.py:175
  (4 shorter events, 0.0 us)
Async XLA Ops:
  0.0 6.4 %collective-permute-start.4 = (bf16[448,128]{1,0:T(8,128)(2,1)}, bf16[448,128]{1,0:T(8,128)(2,1)S(1)}, u32[]{:S(2)}, u32[]{:S(2)}) collective-permute-start(bf16[448,128]{1,0:T(8,128)(2,1)} %bitcast.19), channel_id=1, source_target_pairs={{4,0},{8,4},{12,8},{14,12},{10,14},{6,10},{2,6},{0,2},{5,1},{9,5},... | collective-permute-start | bytes 344072 | tf_op jit(solution)/shard_map/ppermute | solution.py:94
  2.9 5.1 %collective-permute-start = (bf16[448,128]{1,0:T(8,128)(2,1)}, bf16[448,128]{1,0:T(8,128)(2,1)S(1)}, u32[]{:S(2)}, u32[]{:S(2)}) collective-permute-start(bf16[448,128]{1,0:T(8,128)(2,1)} %bitcast.20), channel_id=1, source_target_pairs={{0,4},{4,8},{8,12},{12,14},{14,10},{10,6},{6,2},{2,0},{1,5},{5,9},... | collective-permute-start | bytes 344072 | tf_op jit(solution)/shard_map/ppermute | solution.py:93
  6.4 4.8 %collective-permute-start.5 = (bf16[448,128]{1,0:T(8,128)(2,1)S(1)}, bf16[448,128]{1,0:T(8,128)(2,1)S(1)}, u32[]{:S(2)}, u32[]{:S(2)}) collective-permute-start(bf16[448,128]{1,0:T(8,128)(2,1)S(1)} %collective-permute-done.4.x_b), channel_id=1, source_target_pairs={{4,0},{8,4},{12,8},{14,12},{10,14},{6,10},{2,6},{0,2},{5,1},{9,5},... | collective-permute-start | bytes 344072 | tf_op jit(solution)/shard_map/ppermute | solution.py:94
  8.0 4.8 %collective-permute-start.1 = (bf16[448,128]{1,0:T(8,128)(2,1)S(1)}, bf16[448,128]{1,0:T(8,128)(2,1)S(1)}, u32[]{:S(2)}, u32[]{:S(2)}) collective-permute-start(bf16[448,128]{1,0:T(8,128)(2,1)S(1)} %collective-permute-done.x_f), channel_id=1, source_target_pairs={{0,4},{4,8},{8,12},{12,14},{14,10},{10,6},{6,2},{2,0},{1,5},{5,9},... | collective-permute-start | bytes 344072 | tf_op jit(solution)/shard_map/ppermute | solution.py:93
  11.2 5.2 %collective-permute-start.6 = (bf16[448,128]{1,0:T(8,128)(2,1)S(1)}, bf16[448,128]{1,0:T(8,128)(2,1)S(1)}, u32[]{:S(2)}, u32[]{:S(2)}) collective-permute-start(bf16[448,128]{1,0:T(8,128)(2,1)S(1)} %collective-permute-done.5.x_b), channel_id=1, source_target_pairs={{4,0},{8,4},{12,8},{14,12},{10,14},{6,10},{2,6},{0,2},{5,1},{9,5},... | collective-permute-start | bytes 344072 | tf_op jit(solution)/shard_map/ppermute | solution.py:94
  12.8 5.4 %collective-permute-start.2 = (bf16[448,128]{1,0:T(8,128)(2,1)S(1)}, bf16[448,128]{1,0:T(8,128)(2,1)S(1)}, u32[]{:S(2)}, u32[]{:S(2)}) collective-permute-start(bf16[448,128]{1,0:T(8,128)(2,1)S(1)} %collective-permute-done.1.x_f), channel_id=1, source_target_pairs={{0,4},{4,8},{8,12},{12,14},{14,10},{10,6},{6,2},{2,0},{1,5},{5,9},... | collective-permute-start | bytes 344072 | tf_op jit(solution)/shard_map/ppermute | solution.py:93
  16.4 10.5 %collective-permute-start.7 = (bf16[224,128]{1,0:T(8,128)(2,1)S(1)}, bf16[224,128]{1,0:T(8,128)(2,1)S(1)}, u32[]{:S(2)}, u32[]{:S(2)}) collective-permute-start(bf16[224,128]{1,0:T(8,128)(2,1)S(1)} %slice.9), channel_id=1, source_target_pairs={{4,0},{8,4},{12,8},{14,12},{10,14},{6,10},{2,6},{0,2},{5,1},{9,5},... | collective-permute-start | bytes 172040 | tf_op jit(solution)/shard_map/ppermute | solution.py:102
  18.2 8.7 %collective-permute-start.3 = (bf16[224,128]{1,0:T(8,128)(2,1)S(1)}, bf16[224,128]{1,0:T(8,128)(2,1)S(1)}, u32[]{:S(2)}, u32[]{:S(2)}) collective-permute-start(bf16[224,128]{1,0:T(8,128)(2,1)S(1)} %slice.8), channel_id=1, source_target_pairs={{0,4},{4,8},{8,12},{12,14},{14,10},{10,6},{6,2},{2,0},{1,5},{5,9},... | collective-permute-start | bytes 172040 | tf_op jit(solution)/shard_map/ppermute | solution.py:101
  19.3 2.0 %copy-start = (bf16[3584,512]{1,0:T(8,128)(2,1)S(1)}, bf16[3584,512]{1,0:T(8,128)(2,1)}, u32[]{:S(2)}) copy-start(bf16[3584,512]{1,0:T(8,128)(2,1)} %param.7) | copy-start | bytes 11010052
  21.3 0.9 %copy-start.2 = (bf16[128,448]{0,1:T(8,128)(2,1)S(1)}, bf16[128,448]{0,1:T(8,128)(2,1)}, u32[]{:S(2)}) copy-start(bf16[128,448]{0,1:T(8,128)(2,1)} %param.6) | copy-start | bytes 344068
  22.2 2.0 %copy-start.1 = (bf16[3584,512]{1,0:T(8,128)(2,1)S(1)}, bf16[3584,512]{1,0:T(8,128)(2,1)}, u32[]{:S(2)}) copy-start(bf16[3584,512]{1,0:T(8,128)(2,1)} %param.7) | copy-start | bytes 11010052
  26.0 0.9 %copy-start.3 = (f32[512]{0:T(512)S(1)}, f32[512]{0:T(512)}, u32[]{:S(2)}) copy-start(f32[512]{0:T(512)} %param.8) | copy-start | bytes 6148
  26.0 0.9 %copy-start.4 = (f32[512]{0:T(512)S(1)}, f32[512]{0:T(512)}, u32[]{:S(2)}) copy-start(f32[512]{0:T(512)} %param.9) | copy-start | bytes 6148
  26.9 7.6 %copy-start.5 = (s32[8,4]{0,1:T(4,128)S(1)}, s32[8,4]{0,1:T(4,128)}, u32[]{:S(2)}) copy-start(s32[8,4]{0,1:T(4,128)} %param.10) | copy-start | bytes 388
  28.5 13.4 %all-to-all-start = ((bf16[8,16,512]{2,1,0:T(8,128)(2,1)}), bf16[8,16,512]{2,1,0:T(8,128)(2,1)S(1)}, u32[]{:S(2)}, u32[]{:S(2)}) async-start(bf16[8,16,512]{2,1,0:T(8,128)(2,1)} %bitcast.5), calls=%async_computation | async-start | bytes 262144 | tf_op jit(solution)/shard_map/all_to_all | solution.py:201
  54.4 2.2 %collective-permute-start.9 = (bf16[3,128,512]{2,1,0:T(8,128)(2,1)S(1)}, bf16[3,128,512]{2,1,0:T(8,128)(2,1)S(1)}, u32[]{:S(2)}, u32[]{:S(2)}) collective-permute-start(bf16[3,128,512]{2,1,0:T(8,128)(2,1)S(1)} %bitcast.17), channel_id=1, source_target_pairs={{0,1},{1,0},{2,3},{3,2},{4,5},{5,4},{6,7},{7,6},{8,9},{9,8},{10,11... | collective-permute-start | bytes 1179656 | tf_op jit(solution)/shard_map/ppermute | solution.py:204
  54.6 1.9 %collective-permute-start.8 = (bf16[128,512]{1,0:T(8,128)(2,1)}, bf16[128,512]{1,0:T(8,128)(2,1)S(1)}, u32[]{:S(2)}, u32[]{:S(2)}) collective-permute-start(bf16[128,512]{1,0:T(8,128)(2,1)} %shard_map.68.own), channel_id=1, source_target_pairs={{0,1},{1,0},{2,3},{3,2},{4,5},{5,4},{6,7},{7,6},{8,9},{9,8},{10,11... | collective-permute-start | bytes 393224 | tf_op jit(solution)/shard_map/ppermute | solution.py:200

commit v2 on v1

v2 whole, which is shorter than its diff:
```python
import functools

import jax
import jax.numpy as jnp
import numpy as np
from jax import lax
from jax.experimental import pallas as pl
from jax.experimental.pallas import tpu as pltpu
from jax.sharding import PartitionSpec as P

ramp_width = 0.25
ring_limit = 16
vmem_limit = 32 * 1024 * 1024

rows_by_rows = (((0,), (0,)), ((), ()))


def ring_order(n):
    return list(range(0, n, 2)) + list(range(1, n, 2))[::-1]


def activate(pre_acts, threshold):
    gate = jnp.clip((pre_acts - threshold) / ramp_width + 0.5, 0.0, 1.0)
    return (pre_acts * gate).astype(jnp.bfloat16)


def project(x, w):
    return lax.dot_general(x, w, rows_by_rows, preferred_element_type=jnp.float32)


def first_step(_, x, x_f, x_b, w, w_f, w_b, total):
    total[...] = project(x[...], w[0]) + project(x_f[...], w_f[0]) + project(x_b[...], w_b[0])


def middle_step(_, x_f, x_b, w_f, w_b, before, total):
    total[...] = before[...] + project(x_f[...], w_f[0]) + project(x_b[...], w_b[0])


def last_step(_, x_f, x_b, x_far, w_f, w_b, w_far, before, bias, threshold, acts):
    pre_acts = before[...] + project(x_f[...], w_f[0]) + project(x_b[...], w_b[0])
    pre_acts = pre_acts + project(x_far[...], w_far[0]) + bias[...]
    acts[...] = activate(pre_acts, threshold[...])


def whole(shape):
    return pl.BlockSpec(shape, lambda i, ids: (0,) * len(shape))


def step_call(kernel, ids, places, xs, weights, others, out):
    depth, width = weights.shape[1:]
    picks = [
        pl.BlockSpec((1, depth, width), functools.partial(lambda k, i, ids: (ids[k], 0, 0), k))
        for k in places
    ]
    rows = sum(x.shape[0] for x in xs)
    return pl.pallas_call(
        kernel,
        out_shape=out,
        grid_spec=pltpu.PrefetchScalarGridSpec(
            num_scalar_prefetch=1,
            grid=(1,),
            in_specs=[whole(x.shape) for x in xs] + picks + [whole(o.shape) for o in others],
            out_specs=whole(out.shape),
        ),
        compiler_params=pltpu.CompilerParams(vmem_limit_bytes=vmem_limit),
        cost_estimate=pl.CostEstimate(
            flops=2 * rows * xs[0].shape[1] * width,
            bytes_accessed=2 * rows * width + 8 * xs[0].shape[1] * width,
            transcendentals=0,
        ),
    )(ids, *xs, *([weights] * len(places)), *others)


class Ring:
    def __init__(self, n):
        order = ring_order(n)
        position = {b: i for i, b in enumerate(order)}
        self.n = n
        self.hops = n // 2 - 1
        self.forward = [(order[i], order[(i + 1) % n]) for i in range(n)]
        self.backward = [(d, s) for s, d in self.forward]
        self.across = [(order[i], order[(i + n // 2) % n]) for i in range(n)]
        self.origins = np.array(
            [[order[(position[b] - h) % n] for h in range(n)] for b in range(n)], np.int32
        )

    def ids(self):
        return jnp.asarray(self.origins)[lax.axis_index("lat")]

    def gather(self, x, arrived):
        ahead = lax.ppermute(x, "lat", self.forward)
        behind = lax.ppermute(x, "lat", self.backward)
        far = lax.ppermute(x, "lat", self.across)
        state = None
        for hop in range(1, self.hops):
            now_ahead, now_behind = ahead, behind
            ahead = lax.ppermute(ahead, "lat", self.forward)
            behind = lax.ppermute(behind, "lat", self.backward)
            state = arrived(hop, now_ahead, now_behind, state)
            if hop + 1 < self.hops:
                state, ahead, behind = lax.optimization_barrier((state, ahead, behind))
        return state, ahead, behind, far


def encode_on_ring(residual, enc_weight, enc_bias, threshold, ring, ids):
    tok_rows, depth = residual.shape
    width = enc_weight.shape[1]
    n = ring.n
    x = residual.T
    weights = enc_weight.reshape(n, depth, width)
    total_shape = jax.ShapeDtypeStruct((tok_rows, width), jnp.float32)

    def arrived(hop, ahead, behind, total):
        if hop == 1:
            places, xs, others = [0, 1, n - 1], [x, ahead, behind], []
        else:
            places, xs, others = [hop, n - hop], [ahead, behind], [total]
        kernel = first_step if hop == 1 else middle_step
        return step_call(kernel, ids, places, xs, weights, others, total_shape)

    total, ahead, behind, far = ring.gather(x, arrived)
    return step_call(
        last_step,
        ids,
        [ring.hops, n - ring.hops, n // 2],
        [ahead, behind, far],
        weights,
        [total, enc_bias.reshape(1, width), threshold.reshape(1, width)],
        jax.ShapeDtypeStruct((tok_rows, width), jnp.bfloat16),
    )


def encode_gathered(residual, enc_weight, enc_bias, threshold):
    pre_acts = (
        jnp.dot(
            lax.all_gather(residual, "lat", axis=1, tiled=True),
            enc_weight,
            preferred_element_type=jnp.float32,
        )
        + enc_bias
    )
    return activate(pre_acts, threshold)


def select(slices, partners):
    return jnp.take(slices, jnp.minimum(partners[:, 1:], slices.shape[0] - 1), axis=0)


def choose_kernel(picks, *refs):
    blocks, chosen = refs[:-1], refs[-1]
    for k in range(chosen.shape[0]):
        for i, block in enumerate(blocks):

            @pl.when(picks[k + 1] == i)
            def _():
                chosen[k] = block[...]


def choose(picks, blocks):
    out = (picks.shape[0] - 1,) + blocks[0].shape
    return pl.pallas_call(
        choose_kernel,
        out_shape=jax.ShapeDtypeStruct(out, blocks[0].dtype),
        grid_spec=pltpu.PrefetchScalarGridSpec(
            num_scalar_prefetch=1,
            grid=(1,),
            in_specs=[whole(b.shape) for b in blocks],
            out_specs=whole(out),
        ),
        compiler_params=pltpu.CompilerParams(vmem_limit_bytes=vmem_limit),
    )(picks, *blocks)


def gram_kernel(tok_scale, place, own, own_twin, got, got_twin, tiles):
    rows, width = tiles.shape[2:]
    columns = pl.ds(pl.multiple_of(place[0] * rows, rows), rows)
    k = pl.program_id(0)

    def tile_of(right, right_twin):
        tile = project(own[:, columns], right) + project(own_twin[:, columns], right_twin)
        tiles[0, 0] = (tile * tok_scale).astype(tiles.dtype)

    @pl.when(k == 0)
    def _():
        tile_of(own[...], own_twin[...])

    @pl.when((k > 0) & (place[k] != 0))
    def _():
        tile_of(got[k - 1], got_twin[k - 1])

    @pl.when((k > 0) & (place[k] == 0))
    def _():
        tiles[0, 0] = jnp.zeros((rows, width), tiles.dtype)


def gram(own, own_twin, got, got_twin, place, tok_scale, halves):
    tok_rows, width = own.shape
    slots = got.shape[0] + 1
    rows = width // halves
    return pl.pallas_call(
        functools.partial(gram_kernel, tok_scale),
        out_shape=jax.ShapeDtypeStruct((1, slots, rows, width), own.dtype),
        grid_spec=pltpu.PrefetchScalarGridSpec(
            num_scalar_prefetch=1,
            grid=(slots,),
            in_specs=[whole(a.shape) for a in (own, own_twin, got, got_twin)],
            out_specs=pl.BlockSpec((1, 1, rows, width), lambda i, place: (0, i, 0, 0)),
        ),
        compiler_params=pltpu.CompilerParams(vmem_limit_bytes=vmem_limit),
    )(place, own, own_twin, got, got_twin)


def body(residual, enc_weight, enc_bias, threshold, partners):
    n = lax.axis_size("lat")
    halves = lax.axis_size("tok")
    tok_rows = residual.shape[0]
    width = enc_weight.shape[1]
    slots = partners.shape[1]
    tok_scale = 1.0 / (tok_rows * halves)
    swap = [(i, 1 - i) for i in range(2)]
    row = lax.dynamic_index_in_dim(partners, lax.axis_index("lat"), 0, keepdims=False)
    place = jnp.where(
        jnp.arange(slots) == 0, lax.axis_index("tok"), (row < n).astype(jnp.int32)
    ).astype(jnp.int32)
    if n <= ring_limit:
        ring = Ring(n)
        ids = ring.ids()
        acts = encode_on_ring(residual, enc_weight, enc_bias, threshold, ring, ids)
        acts_twin = lax.ppermute(acts, "tok", swap)
        blocks = {0: acts}

        def arrived(hop, ahead, behind, state):
            blocks[hop], blocks[n - hop] = ahead, behind
            return acts_twin

        acts_twin, ahead, behind, far = ring.gather(acts, arrived)
        blocks[ring.hops], blocks[n - ring.hops], blocks[n // 2] = ahead, behind, far
        picks = jnp.sum(jnp.where(row[:, None] == ids[None, :], jnp.arange(n), 0), axis=1)
        got = choose(picks.astype(jnp.int32), [blocks[i] for i in range(n)])
    else:
        acts = encode_gathered(residual, enc_weight, enc_bias, threshold)
        acts_twin = lax.ppermute(acts, "tok", swap)
        slices = lax.all_to_all(acts.reshape(n, tok_rows // n, width), "lat", 0, 0)
        got = lax.all_to_all(select(slices, partners), "lat", 0, 0)
        got = got.transpose(1, 0, 2, 3).reshape(slots - 1, tok_rows, width)
    got_twin = lax.ppermute(got, "tok", swap)
    return gram(acts, acts_twin, got, got_twin, place, tok_scale, halves)


def solution(mesh):
    return jax.shard_map(
        body,
        mesh=mesh,
        in_specs=(P(("parts", "tok"), "lat"), P(None, "lat"), P("lat"), P("lat"), P()),
        out_specs=P(("parts", "lat"), None, "tok", None),
        check_vma=False,
    )
```

time: 60.3 us -> 47.8 us (0.79)
  blocking collectives: 11.8 us -> 0 us
  starting transfers between devices: 15.9 us -> 26.4 us
  waiting for transfers between devices: 18 us -> 10.9 us
  Pallas kernels: 8.57 us -> 6.2 us
  local copies, waits for them, and re-layouts: 5.01 us -> 3.83 us
    ppermute x8 -> x14, starting transfers between devices: 9.2 us -> 26.3 us  [the longest x2 12.2 us: gather(): far = lax.ppermute(x, 'lat', self.across)]
    all_to_all x1 -> x0, blocking collectives: 11.8 us -> none  [body(): got = lax.all_to_all(select(slices, partners), 'lat', 0, 0)]
    all_to_all x1 -> x0, waiting for transfers between devices: 7.26 us -> none  [body(): slices = lax.all_to_all(acts.reshape(n, tok_rows // n, width), 'lat', 0, 0)]
    all_to_all x1 -> x0, starting transfers between devices: 6.03 us -> none  [body(): slices = lax.all_to_all(acts.reshape(n, tok_rows // n, width), 'lat', 0, 0)]
    pallas_call x5 -> x3, Pallas kernels: 4.86 us -> 2.75 us  [step_call(): pl.pallas_call(kernel, out_shape=out, grid_spec=pltpu.PrefetchScalarGridS...]
    ppermute x1, waiting for transfers between devices: 0.01 us -> 1.69 us  [body(): got_twin = lax.ppermute(got, 'tok', swap)]
    ppermute x1, waiting for transfers between devices: 1.36 us -> 0.01 us  [body(): acts_twin = lax.ppermute(acts, 'tok', swap)]
    unnamed x13 -> x12, local copies, waits for them, and re-layouts: 4.29 us -> 2.96 us
  transfers between devices with their start and end apart: 11 -> 16, of which waited for: 6 -> 7; matrix products, arithmetic and copies ran while one was open for 2% -> 2% of each run, Pallas kernels for 6% -> 4%
where the time goes in v2:
time: 47.8 us; the launch traced here: 47.6 us
  starting transfers between devices  26.4 us (55%)
  waiting for transfers between devices  10.9 us (23%)
  Pallas kernels  6.2 us (13%)
  local copies, waits for them, and re-layouts  3.83 us (8%)
    ppermute x2, starting transfers between devices, gather(): far = lax.ppermute(x, 'lat', self.across)  12.2 us
    ppermute x4, starting transfers between devices, gather(): behind = lax.ppermute(behind, 'lat', self.backward)  6.37 us
    ppermute x2, starting transfers between devices, gather(): behind = lax.ppermute(x, 'lat', self.backward)  4.72 us
    ppermute x2, waiting for transfers between devices, gather(): far = lax.ppermute(x, 'lat', self.across)  3.09 us
    unnamed x12, local copies, waits for them, and re-layouts  2.96 us
    ppermute x2, waiting for transfers between devices, gather(): behind = lax.ppermute(x, 'lat', self.backward)  2.92 us
    ppermute x4, waiting for transfers between devices, gather(): ahead = lax.ppermute(ahead, 'lat', self.forward)  2.75 us
    pallas_call x3, Pallas kernels, step_call(): pl.pallas_call(kernel, out_shape=out, grid_spec=pltpu.PrefetchScalarGridS...  2.75 us
  transfers between devices with their start and end apart: 16, of which 7 were waited for; matrix products, arithmetic and copies ran while one was open for 2% of the time, Pallas kernels for 4%

profile of v2, /device:TPU:0, one launch (start us, length us, event | category | flops | bytes accessed | tf_op | source)
XLA Modules:
  0.0 47.6 jit_solution(6551854835859705304)
XLA Ops:
  0.0 0.0 copy-start
  0.0 2.9 %collective-permute-start.1 = (bf16[448,128]{1,0:T(8,128)(2,1)}, bf16[448,128]{1,0:T(8,128)(2,1)S(1)}, u32[]{:S(2)}, u32[]{:S(2)}) collective-permute-start(bf16[448,128]{1,0:T(8,128)(2,1)} %bitcast.14), channel_id=1, source_target_pairs={{4,0},{8,4},{12,8},{14,12},{10,14},{6,10},{2,6},{0,2},{5,1},{9,5},... | collective-permute-start | bytes 344072 | tf_op jit(solution)/shard_map/ppermute | solution.py:92
  2.9 0.1 collective-permute-start
  3.1 4.9 %collective-permute-start.6 = (bf16[448,128]{1,0:T(8,128)(2,1)}, bf16[448,128]{1,0:T(8,128)(2,1)S(1)}, u32[]{:S(2)}, u32[]{:S(2)}) collective-permute-start(bf16[448,128]{1,0:T(8,128)(2,1)} %bitcast.16), channel_id=1, source_target_pairs={{0,14},{4,10},{8,6},{12,2},{14,0},{10,4},{6,8},{2,12},{1,15},{5,11... | collective-permute-start | bytes 344072 | tf_op jit(solution)/shard_map/ppermute | solution.py:93
  8.0 0.0 collective-permute-done.1.x_b
  8.0 0.5 %collective-permute-start.3 = (bf16[448,128]{1,0:T(8,128)(2,1)S(1)}, bf16[448,128]{1,0:T(8,128)(2,1)S(1)}, u32[]{:S(2)}, u32[]{:S(2)}) collective-permute-start(bf16[448,128]{1,0:T(8,128)(2,1)S(1)} %collective-permute-done.1.x_b), channel_id=1, source_target_pairs={{4,0},{8,4},{12,8},{14,12},{10,14},{6,10},{2,6},{0,2},{5,1},{9,5},... | collective-permute-start | bytes 344072 | tf_op jit(solution)/shard_map/ppermute | solution.py:98
  8.5 0.0 collective-permute-done.x_f
  8.5 1.5 %collective-permute-start.2 = (bf16[448,128]{1,0:T(8,128)(2,1)S(1)}, bf16[448,128]{1,0:T(8,128)(2,1)S(1)}, u32[]{:S(2)}, u32[]{:S(2)}) collective-permute-start(bf16[448,128]{1,0:T(8,128)(2,1)S(1)} %collective-permute-done.x_f), channel_id=1, source_target_pairs={{0,4},{4,8},{8,12},{12,14},{14,10},{10,6},{6,2},{2,0},{1,5},{5,9},... | collective-permute-start | bytes 344072 | tf_op jit(solution)/shard_map/ppermute | solution.py:97
  10.0 0.7 %dynamic-slice_bitcast_fusion._ = s32[8]{0:T(128)S(1)} fusion(s32[8,8]{1,0:T(8,128)} %constant.20.clone, s32[]{:T(128)S(6)} %select_n.13), kind=kLoop, calls=%fused_computation.4 | loop fusion | bytes 68 | tf_op jit(solution)/shard_map/squeeze | solution.py:88
  10.7 2.0 %copy-done.1 = bf16[3584,512]{1,0:T(8,128)(2,1)S(1)} copy-done((bf16[3584,512]{1,0:T(8,128)(2,1)S(1)}, bf16[3584,512]{1,0:T(8,128)(2,1)}, u32[]{:S(2)}) %copy-start.1) | copy-done | bytes 3670040
  12.8 0.9 %copy-done.3 = bf16[128,448]{0,1:T(8,128)(2,1)S(1)} copy-done((bf16[128,448]{0,1:T(8,128)(2,1)S(1)}, bf16[128,448]{0,1:T(8,128)(2,1)}, u32[]{:S(2)}) %copy-start.3) | copy-done | bytes 114712
  13.7 0.9 %shard_map.64.before = f32[128,512]{1,0:T(8,128)S(1)} custom-call(s32[8]{0:T(128)S(1)} %dynamic-slice_bitcast_fusion._, bf16[448,128]{1,0:T(8,128)(2,1)S(1)} %bitcast.17, bf16[448,128]{1,0:T(8,128)(2,1)S(1)} %collective-permute-done.x_f, bf16[448,128]{1,0:T(8,128)(2,1)S(1)} %collective-permute-done.1.x_b, bf16[8,448,512]{2,1,0:T(8,128)(2,1)S(1)} %bitcast.6, ...), custom_call_target="tpu_custom_call" | custom-call | flops 176160768 | bytes 1900544 | tf_op jit(solution)/shard_map/pallas_call | solution.py:56
  14.6 0.0 copy-start.4
  14.6 0.0 copy-start.5
  14.6 0.0 collective-permute-done.3.x_b
  14.6 0.0 collective-permute-done.2.x_f
  14.6 0.9 %collective-permute-start.4 = (bf16[448,128]{1,0:T(8,128)(2,1)S(1)}, bf16[448,128]{1,0:T(8,128)(2,1)S(1)}, u32[]{:S(2)}, u32[]{:S(2)}) collective-permute-start(bf16[448,128]{1,0:T(8,128)(2,1)S(1)} %collective-permute-done.2.x_f), channel_id=1, source_target_pairs={{0,4},{4,8},{8,12},{12,14},{14,10},{10,6},{6,2},{2,0},{1,5},{5,9},... | collective-permute-start | bytes 344072 | tf_op jit(solution)/shard_map/ppermute | solution.py:97
  15.5 1.7 %collective-permute-start.5 = (bf16[448,128]{1,0:T(8,128)(2,1)S(1)}, bf16[448,128]{1,0:T(8,128)(2,1)S(1)}, u32[]{:S(2)}, u32[]{:S(2)}) collective-permute-start(bf16[448,128]{1,0:T(8,128)(2,1)S(1)} %collective-permute-done.3.x_b), channel_id=1, source_target_pairs={{4,0},{8,4},{12,8},{14,12},{10,14},{6,10},{2,6},{0,2},{5,1},{9,5},... | collective-permute-start | bytes 344072 | tf_op jit(solution)/shard_map/ppermute | solution.py:98
  17.2 0.0 copy-done.2
  17.2 0.9 %shard_map.65.before = f32[128,512]{1,0:T(8,128)S(1)} custom-call(s32[8]{0:T(128)S(1)} %dynamic-slice_bitcast_fusion._, bf16[448,128]{1,0:T(8,128)(2,1)S(1)} %collective-permute-done.2.x_f, bf16[448,128]{1,0:T(8,128)(2,1)S(1)} %collective-permute-done.3.x_b, bf16[8,448,512]{2,1,0:T(8,128)(2,1)S(1)} %bitcast.9, bf16[8,448,512]{2,1,0:T(8,128)(2,1)S(1)} %bitcast.10, ...), custom_call_target="tpu_custom_call" | custom-call | flops 117440512 | bytes 1441792 | tf_op jit(solution)/shard_map/pallas_call | solution.py:56
  18.1 0.0 collective-permute-done.6.x_far
  18.1 1.9 %collective-permute-done.4.x_f = bf16[448,128]{1,0:T(8,128)(2,1)S(1)} collective-permute-done((bf16[448,128]{1,0:T(8,128)(2,1)S(1)}, bf16[448,128]{1,0:T(8,128)(2,1)S(1)}, u32[]{:S(2)}, u32[]{:S(2)}) %collective-permute-start.4) | collective-permute-done | bytes 114720 | tf_op jit(solution)/shard_map/ppermute | solution.py:97
  20.0 0.3 collective-permute-done.5.x_b
  20.3 0.0 copy-done.4
  20.3 0.0 copy-done.5
  20.3 1.0 %shard_map.66.refs_0_.own = bf16[128,512]{1,0:T(8,128)(2,1)S(1)} custom-call(s32[8]{0:T(128)S(1)} %dynamic-slice_bitcast_fusion._, bf16[448,128]{1,0:T(8,128)(2,1)S(1)} %collective-permute-done.4.x_f, bf16[448,128]{1,0:T(8,128)(2,1)S(1)} %collective-permute-done.5.x_b, bf16[448,128]{1,0:T(8,128)(2,1)S(1)} %collective-permute-done.6.x_far, ...), custom_call_target="tpu_custom_call" | custom-call | flops 176160768 | bytes 1900544 | tf_op jit(solution)/shard_map/pallas_call | solution.py:56
  21.3 1.8 %collective-permute-start.10 = (bf16[128,512]{1,0:T(8,128)(2,1)S(1)}, bf16[128,512]{1,0:T(8,128)(2,1)S(1)}, u32[]{:S(2)}, u32[]{:S(2)}) collective-permute-start(bf16[128,512]{1,0:T(8,128)(2,1)S(1)} %shard_map.66.refs_0_.own), channel_id=1, source_target_pairs={{4,0},{8,4},{12,8},{14,12},{10,14},{6,10},{2,6},{0,2},{5,1},{9,5},... | collective-permute-start | bytes 393224 | tf_op jit(solution)/shard_map/ppermute | solution.py:92
  23.1 0.3 collective-permute-start.8
  23.4 0.0 collective-permute-start.7
  23.4 2.9 %collective-permute-done.10.refs_7_ = bf16[128,512]{1,0:T(8,128)(2,1)S(1)} collective-permute-done((bf16[128,512]{1,0:T(8,128)(2,1)S(1)}, bf16[128,512]{1,0:T(8,128)(2,1)S(1)}, u32[]{:S(2)}, u32[]{:S(2)}) %collective-permute-start.10) | collective-permute-done | bytes 131104 | tf_op jit(solution)/shard_map/ppermute | solution.py:92
  26.3 1.7 %collective-permute-start.11 = (bf16[128,512]{1,0:T(8,128)(2,1)S(1)}, bf16[128,512]{1,0:T(8,128)(2,1)S(1)}, u32[]{:S(2)}, u32[]{:S(2)}) collective-permute-start(bf16[128,512]{1,0:T(8,128)(2,1)S(1)} %collective-permute-done.10.refs_7_), channel_id=1, source_target_pairs={{4,0},{8,4},{12,8},{14,12},{10,14},{6,10},{2,6},{0,2},{5,1},{9,5},... | collective-permute-start | bytes 393224 | tf_op jit(solution)/shard_map/ppermute | solution.py:98
  28.0 0.1 collective-permute-done.8.refs_1_
  28.1 0.2 collective-permute-start.9
  28.3 7.2 %collective-permute-start.13 = (bf16[128,512]{1,0:T(8,128)(2,1)S(1)}, bf16[128,512]{1,0:T(8,128)(2,1)S(1)}, u32[]{:S(2)}, u32[]{:S(2)}) collective-permute-start(bf16[128,512]{1,0:T(8,128)(2,1)S(1)} %shard_map.66.refs_0_.own), channel_id=1, source_target_pairs={{0,14},{4,10},{8,6},{12,2},{14,0},{10,4},{6,8},{2,12},{1,15},{5,11... | collective-permute-start | bytes 393224 | tf_op jit(solution)/shard_map/ppermute | solution.py:93
  35.6 0.0 collective-permute-done.7.own_twin
  35.6 0.0 collective-permute-done.11.refs_6_
  35.6 0.0 collective-permute-done.9.refs_2_
  35.6 0.1 collective-permute-start.12
  35.7 2.4 %collective-permute-start.14 = (bf16[128,512]{1,0:T(8,128)(2,1)S(1)}, bf16[128,512]{1,0:T(8,128)(2,1)S(1)}, u32[]{:S(2)}, u32[]{:S(2)}) collective-permute-start(bf16[128,512]{1,0:T(8,128)(2,1)S(1)} %collective-permute-done.11.refs_6_), channel_id=1, source_target_pairs={{4,0},{8,4},{12,8},{14,12},{10,14},{6,10},{2,6},{0,2},{5,1},{9,5},... | collective-permute-start | bytes 393224 | tf_op jit(solution)/shard_map/ppermute | solution.py:98
  38.1 0.2 dynamic-slice_reduce_fusion
  38.2 0.2 select_reduce_fusion.picks
  38.4 3.1 %collective-permute-done.13.refs_4_ = bf16[128,512]{1,0:T(8,128)(2,1)S(1)} collective-permute-done((bf16[128,512]{1,0:T(8,128)(2,1)S(1)}, bf16[128,512]{1,0:T(8,128)(2,1)S(1)}, u32[]{:S(2)}, u32[]{:S(2)}) %collective-permute-start.13) | collective-permute-done | bytes 131104 | tf_op jit(solution)/shard_map/ppermute | solution.py:93
  41.5 0.9 %collective-permute-done.12.refs_3_ = bf16[128,512]{1,0:T(8,128)(2,1)S(1)} collective-permute-done((bf16[128,512]{1,0:T(8,128)(2,1)S(1)}, bf16[128,512]{1,0:T(8,128)(2,1)S(1)}, u32[]{:S(2)}, u32[]{:S(2)}) %collective-permute-start.12) | collective-permute-done | bytes 131104 | tf_op jit(solution)/shard_map/ppermute | solution.py:97
  42.4 0.0 collective-permute-done.14.refs_5_
  42.4 0.7 %shard_map.67.got = bf16[3,128,512]{2,1,0:T(8,128)(2,1)S(1)} custom-call(s32[4]{0:T(128)S(1)} %select_reduce_fusion.picks, bf16[128,512]{1,0:T(8,128)(2,1)S(1)} %shard_map.66.refs_0_.own, bf16[128,512]{1,0:T(8,128)(2,1)S(1)} %collective-permute-done.8.refs_1_, bf16[128,512]{1,0:T(8,128)(2,1)S(1)} %collective-permute-done.9.refs_2_, ...), custom_call_target="tpu_custom_call" | custom-call | tf_op jit(solution)/shard_map/pallas_call | solution.py:161
  43.1 0.1 collective-permute-start.15
  43.2 1.7 %collective-permute-done.15.got_twin = bf16[3,128,512]{2,1,0:T(8,128)(2,1)S(1)} collective-permute-done((bf16[3,128,512]{2,1,0:T(8,128)(2,1)S(1)}, bf16[3,128,512]{2,1,0:T(8,128)(2,1)S(1)}, u32[]{:S(2)}, u32[]{:S(2)}) %collective-permute-start.15) | collective-permute-done | bytes 393248 | tf_op jit(solution)/shard_map/ppermute | solution.py:246
  44.9 2.7 %shard_map.68 = bf16[1,4,256,512]{3,2,1,0:T(8,128)(2,1)} custom-call(s32[4]{0:T(128)S(1)} %compare_select_fusion.place, bf16[128,512]{1,0:T(8,128)(2,1)S(1)} %shard_map.66.refs_0_.own, bf16[128,512]{1,0:T(8,128)(2,1)S(1)} %collective-permute-done.7.own_twin, bf16[3,128,512]{2,1,0:T(8,128)(2,1)S(1)} %shard_map.67.got, ...), custom_call_target="tpu_custom_call" | custom-call | tf_op jit(solution)/shard_map/pallas_call | solution.py:200
  (5 shorter events, 0.0 us)
Async XLA Ops:
  0.0 38.1 %copy-start = (s32[8,4]{0,1:T(4,128)S(1)}, s32[8,4]{0,1:T(4,128)}, u32[]{:S(2)}) copy-start(s32[8,4]{0,1:T(4,128)} %param.10) | copy-start | bytes 388
  0.0 8.0 %collective-permute-start.1 = (bf16[448,128]{1,0:T(8,128)(2,1)}, bf16[448,128]{1,0:T(8,128)(2,1)S(1)}, u32[]{:S(2)}, u32[]{:S(2)}) collective-permute-start(bf16[448,128]{1,0:T(8,128)(2,1)} %bitcast.14), channel_id=1, source_target_pairs={{4,0},{8,4},{12,8},{14,12},{10,14},{6,10},{2,6},{0,2},{5,1},{9,5},... | collective-permute-start | bytes 344072 | tf_op jit(solution)/shard_map/ppermute | solution.py:92
  2.9 5.6 %collective-permute-start = (bf16[448,128]{1,0:T(8,128)(2,1)}, bf16[448,128]{1,0:T(8,128)(2,1)S(1)}, u32[]{:S(2)}, u32[]{:S(2)}) collective-permute-start(bf16[448,128]{1,0:T(8,128)(2,1)} %bitcast.15), channel_id=1, source_target_pairs={{0,4},{4,8},{8,12},{12,14},{14,10},{10,6},{6,2},{2,0},{1,5},{5,9},... | collective-permute-start | bytes 344072 | tf_op jit(solution)/shard_map/ppermute | solution.py:91
  3.1 15.0 %collective-permute-start.6 = (bf16[448,128]{1,0:T(8,128)(2,1)}, bf16[448,128]{1,0:T(8,128)(2,1)S(1)}, u32[]{:S(2)}, u32[]{:S(2)}) collective-permute-start(bf16[448,128]{1,0:T(8,128)(2,1)} %bitcast.16), channel_id=1, source_target_pairs={{0,14},{4,10},{8,6},{12,2},{14,0},{10,4},{6,8},{2,12},{1,15},{5,11... | collective-permute-start | bytes 344072 | tf_op jit(solution)/shard_map/ppermute | solution.py:93
  8.0 6.6 %collective-permute-start.3 = (bf16[448,128]{1,0:T(8,128)(2,1)S(1)}, bf16[448,128]{1,0:T(8,128)(2,1)S(1)}, u32[]{:S(2)}, u32[]{:S(2)}) collective-permute-start(bf16[448,128]{1,0:T(8,128)(2,1)S(1)} %collective-permute-done.1.x_b), channel_id=1, source_target_pairs={{4,0},{8,4},{12,8},{14,12},{10,14},{6,10},{2,6},{0,2},{5,1},{9,5},... | collective-permute-start | bytes 344072 | tf_op jit(solution)/shard_map/ppermute | solution.py:98
  8.5 6.1 %collective-permute-start.2 = (bf16[448,128]{1,0:T(8,128)(2,1)S(1)}, bf16[448,128]{1,0:T(8,128)(2,1)S(1)}, u32[]{:S(2)}, u32[]{:S(2)}) collective-permute-start(bf16[448,128]{1,0:T(8,128)(2,1)S(1)} %collective-permute-done.x_f), channel_id=1, source_target_pairs={{0,4},{4,8},{8,12},{12,14},{14,10},{10,6},{6,2},{2,0},{1,5},{5,9},... | collective-permute-start | bytes 344072 | tf_op jit(solution)/shard_map/ppermute | solution.py:97
  10.7 2.0 %copy-start.1 = (bf16[3584,512]{1,0:T(8,128)(2,1)S(1)}, bf16[3584,512]{1,0:T(8,128)(2,1)}, u32[]{:S(2)}) copy-start(bf16[3584,512]{1,0:T(8,128)(2,1)} %param.7) | copy-start | bytes 11010052
  12.8 0.9 %copy-start.3 = (bf16[128,448]{0,1:T(8,128)(2,1)S(1)}, bf16[128,448]{0,1:T(8,128)(2,1)}, u32[]{:S(2)}) copy-start(bf16[128,448]{0,1:T(8,128)(2,1)} %param.6) | copy-start | bytes 344068
  13.7 3.6 %copy-start.2 = (bf16[3584,512]{1,0:T(8,128)(2,1)S(1)}, bf16[3584,512]{1,0:T(8,128)(2,1)}, u32[]{:S(2)}) copy-start(bf16[3584,512]{1,0:T(8,128)(2,1)} %param.7) | copy-start | bytes 11010052
  14.6 5.7 %copy-start.4 = (f32[512]{0:T(512)S(1)}, f32[512]{0:T(512)}, u32[]{:S(2)}) copy-start(f32[512]{0:T(512)} %param.8) | copy-start | bytes 6148
  14.6 5.7 %copy-start.5 = (f32[512]{0:T(512)S(1)}, f32[512]{0:T(512)}, u32[]{:S(2)}) copy-start(f32[512]{0:T(512)} %param.9) | copy-start | bytes 6148
  14.6 5.3 %collective-permute-start.4 = (bf16[448,128]{1,0:T(8,128)(2,1)S(1)}, bf16[448,128]{1,0:T(8,128)(2,1)S(1)}, u32[]{:S(2)}, u32[]{:S(2)}) collective-permute-start(bf16[448,128]{1,0:T(8,128)(2,1)S(1)} %collective-permute-done.2.x_f), channel_id=1, source_target_pairs={{0,4},{4,8},{8,12},{12,14},{14,10},{10,6},{6,2},{2,0},{1,5},{5,9},... | collective-permute-start | bytes 344072 | tf_op jit(solution)/shard_map/ppermute | solution.py:97
  15.5 4.8 %collective-permute-start.5 = (bf16[448,128]{1,0:T(8,128)(2,1)S(1)}, bf16[448,128]{1,0:T(8,128)(2,1)S(1)}, u32[]{:S(2)}, u32[]{:S(2)}) collective-permute-start(bf16[448,128]{1,0:T(8,128)(2,1)S(1)} %collective-permute-done.3.x_b), channel_id=1, source_target_pairs={{4,0},{8,4},{12,8},{14,12},{10,14},{6,10},{2,6},{0,2},{5,1},{9,5},... | collective-permute-start | bytes 344072 | tf_op jit(solution)/shard_map/ppermute | solution.py:98
  21.3 5.0 %collective-permute-start.10 = (bf16[128,512]{1,0:T(8,128)(2,1)S(1)}, bf16[128,512]{1,0:T(8,128)(2,1)S(1)}, u32[]{:S(2)}, u32[]{:S(2)}) collective-permute-start(bf16[128,512]{1,0:T(8,128)(2,1)S(1)} %shard_map.66.refs_0_.own), channel_id=1, source_target_pairs={{4,0},{8,4},{12,8},{14,12},{10,14},{6,10},{2,6},{0,2},{5,1},{9,5},... | collective-permute-start | bytes 393224 | tf_op jit(solution)/shard_map/ppermute | solution.py:92
  23.1 5.1 %collective-permute-start.8 = (bf16[128,512]{1,0:T(8,128)(2,1)S(1)}, bf16[128,512]{1,0:T(8,128)(2,1)S(1)}, u32[]{:S(2)}, u32[]{:S(2)}) collective-permute-start(bf16[128,512]{1,0:T(8,128)(2,1)S(1)} %shard_map.66.refs_0_.own), channel_id=1, source_target_pairs={{0,4},{4,8},{8,12},{12,14},{14,10},{10,6},{6,2},{2,0},{1,5},{5,9},... | collective-permute-start | bytes 393224 | tf_op jit(solution)/shard_map/ppermute | solution.py:91
  23.4 12.2 %collective-permute-start.7 = (bf16[128,512]{1,0:T(8,128)(2,1)S(1)}, bf16[128,512]{1,0:T(8,128)(2,1)S(1)}, u32[]{:S(2)}, u32[]{:S(2)}) collective-permute-start(bf16[128,512]{1,0:T(8,128)(2,1)S(1)} %shard_map.66.refs_0_.own), channel_id=1, source_target_pairs={{0,1},{1,0},{2,3},{3,2},{4,5},{5,4},{6,7},{7,6},{8,9},{9,8},{10,11... | collective-permute-start | bytes 393224 | tf_op jit(solution)/shard_map/ppermute | solution.py:229
  26.3 9.3 %collective-permute-start.11 = (bf16[128,512]{1,0:T(8,128)(2,1)S(1)}, bf16[128,512]{1,0:T(8,128)(2,1)S(1)}, u32[]{:S(2)}, u32[]{:S(2)}) collective-permute-start(bf16[128,512]{1,0:T(8,128)(2,1)S(1)} %collective-permute-done.10.refs_7_), channel_id=1, source_target_pairs={{4,0},{8,4},{12,8},{14,12},{10,14},{6,10},{2,6},{0,2},{5,1},{9,5},... | collective-permute-start | bytes 393224 | tf_op jit(solution)/shard_map/ppermute | solution.py:98
  28.1 7.5 %collective-permute-start.9 = (bf16[128,512]{1,0:T(8,128)(2,1)S(1)}, bf16[128,512]{1,0:T(8,128)(2,1)S(1)}, u32[]{:S(2)}, u32[]{:S(2)}) collective-permute-start(bf16[128,512]{1,0:T(8,128)(2,1)S(1)} %collective-permute-done.8.refs_1_), channel_id=1, source_target_pairs={{0,4},{4,8},{8,12},{12,14},{14,10},{10,6},{6,2},{2,0},{1,5},{5,9},... | collective-permute-start | bytes 393224 | tf_op jit(solution)/shard_map/ppermute | solution.py:97
  28.3 13.2 %collective-permute-start.13 = (bf16[128,512]{1,0:T(8,128)(2,1)S(1)}, bf16[128,512]{1,0:T(8,128)(2,1)S(1)}, u32[]{:S(2)}, u32[]{:S(2)}) collective-permute-start(bf16[128,512]{1,0:T(8,128)(2,1)S(1)} %shard_map.66.refs_0_.own), channel_id=1, source_target_pairs={{0,14},{4,10},{8,6},{12,2},{14,0},{10,4},{6,8},{2,12},{1,15},{5,11... | collective-permute-start | bytes 393224 | tf_op jit(solution)/shard_map/ppermute | solution.py:93
  35.6 6.8 %collective-permute-start.12 = (bf16[128,512]{1,0:T(8,128)(2,1)S(1)}, bf16[128,512]{1,0:T(8,128)(2,1)S(1)}, u32[]{:S(2)}, u32[]{:S(2)}) collective-permute-start(bf16[128,512]{1,0:T(8,128)(2,1)S(1)} %collective-permute-done.9.refs_2_), channel_id=1, source_target_pairs={{0,4},{4,8},{8,12},{12,14},{14,10},{10,6},{6,2},{2,0},{1,5},{5,9},... | collective-permute-start | bytes 393224 | tf_op jit(solution)/shard_map/ppermute | solution.py:97
  35.7 6.7 %collective-permute-start.14 = (bf16[128,512]{1,0:T(8,128)(2,1)S(1)}, bf16[128,512]{1,0:T(8,128)(2,1)S(1)}, u32[]{:S(2)}, u32[]{:S(2)}) collective-permute-start(bf16[128,512]{1,0:T(8,128)(2,1)S(1)} %collective-permute-done.11.refs_6_), channel_id=1, source_target_pairs={{4,0},{8,4},{12,8},{14,12},{10,14},{6,10},{2,6},{0,2},{5,1},{9,5},... | collective-permute-start | bytes 393224 | tf_op jit(solution)/shard_map/ppermute | solution.py:98
  43.1 1.8 %collective-permute-start.15 = (bf16[3,128,512]{2,1,0:T(8,128)(2,1)S(1)}, bf16[3,128,512]{2,1,0:T(8,128)(2,1)S(1)}, u32[]{:S(2)}, u32[]{:S(2)}) collective-permute-start(bf16[3,128,512]{2,1,0:T(8,128)(2,1)S(1)} %shard_map.67.got), channel_id=1, source_target_pairs={{0,1},{1,0},{2,3},{3,2},{4,5},{5,4},{6,7},{7,6},{8,9},{9,8},{10,11... | collective-permute-start | bytes 1179656 | tf_op jit(solution)/shard_map/ppermute | solution.py:246

commit v3 on v0

v3 whole, which is shorter than its diff:
```python
import functools

import jax
import jax.numpy as jnp
from jax import lax
from jax.experimental import pallas as pl
from jax.experimental.pallas import tpu as pltpu
from jax.sharding import PartitionSpec as P

ramp_width = 0.25
ring_limit = 16

in_vmem = pl.BlockSpec(memory_space=pltpu.VMEM)
in_smem = pl.BlockSpec(memory_space=pltpu.SMEM)
in_hbm = pl.BlockSpec(memory_space=pltpu.HBM)
params = pltpu.CompilerParams(vmem_limit_bytes=24 * 1024 * 1024)

rows_by_rows = (((0,), (0,)), ((), ()))


def place_on_ring(block, n):
    half = block // 2
    return half + (block % 2) * (n - 1 - 2 * half)


def block_at(place, n):
    up = 2 * place
    if isinstance(place, int):
        return up if place < n // 2 else 2 * n - 1 - up
    return jnp.where(place < n // 2, up, 2 * n - 1 - up)


def origin(hop, n):
    me = place_on_ring(lax.axis_index("lat"), n)
    return block_at(lax.rem(me + n - hop, n), n)


def activate(pre_acts, threshold):
    gate = jnp.clip((pre_acts - threshold) / ramp_width + 0.5, 0.0, 1.0)
    return (pre_acts * gate).astype(jnp.bfloat16)


def project(x, w):
    return lax.dot_general(x, w, rows_by_rows, preferred_element_type=jnp.float32)


def first_step(x_f, x_b, weights, total):
    n = weights.shape[0]
    total[...] = project(x_f[...], weights[origin(1, n)]) + project(x_b[...], weights[origin(-1, n)])


def middle_step(hops, x, x_f, x_b, before, weights, total):
    n = weights.shape[0]
    total[...] = before[...]
    for hop, arrived in zip(hops, (x_f, x_b, x)):
        total[...] += project(arrived[...], weights[origin(hop, n)])


def last_step(hops, x_f, x_b, x_far, before, weights, bias, threshold, acts):
    n = weights.shape[0]
    pre_acts = before[...] + bias[...]
    for hop, arrived in zip(hops, (x_f, x_b, x_far)):
        pre_acts = pre_acts + project(arrived[...], weights[origin(hop, n)])
    acts[...] = activate(pre_acts, threshold[...])


def cost(rows, depth, width, blocks):
    return pl.CostEstimate(
        flops=2 * rows * depth * width * blocks,
        bytes_accessed=2 * depth * (rows + width) * blocks + 8 * rows * width,
        transcendentals=0,
    )


class Ring:
    def __init__(self, n):
        walk = [block_at(i, n) for i in range(n)]
        self.n = n
        self.hops = n // 2 - 1
        self.forward = [(walk[i], walk[(i + 1) % n]) for i in range(n)]
        self.backward = [(d, s) for s, d in self.forward]
        self.across = [(walk[i], walk[(i + n // 2) % n]) for i in range(n)]

    def gather(self, x, arrived):
        ahead = lax.ppermute(x, "lat", self.forward)
        behind = lax.ppermute(x, "lat", self.backward)
        far = lax.ppermute(x, "lat", self.across)
        state = None
        for hop in range(1, self.hops):
            now_ahead, now_behind = ahead, behind
            ahead = lax.ppermute(ahead, "lat", self.forward)
            behind = lax.ppermute(behind, "lat", self.backward)
            state = arrived(hop, now_ahead, now_behind, state)
            if hop + 1 < self.hops:
                state, ahead, behind, far = lax.optimization_barrier(
                    (state, ahead, behind, far)
                )
        return state, ahead, behind, far


def encode_on_ring(residual, enc_weight, enc_bias, threshold, ring):
    tok_rows, depth = residual.shape
    width = enc_weight.shape[1]
    n = ring.n
    x = residual.T
    weights = enc_weight.reshape(n, depth, width)
    total_shape = jax.ShapeDtypeStruct((tok_rows, width), jnp.float32)

    def arrived(hop, ahead, behind, total):
        if hop == 1:
            kernel, operands = first_step, (ahead, behind, weights)
        elif hop == 2:
            kernel = functools.partial(middle_step, (2, -2, 0))
            operands = (x, ahead, behind, total, weights)
        else:
            kernel = functools.partial(middle_step, (hop, -hop))
            operands = (x, ahead, behind, total, weights)
        return pl.pallas_call(
            kernel,
            out_shape=total_shape,
            in_specs=[in_vmem] * len(operands),
            out_specs=in_vmem,
            compiler_params=params,
            cost_estimate=cost(tok_rows, depth, width, 3),
        )(*operands)

    total, ahead, behind, far = ring.gather(x, arrived)
    return pl.pallas_call(
        functools.partial(last_step, (ring.hops, -ring.hops, n // 2)),
        out_shape=jax.ShapeDtypeStruct((tok_rows, width), jnp.bfloat16),
        in_specs=[in_vmem] * 7,
        out_specs=in_vmem,
        compiler_params=params,
        cost_estimate=cost(tok_rows, depth, width, 3),
    )(
        ahead,
        behind,
        far,
        total,
        weights,
        enc_bias.reshape(1, width),
        threshold.reshape(1, width),
    )


def encode_gathered(residual, enc_weight, enc_bias, threshold):
    pre_acts = (
        jnp.dot(
            lax.all_gather(residual, "lat", axis=1, tiled=True),
            enc_weight,
            preferred_element_type=jnp.float32,
        )
        + enc_bias
    )
    return activate(pre_acts, threshold)


def choose_kernel(partners, *refs):
    blocks, chosen = refs[:-1], refs[-1]
    n = len(blocks)
    me = lax.axis_index("lat")
    for k in range(chosen.shape[0]):
        listed = partners[k + 1, me]
        hop = lax.rem(place_on_ring(me, n) + n - place_on_ring(jnp.minimum(listed, n - 1), n), n)
        for i, block in enumerate(blocks):

            @pl.when(hop == i)
            def _():
                chosen[k] = block[...]


def choose(partners, blocks):
    return pl.pallas_call(
        choose_kernel,
        out_shape=jax.ShapeDtypeStruct((partners.shape[0] - 1,) + blocks[0].shape, blocks[0].dtype),
        in_specs=[in_smem] + [in_vmem] * len(blocks),
        out_specs=in_vmem,
        compiler_params=params,
    )(partners, *blocks)


def gram_kernel(tok_scale, n, partners, own, own_twin, got, got_twin, out, tiles, sems):
    slots, rows, width = tiles.shape
    me = lax.axis_index("lat")
    columns = pl.ds(pl.multiple_of(lax.axis_index("tok") * rows, rows), rows)
    left = jnp.concatenate([own[:, columns], own_twin[:, columns]], axis=0)

    def tile_of(right, right_twin):
        tile = project(left, jnp.concatenate([right, right_twin], axis=0))
        return (tile * tok_scale).astype(tiles.dtype)

    copies = [pltpu.make_async_copy(tiles.at[k], out.at[0, k], sems.at[k]) for k in range(slots)]
    tiles[0] = tile_of(own[...], own_twin[...])
    copies[0].start()
    for k in range(1, slots):
        live = partners[k, me] < n

        @pl.when(live)
        def _():
            tiles[k] = tile_of(got[k - 1], got_twin[k - 1])

        @pl.when(jnp.logical_not(live))
        def _():
            tiles[k] = jnp.zeros((rows, width), tiles.dtype)

        copies[k].start()
    for copy in copies:
        copy.wait()


def gram(partners, own, own_twin, got, got_twin, tok_scale, halves, n):
    tok_rows, width = own.shape
    slots = partners.shape[0]
    rows = width // halves
    return pl.pallas_call(
        functools.partial(gram_kernel, tok_scale, n),
        out_shape=jax.ShapeDtypeStruct((1, slots, rows, width), own.dtype),
        in_specs=[in_smem] + [in_vmem] * 4,
        out_specs=in_hbm,
        scratch_shapes=[
            pltpu.VMEM((slots, rows, width), own.dtype),
            pltpu.SemaphoreType.DMA((slots,)),
        ],
        compiler_params=params,
    )(partners, own, own_twin, got, got_twin)


def body(residual, enc_weight, enc_bias, threshold, partners):
    n = lax.axis_size("lat")
    halves = lax.axis_size("tok")
    tok_rows = residual.shape[0]
    width = enc_weight.shape[1]
    slots = partners.shape[1]
    tok_scale = 1.0 / (tok_rows * halves)
    swap = [(i, 1 - i) for i in range(2)]
    by_slot = partners.T
    if 8 <= n <= ring_limit:
        ring = Ring(n)
        acts = encode_on_ring(residual, enc_weight, enc_bias, threshold, ring)
        acts_twin = lax.ppermute(acts, "tok", swap)
        blocks = {0: acts}

        def arrived(hop, ahead, behind, state):
            blocks[hop], blocks[n - hop] = ahead, behind
            return acts_twin

        acts_twin, ahead, behind, far = ring.gather(acts, arrived)
        blocks[ring.hops], blocks[n - ring.hops], blocks[n // 2] = ahead, behind, far
        got = choose(by_slot, [blocks[i] for i in range(n)])
    else:
        acts = encode_gathered(residual, enc_weight, enc_bias, threshold)
        acts_twin = lax.ppermute(acts, "tok", swap)
        slices = lax.all_to_all(acts.reshape(n, tok_rows // n, width), "lat", 0, 0)
        outgoing = jnp.take(slices, jnp.minimum(partners[:, 1:], n - 1), axis=0)
        got = lax.all_to_all(outgoing, "lat", 0, 0)
        got = got.transpose(1, 0, 2, 3).reshape(slots - 1, tok_rows, width)
    got_twin = lax.ppermute(got, "tok", swap)
    return gram(by_slot, acts, acts_twin, got, got_twin, tok_scale, halves, n)


def solution(mesh):
    return jax.shard_map(
        body,
        mesh=mesh,
        in_specs=(P(("parts", "tok"), "lat"), P(None, "lat"), P("lat"), P("lat"), P()),
        out_specs=P(("parts", "lat"), None, "tok", None),
        check_vma=False,
    )
```

time: 97.5 us -> 45.9 us (0.47)
  blocking collectives: 47.2 us -> 0 us
  starting transfers between devices: 5.55 us -> 23 us
  between operations: 13.5 us -> 0.07 us
  matrix products: 5.44 us -> 0 us
  Pallas kernels: 0 us -> 3.72 us
  other arithmetic: 3.31 us -> 0 us
  local copies, waits for them, and re-layouts: 3.81 us -> 2.06 us
  waiting for transfers between devices: 18.3 us -> 16.7 us
    all_gather x1 -> x0, blocking collectives: 34.5 us -> none  [body(): lax.all_gather(residual, 'lat', axis=1, tiled=True)]
    ppermute x0 -> x16, starting transfers between devices: none -> 23 us  [the longest x2 9.08 us: gather(): far = lax.ppermute(x, 'lat', self.across)]
    ppermute x0 -> x16, waiting for transfers between devices: none -> 16.7 us  [the longest x4 6.81 us: gather(): ahead = lax.ppermute(ahead, 'lat', self.forward)]
    all_to_all x1 -> x0, blocking collectives: 12.7 us -> none  [body(): lax.all_to_all(outgoing, 'lat', split_axis=0, concat_axis=2, tiled=True)[0]]
    reduce_scatter x1 -> x0, waiting for transfers between devices: 11.2 us -> none  [body(): lax.psum_scatter(partial_value, 'tok', scatter_dimension=2, tiled=True)]
    all_to_all x1 -> x0, waiting for transfers between devices: 7.1 us -> none  [body(): lax.all_to_all(activations.reshape(1, tok_rows, lat_width), 'lat', split_...]
    all_to_all x1 -> x0, starting transfers between devices: 5.51 us -> none  [body(): lax.all_to_all(activations.reshape(1, tok_rows, lat_width), 'lat', split_...]
    dot_general x2 -> x0, matrix products: 5.44 us -> none  [the longest x1 2.77 us: body(): jnp.dot(lax.all_gather(residual, 'lat', axis=1, tiled=True), enc_weight,...]
  transfers between devices with their start and end apart: 2 -> 16, of which waited for: 2 -> 10; matrix products, arithmetic and copies ran while one was open for 0% -> 0% of each run, Pallas kernels for 0% -> 2%
where the time goes in v3:
time: 45.9 us; the launch traced here: 45.5 us
  starting transfers between devices  23 us (50%)
  waiting for transfers between devices  16.7 us (36%)
  Pallas kernels  3.72 us (8%)
  local copies, waits for them, and re-layouts  2.06 us (4%)
    ppermute x2, starting transfers between devices, gather(): far = lax.ppermute(x, 'lat', self.across)  9.08 us
    ppermute x4, waiting for transfers between devices, gather(): ahead = lax.ppermute(ahead, 'lat', self.forward)  6.81 us
    ppermute x4, starting transfers between devices, gather(): ahead = lax.ppermute(ahead, 'lat', self.forward)  5.58 us
    ppermute x2, waiting for transfers between devices, gather(): far = lax.ppermute(x, 'lat', self.across)  4.79 us
    ppermute x2, starting transfers between devices, gather(): behind = lax.ppermute(x, 'lat', self.backward)  4.11 us
    ppermute x4, waiting for transfers between devices, gather(): behind = lax.ppermute(behind, 'lat', self.backward)  3.38 us
    ppermute x4, starting transfers between devices, gather(): behind = lax.ppermute(behind, 'lat', self.backward)  3.13 us
    unnamed x12, local copies, waits for them, and re-layouts  2.06 us
  transfers between devices with their start and end apart: 16, of which 10 were waited for; matrix products, arithmetic and copies ran while one was open for 0% of the time, Pallas kernels for 2%

profile of v3, /device:TPU:0, one launch (start us, length us, event | category | flops | bytes accessed | tf_op | source)
XLA Modules:
  0.0 45.5 jit_solution(4819813523652464207)
XLA Ops:
  0.0 2.9 %collective-permute-start.1 = (bf16[448,128]{1,0:T(8,128)(2,1)}, bf16[448,128]{1,0:T(8,128)(2,1)S(1)}, u32[]{:S(2)}, u32[]{:S(2)}) collective-permute-start(bf16[448,128]{1,0:T(8,128)(2,1)} %bitcast.8), channel_id=1, source_target_pairs={{4,0},{8,4},{12,8},{14,12},{10,14},{6,10},{2,6},{0,2},{5,1},{9,5},... | collective-permute-start | bytes 344072 | tf_op jit(solution)/shard_map/ppermute | solution.py:86
  2.9 0.1 collective-permute-start
  3.0 5.0 %collective-permute-start.4 = (bf16[448,128]{1,0:T(8,128)(2,1)}, bf16[448,128]{1,0:T(8,128)(2,1)S(1)}, u32[]{:S(2)}, u32[]{:S(2)}) collective-permute-start(bf16[448,128]{1,0:T(8,128)(2,1)} %bitcast.10), channel_id=1, source_target_pairs={{0,14},{4,10},{8,6},{12,2},{14,0},{10,4},{6,8},{2,12},{1,15},{5,11... | collective-permute-start | bytes 344072 | tf_op jit(solution)/shard_map/ppermute | solution.py:87
  8.0 0.0 collective-permute-done.1.x_b
  8.0 0.5 %collective-permute-start.3 = (bf16[448,128]{1,0:T(8,128)(2,1)S(1)}, bf16[448,128]{1,0:T(8,128)(2,1)S(1)}, u32[]{:S(2)}, u32[]{:S(2)}) collective-permute-start(bf16[448,128]{1,0:T(8,128)(2,1)S(1)} %collective-permute-done.1.x_b), channel_id=1, source_target_pairs={{4,0},{8,4},{12,8},{14,12},{10,14},{6,10},{2,6},{0,2},{5,1},{9,5},... | collective-permute-start | bytes 344072 | tf_op jit(solution)/shard_map/ppermute | solution.py:92
  8.5 0.0 collective-permute-done.x_f
  8.5 1.5 %collective-permute-start.2 = (bf16[448,128]{1,0:T(8,128)(2,1)S(1)}, bf16[448,128]{1,0:T(8,128)(2,1)S(1)}, u32[]{:S(2)}, u32[]{:S(2)}) collective-permute-start(bf16[448,128]{1,0:T(8,128)(2,1)S(1)} %collective-permute-done.x_f), channel_id=1, source_target_pairs={{0,4},{4,8},{8,12},{12,14},{14,10},{10,6},{6,2},{2,0},{1,5},{5,9},... | collective-permute-start | bytes 344072 | tf_op jit(solution)/shard_map/ppermute | solution.py:91
  10.0 0.0 copy-start
  10.0 2.0 %copy-done = bf16[3584,512]{1,0:T(8,128)(2,1)S(1)} copy-done((bf16[3584,512]{1,0:T(8,128)(2,1)S(1)}, bf16[3584,512]{1,0:T(8,128)(2,1)}, u32[]{:S(2)}) %copy-start) | copy-done | bytes 3670040
  12.1 0.0 copy-start.1
  12.1 0.0 copy-start.2
  12.1 0.0 copy-start.4
  12.1 0.3 shard_map.55.before
  12.4 0.0 copy-start.3
  12.4 1.6 %collective-permute-done.4.x_far = bf16[448,128]{1,0:T(8,128)(2,1)S(1)} collective-permute-done((bf16[448,128]{1,0:T(8,128)(2,1)}, bf16[448,128]{1,0:T(8,128)(2,1)S(1)}, u32[]{:S(2)}, u32[]{:S(2)}) %collective-permute-start.4) | collective-permute-done | bytes 114720 | tf_op jit(solution)/shard_map/ppermute | solution.py:87
  14.1 0.0 collective-permute-done.3.x_b
  14.1 0.5 %collective-permute-done.2.x_f = bf16[448,128]{1,0:T(8,128)(2,1)S(1)} collective-permute-done((bf16[448,128]{1,0:T(8,128)(2,1)S(1)}, bf16[448,128]{1,0:T(8,128)(2,1)S(1)}, u32[]{:S(2)}, u32[]{:S(2)}) %collective-permute-start.2) | collective-permute-done | bytes 114720 | tf_op jit(solution)/shard_map/ppermute | solution.py:91
  14.6 1.9 %collective-permute-start.5 = (bf16[448,128]{1,0:T(8,128)(2,1)S(1)}, bf16[448,128]{1,0:T(8,128)(2,1)S(1)}, u32[]{:S(2)}, u32[]{:S(2)}) collective-permute-start(bf16[448,128]{1,0:T(8,128)(2,1)S(1)} %collective-permute-done.2.x_f), channel_id=1, source_target_pairs={{0,4},{4,8},{8,12},{12,14},{14,10},{10,6},{6,2},{2,0},{1,5},{5,9},... | collective-permute-start | bytes 344072 | tf_op jit(solution)/shard_map/ppermute | solution.py:91
  16.5 0.7 %collective-permute-start.6 = (bf16[448,128]{1,0:T(8,128)(2,1)S(1)}, bf16[448,128]{1,0:T(8,128)(2,1)S(1)}, u32[]{:S(2)}, u32[]{:S(2)}) collective-permute-start(bf16[448,128]{1,0:T(8,128)(2,1)S(1)} %collective-permute-done.3.x_b), channel_id=1, source_target_pairs={{4,0},{8,4},{12,8},{14,12},{10,14},{6,10},{2,6},{0,2},{5,1},{9,5},... | collective-permute-start | bytes 344072 | tf_op jit(solution)/shard_map/ppermute | solution.py:92
  17.2 0.0 copy-done.1
  17.2 0.0 copy-done.2
  17.2 0.4 shard_map.56.before
  17.6 2.4 %collective-permute-done.5.x_f = bf16[448,128]{1,0:T(8,128)(2,1)S(1)} collective-permute-done((bf16[448,128]{1,0:T(8,128)(2,1)S(1)}, bf16[448,128]{1,0:T(8,128)(2,1)S(1)}, u32[]{:S(2)}, u32[]{:S(2)}) %collective-permute-start.5) | collective-permute-done | bytes 114720 | tf_op jit(solution)/shard_map/ppermute | solution.py:91
  20.0 1.3 %collective-permute-done.6.x_b = bf16[448,128]{1,0:T(8,128)(2,1)S(1)} collective-permute-done((bf16[448,128]{1,0:T(8,128)(2,1)S(1)}, bf16[448,128]{1,0:T(8,128)(2,1)S(1)}, u32[]{:S(2)}, u32[]{:S(2)}) %collective-permute-start.6) | collective-permute-done | bytes 114720 | tf_op jit(solution)/shard_map/ppermute | solution.py:92
  21.3 0.0 copy-done.4
  21.3 0.0 copy-done.5
  21.3 0.4 shard_map.57.refs_0_.own
  21.7 1.2 %collective-permute-start.10 = (bf16[128,512]{1,0:T(8,128)(2,1)S(1)}, bf16[128,512]{1,0:T(8,128)(2,1)S(1)}, u32[]{:S(2)}, u32[]{:S(2)}) collective-permute-start(bf16[128,512]{1,0:T(8,128)(2,1)S(1)} %shard_map.57.refs_0_.own), channel_id=1, source_target_pairs={{4,0},{8,4},{12,8},{14,12},{10,14},{6,10},{2,6},{0,2},{5,1},{9,5},... | collective-permute-start | bytes 393224 | tf_op jit(solution)/shard_map/ppermute | solution.py:86
  22.9 0.9 %collective-permute-start.8 = (bf16[128,512]{1,0:T(8,128)(2,1)S(1)}, bf16[128,512]{1,0:T(8,128)(2,1)S(1)}, u32[]{:S(2)}, u32[]{:S(2)}) collective-permute-start(bf16[128,512]{1,0:T(8,128)(2,1)S(1)} %shard_map.57.refs_0_.own), channel_id=1, source_target_pairs={{0,4},{4,8},{8,12},{12,14},{14,10},{10,6},{6,2},{2,0},{1,5},{5,9},... | collective-permute-start | bytes 393224 | tf_op jit(solution)/shard_map/ppermute | solution.py:85
  23.8 4.1 %collective-permute-start.12 = (bf16[128,512]{1,0:T(8,128)(2,1)S(1)}, bf16[128,512]{1,0:T(8,128)(2,1)S(1)}, u32[]{:S(2)}, u32[]{:S(2)}) collective-permute-start(bf16[128,512]{1,0:T(8,128)(2,1)S(1)} %shard_map.57.refs_0_.own), channel_id=1, source_target_pairs={{0,14},{4,10},{8,6},{12,2},{14,0},{10,4},{6,8},{2,12},{1,15},{5,11... | collective-permute-start | bytes 393224 | tf_op jit(solution)/shard_map/ppermute | solution.py:87
  27.9 0.0 collective-permute-start.7
  27.9 0.0 collective-permute-done.10.refs_7_
  27.9 0.9 %collective-permute-start.11 = (bf16[128,512]{1,0:T(8,128)(2,1)S(1)}, bf16[128,512]{1,0:T(8,128)(2,1)S(1)}, u32[]{:S(2)}, u32[]{:S(2)}) collective-permute-start(bf16[128,512]{1,0:T(8,128)(2,1)S(1)} %collective-permute-done.10.refs_7_), channel_id=1, source_target_pairs={{4,0},{8,4},{12,8},{14,12},{10,14},{6,10},{2,6},{0,2},{5,1},{9,5},... | collective-permute-start | bytes 393224 | tf_op jit(solution)/shard_map/ppermute | solution.py:92
  28.8 0.0 collective-permute-done.8.refs_1_
  28.8 1.2 %collective-permute-start.9 = (bf16[128,512]{1,0:T(8,128)(2,1)S(1)}, bf16[128,512]{1,0:T(8,128)(2,1)S(1)}, u32[]{:S(2)}, u32[]{:S(2)}) collective-permute-start(bf16[128,512]{1,0:T(8,128)(2,1)S(1)} %collective-permute-done.8.refs_1_), channel_id=1, source_target_pairs={{0,4},{4,8},{8,12},{12,14},{14,10},{10,6},{6,2},{2,0},{1,5},{5,9},... | collective-permute-start | bytes 393224 | tf_op jit(solution)/shard_map/ppermute | solution.py:91
  29.9 3.1 %collective-permute-done.12.refs_4_ = bf16[128,512]{1,0:T(8,128)(2,1)S(1)} collective-permute-done((bf16[128,512]{1,0:T(8,128)(2,1)S(1)}, bf16[128,512]{1,0:T(8,128)(2,1)S(1)}, u32[]{:S(2)}, u32[]{:S(2)}) %collective-permute-start.12) | collective-permute-done | bytes 131104 | tf_op jit(solution)/shard_map/ppermute | solution.py:87
  33.1 0.0 collective-permute-done.7.own_twin
  33.1 1.3 %collective-permute-done.11.refs_6_ = bf16[128,512]{1,0:T(8,128)(2,1)S(1)} collective-permute-done((bf16[128,512]{1,0:T(8,128)(2,1)S(1)}, bf16[128,512]{1,0:T(8,128)(2,1)S(1)}, u32[]{:S(2)}, u32[]{:S(2)}) %collective-permute-start.11) | collective-permute-done | bytes 131104 | tf_op jit(solution)/shard_map/ppermute | solution.py:92
  34.4 0.8 %collective-permute-done.9.refs_2_ = bf16[128,512]{1,0:T(8,128)(2,1)S(1)} collective-permute-done((bf16[128,512]{1,0:T(8,128)(2,1)S(1)}, bf16[128,512]{1,0:T(8,128)(2,1)S(1)}, u32[]{:S(2)}, u32[]{:S(2)}) %collective-permute-start.9) | collective-permute-done | bytes 131104 | tf_op jit(solution)/shard_map/ppermute | solution.py:91
  35.2 1.0 %collective-permute-start.13 = (bf16[128,512]{1,0:T(8,128)(2,1)S(1)}, bf16[128,512]{1,0:T(8,128)(2,1)S(1)}, u32[]{:S(2)}, u32[]{:S(2)}) collective-permute-start(bf16[128,512]{1,0:T(8,128)(2,1)S(1)} %collective-permute-done.9.refs_2_), channel_id=1, source_target_pairs={{0,4},{4,8},{8,12},{12,14},{14,10},{10,6},{6,2},{2,0},{1,5},{5,9},... | collective-permute-start | bytes 393224 | tf_op jit(solution)/shard_map/ppermute | solution.py:91
  36.2 1.0 %collective-permute-start.14 = (bf16[128,512]{1,0:T(8,128)(2,1)S(1)}, bf16[128,512]{1,0:T(8,128)(2,1)S(1)}, u32[]{:S(2)}, u32[]{:S(2)}) collective-permute-start(bf16[128,512]{1,0:T(8,128)(2,1)S(1)} %collective-permute-done.11.refs_6_), channel_id=1, source_target_pairs={{4,0},{8,4},{12,8},{14,12},{10,14},{6,10},{2,6},{0,2},{5,1},{9,5},... | collective-permute-start | bytes 393224 | tf_op jit(solution)/shard_map/ppermute | solution.py:92
  37.2 3.1 %collective-permute-done.13.refs_3_ = bf16[128,512]{1,0:T(8,128)(2,1)S(1)} collective-permute-done((bf16[128,512]{1,0:T(8,128)(2,1)S(1)}, bf16[128,512]{1,0:T(8,128)(2,1)S(1)}, u32[]{:S(2)}, u32[]{:S(2)}) %collective-permute-start.13) | collective-permute-done | bytes 131104 | tf_op jit(solution)/shard_map/ppermute | solution.py:91
  40.3 0.8 %collective-permute-done.14.refs_5_ = bf16[128,512]{1,0:T(8,128)(2,1)S(1)} collective-permute-done((bf16[128,512]{1,0:T(8,128)(2,1)S(1)}, bf16[128,512]{1,0:T(8,128)(2,1)S(1)}, u32[]{:S(2)}, u32[]{:S(2)}) %collective-permute-start.14) | collective-permute-done | bytes 131104 | tf_op jit(solution)/shard_map/ppermute | solution.py:92
  41.2 0.0 copy-done.3
  41.2 0.8 %shard_map.58.got = bf16[3,128,512]{2,1,0:T(8,128)(2,1)S(1)} custom-call(s32[4,8]{1,0:T(4,128)S(1)} %bitcast.12, bf16[128,512]{1,0:T(8,128)(2,1)S(1)} %shard_map.57.refs_0_.own, bf16[128,512]{1,0:T(8,128)(2,1)S(1)} %collective-permute-done.8.refs_1_, bf16[128,512]{1,0:T(8,128)(2,1)S(1)} %collective-permute-done.9.refs_2_, ...), custom_call_target="tpu_custom_call" | custom-call | tf_op jit(solution)/shard_map/pallas_call | solution.py:173
  41.9 0.1 collective-permute-start.15
  42.0 1.7 %collective-permute-done.15.got_twin = bf16[3,128,512]{2,1,0:T(8,128)(2,1)S(1)} collective-permute-done((bf16[3,128,512]{2,1,0:T(8,128)(2,1)S(1)}, bf16[3,128,512]{2,1,0:T(8,128)(2,1)S(1)}, u32[]{:S(2)}, u32[]{:S(2)}) %collective-permute-start.15) | collective-permute-done | bytes 393248 | tf_op jit(solution)/shard_map/ppermute | solution.py:257
  43.7 1.8 %shard_map.59 = bf16[1,4,256,512]{3,2,1,0:T(8,128)(2,1)} custom-call(s32[4,8]{1,0:T(4,128)S(1)} %bitcast.13, bf16[128,512]{1,0:T(8,128)(2,1)S(1)} %shard_map.57.refs_0_.own, bf16[128,512]{1,0:T(8,128)(2,1)S(1)} %collective-permute-done.7.own_twin, bf16[3,128,512]{2,1,0:T(8,128)(2,1)S(1)} %shard_map.58.got, ...), custom_call_target="tpu_custom_call" | custom-call | tf_op jit(solution)/shard_map/pallas_call | solution.py:215
  (1 shorter events, 0.0 us)
Async XLA Ops:
  0.0 8.0 %collective-permute-start.1 = (bf16[448,128]{1,0:T(8,128)(2,1)}, bf16[448,128]{1,0:T(8,128)(2,1)S(1)}, u32[]{:S(2)}, u32[]{:S(2)}) collective-permute-start(bf16[448,128]{1,0:T(8,128)(2,1)} %bitcast.8), channel_id=1, source_target_pairs={{4,0},{8,4},{12,8},{14,12},{10,14},{6,10},{2,6},{0,2},{5,1},{9,5},... | collective-permute-start | bytes 344072 | tf_op jit(solution)/shard_map/ppermute | solution.py:86
  2.9 5.6 %collective-permute-start = (bf16[448,128]{1,0:T(8,128)(2,1)}, bf16[448,128]{1,0:T(8,128)(2,1)S(1)}, u32[]{:S(2)}, u32[]{:S(2)}) collective-permute-start(bf16[448,128]{1,0:T(8,128)(2,1)} %bitcast.9), channel_id=1, source_target_pairs={{0,4},{4,8},{8,12},{12,14},{14,10},{10,6},{6,2},{2,0},{1,5},{5,9},... | collective-permute-start | bytes 344072 | tf_op jit(solution)/shard_map/ppermute | solution.py:85
  3.0 11.1 %collective-permute-start.4 = (bf16[448,128]{1,0:T(8,128)(2,1)}, bf16[448,128]{1,0:T(8,128)(2,1)S(1)}, u32[]{:S(2)}, u32[]{:S(2)}) collective-permute-start(bf16[448,128]{1,0:T(8,128)(2,1)} %bitcast.10), channel_id=1, source_target_pairs={{0,14},{4,10},{8,6},{12,2},{14,0},{10,4},{6,8},{2,12},{1,15},{5,11... | collective-permute-start | bytes 344072 | tf_op jit(solution)/shard_map/ppermute | solution.py:87
  8.0 6.1 %collective-permute-start.3 = (bf16[448,128]{1,0:T(8,128)(2,1)S(1)}, bf16[448,128]{1,0:T(8,128)(2,1)S(1)}, u32[]{:S(2)}, u32[]{:S(2)}) collective-permute-start(bf16[448,128]{1,0:T(8,128)(2,1)S(1)} %collective-permute-done.1.x_b), channel_id=1, source_target_pairs={{4,0},{8,4},{12,8},{14,12},{10,14},{6,10},{2,6},{0,2},{5,1},{9,5},... | collective-permute-start | bytes 344072 | tf_op jit(solution)/shard_map/ppermute | solution.py:92
  8.5 6.0 %collective-permute-start.2 = (bf16[448,128]{1,0:T(8,128)(2,1)S(1)}, bf16[448,128]{1,0:T(8,128)(2,1)S(1)}, u32[]{:S(2)}, u32[]{:S(2)}) collective-permute-start(bf16[448,128]{1,0:T(8,128)(2,1)S(1)} %collective-permute-done.x_f), channel_id=1, source_target_pairs={{0,4},{4,8},{8,12},{12,14},{14,10},{10,6},{6,2},{2,0},{1,5},{5,9},... | collective-permute-start | bytes 344072 | tf_op jit(solution)/shard_map/ppermute | solution.py:91
  10.0 2.0 %copy-start = (bf16[3584,512]{1,0:T(8,128)(2,1)S(1)}, bf16[3584,512]{1,0:T(8,128)(2,1)}, u32[]{:S(2)}) copy-start(bf16[3584,512]{1,0:T(8,128)(2,1)} %param.6) | copy-start | bytes 11010052
  12.1 5.1 %copy-start.1 = (bf16[3584,512]{1,0:T(8,128)(2,1)S(1)}, bf16[3584,512]{1,0:T(8,128)(2,1)}, u32[]{:S(2)}) copy-start(bf16[3584,512]{1,0:T(8,128)(2,1)} %param.6) | copy-start | bytes 11010052
  12.1 5.1 %copy-start.2 = (bf16[128,448]{0,1:T(8,128)(2,1)S(1)}, bf16[128,448]{0,1:T(8,128)(2,1)}, u32[]{:S(2)}) copy-start(bf16[128,448]{0,1:T(8,128)(2,1)} %param.5) | copy-start | bytes 344068
  12.1 9.2 %copy-start.4 = (f32[512]{0:T(512)S(1)}, f32[512]{0:T(512)}, u32[]{:S(2)}) copy-start(f32[512]{0:T(512)} %param.7) | copy-start | bytes 6148
  12.1 9.2 %copy-start.5 = (f32[512]{0:T(512)S(1)}, f32[512]{0:T(512)}, u32[]{:S(2)}) copy-start(f32[512]{0:T(512)} %param.8) | copy-start | bytes 6148
  12.4 28.7 %copy-start.3 = (s32[8,4]{0,1:T(4,128)S(1)}, s32[8,4]{0,1:T(4,128)}, u32[]{:S(2)}) copy-start(s32[8,4]{0,1:T(4,128)} %param.9) | copy-start | bytes 388
  14.6 5.4 %collective-permute-start.5 = (bf16[448,128]{1,0:T(8,128)(2,1)S(1)}, bf16[448,128]{1,0:T(8,128)(2,1)S(1)}, u32[]{:S(2)}, u32[]{:S(2)}) collective-permute-start(bf16[448,128]{1,0:T(8,128)(2,1)S(1)} %collective-permute-done.2.x_f), channel_id=1, source_target_pairs={{0,4},{4,8},{8,12},{12,14},{14,10},{10,6},{6,2},{2,0},{1,5},{5,9},... | collective-permute-start | bytes 344072 | tf_op jit(solution)/shard_map/ppermute | solution.py:91
  16.5 4.8 %collective-permute-start.6 = (bf16[448,128]{1,0:T(8,128)(2,1)S(1)}, bf16[448,128]{1,0:T(8,128)(2,1)S(1)}, u32[]{:S(2)}, u32[]{:S(2)}) collective-permute-start(bf16[448,128]{1,0:T(8,128)(2,1)S(1)} %collective-permute-done.3.x_b), channel_id=1, source_target_pairs={{4,0},{8,4},{12,8},{14,12},{10,14},{6,10},{2,6},{0,2},{5,1},{9,5},... | collective-permute-start | bytes 344072 | tf_op jit(solution)/shard_map/ppermute | solution.py:92
  21.7 6.2 %collective-permute-start.10 = (bf16[128,512]{1,0:T(8,128)(2,1)S(1)}, bf16[128,512]{1,0:T(8,128)(2,1)S(1)}, u32[]{:S(2)}, u32[]{:S(2)}) collective-permute-start(bf16[128,512]{1,0:T(8,128)(2,1)S(1)} %shard_map.57.refs_0_.own), channel_id=1, source_target_pairs={{4,0},{8,4},{12,8},{14,12},{10,14},{6,10},{2,6},{0,2},{5,1},{9,5},... | collective-permute-start | bytes 393224 | tf_op jit(solution)/shard_map/ppermute | solution.py:86
  22.9 5.9 %collective-permute-start.8 = (bf16[128,512]{1,0:T(8,128)(2,1)S(1)}, bf16[128,512]{1,0:T(8,128)(2,1)S(1)}, u32[]{:S(2)}, u32[]{:S(2)}) collective-permute-start(bf16[128,512]{1,0:T(8,128)(2,1)S(1)} %shard_map.57.refs_0_.own), channel_id=1, source_target_pairs={{0,4},{4,8},{8,12},{12,14},{14,10},{10,6},{6,2},{2,0},{1,5},{5,9},... | collective-permute-start | bytes 393224 | tf_op jit(solution)/shard_map/ppermute | solution.py:85
  23.8 9.3 %collective-permute-start.12 = (bf16[128,512]{1,0:T(8,128)(2,1)S(1)}, bf16[128,512]{1,0:T(8,128)(2,1)S(1)}, u32[]{:S(2)}, u32[]{:S(2)}) collective-permute-start(bf16[128,512]{1,0:T(8,128)(2,1)S(1)} %shard_map.57.refs_0_.own), channel_id=1, source_target_pairs={{0,14},{4,10},{8,6},{12,2},{14,0},{10,4},{6,8},{2,12},{1,15},{5,11... | collective-permute-start | bytes 393224 | tf_op jit(solution)/shard_map/ppermute | solution.py:87
  27.9 5.2 %collective-permute-start.7 = (bf16[128,512]{1,0:T(8,128)(2,1)S(1)}, bf16[128,512]{1,0:T(8,128)(2,1)S(1)}, u32[]{:S(2)}, u32[]{:S(2)}) collective-permute-start(bf16[128,512]{1,0:T(8,128)(2,1)S(1)} %shard_map.57.refs_0_.own), channel_id=1, source_target_pairs={{0,1},{1,0},{2,3},{3,2},{4,5},{5,4},{6,7},{7,6},{8,9},{9,8},{10,11... | collective-permute-start | bytes 393224 | tf_op jit(solution)/shard_map/ppermute | solution.py:240
  27.9 6.4 %collective-permute-start.11 = (bf16[128,512]{1,0:T(8,128)(2,1)S(1)}, bf16[128,512]{1,0:T(8,128)(2,1)S(1)}, u32[]{:S(2)}, u32[]{:S(2)}) collective-permute-start(bf16[128,512]{1,0:T(8,128)(2,1)S(1)} %collective-permute-done.10.refs_7_), channel_id=1, source_target_pairs={{4,0},{8,4},{12,8},{14,12},{10,14},{6,10},{2,6},{0,2},{5,1},{9,5},... | collective-permute-start | bytes 393224 | tf_op jit(solution)/shard_map/ppermute | solution.py:92
  28.8 6.4 %collective-permute-start.9 = (bf16[128,512]{1,0:T(8,128)(2,1)S(1)}, bf16[128,512]{1,0:T(8,128)(2,1)S(1)}, u32[]{:S(2)}, u32[]{:S(2)}) collective-permute-start(bf16[128,512]{1,0:T(8,128)(2,1)S(1)} %collective-permute-done.8.refs_1_), channel_id=1, source_target_pairs={{0,4},{4,8},{8,12},{12,14},{14,10},{10,6},{6,2},{2,0},{1,5},{5,9},... | collective-permute-start | bytes 393224 | tf_op jit(solution)/shard_map/ppermute | solution.py:91
  35.2 5.2 %collective-permute-start.13 = (bf16[128,512]{1,0:T(8,128)(2,1)S(1)}, bf16[128,512]{1,0:T(8,128)(2,1)S(1)}, u32[]{:S(2)}, u32[]{:S(2)}) collective-permute-start(bf16[128,512]{1,0:T(8,128)(2,1)S(1)} %collective-permute-done.9.refs_2_), channel_id=1, source_target_pairs={{0,4},{4,8},{8,12},{12,14},{14,10},{10,6},{6,2},{2,0},{1,5},{5,9},... | collective-permute-start | bytes 393224 | tf_op jit(solution)/shard_map/ppermute | solution.py:91
  36.2 5.0 %collective-permute-start.14 = (bf16[128,512]{1,0:T(8,128)(2,1)S(1)}, bf16[128,512]{1,0:T(8,128)(2,1)S(1)}, u32[]{:S(2)}, u32[]{:S(2)}) collective-permute-start(bf16[128,512]{1,0:T(8,128)(2,1)S(1)} %collective-permute-done.11.refs_6_), channel_id=1, source_target_pairs={{4,0},{8,4},{12,8},{14,12},{10,14},{6,10},{2,6},{0,2},{5,1},{9,5},... | collective-permute-start | bytes 393224 | tf_op jit(solution)/shard_map/ppermute | solution.py:92
  41.9 1.8 %collective-permute-start.15 = (bf16[3,128,512]{2,1,0:T(8,128)(2,1)S(1)}, bf16[3,128,512]{2,1,0:T(8,128)(2,1)S(1)}, u32[]{:S(2)}, u32[]{:S(2)}) collective-permute-start(bf16[3,128,512]{2,1,0:T(8,128)(2,1)S(1)} %shard_map.58.got), channel_id=1, source_target_pairs={{0,1},{1,0},{2,3},{3,2},{4,5},{5,4},{6,7},{7,6},{8,9},{9,8},{10,11... | collective-permute-start | bytes 1179656 | tf_op jit(solution)/shard_map/ppermute | solution.py:257

commit v4 on v3

--- a/solution.py
+++ b/solution.py
@@ -8,7 +8,7 @@
 from jax.sharding import PartitionSpec as P
 
 ramp_width = 0.25
-ring_limit = 16
+ring_size = 8
 
 in_vmem = pl.BlockSpec(memory_space=pltpu.VMEM)
 in_smem = pl.BlockSpec(memory_space=pltpu.SMEM)
@@ -79,22 +79,27 @@
         self.hops = n // 2 - 1
         self.forward = [(walk[i], walk[(i + 1) % n]) for i in range(n)]
         self.backward = [(d, s) for s, d in self.forward]
-        self.across = [(walk[i], walk[(i + n // 2) % n]) for i in range(n)]
+        mates = {i: (i + 4) % n if i % 4 in (0, 3) else n - 1 - i for i in range(n)}
+        self.across = [(walk[i], walk[mates[i]]) for i in range(n)]
+
+    def to_cross(self, x, ahead, behind):
+        place = place_on_ring(lax.axis_index("lat"), self.n) % 4
+        return jnp.where(place == 1, behind, jnp.where(place == 2, ahead, x))
 
     def gather(self, x, arrived):
         ahead = lax.ppermute(x, "lat", self.forward)
         behind = lax.ppermute(x, "lat", self.backward)
-        far = lax.ppermute(x, "lat", self.across)
         state = None
         for hop in range(1, self.hops):
             now_ahead, now_behind = ahead, behind
             ahead = lax.ppermute(ahead, "lat", self.forward)
             behind = lax.ppermute(behind, "lat", self.backward)
+            if hop == 1:
+                cross = self.to_cross(x, now_ahead, now_behind)
+                far = lax.ppermute(cross, "lat", self.across)
             state = arrived(hop, now_ahead, now_behind, state)
             if hop + 1 < self.hops:
-                state, ahead, behind, far = lax.optimization_barrier(
-                    (state, ahead, behind, far)
-                )
+                state, ahead, behind = lax.optimization_barrier((state, ahead, behind))
         return state, ahead, behind, far
 
 
@@ -234,7 +239,7 @@
     tok_scale = 1.0 / (tok_rows * halves)
     swap = [(i, 1 - i) for i in range(2)]
     by_slot = partners.T
-    if 8 <= n <= ring_limit:
+    if n == ring_size:
         ring = Ring(n)
         acts = encode_on_ring(residual, enc_weight, enc_bias, threshold, ring)
         acts_twin = lax.ppermute(acts, "tok", swap)

time: 45.9 us -> 45.8 us (level)
  starting transfers between devices: 23 us -> 21.3 us
  other arithmetic: 0 us -> 0.95 us
  waiting for transfers between devices: 16.7 us -> 17.2 us
    ppermute x2, waiting for transfers between devices: 0.01 us -> 6.14 us  [gather(): behind = lax.ppermute(x, 'lat', self.backward)]
    ppermute x4, starting transfers between devices: 5.58 us -> 0.5 us  [gather(): ahead = lax.ppermute(ahead, 'lat', self.forward)]
    ppermute x2, waiting for transfers between devices: 4.79 us -> 0.01 us  [gather(): far = lax.ppermute(cross, 'lat', self.across)]
    ppermute x4, starting transfers between devices: 3.13 us -> 7.82 us  [gather(): behind = lax.ppermute(behind, 'lat', self.backward)]
    ppermute x4, waiting for transfers between devices: 3.38 us -> 0.96 us  [gather(): behind = lax.ppermute(behind, 'lat', self.backward)]
    ppermute x2, starting transfers between devices: 9.08 us -> 7.56 us  [gather(): far = lax.ppermute(cross, 'lat', self.across)]
    ppermute x4, waiting for transfers between devices: 6.81 us -> 8.28 us  [gather(): ahead = lax.ppermute(ahead, 'lat', self.forward)]
    ppermute x2, starting transfers between devices: 4.11 us -> 5.18 us  [gather(): behind = lax.ppermute(x, 'lat', self.backward)]
  transfers between devices with their start and end apart: 16 -> 16, of which waited for: 10 -> 9; matrix products, arithmetic and copies ran while one was open for 0% -> 2% of each run, Pallas kernels for 2% -> 2%
where the time goes in v4:
time: 45.8 us; the launch traced here: 45.7 us
  starting transfers between devices  21.3 us (47%)
  waiting for transfers between devices  17.2 us (38%)
  Pallas kernels  4.15 us (9%)
  local copies, waits for them, and re-layouts  2.06 us (4%)
  other arithmetic  0.95 us (2%)
    ppermute x4, waiting for transfers between devices, gather(): ahead = lax.ppermute(ahead, 'lat', self.forward)  8.28 us
    ppermute x4, starting transfers between devices, gather(): behind = lax.ppermute(behind, 'lat', self.backward)  7.82 us
    ppermute x2, starting transfers between devices, gather(): far = lax.ppermute(cross, 'lat', self.across)  7.56 us
    ppermute x2, waiting for transfers between devices, gather(): behind = lax.ppermute(x, 'lat', self.backward)  6.14 us
    ppermute x2, starting transfers between devices, gather(): behind = lax.ppermute(x, 'lat', self.backward)  5.18 us
    pallas_call x1, Pallas kernels, gram(): pl.pallas_call(functools.partial(gram_kernel, tok_scale, n), out_shape=ja...  2.25 us
    unnamed x12, local copies, waits for them, and re-layouts  2.06 us
    ppermute x1, waiting for transfers between devices, body(): got_twin = lax.ppermute(got, 'tok', swap)  1.71 us
  transfers between devices with their start and end apart: 16, of which 9 were waited for; matrix products, arithmetic and copies ran while one was open for 2% of the time, Pallas kernels for 2%

profile of v4, /device:TPU:0, one launch (start us, length us, event | category | flops | bytes accessed | tf_op | source)
XLA Modules:
  0.0 45.7 jit_solution(15860160706131451880)
XLA Ops:
  0.0 0.0 copy-start.2
  0.0 2.9 %collective-permute-start.1 = (bf16[448,128]{1,0:T(8,128)(2,1)}, bf16[448,128]{1,0:T(8,128)(2,1)S(1)}, u32[]{:S(2)}, u32[]{:S(2)}) collective-permute-start(bf16[448,128]{1,0:T(8,128)(2,1)} %bitcast.9), channel_id=1, source_target_pairs={{4,0},{8,4},{12,8},{14,12},{10,14},{6,10},{2,6},{0,2},{5,1},{9,5},... | collective-permute-start | bytes 344072 | tf_op jit(solution)/shard_map/ppermute | solution.py:91
  2.9 0.1 collective-permute-start
  3.1 3.4 %collective-permute-done.1.x_b = bf16[448,128]{1,0:T(8,128)(2,1)S(1)} collective-permute-done((bf16[448,128]{1,0:T(8,128)(2,1)}, bf16[448,128]{1,0:T(8,128)(2,1)S(1)}, u32[]{:S(2)}, u32[]{:S(2)}) %collective-permute-start.1) | collective-permute-done | bytes 114720 | tf_op jit(solution)/shard_map/ppermute | solution.py:91
  6.5 1.6 %collective-permute-start.3 = (bf16[448,128]{1,0:T(8,128)(2,1)S(1)}, bf16[448,128]{1,0:T(8,128)(2,1)S(1)}, u32[]{:S(2)}, u32[]{:S(2)}) collective-permute-start(bf16[448,128]{1,0:T(8,128)(2,1)S(1)} %collective-permute-done.1.x_b), channel_id=1, source_target_pairs={{4,0},{8,4},{12,8},{14,12},{10,14},{6,10},{2,6},{0,2},{5,1},{9,5},... | collective-permute-start | bytes 344072 | tf_op jit(solution)/shard_map/ppermute | solution.py:96
  8.0 0.0 collective-permute-done.x_f
  8.0 0.4 collective-permute-start.2
  8.5 0.9 %select_select_fusion.1 = bf16[448,128]{1,0:T(8,128)(2,1)S(1)} fusion(bf16[448,128]{1,0:T(8,128)(2,1)S(1)} %collective-permute-done.1.x_b, bf16[448,128]{1,0:T(8,128)(2,1)S(1)} %collective-permute-done.x_f, pred[]{:T(512)S(6)} %eq.14, pred[]{:T(512)S(6)} %eq.13, bf16[128,448]{0,1:T(8,128)(2,1)} %param.5), kind=kLoop, calls=%fused_computation.1 | loop fusion | flops 114688 | bytes 458754 | tf_op jit(solution)/shard_map/jit(_where)/select_n | solution.py:87
  9.4 4.7 %collective-permute-start.6 = (bf16[448,128]{1,0:T(8,128)(2,1)S(1)}, bf16[448,128]{1,0:T(8,128)(2,1)S(1)}, u32[]{:S(2)}, u32[]{:S(2)}) collective-permute-start(bf16[448,128]{1,0:T(8,128)(2,1)S(1)} %select_select_fusion.1), channel_id=1, source_target_pairs={{0,14},{4,6},{8,10},{12,2},{14,0},{10,8},{6,4},{2,12},{1,15},{5,7}... | collective-permute-start | bytes 344072 | tf_op jit(solution)/shard_map/ppermute | solution.py:99
  14.1 0.0 copy-start
  14.1 2.0 %copy-done = bf16[3584,512]{1,0:T(8,128)(2,1)S(1)} copy-done((bf16[3584,512]{1,0:T(8,128)(2,1)S(1)}, bf16[3584,512]{1,0:T(8,128)(2,1)}, u32[]{:S(2)}) %copy-start) | copy-done | bytes 3670040
  16.1 0.0 copy-start.1
  16.1 0.3 shard_map.55.before
  16.5 0.0 copy-start.3
  16.5 0.0 collective-permute-done.3.x_b
  16.5 0.0 collective-permute-done.2.x_f
  16.5 0.1 collective-permute-start.4
  16.6 2.0 %collective-permute-start.5 = (bf16[448,128]{1,0:T(8,128)(2,1)S(1)}, bf16[448,128]{1,0:T(8,128)(2,1)S(1)}, u32[]{:S(2)}, u32[]{:S(2)}) collective-permute-start(bf16[448,128]{1,0:T(8,128)(2,1)S(1)} %collective-permute-done.3.x_b), channel_id=1, source_target_pairs={{4,0},{8,4},{12,8},{14,12},{10,14},{6,10},{2,6},{0,2},{5,1},{9,5},... | collective-permute-start | bytes 344072 | tf_op jit(solution)/shard_map/ppermute | solution.py:96
  18.6 0.0 copy-done.2
  18.6 0.0 copy-done.1
  18.6 0.4 shard_map.56.before
  19.0 0.0 collective-permute-done.6.x_far
  19.0 2.3 %collective-permute-done.4.x_f = bf16[448,128]{1,0:T(8,128)(2,1)S(1)} collective-permute-done((bf16[448,128]{1,0:T(8,128)(2,1)S(1)}, bf16[448,128]{1,0:T(8,128)(2,1)S(1)}, u32[]{:S(2)}, u32[]{:S(2)}) %collective-permute-start.4) | collective-permute-done | bytes 114720 | tf_op jit(solution)/shard_map/ppermute | solution.py:95
  21.3 0.1 collective-permute-done.5.x_b
  21.4 0.0 copy-done.4
  21.4 0.0 copy-done.5
  21.4 0.4 shard_map.57.refs_0_.own
  21.9 2.2 %collective-permute-start.10 = (bf16[128,512]{1,0:T(8,128)(2,1)S(1)}, bf16[128,512]{1,0:T(8,128)(2,1)S(1)}, u32[]{:S(2)}, u32[]{:S(2)}) collective-permute-start(bf16[128,512]{1,0:T(8,128)(2,1)S(1)} %shard_map.57.refs_0_.own), channel_id=1, source_target_pairs={{4,0},{8,4},{12,8},{14,12},{10,14},{6,10},{2,6},{0,2},{5,1},{9,5},... | collective-permute-start | bytes 393224 | tf_op jit(solution)/shard_map/ppermute | solution.py:91
  24.1 0.0 collective-permute-start.8
  24.1 0.0 collective-permute-start.7
  24.1 2.8 %collective-permute-done.10.refs_7_ = bf16[128,512]{1,0:T(8,128)(2,1)S(1)} collective-permute-done((bf16[128,512]{1,0:T(8,128)(2,1)S(1)}, bf16[128,512]{1,0:T(8,128)(2,1)S(1)}, u32[]{:S(2)}, u32[]{:S(2)}) %collective-permute-start.10) | collective-permute-done | bytes 131104 | tf_op jit(solution)/shard_map/ppermute | solution.py:91
  26.9 2.2 %collective-permute-start.11 = (bf16[128,512]{1,0:T(8,128)(2,1)S(1)}, bf16[128,512]{1,0:T(8,128)(2,1)S(1)}, u32[]{:S(2)}, u32[]{:S(2)}) collective-permute-start(bf16[128,512]{1,0:T(8,128)(2,1)S(1)} %collective-permute-done.10.refs_7_), channel_id=1, source_target_pairs={{4,0},{8,4},{12,8},{14,12},{10,14},{6,10},{2,6},{0,2},{5,1},{9,5},... | collective-permute-start | bytes 393224 | tf_op jit(solution)/shard_map/ppermute | solution.py:96
  29.1 0.1 collective-permute-done.8.refs_1_
  29.1 0.0 collective-permute-start.9
  29.2 2.9 %collective-permute-start.13 = (bf16[128,512]{1,0:T(8,128)(2,1)S(1)}, bf16[128,512]{1,0:T(8,128)(2,1)S(1)}, u32[]{:S(2)}, u32[]{:S(2)}) collective-permute-start(bf16[128,512]{1,0:T(8,128)(2,1)S(1)} %select_select_fusion), channel_id=1, source_target_pairs={{0,14},{4,6},{8,10},{12,2},{14,0},{10,8},{6,4},{2,12},{1,15},{5,7}... | collective-permute-start | bytes 393224 | tf_op jit(solution)/shard_map/ppermute | solution.py:99
  32.0 0.0 collective-permute-done.7.own_twin
  32.0 0.9 %collective-permute-done.11.refs_6_ = bf16[128,512]{1,0:T(8,128)(2,1)S(1)} collective-permute-done((bf16[128,512]{1,0:T(8,128)(2,1)S(1)}, bf16[128,512]{1,0:T(8,128)(2,1)S(1)}, u32[]{:S(2)}, u32[]{:S(2)}) %collective-permute-start.11) | collective-permute-done | bytes 131104 | tf_op jit(solution)/shard_map/ppermute | solution.py:96
  32.9 3.0 %collective-permute-done.9.refs_2_ = bf16[128,512]{1,0:T(8,128)(2,1)S(1)} collective-permute-done((bf16[128,512]{1,0:T(8,128)(2,1)S(1)}, bf16[128,512]{1,0:T(8,128)(2,1)S(1)}, u32[]{:S(2)}, u32[]{:S(2)}) %collective-permute-start.9) | collective-permute-done | bytes 131104 | tf_op jit(solution)/shard_map/ppermute | solution.py:95
  35.9 0.0 collective-permute-start.12
  35.9 2.0 %collective-permute-start.14 = (bf16[128,512]{1,0:T(8,128)(2,1)S(1)}, bf16[128,512]{1,0:T(8,128)(2,1)S(1)}, u32[]{:S(2)}, u32[]{:S(2)}) collective-permute-start(bf16[128,512]{1,0:T(8,128)(2,1)S(1)} %collective-permute-done.11.refs_6_), channel_id=1, source_target_pairs={{4,0},{8,4},{12,8},{14,12},{10,14},{6,10},{2,6},{0,2},{5,1},{9,5},... | collective-permute-start | bytes 393224 | tf_op jit(solution)/shard_map/ppermute | solution.py:96
  38.0 0.0 collective-permute-done.13.refs_4_
  38.0 2.9 %collective-permute-done.12.refs_3_ = bf16[128,512]{1,0:T(8,128)(2,1)S(1)} collective-permute-done((bf16[128,512]{1,0:T(8,128)(2,1)S(1)}, bf16[128,512]{1,0:T(8,128)(2,1)S(1)}, u32[]{:S(2)}, u32[]{:S(2)}) %collective-permute-start.12) | collective-permute-done | bytes 131104 | tf_op jit(solution)/shard_map/ppermute | solution.py:95
  40.9 0.0 collective-permute-done.14.refs_5_
  40.9 0.0 copy-done.3
  40.9 0.8 %shard_map.58.got = bf16[3,128,512]{2,1,0:T(8,128)(2,1)S(1)} custom-call(s32[4,8]{1,0:T(4,128)S(1)} %bitcast.12, bf16[128,512]{1,0:T(8,128)(2,1)S(1)} %shard_map.57.refs_0_.own, bf16[128,512]{1,0:T(8,128)(2,1)S(1)} %collective-permute-done.8.refs_1_, bf16[128,512]{1,0:T(8,128)(2,1)S(1)} %collective-permute-done.9.refs_2_, ...), custom_call_target="tpu_custom_call" | custom-call | tf_op jit(solution)/shard_map/pallas_call | solution.py:178
  41.7 0.1 collective-permute-start.15
  41.8 1.7 %collective-permute-done.15.got_twin = bf16[3,128,512]{2,1,0:T(8,128)(2,1)S(1)} collective-permute-done((bf16[3,128,512]{2,1,0:T(8,128)(2,1)S(1)}, bf16[3,128,512]{2,1,0:T(8,128)(2,1)S(1)}, u32[]{:S(2)}, u32[]{:S(2)}) %collective-permute-start.15) | collective-permute-done | bytes 393248 | tf_op jit(solution)/shard_map/ppermute | solution.py:262
  43.5 2.2 %shard_map.59 = bf16[1,4,256,512]{3,2,1,0:T(8,128)(2,1)} custom-call(s32[4,8]{1,0:T(4,128)S(1)} %bitcast.13, bf16[128,512]{1,0:T(8,128)(2,1)S(1)} %shard_map.57.refs_0_.own, bf16[128,512]{1,0:T(8,128)(2,1)S(1)} %collective-permute-done.7.own_twin, bf16[3,128,512]{2,1,0:T(8,128)(2,1)S(1)} %shard_map.58.got, ...), custom_call_target="tpu_custom_call" | custom-call | tf_op jit(solution)/shard_map/pallas_call | solution.py:220
  (3 shorter events, 0.0 us)
Async XLA Ops:
  0.0 18.6 %copy-start.2 = (bf16[128,448]{0,1:T(8,128)(2,1)S(1)}, bf16[128,448]{0,1:T(8,128)(2,1)}, u32[]{:S(2)}) copy-start(bf16[128,448]{0,1:T(8,128)(2,1)} %param.5) | copy-start | bytes 344068
  0.0 6.4 %collective-permute-start.1 = (bf16[448,128]{1,0:T(8,128)(2,1)}, bf16[448,128]{1,0:T(8,128)(2,1)S(1)}, u32[]{:S(2)}, u32[]{:S(2)}) collective-permute-start(bf16[448,128]{1,0:T(8,128)(2,1)} %bitcast.9), channel_id=1, source_target_pairs={{4,0},{8,4},{12,8},{14,12},{10,14},{6,10},{2,6},{0,2},{5,1},{9,5},... | collective-permute-start | bytes 344072 | tf_op jit(solution)/shard_map/ppermute | solution.py:91
  2.9 5.1 %collective-permute-start = (bf16[448,128]{1,0:T(8,128)(2,1)}, bf16[448,128]{1,0:T(8,128)(2,1)S(1)}, u32[]{:S(2)}, u32[]{:S(2)}) collective-permute-start(bf16[448,128]{1,0:T(8,128)(2,1)} %bitcast.10), channel_id=1, source_target_pairs={{0,4},{4,8},{8,12},{12,14},{14,10},{10,6},{6,2},{2,0},{1,5},{5,9},... | collective-permute-start | bytes 344072 | tf_op jit(solution)/shard_map/ppermute | solution.py:90
  6.5 10.0 %collective-permute-start.3 = (bf16[448,128]{1,0:T(8,128)(2,1)S(1)}, bf16[448,128]{1,0:T(8,128)(2,1)S(1)}, u32[]{:S(2)}, u32[]{:S(2)}) collective-permute-start(bf16[448,128]{1,0:T(8,128)(2,1)S(1)} %collective-permute-done.1.x_b), channel_id=1, source_target_pairs={{4,0},{8,4},{12,8},{14,12},{10,14},{6,10},{2,6},{0,2},{5,1},{9,5},... | collective-permute-start | bytes 344072 | tf_op jit(solution)/shard_map/ppermute | solution.py:96
  8.0 8.5 %collective-permute-start.2 = (bf16[448,128]{1,0:T(8,128)(2,1)S(1)}, bf16[448,128]{1,0:T(8,128)(2,1)S(1)}, u32[]{:S(2)}, u32[]{:S(2)}) collective-permute-start(bf16[448,128]{1,0:T(8,128)(2,1)S(1)} %collective-permute-done.x_f), channel_id=1, source_target_pairs={{0,4},{4,8},{8,12},{12,14},{14,10},{10,6},{6,2},{2,0},{1,5},{5,9},... | collective-permute-start | bytes 344072 | tf_op jit(solution)/shard_map/ppermute | solution.py:95
  9.4 9.6 %collective-permute-start.6 = (bf16[448,128]{1,0:T(8,128)(2,1)S(1)}, bf16[448,128]{1,0:T(8,128)(2,1)S(1)}, u32[]{:S(2)}, u32[]{:S(2)}) collective-permute-start(bf16[448,128]{1,0:T(8,128)(2,1)S(1)} %select_select_fusion.1), channel_id=1, source_target_pairs={{0,14},{4,6},{8,10},{12,2},{14,0},{10,8},{6,4},{2,12},{1,15},{5,7}... | collective-permute-start | bytes 344072 | tf_op jit(solution)/shard_map/ppermute | solution.py:99
  14.1 2.0 %copy-start = (bf16[3584,512]{1,0:T(8,128)(2,1)S(1)}, bf16[3584,512]{1,0:T(8,128)(2,1)}, u32[]{:S(2)}) copy-start(bf16[3584,512]{1,0:T(8,128)(2,1)} %param.6) | copy-start | bytes 11010052
  16.1 2.5 %copy-start.1 = (bf16[3584,512]{1,0:T(8,128)(2,1)S(1)}, bf16[3584,512]{1,0:T(8,128)(2,1)}, u32[]{:S(2)}) copy-start(bf16[3584,512]{1,0:T(8,128)(2,1)} %param.6) | copy-start | bytes 11010052
  16.1 5.3 %copy-start.4 = (f32[512]{0:T(512)S(1)}, f32[512]{0:T(512)}, u32[]{:S(2)}) copy-start(f32[512]{0:T(512)} %param.7) | copy-start | bytes 6148
  16.1 5.3 %copy-start.5 = (f32[512]{0:T(512)S(1)}, f32[512]{0:T(512)}, u32[]{:S(2)}) copy-start(f32[512]{0:T(512)} %param.8) | copy-start | bytes 6148
  16.5 24.4 %copy-start.3 = (s32[8,4]{0,1:T(4,128)S(1)}, s32[8,4]{0,1:T(4,128)}, u32[]{:S(2)}) copy-start(s32[8,4]{0,1:T(4,128)} %param.9) | copy-start | bytes 388
  16.5 4.8 %collective-permute-start.4 = (bf16[448,128]{1,0:T(8,128)(2,1)S(1)}, bf16[448,128]{1,0:T(8,128)(2,1)S(1)}, u32[]{:S(2)}, u32[]{:S(2)}) collective-permute-start(bf16[448,128]{1,0:T(8,128)(2,1)S(1)} %collective-permute-done.2.x_f), channel_id=1, source_target_pairs={{0,4},{4,8},{8,12},{12,14},{14,10},{10,6},{6,2},{2,0},{1,5},{5,9},... | collective-permute-start | bytes 344072 | tf_op jit(solution)/shard_map/ppermute | solution.py:95
  16.6 4.8 %collective-permute-start.5 = (bf16[448,128]{1,0:T(8,128)(2,1)S(1)}, bf16[448,128]{1,0:T(8,128)(2,1)S(1)}, u32[]{:S(2)}, u32[]{:S(2)}) collective-permute-start(bf16[448,128]{1,0:T(8,128)(2,1)S(1)} %collective-permute-done.3.x_b), channel_id=1, source_target_pairs={{4,0},{8,4},{12,8},{14,12},{10,14},{6,10},{2,6},{0,2},{5,1},{9,5},... | collective-permute-start | bytes 344072 | tf_op jit(solution)/shard_map/ppermute | solution.py:96
  21.9 5.0 %collective-permute-start.10 = (bf16[128,512]{1,0:T(8,128)(2,1)S(1)}, bf16[128,512]{1,0:T(8,128)(2,1)S(1)}, u32[]{:S(2)}, u32[]{:S(2)}) collective-permute-start(bf16[128,512]{1,0:T(8,128)(2,1)S(1)} %shard_map.57.refs_0_.own), channel_id=1, source_target_pairs={{4,0},{8,4},{12,8},{14,12},{10,14},{6,10},{2,6},{0,2},{5,1},{9,5},... | collective-permute-start | bytes 393224 | tf_op jit(solution)/shard_map/ppermute | solution.py:91
  24.1 5.0 %collective-permute-start.8 = (bf16[128,512]{1,0:T(8,128)(2,1)S(1)}, bf16[128,512]{1,0:T(8,128)(2,1)S(1)}, u32[]{:S(2)}, u32[]{:S(2)}) collective-permute-start(bf16[128,512]{1,0:T(8,128)(2,1)S(1)} %shard_map.57.refs_0_.own), channel_id=1, source_target_pairs={{0,4},{4,8},{8,12},{12,14},{14,10},{10,6},{6,2},{2,0},{1,5},{5,9},... | collective-permute-start | bytes 393224 | tf_op jit(solution)/shard_map/ppermute | solution.py:90
  24.1 7.9 %collective-permute-start.7 = (bf16[128,512]{1,0:T(8,128)(2,1)S(1)}, bf16[128,512]{1,0:T(8,128)(2,1)S(1)}, u32[]{:S(2)}, u32[]{:S(2)}) collective-permute-start(bf16[128,512]{1,0:T(8,128)(2,1)S(1)} %shard_map.57.refs_0_.own), channel_id=1, source_target_pairs={{0,1},{1,0},{2,3},{3,2},{4,5},{5,4},{6,7},{7,6},{8,9},{9,8},{10,11... | collective-permute-start | bytes 393224 | tf_op jit(solution)/shard_map/ppermute | solution.py:245
  26.9 6.1 %collective-permute-start.11 = (bf16[128,512]{1,0:T(8,128)(2,1)S(1)}, bf16[128,512]{1,0:T(8,128)(2,1)S(1)}, u32[]{:S(2)}, u32[]{:S(2)}) collective-permute-start(bf16[128,512]{1,0:T(8,128)(2,1)S(1)} %collective-permute-done.10.refs_7_), channel_id=1, source_target_pairs={{4,0},{8,4},{12,8},{14,12},{10,14},{6,10},{2,6},{0,2},{5,1},{9,5},... | collective-permute-start | bytes 393224 | tf_op jit(solution)/shard_map/ppermute | solution.py:96
  29.1 6.8 %collective-permute-start.9 = (bf16[128,512]{1,0:T(8,128)(2,1)S(1)}, bf16[128,512]{1,0:T(8,128)(2,1)S(1)}, u32[]{:S(2)}, u32[]{:S(2)}) collective-permute-start(bf16[128,512]{1,0:T(8,128)(2,1)S(1)} %collective-permute-done.8.refs_1_), channel_id=1, source_target_pairs={{0,4},{4,8},{8,12},{12,14},{14,10},{10,6},{6,2},{2,0},{1,5},{5,9},... | collective-permute-start | bytes 393224 | tf_op jit(solution)/shard_map/ppermute | solution.py:95
  29.2 8.8 %collective-permute-start.13 = (bf16[128,512]{1,0:T(8,128)(2,1)S(1)}, bf16[128,512]{1,0:T(8,128)(2,1)S(1)}, u32[]{:S(2)}, u32[]{:S(2)}) collective-permute-start(bf16[128,512]{1,0:T(8,128)(2,1)S(1)} %select_select_fusion), channel_id=1, source_target_pairs={{0,14},{4,6},{8,10},{12,2},{14,0},{10,8},{6,4},{2,12},{1,15},{5,7}... | collective-permute-start | bytes 393224 | tf_op jit(solution)/shard_map/ppermute | solution.py:99
  35.9 5.0 %collective-permute-start.12 = (bf16[128,512]{1,0:T(8,128)(2,1)S(1)}, bf16[128,512]{1,0:T(8,128)(2,1)S(1)}, u32[]{:S(2)}, u32[]{:S(2)}) collective-permute-start(bf16[128,512]{1,0:T(8,128)(2,1)S(1)} %collective-permute-done.9.refs_2_), channel_id=1, source_target_pairs={{0,4},{4,8},{8,12},{12,14},{14,10},{10,6},{6,2},{2,0},{1,5},{5,9},... | collective-permute-start | bytes 393224 | tf_op jit(solution)/shard_map/ppermute | solution.py:95
  35.9 5.0 %collective-permute-start.14 = (bf16[128,512]{1,0:T(8,128)(2,1)S(1)}, bf16[128,512]{1,0:T(8,128)(2,1)S(1)}, u32[]{:S(2)}, u32[]{:S(2)}) collective-permute-start(bf16[128,512]{1,0:T(8,128)(2,1)S(1)} %collective-permute-done.11.refs_6_), channel_id=1, source_target_pairs={{4,0},{8,4},{12,8},{14,12},{10,14},{6,10},{2,6},{0,2},{5,1},{9,5},... | collective-permute-start | bytes 393224 | tf_op jit(solution)/shard_map/ppermute | solution.py:96
  41.7 1.8 %collective-permute-start.15 = (bf16[3,128,512]{2,1,0:T(8,128)(2,1)S(1)}, bf16[3,128,512]{2,1,0:T(8,128)(2,1)S(1)}, u32[]{:S(2)}, u32[]{:S(2)}) collective-permute-start(bf16[3,128,512]{2,1,0:T(8,128)(2,1)S(1)} %shard_map.58.got), channel_id=1, source_target_pairs={{0,1},{1,0},{2,3},{3,2},{4,5},{5,4},{6,7},{7,6},{8,9},{9,8},{10,11... | collective-permute-start | bytes 1179656 | tf_op jit(solution)/shard_map/ppermute | solution.py:262

commit v5 on v4

--- a/solution.py
+++ b/solution.py
@@ -44,23 +44,25 @@
     return lax.dot_general(x, w, rows_by_rows, preferred_element_type=jnp.float32)
 
 
-def first_step(x_f, x_b, weights, total):
+def on_corner(n):
+    return place_on_ring(lax.axis_index("lat"), n) % (n // 2) % (n // 2 - 1) == 0
+
+
+def first_step(hops, *refs):
+    xs, weights, total = refs[:-2], refs[-2], refs[-1]
     n = weights.shape[0]
-    total[...] = project(x_f[...], weights[origin(1, n)]) + project(x_b[...], weights[origin(-1, n)])
-
-
-def middle_step(hops, x, x_f, x_b, before, weights, total):
+    total[...] = project(xs[0][...], weights[origin(hops[0], n)])
+    for hop, x in zip(hops[1:], xs[1:]):
+        total[...] += project(x[...], weights[origin(hop, n)])
+
+
+def last_step(x, x_f, x_b, x_corner, x_middle, before, weights, bias, threshold, acts):
     n = weights.shape[0]
-    total[...] = before[...]
-    for hop, arrived in zip(hops, (x_f, x_b, x)):
-        total[...] += project(arrived[...], weights[origin(hop, n)])
-
-
-def last_step(hops, x_f, x_b, x_far, before, weights, bias, threshold, acts):
-    n = weights.shape[0]
+    hops = n // 2 - 1
+    x_far = jnp.where(on_corner(n), x_corner[...], x_middle[...])
     pre_acts = before[...] + bias[...]
-    for hop, arrived in zip(hops, (x_f, x_b, x_far)):
-        pre_acts = pre_acts + project(arrived[...], weights[origin(hop, n)])
+    for hop, part in ((0, x[...]), (hops, x_f[...]), (-hops, x_b[...]), (n // 2, x_far)):
+        pre_acts = pre_acts + project(part, weights[origin(hop, n)])
     acts[...] = activate(pre_acts, threshold[...])
 
 
@@ -76,71 +78,59 @@
     def __init__(self, n):
         walk = [block_at(i, n) for i in range(n)]
         self.n = n
-        self.hops = n // 2 - 1
         self.forward = [(walk[i], walk[(i + 1) % n]) for i in range(n)]
         self.backward = [(d, s) for s, d in self.forward]
-        mates = {i: (i + 4) % n if i % 4 in (0, 3) else n - 1 - i for i in range(n)}
-        self.across = [(walk[i], walk[mates[i]]) for i in range(n)]
-
-    def to_cross(self, x, ahead, behind):
-        place = place_on_ring(lax.axis_index("lat"), self.n) % 4
-        return jnp.where(place == 1, behind, jnp.where(place == 2, ahead, x))
-
-    def gather(self, x, arrived):
+        beside = [(i, n - 1 - i) for i in range(n) if i % 4 in (1, 2)]
+        across = [(i, (i + 4) % n) for i in range(n) if i % 4 in (0, 3)]
+        self.beside = [(walk[i], walk[j]) for i, j in beside]
+        self.across = [(walk[i], walk[j]) for i, j in across + beside]
+
+    def gather(self, x, beside_last):
         ahead = lax.ppermute(x, "lat", self.forward)
         behind = lax.ppermute(x, "lat", self.backward)
-        state = None
-        for hop in range(1, self.hops):
-            now_ahead, now_behind = ahead, behind
-            ahead = lax.ppermute(ahead, "lat", self.forward)
-            behind = lax.ppermute(behind, "lat", self.backward)
-            if hop == 1:
-                cross = self.to_cross(x, now_ahead, now_behind)
-                far = lax.ppermute(cross, "lat", self.across)
-            state = arrived(hop, now_ahead, now_behind, state)
-            if hop + 1 < self.hops:
-                state, ahead, behind = lax.optimization_barrier((state, ahead, behind))
-        return state, ahead, behind, far
+        corner = lax.ppermute(x, "lat", self.across)
+        ahead_2 = lax.ppermute(ahead, "lat", self.forward)
+        behind_2 = lax.ppermute(behind, "lat", self.backward)
+        odd = place_on_ring(lax.axis_index("lat"), self.n) % 2 == 1
+        middle = lax.ppermute(jnp.where(odd, behind, ahead), "lat", self.beside)
+        ahead_2, behind_2, corner = lax.optimization_barrier((ahead_2, behind_2, corner))
+        ahead_3 = lax.ppermute(ahead_2, "lat", self.forward)
+        behind_3 = lax.ppermute(behind_2, "lat", self.backward)
+        done = beside_last(x, ahead, behind, ahead_2, behind_2)
+        return done, ahead_3, behind_3, corner, middle
 
 
 def encode_on_ring(residual, enc_weight, enc_bias, threshold, ring):
     tok_rows, depth = residual.shape
     width = enc_weight.shape[1]
     n = ring.n
-    x = residual.T
     weights = enc_weight.reshape(n, depth, width)
-    total_shape = jax.ShapeDtypeStruct((tok_rows, width), jnp.float32)
-
-    def arrived(hop, ahead, behind, total):
-        if hop == 1:
-            kernel, operands = first_step, (ahead, behind, weights)
-        elif hop == 2:
-            kernel = functools.partial(middle_step, (2, -2, 0))
-            operands = (x, ahead, behind, total, weights)
-        else:
-            kernel = functools.partial(middle_step, (hop, -hop))
-            operands = (x, ahead, behind, total, weights)
+
+    def beside_last(_, *blocks):
         return pl.pallas_call(
-            kernel,
-            out_shape=total_shape,
-            in_specs=[in_vmem] * len(operands),
+            functools.partial(first_step, (1, -1, 2, -2)),
+            out_shape=jax.ShapeDtypeStruct((tok_rows, width), jnp.float32),
+            in_specs=[in_vmem] * (len(blocks) + 1),
             out_specs=in_vmem,
             compiler_params=params,
-            cost_estimate=cost(tok_rows, depth, width, 3),
-        )(*operands)
-
-    total, ahead, behind, far = ring.gather(x, arrived)
+            cost_estimate=cost(tok_rows, depth, width, 4),
+        )(*blocks, weights)
+
+    x = residual.T
+    total, ahead, behind, corner, middle = ring.gather(x, beside_last)
     return pl.pallas_call(
-        functools.partial(last_step, (ring.hops, -ring.hops, n // 2)),
+        last_step,
         out_shape=jax.ShapeDtypeStruct((tok_rows, width), jnp.bfloat16),
-        in_specs=[in_vmem] * 7,
+        in_specs=[in_vmem] * 9,
         out_specs=in_vmem,
         compiler_params=params,
-        cost_estimate=cost(tok_rows, depth, width, 3),
+        cost_estimate=cost(tok_rows, depth, width, 4),
     )(
+        x,
         ahead,
         behind,
-        far,
+        corner,
+        middle,
         total,
         weights,
         enc_bias.reshape(1, width),
@@ -160,23 +150,25 @@
     return activate(pre_acts, threshold)
 
 
-def choose_kernel(partners, *refs):
+def choose_kernel(hops, partners, *refs):
     blocks, chosen = refs[:-1], refs[-1]
-    n = len(blocks)
+    n = ring_size
     me = lax.axis_index("lat")
+    corner = on_corner(n)
     for k in range(chosen.shape[0]):
-        listed = partners[k + 1, me]
-        hop = lax.rem(place_on_ring(me, n) + n - place_on_ring(jnp.minimum(listed, n - 1), n), n)
-        for i, block in enumerate(blocks):
+        listed = jnp.minimum(partners[k + 1, me], n - 1)
+        hop = lax.rem(place_on_ring(me, n) + n - place_on_ring(listed, n), n)
+        hop = jnp.where((hop == n // 2) & jnp.logical_not(corner), n, hop)
+        for i, block in zip(hops, blocks):
 
             @pl.when(hop == i)
             def _():
                 chosen[k] = block[...]
 
 
-def choose(partners, blocks):
+def choose(partners, hops, blocks):
     return pl.pallas_call(
-        choose_kernel,
+        functools.partial(choose_kernel, hops),
         out_shape=jax.ShapeDtypeStruct((partners.shape[0] - 1,) + blocks[0].shape, blocks[0].dtype),
         in_specs=[in_smem] + [in_vmem] * len(blocks),
         out_specs=in_vmem,
@@ -243,15 +235,8 @@
         ring = Ring(n)
         acts = encode_on_ring(residual, enc_weight, enc_bias, threshold, ring)
         acts_twin = lax.ppermute(acts, "tok", swap)
-        blocks = {0: acts}
-
-        def arrived(hop, ahead, behind, state):
-            blocks[hop], blocks[n - hop] = ahead, behind
-            return acts_twin
-
-        acts_twin, ahead, behind, far = ring.gather(acts, arrived)
-        blocks[ring.hops], blocks[n - ring.hops], blocks[n // 2] = ahead, behind, far
-        got = choose(by_slot, [blocks[i] for i in range(n)])
+        early, *late = ring.gather(acts, lambda *blocks: blocks)
+        got = choose(by_slot, (0, 1, n - 1, 2, n - 2, 3, n - 3, 4, n), [*early, *late])
     else:
         acts = encode_gathered(residual, enc_weight, enc_bias, threshold)
         acts_twin = lax.ppermute(acts, "tok", swap)

time: 45.8 us -> 45.1 us (0.985)
  waiting for transfers between devices: 17.2 us -> 14 us
  starting transfers between devices: 21.3 us -> 24 us
  other arithmetic: 0.95 us -> 0.04 us
  local copies, waits for them, and re-layouts: 2.06 us -> 2.9 us
  Pallas kernels: 4.15 us -> 3.55 us
    ppermute x2, waiting for transfers between devices: 6.14 us -> 0.17 us  [gather(): behind = lax.ppermute(x, 'lat', self.backward)]
    ppermute x10 -> x12, waiting for transfers between devices: 9.25 us -> 12.5 us  [the longest x2 6.11 us: gather(): corner = lax.ppermute(x, 'lat', self.across)]
    ppermute x10 -> x12, starting transfers between devices: 15.9 us -> 18.2 us  [the longest x2 8.13 us: gather(): corner = lax.ppermute(x, 'lat', self.across)]
    ppermute x1, waiting for transfers between devices: 1.71 us -> 0.01 us  [body(): got_twin = lax.ppermute(got, 'tok', swap)]
    ppermute x1, waiting for transfers between devices: 0.01 us -> 1.4 us  [body(): acts_twin = lax.ppermute(acts, 'tok', swap)]
    ppermute x2, starting transfers between devices: 5.18 us -> 3.8 us  [gather(): behind = lax.ppermute(x, 'lat', self.backward)]
    ppermute x2, starting transfers between devices: 0.14 us -> 1.42 us  [gather(): ahead = lax.ppermute(x, 'lat', self.forward)]
    select_n x2, other arithmetic: 0.95 us -> 0.04 us  [gather(): middle = lax.ppermute(jnp.where(odd, behind, ahead), 'lat', self.beside)]
  transfers between devices with their start and end apart: 16 -> 18, of which waited for: 9 -> 10; matrix products, arithmetic and copies ran while one was open for 2% -> 0% of each run, Pallas kernels for 2% -> 1%
where the time goes in v5:
time: 45.1 us; the launch traced here: 44.6 us
  starting transfers between devices  24 us (53%)
  waiting for transfers between devices  14 us (31%)
  Pallas kernels  3.55 us (8%)
  local copies, waits for them, and re-layouts  2.9 us (6%)
    ppermute x2, starting transfers between devices, gather(): corner = lax.ppermute(x, 'lat', self.across)  8.13 us
    ppermute x2, waiting for transfers between devices, gather(): corner = lax.ppermute(x, 'lat', self.across)  6.11 us
    ppermute x2, starting transfers between devices, gather(): behind = lax.ppermute(x, 'lat', self.backward)  3.8 us
    ppermute x2, starting transfers between devices, gather(): ahead_2 = lax.ppermute(ahead, 'lat', self.forward)  3.5 us
    ppermute x2, starting transfers between devices, gather(): behind_3 = lax.ppermute(behind_2, 'lat', self.backward)  3.45 us
    ppermute x2, waiting for transfers between devices, gather(): ahead_3 = lax.ppermute(ahead_2, 'lat', self.forward)  3.19 us
    unnamed x12, local copies, waits for them, and re-layouts  2.9 us
    ppermute x2, waiting for transfers between devices, gather(): ahead_2 = lax.ppermute(ahead, 'lat', self.forward)  2.56 us
  transfers between devices with their start and end apart: 18, of which 10 were waited for; matrix products, arithmetic and copies ran while one was open for 0% of the time, Pallas kernels for 1%

profile of v5, /device:TPU:0, one launch (start us, length us, event | category | flops | bytes accessed | tf_op | source)
XLA Modules:
  0.0 44.6 jit_solution(6714770259781124574)
XLA Ops:
  0.0 0.0 copy-start.2
  0.0 0.0 copy-start.5
  0.0 3.0 %collective-permute-start.2 = (bf16[448,128]{1,0:T(8,128)(2,1)}, bf16[448,128]{1,0:T(8,128)(2,1)S(1)}, u32[]{:S(2)}, u32[]{:S(2)}) collective-permute-start(bf16[448,128]{1,0:T(8,128)(2,1)} %bitcast.7), channel_id=1, source_target_pairs={{4,0},{8,4},{12,8},{14,12},{10,14},{6,10},{2,6},{0,2},{5,1},{9,5},... | collective-permute-start | bytes 344072 | tf_op jit(solution)/shard_map/ppermute | solution.py:90
  3.0 0.1 collective-permute-start
  3.2 4.9 %collective-permute-start.4 = (bf16[448,128]{1,0:T(8,128)(2,1)}, bf16[448,128]{1,0:T(8,128)(2,1)S(1)}, u32[]{:S(2)}, u32[]{:S(2)}) collective-permute-start(bf16[448,128]{1,0:T(8,128)(2,1)} %bitcast.9), channel_id=1, source_target_pairs={{0,14},{12,2},{14,0},{2,12},{4,6},{8,10},{10,8},{6,4},{1,15},{13,3... | collective-permute-start | bytes 344072 | tf_op jit(solution)/shard_map/ppermute | solution.py:91
  8.1 0.0 collective-permute-done.2.refs_1_
  8.1 0.5 %collective-permute-start.3 = (bf16[448,128]{1,0:T(8,128)(2,1)S(1)}, bf16[448,128]{1,0:T(8,128)(2,1)S(1)}, u32[]{:S(2)}, u32[]{:S(2)}) collective-permute-start(bf16[448,128]{1,0:T(8,128)(2,1)S(1)} %collective-permute-done.2.refs_1_), channel_id=1, source_target_pairs={{4,0},{8,4},{12,8},{14,12},{10,14},{6,10},{2,6},{0,2},{5,1},{9,5},... | collective-permute-start | bytes 344072 | tf_op jit(solution)/shard_map/ppermute | solution.py:93
  8.6 0.0 collective-permute-done.refs_0_
  8.6 1.5 %collective-permute-start.1 = (bf16[448,128]{1,0:T(8,128)(2,1)S(1)}, bf16[448,128]{1,0:T(8,128)(2,1)S(1)}, u32[]{:S(2)}, u32[]{:S(2)}) collective-permute-start(bf16[448,128]{1,0:T(8,128)(2,1)S(1)} %collective-permute-done.refs_0_), channel_id=1, source_target_pairs={{0,4},{4,8},{8,12},{12,14},{14,10},{10,6},{6,2},{2,0},{1,5},{5,9},... | collective-permute-start | bytes 344072 | tf_op jit(solution)/shard_map/ppermute | solution.py:92
  10.1 0.7 %collective-permute-start.7 = (bf16[448,128]{1,0:T(8,128)(2,1)S(1)}, bf16[448,128]{1,0:T(8,128)(2,1)S(1)}, u32[]{:S(2)}, u32[]{:S(2)}) collective-permute-start(bf16[448,128]{1,0:T(8,128)(2,1)S(1)} %broadcast_select_fusion.1), channel_id=1, source_target_pairs={{4,6},{8,10},{10,8},{6,4},{5,7},{9,11},{11,9},{7,5},{20,22},{24,26... | collective-permute-start | bytes 344072 | tf_op jit(solution)/shard_map/ppermute | solution.py:95
  10.8 3.4 %collective-permute-done.4.x_corner = bf16[448,128]{1,0:T(8,128)(2,1)S(1)} collective-permute-done((bf16[448,128]{1,0:T(8,128)(2,1)}, bf16[448,128]{1,0:T(8,128)(2,1)S(1)}, u32[]{:S(2)}, u32[]{:S(2)}) %collective-permute-start.4) | collective-permute-done | bytes 114720 | tf_op jit(solution)/shard_map/ppermute | solution.py:91
  14.1 0.0 collective-permute-done.3.refs_3_
  14.1 0.5 %collective-permute-done.1.refs_2_ = bf16[448,128]{1,0:T(8,128)(2,1)S(1)} collective-permute-done((bf16[448,128]{1,0:T(8,128)(2,1)S(1)}, bf16[448,128]{1,0:T(8,128)(2,1)S(1)}, u32[]{:S(2)}, u32[]{:S(2)}) %collective-permute-start.1) | collective-permute-done | bytes 114720 | tf_op jit(solution)/shard_map/ppermute | solution.py:92
  14.6 0.5 %collective-permute-start.5 = (bf16[448,128]{1,0:T(8,128)(2,1)S(1)}, bf16[448,128]{1,0:T(8,128)(2,1)S(1)}, u32[]{:S(2)}, u32[]{:S(2)}) collective-permute-start(bf16[448,128]{1,0:T(8,128)(2,1)S(1)} %collective-permute-done.1.refs_2_), channel_id=1, source_target_pairs={{0,4},{4,8},{8,12},{12,14},{14,10},{10,6},{6,2},{2,0},{1,5},{5,9},... | collective-permute-start | bytes 344072 | tf_op jit(solution)/shard_map/ppermute | solution.py:97
  15.1 1.6 %collective-permute-start.6 = (bf16[448,128]{1,0:T(8,128)(2,1)S(1)}, bf16[448,128]{1,0:T(8,128)(2,1)S(1)}, u32[]{:S(2)}, u32[]{:S(2)}) collective-permute-start(bf16[448,128]{1,0:T(8,128)(2,1)S(1)} %collective-permute-done.3.refs_3_), channel_id=1, source_target_pairs={{4,0},{8,4},{12,8},{14,12},{10,14},{6,10},{2,6},{0,2},{5,1},{9,5},... | collective-permute-start | bytes 344072 | tf_op jit(solution)/shard_map/ppermute | solution.py:98
  16.7 2.0 %copy-done = bf16[3584,512]{1,0:T(8,128)(2,1)S(1)} copy-done((bf16[3584,512]{1,0:T(8,128)(2,1)S(1)}, bf16[3584,512]{1,0:T(8,128)(2,1)}, u32[]{:S(2)}) %copy-start) | copy-done | bytes 3670040
  18.7 0.5 %shard_map.55.before = f32[128,512]{1,0:T(8,128)S(1)} custom-call(bf16[448,128]{1,0:T(8,128)(2,1)S(1)} %collective-permute-done.refs_0_, bf16[448,128]{1,0:T(8,128)(2,1)S(1)} %collective-permute-done.2.refs_1_, bf16[448,128]{1,0:T(8,128)(2,1)S(1)} %collective-permute-done.1.refs_2_, bf16[448,128]{1,0:T(8,128)(2,1)S(1)} %collective-permute-done.3.refs_3_, ...), custom_call_target="tpu_custom_call" | custom-call | flops 234881024 | bytes 2818048 | tf_op jit(solution)/shard_map/pallas_call | solution.py:110
  19.2 0.0 collective-permute-done.7.x_middle
  19.2 0.2 collective-permute-done.5.x_f
  19.4 0.5 %collective-permute-done.6.x_b = bf16[448,128]{1,0:T(8,128)(2,1)S(1)} collective-permute-done((bf16[448,128]{1,0:T(8,128)(2,1)S(1)}, bf16[448,128]{1,0:T(8,128)(2,1)S(1)}, u32[]{:S(2)}, u32[]{:S(2)}) %collective-permute-start.6) | collective-permute-done | bytes 114720 | tf_op jit(solution)/shard_map/ppermute | solution.py:98
  19.9 0.0 copy-done.2
  19.9 0.0 copy-done.5
  19.9 0.0 copy-done.4
  19.9 0.8 %copy-done.1 = bf16[3584,512]{1,0:T(8,128)(2,1)S(1)} copy-done((bf16[3584,512]{1,0:T(8,128)(2,1)S(1)}, bf16[3584,512]{1,0:T(8,128)(2,1)}, u32[]{:S(2)}) %copy-start.1) | copy-done | bytes 3670040
  20.7 0.5 %shard_map.56.refs_0_.own = bf16[128,512]{1,0:T(8,128)(2,1)S(1)} custom-call(bf16[448,128]{1,0:T(8,128)(2,1)S(1)} %bitcast.10, bf16[448,128]{1,0:T(8,128)(2,1)S(1)} %collective-permute-done.5.x_f, bf16[448,128]{1,0:T(8,128)(2,1)S(1)} %collective-permute-done.6.x_b, bf16[448,128]{1,0:T(8,128)(2,1)S(1)} %collective-permute-done.4.x_corner, ...), custom_call_target="tpu_custom_call" | custom-call | flops 234881024 | bytes 2818048 | tf_op jit(solution)/shard_map/pallas_call | solution.py:121
  21.2 0.8 %collective-permute-start.10 = (bf16[128,512]{1,0:T(8,128)(2,1)S(1)}, bf16[128,512]{1,0:T(8,128)(2,1)S(1)}, u32[]{:S(2)}, u32[]{:S(2)}) collective-permute-start(bf16[128,512]{1,0:T(8,128)(2,1)S(1)} %shard_map.56.refs_0_.own), channel_id=1, source_target_pairs={{4,0},{8,4},{12,8},{14,12},{10,14},{6,10},{2,6},{0,2},{5,1},{9,5},... | collective-permute-start | bytes 393224 | tf_op jit(solution)/shard_map/ppermute | solution.py:90
  22.1 1.3 %collective-permute-start.9 = (bf16[128,512]{1,0:T(8,128)(2,1)S(1)}, bf16[128,512]{1,0:T(8,128)(2,1)S(1)}, u32[]{:S(2)}, u32[]{:S(2)}) collective-permute-start(bf16[128,512]{1,0:T(8,128)(2,1)S(1)} %shard_map.56.refs_0_.own), channel_id=1, source_target_pairs={{0,4},{4,8},{8,12},{12,14},{14,10},{10,6},{6,2},{2,0},{1,5},{5,9},... | collective-permute-start | bytes 393224 | tf_op jit(solution)/shard_map/ppermute | solution.py:89
  23.3 3.2 %collective-permute-start.13 = (bf16[128,512]{1,0:T(8,128)(2,1)S(1)}, bf16[128,512]{1,0:T(8,128)(2,1)S(1)}, u32[]{:S(2)}, u32[]{:S(2)}) collective-permute-start(bf16[128,512]{1,0:T(8,128)(2,1)S(1)} %shard_map.56.refs_0_.own), channel_id=1, source_target_pairs={{0,14},{12,2},{14,0},{2,12},{4,6},{8,10},{10,8},{6,4},{1,15},{13,3... | collective-permute-start | bytes 393224 | tf_op jit(solution)/shard_map/ppermute | solution.py:91
  26.5 0.2 collective-permute-done.10.refs_2_
  26.7 0.6 %collective-permute-start.12 = (bf16[128,512]{1,0:T(8,128)(2,1)S(1)}, bf16[128,512]{1,0:T(8,128)(2,1)S(1)}, u32[]{:S(2)}, u32[]{:S(2)}) collective-permute-start(bf16[128,512]{1,0:T(8,128)(2,1)S(1)} %collective-permute-done.10.refs_2_), channel_id=1, source_target_pairs={{4,0},{8,4},{12,8},{14,12},{10,14},{6,10},{2,6},{0,2},{5,1},{9,5},... | collective-permute-start | bytes 393224 | tf_op jit(solution)/shard_map/ppermute | solution.py:93
  27.3 0.0 collective-permute-done.9.refs_1_
  27.3 2.0 %collective-permute-start.11 = (bf16[128,512]{1,0:T(8,128)(2,1)S(1)}, bf16[128,512]{1,0:T(8,128)(2,1)S(1)}, u32[]{:S(2)}, u32[]{:S(2)}) collective-permute-start(bf16[128,512]{1,0:T(8,128)(2,1)S(1)} %collective-permute-done.9.refs_1_), channel_id=1, source_target_pairs={{0,4},{4,8},{8,12},{12,14},{14,10},{10,6},{6,2},{2,0},{1,5},{5,9},... | collective-permute-start | bytes 393224 | tf_op jit(solution)/shard_map/ppermute | solution.py:92
  29.3 0.7 %collective-permute-start.16 = (bf16[128,512]{1,0:T(8,128)(2,1)S(1)}, bf16[128,512]{1,0:T(8,128)(2,1)S(1)}, u32[]{:S(2)}, u32[]{:S(2)}) collective-permute-start(bf16[128,512]{1,0:T(8,128)(2,1)S(1)} %broadcast_select_fusion), channel_id=1, source_target_pairs={{4,6},{8,10},{10,8},{6,4},{5,7},{9,11},{11,9},{7,5},{20,22},{24,26... | collective-permute-start | bytes 393224 | tf_op jit(solution)/shard_map/ppermute | solution.py:95
  30.0 2.8 %collective-permute-done.13.refs_7_ = bf16[128,512]{1,0:T(8,128)(2,1)S(1)} collective-permute-done((bf16[128,512]{1,0:T(8,128)(2,1)S(1)}, bf16[128,512]{1,0:T(8,128)(2,1)S(1)}, u32[]{:S(2)}, u32[]{:S(2)}) %collective-permute-start.13) | collective-permute-done | bytes 131104 | tf_op jit(solution)/shard_map/ppermute | solution.py:91
  32.8 0.0 collective-permute-done.12.refs_4_
  32.8 2.1 %collective-permute-done.11.refs_3_ = bf16[128,512]{1,0:T(8,128)(2,1)S(1)} collective-permute-done((bf16[128,512]{1,0:T(8,128)(2,1)S(1)}, bf16[128,512]{1,0:T(8,128)(2,1)S(1)}, u32[]{:S(2)}, u32[]{:S(2)}) %collective-permute-start.11) | collective-permute-done | bytes 131104 | tf_op jit(solution)/shard_map/ppermute | solution.py:92
  34.8 0.2 collective-permute-start.14
  35.0 1.9 %collective-permute-start.15 = (bf16[128,512]{1,0:T(8,128)(2,1)S(1)}, bf16[128,512]{1,0:T(8,128)(2,1)S(1)}, u32[]{:S(2)}, u32[]{:S(2)}) collective-permute-start(bf16[128,512]{1,0:T(8,128)(2,1)S(1)} %collective-permute-done.12.refs_4_), channel_id=1, source_target_pairs={{4,0},{8,4},{12,8},{14,12},{10,14},{6,10},{2,6},{0,2},{5,1},{9,5},... | collective-permute-start | bytes 393224 | tf_op jit(solution)/shard_map/ppermute | solution.py:98
  36.9 0.0 collective-permute-done.16.refs_8_
  36.9 2.9 %collective-permute-done.14.refs_5_ = bf16[128,512]{1,0:T(8,128)(2,1)S(1)} collective-permute-done((bf16[128,512]{1,0:T(8,128)(2,1)S(1)}, bf16[128,512]{1,0:T(8,128)(2,1)S(1)}, u32[]{:S(2)}, u32[]{:S(2)}) %collective-permute-start.14) | collective-permute-done | bytes 131104 | tf_op jit(solution)/shard_map/ppermute | solution.py:97
  39.9 0.1 collective-permute-done.15.refs_6_
  40.0 0.0 copy-done.3
  40.0 0.8 %shard_map.57.got = bf16[3,128,512]{2,1,0:T(8,128)(2,1)S(1)} custom-call(s32[4,8]{1,0:T(4,128)S(1)} %bitcast.11, bf16[128,512]{1,0:T(8,128)(2,1)S(1)} %shard_map.56.refs_0_.own, bf16[128,512]{1,0:T(8,128)(2,1)S(1)} %collective-permute-done.9.refs_1_, bf16[128,512]{1,0:T(8,128)(2,1)S(1)} %collective-permute-done.10.refs_2_, ...), custom_call_target="tpu_custom_call" | custom-call | tf_op jit(solution)/shard_map/pallas_call | solution.py:170
  40.8 0.1 collective-permute-start.17
  40.9 0.5 %collective-permute-start.8 = (bf16[128,512]{1,0:T(8,128)(2,1)S(1)}, bf16[128,512]{1,0:T(8,128)(2,1)S(1)}, u32[]{:S(2)}, u32[]{:S(2)}) collective-permute-start(bf16[128,512]{1,0:T(8,128)(2,1)S(1)} %shard_map.56.refs_0_.own), channel_id=1, source_target_pairs={{0,1},{1,0},{2,3},{3,2},{4,5},{5,4},{6,7},{7,6},{8,9},{9,8},{10,11... | collective-permute-start | bytes 393224 | tf_op jit(solution)/shard_map/ppermute | solution.py:237
  41.4 1.4 %collective-permute-done.8.own_twin = bf16[128,512]{1,0:T(8,128)(2,1)S(1)} collective-permute-done((bf16[128,512]{1,0:T(8,128)(2,1)S(1)}, bf16[128,512]{1,0:T(8,128)(2,1)S(1)}, u32[]{:S(2)}, u32[]{:S(2)}) %collective-permute-start.8) | collective-permute-done | bytes 131104 | tf_op jit(solution)/shard_map/ppermute | solution.py:237
  42.8 0.0 collective-permute-done.17.got_twin
  42.8 1.8 %shard_map.58 = bf16[1,4,256,512]{3,2,1,0:T(8,128)(2,1)} custom-call(s32[4,8]{1,0:T(4,128)S(1)} %bitcast.12, bf16[128,512]{1,0:T(8,128)(2,1)S(1)} %shard_map.56.refs_0_.own, bf16[128,512]{1,0:T(8,128)(2,1)S(1)} %collective-permute-done.8.own_twin, bf16[3,128,512]{2,1,0:T(8,128)(2,1)S(1)} %shard_map.57.got, ...), custom_call_target="tpu_custom_call" | custom-call | tf_op jit(solution)/shard_map/pallas_call | solution.py:212
  (6 shorter events, 0.0 us)
Async XLA Ops:
  0.0 19.9 %copy-start.2 = (bf16[128,448]{0,1:T(8,128)(2,1)S(1)}, bf16[128,448]{0,1:T(8,128)(2,1)}, u32[]{:S(2)}) copy-start(bf16[128,448]{0,1:T(8,128)(2,1)} %param.5) | copy-start | bytes 344068
  0.0 19.9 %copy-start.5 = (f32[512]{0:T(512)S(1)}, f32[512]{0:T(512)}, u32[]{:S(2)}) copy-start(f32[512]{0:T(512)} %param.8) | copy-start | bytes 6148
  0.0 19.9 %copy-start.4 = (f32[512]{0:T(512)S(1)}, f32[512]{0:T(512)}, u32[]{:S(2)}) copy-start(f32[512]{0:T(512)} %param.7) | copy-start | bytes 6148
  0.0 8.1 %collective-permute-start.2 = (bf16[448,128]{1,0:T(8,128)(2,1)}, bf16[448,128]{1,0:T(8,128)(2,1)S(1)}, u32[]{:S(2)}, u32[]{:S(2)}) collective-permute-start(bf16[448,128]{1,0:T(8,128)(2,1)} %bitcast.7), channel_id=1, source_target_pairs={{4,0},{8,4},{12,8},{14,12},{10,14},{6,10},{2,6},{0,2},{5,1},{9,5},... | collective-permute-start | bytes 344072 | tf_op jit(solution)/shard_map/ppermute | solution.py:90
  3.0 5.6 %collective-permute-start = (bf16[448,128]{1,0:T(8,128)(2,1)}, bf16[448,128]{1,0:T(8,128)(2,1)S(1)}, u32[]{:S(2)}, u32[]{:S(2)}) collective-permute-start(bf16[448,128]{1,0:T(8,128)(2,1)} %bitcast.8), channel_id=1, source_target_pairs={{0,4},{4,8},{8,12},{12,14},{14,10},{10,6},{6,2},{2,0},{1,5},{5,9},... | collective-permute-start | bytes 344072 | tf_op jit(solution)/shard_map/ppermute | solution.py:89
  3.2 11.0 %collective-permute-start.4 = (bf16[448,128]{1,0:T(8,128)(2,1)}, bf16[448,128]{1,0:T(8,128)(2,1)S(1)}, u32[]{:S(2)}, u32[]{:S(2)}) collective-permute-start(bf16[448,128]{1,0:T(8,128)(2,1)} %bitcast.9), channel_id=1, source_target_pairs={{0,14},{12,2},{14,0},{2,12},{4,6},{8,10},{10,8},{6,4},{1,15},{13,3... | collective-permute-start | bytes 344072 | tf_op jit(solution)/shard_map/ppermute | solution.py:91
  8.1 6.1 %collective-permute-start.3 = (bf16[448,128]{1,0:T(8,128)(2,1)S(1)}, bf16[448,128]{1,0:T(8,128)(2,1)S(1)}, u32[]{:S(2)}, u32[]{:S(2)}) collective-permute-start(bf16[448,128]{1,0:T(8,128)(2,1)S(1)} %collective-permute-done.2.refs_1_), channel_id=1, source_target_pairs={{4,0},{8,4},{12,8},{14,12},{10,14},{6,10},{2,6},{0,2},{5,1},{9,5},... | collective-permute-start | bytes 344072 | tf_op jit(solution)/shard_map/ppermute | solution.py:93
  8.6 6.0 %collective-permute-start.1 = (bf16[448,128]{1,0:T(8,128)(2,1)S(1)}, bf16[448,128]{1,0:T(8,128)(2,1)S(1)}, u32[]{:S(2)}, u32[]{:S(2)}) collective-permute-start(bf16[448,128]{1,0:T(8,128)(2,1)S(1)} %collective-permute-done.refs_0_), channel_id=1, source_target_pairs={{0,4},{4,8},{8,12},{12,14},{14,10},{10,6},{6,2},{2,0},{1,5},{5,9},... | collective-permute-start | bytes 344072 | tf_op jit(solution)/shard_map/ppermute | solution.py:92
  10.1 9.1 %collective-permute-start.7 = (bf16[448,128]{1,0:T(8,128)(2,1)S(1)}, bf16[448,128]{1,0:T(8,128)(2,1)S(1)}, u32[]{:S(2)}, u32[]{:S(2)}) collective-permute-start(bf16[448,128]{1,0:T(8,128)(2,1)S(1)} %broadcast_select_fusion.1), channel_id=1, source_target_pairs={{4,6},{8,10},{10,8},{6,4},{5,7},{9,11},{11,9},{7,5},{20,22},{24,26... | collective-permute-start | bytes 344072 | tf_op jit(solution)/shard_map/ppermute | solution.py:95
  14.6 4.8 %collective-permute-start.5 = (bf16[448,128]{1,0:T(8,128)(2,1)S(1)}, bf16[448,128]{1,0:T(8,128)(2,1)S(1)}, u32[]{:S(2)}, u32[]{:S(2)}) collective-permute-start(bf16[448,128]{1,0:T(8,128)(2,1)S(1)} %collective-permute-done.1.refs_2_), channel_id=1, source_target_pairs={{0,4},{4,8},{8,12},{12,14},{14,10},{10,6},{6,2},{2,0},{1,5},{5,9},... | collective-permute-start | bytes 344072 | tf_op jit(solution)/shard_map/ppermute | solution.py:97
  15.1 4.8 %collective-permute-start.6 = (bf16[448,128]{1,0:T(8,128)(2,1)S(1)}, bf16[448,128]{1,0:T(8,128)(2,1)S(1)}, u32[]{:S(2)}, u32[]{:S(2)}) collective-permute-start(bf16[448,128]{1,0:T(8,128)(2,1)S(1)} %collective-permute-done.3.refs_3_), channel_id=1, source_target_pairs={{4,0},{8,4},{12,8},{14,12},{10,14},{6,10},{2,6},{0,2},{5,1},{9,5},... | collective-permute-start | bytes 344072 | tf_op jit(solution)/shard_map/ppermute | solution.py:98
  16.7 2.0 %copy-start = (bf16[3584,512]{1,0:T(8,128)(2,1)S(1)}, bf16[3584,512]{1,0:T(8,128)(2,1)}, u32[]{:S(2)}) copy-start(bf16[3584,512]{1,0:T(8,128)(2,1)} %param.6) | copy-start | bytes 11010052
  18.7 2.0 %copy-start.1 = (bf16[3584,512]{1,0:T(8,128)(2,1)S(1)}, bf16[3584,512]{1,0:T(8,128)(2,1)}, u32[]{:S(2)}) copy-start(bf16[3584,512]{1,0:T(8,128)(2,1)} %param.6) | copy-start | bytes 11010052
  18.7 21.3 %copy-start.3 = (s32[8,4]{0,1:T(4,128)S(1)}, s32[8,4]{0,1:T(4,128)}, u32[]{:S(2)}) copy-start(s32[8,4]{0,1:T(4,128)} %param.9) | copy-start | bytes 388
  21.2 5.5 %collective-permute-start.10 = (bf16[128,512]{1,0:T(8,128)(2,1)S(1)}, bf16[128,512]{1,0:T(8,128)(2,1)S(1)}, u32[]{:S(2)}, u32[]{:S(2)}) collective-permute-start(bf16[128,512]{1,0:T(8,128)(2,1)S(1)} %shard_map.56.refs_0_.own), channel_id=1, source_target_pairs={{4,0},{8,4},{12,8},{14,12},{10,14},{6,10},{2,6},{0,2},{5,1},{9,5},... | collective-permute-start | bytes 393224 | tf_op jit(solution)/shard_map/ppermute | solution.py:90
  22.1 5.2 %collective-permute-start.9 = (bf16[128,512]{1,0:T(8,128)(2,1)S(1)}, bf16[128,512]{1,0:T(8,128)(2,1)S(1)}, u32[]{:S(2)}, u32[]{:S(2)}) collective-permute-start(bf16[128,512]{1,0:T(8,128)(2,1)S(1)} %shard_map.56.refs_0_.own), channel_id=1, source_target_pairs={{0,4},{4,8},{8,12},{12,14},{14,10},{10,6},{6,2},{2,0},{1,5},{5,9},... | collective-permute-start | bytes 393224 | tf_op jit(solution)/shard_map/ppermute | solution.py:89
  23.3 9.4 %collective-permute-start.13 = (bf16[128,512]{1,0:T(8,128)(2,1)S(1)}, bf16[128,512]{1,0:T(8,128)(2,1)S(1)}, u32[]{:S(2)}, u32[]{:S(2)}) collective-permute-start(bf16[128,512]{1,0:T(8,128)(2,1)S(1)} %shard_map.56.refs_0_.own), channel_id=1, source_target_pairs={{0,14},{12,2},{14,0},{2,12},{4,6},{8,10},{10,8},{6,4},{1,15},{13,3... | collective-permute-start | bytes 393224 | tf_op jit(solution)/shard_map/ppermute | solution.py:91
  26.7 6.0 %collective-permute-start.12 = (bf16[128,512]{1,0:T(8,128)(2,1)S(1)}, bf16[128,512]{1,0:T(8,128)(2,1)S(1)}, u32[]{:S(2)}, u32[]{:S(2)}) collective-permute-start(bf16[128,512]{1,0:T(8,128)(2,1)S(1)} %collective-permute-done.10.refs_2_), channel_id=1, source_target_pairs={{4,0},{8,4},{12,8},{14,12},{10,14},{6,10},{2,6},{0,2},{5,1},{9,5},... | collective-permute-start | bytes 393224 | tf_op jit(solution)/shard_map/ppermute | solution.py:93
  27.3 7.5 %collective-permute-start.11 = (bf16[128,512]{1,0:T(8,128)(2,1)S(1)}, bf16[128,512]{1,0:T(8,128)(2,1)S(1)}, u32[]{:S(2)}, u32[]{:S(2)}) collective-permute-start(bf16[128,512]{1,0:T(8,128)(2,1)S(1)} %collective-permute-done.9.refs_1_), channel_id=1, source_target_pairs={{0,4},{4,8},{8,12},{12,14},{14,10},{10,6},{6,2},{2,0},{1,5},{5,9},... | collective-permute-start | bytes 393224 | tf_op jit(solution)/shard_map/ppermute | solution.py:92
  29.3 7.6 %collective-permute-start.16 = (bf16[128,512]{1,0:T(8,128)(2,1)S(1)}, bf16[128,512]{1,0:T(8,128)(2,1)S(1)}, u32[]{:S(2)}, u32[]{:S(2)}) collective-permute-start(bf16[128,512]{1,0:T(8,128)(2,1)S(1)} %broadcast_select_fusion), channel_id=1, source_target_pairs={{4,6},{8,10},{10,8},{6,4},{5,7},{9,11},{11,9},{7,5},{20,22},{24,26... | collective-permute-start | bytes 393224 | tf_op jit(solution)/shard_map/ppermute | solution.py:95
  34.8 5.0 %collective-permute-start.14 = (bf16[128,512]{1,0:T(8,128)(2,1)S(1)}, bf16[128,512]{1,0:T(8,128)(2,1)S(1)}, u32[]{:S(2)}, u32[]{:S(2)}) collective-permute-start(bf16[128,512]{1,0:T(8,128)(2,1)S(1)} %collective-permute-done.11.refs_3_), channel_id=1, source_target_pairs={{0,4},{4,8},{8,12},{12,14},{14,10},{10,6},{6,2},{2,0},{1,5},{5,9},... | collective-permute-start | bytes 393224 | tf_op jit(solution)/shard_map/ppermute | solution.py:97
  35.0 5.0 %collective-permute-start.15 = (bf16[128,512]{1,0:T(8,128)(2,1)S(1)}, bf16[128,512]{1,0:T(8,128)(2,1)S(1)}, u32[]{:S(2)}, u32[]{:S(2)}) collective-permute-start(bf16[128,512]{1,0:T(8,128)(2,1)S(1)} %collective-permute-done.12.refs_4_), channel_id=1, source_target_pairs={{4,0},{8,4},{12,8},{14,12},{10,14},{6,10},{2,6},{0,2},{5,1},{9,5},... | collective-permute-start | bytes 393224 | tf_op jit(solution)/shard_map/ppermute | solution.py:98
  40.8 2.0 %collective-permute-start.17 = (bf16[3,128,512]{2,1,0:T(8,128)(2,1)S(1)}, bf16[3,128,512]{2,1,0:T(8,128)(2,1)S(1)}, u32[]{:S(2)}, u32[]{:S(2)}) collective-permute-start(bf16[3,128,512]{2,1,0:T(8,128)(2,1)S(1)} %shard_map.57.got), channel_id=1, source_target_pairs={{0,1},{1,0},{2,3},{3,2},{4,5},{5,4},{6,7},{7,6},{8,9},{9,8},{10,11... | collective-permute-start | bytes 1179656 | tf_op jit(solution)/shard_map/ppermute | solution.py:247
  40.9 1.9 %collective-permute-start.8 = (bf16[128,512]{1,0:T(8,128)(2,1)S(1)}, bf16[128,512]{1,0:T(8,128)(2,1)S(1)}, u32[]{:S(2)}, u32[]{:S(2)}) collective-permute-start(bf16[128,512]{1,0:T(8,128)(2,1)S(1)} %shard_map.56.refs_0_.own), channel_id=1, source_target_pairs={{0,1},{1,0},{2,3},{3,2},{4,5},{5,4},{6,7},{7,6},{8,9},{9,8},{10,11... | collective-permute-start | bytes 393224 | tf_op jit(solution)/shard_map/ppermute | solution.py:237

commit v6 on v5

--- a/solution.py
+++ b/solution.py
@@ -85,7 +85,7 @@
         self.beside = [(walk[i], walk[j]) for i, j in beside]
         self.across = [(walk[i], walk[j]) for i, j in across + beside]
 
-    def gather(self, x, beside_last):
+    def gather(self, x, beside_second=None, beside_third=None):
         ahead = lax.ppermute(x, "lat", self.forward)
         behind = lax.ppermute(x, "lat", self.backward)
         corner = lax.ppermute(x, "lat", self.across)
@@ -93,10 +93,13 @@
         behind_2 = lax.ppermute(behind, "lat", self.backward)
         odd = place_on_ring(lax.axis_index("lat"), self.n) % 2 == 1
         middle = lax.ppermute(jnp.where(odd, behind, ahead), "lat", self.beside)
-        ahead_2, behind_2, corner = lax.optimization_barrier((ahead_2, behind_2, corner))
+        done = beside_second(ahead, behind) if beside_second else ()
+        ahead_2, behind_2, corner, done = lax.optimization_barrier(
+            (ahead_2, behind_2, corner, done)
+        )
         ahead_3 = lax.ppermute(ahead_2, "lat", self.forward)
         behind_3 = lax.ppermute(behind_2, "lat", self.backward)
-        done = beside_last(x, ahead, behind, ahead_2, behind_2)
+        done = beside_third(ahead, behind, ahead_2, behind_2, corner, done)
         return done, ahead_3, behind_3, corner, middle
 
 
@@ -106,7 +109,8 @@
     n = ring.n
     weights = enc_weight.reshape(n, depth, width)
 
-    def beside_last(_, *blocks):
+    def beside_third(*blocks):
+        blocks = blocks[:4]
         return pl.pallas_call(
             functools.partial(first_step, (1, -1, 2, -2)),
             out_shape=jax.ShapeDtypeStruct((tok_rows, width), jnp.float32),
@@ -117,7 +121,7 @@
         )(*blocks, weights)
 
     x = residual.T
-    total, ahead, behind, corner, middle = ring.gather(x, beside_last)
+    total, ahead, behind, corner, middle = ring.gather(x, beside_third=beside_third)
     return pl.pallas_call(
         last_step,
         out_shape=jax.ShapeDtypeStruct((tok_rows, width), jnp.bfloat16),
@@ -150,32 +154,6 @@
     return activate(pre_acts, threshold)
 
 
-def choose_kernel(hops, partners, *refs):
-    blocks, chosen = refs[:-1], refs[-1]
-    n = ring_size
-    me = lax.axis_index("lat")
-    corner = on_corner(n)
-    for k in range(chosen.shape[0]):
-        listed = jnp.minimum(partners[k + 1, me], n - 1)
-        hop = lax.rem(place_on_ring(me, n) + n - place_on_ring(listed, n), n)
-        hop = jnp.where((hop == n // 2) & jnp.logical_not(corner), n, hop)
-        for i, block in zip(hops, blocks):
-
-            @pl.when(hop == i)
-            def _():
-                chosen[k] = block[...]
-
-
-def choose(partners, hops, blocks):
-    return pl.pallas_call(
-        functools.partial(choose_kernel, hops),
-        out_shape=jax.ShapeDtypeStruct((partners.shape[0] - 1,) + blocks[0].shape, blocks[0].dtype),
-        in_specs=[in_smem] + [in_vmem] * len(blocks),
-        out_specs=in_vmem,
-        compiler_params=params,
-    )(partners, *blocks)
-
-
 def gram_kernel(tok_scale, n, partners, own, own_twin, got, got_twin, out, tiles, sems):
     slots, rows, width = tiles.shape
     me = lax.axis_index("lat")
@@ -222,6 +200,81 @@
     )(partners, own, own_twin, got, got_twin)
 
 
+def hop_of_slot(partners, k, n):
+    me = lax.axis_index("lat")
+    listed = partners[k, me]
+    hop = lax.rem(place_on_ring(me, n) + n - place_on_ring(jnp.minimum(listed, n - 1), n), n)
+    hop = jnp.where((hop == n // 2) & jnp.logical_not(on_corner(n)), n, hop)
+    return jnp.where(listed < n, hop, -1)
+
+
+def tiles_kernel(tok_scale, n, hops, is_first, partners, own, own_twin, *refs):
+    count = len(hops)
+    blocks, twins = refs[:count], refs[count : 2 * count]
+    out, tiles, sems = refs[-3:]
+    rows, width = tiles.shape[1:]
+    slots = partners.shape[0]
+    columns = pl.ds(pl.multiple_of(lax.axis_index("tok") * rows, rows), rows)
+    left = jnp.concatenate([own[:, columns], own_twin[:, columns]], axis=0)
+
+    def tile_of(right, right_twin):
+        tile = project(left, jnp.concatenate([right[...], right_twin[...]], axis=0))
+        return (tile * tok_scale).astype(tiles.dtype)
+
+    slot_hops = [hop_of_slot(partners, k, n) for k in range(1, slots)]
+    copies = []
+
+    def send(place, slot, when, value):
+        copy = pltpu.make_async_copy(tiles.at[place], out.at[0, slot], sems.at[len(copies)])
+        copies.append((copy, when))
+
+        @pl.when(when)
+        def _():
+            if value is not None:
+                tiles[place] = value()
+            copy.start()
+
+    if is_first:
+        always = lax.axis_index("lat") >= 0
+        send(count, 0, always, lambda: tile_of(own, own_twin))
+        tiles[count + 1] = jnp.zeros((rows, width), tiles.dtype)
+        for k, hop in enumerate(slot_hops):
+            send(count + 1, k + 1, hop < 0, None)
+    for j, hop in enumerate(hops):
+        slot = jnp.int32(0)
+        for k, h in enumerate(slot_hops):
+            slot = jnp.where(h == hop, jnp.int32(k + 1), slot)
+        send(j, slot, slot > 0, functools.partial(tile_of, blocks[j], twins[j]))
+    for copy, when in copies:
+        pl.when(when)(copy.wait)
+
+
+def tiles_of(partners, own, own_twin, hops, blocks, twins, before, tok_scale, halves, n):
+    width = own.shape[1]
+    slots = partners.shape[0]
+    rows = width // halves
+    first = before is None
+    operands = (partners, own, own_twin, *blocks, *twins) + (() if first else (before,))
+    specs = [in_smem] + [in_vmem] * (2 + 2 * len(hops)) + ([] if first else [in_hbm])
+    return pl.pallas_call(
+        functools.partial(tiles_kernel, tok_scale, n, hops, first),
+        out_shape=jax.ShapeDtypeStruct((1, slots, rows, width), own.dtype),
+        in_specs=specs,
+        out_specs=in_hbm,
+        input_output_aliases={} if first else {len(operands) - 1: 0},
+        scratch_shapes=[
+            pltpu.VMEM((len(hops) + (2 if first else 0), rows, width), own.dtype),
+            pltpu.SemaphoreType.DMA((len(hops) + (slots if first else 0),)),
+        ],
+        compiler_params=params,
+        cost_estimate=pl.CostEstimate(
+            flops=4 * rows * width * own.shape[0] * len(hops),
+            bytes_accessed=4 * rows * width * len(hops),
+            transcendentals=0,
+        ),
+    )(*operands)
+
+
 def body(residual, enc_weight, enc_bias, threshold, partners):
     n = lax.axis_size("lat")
     halves = lax.axis_size("tok")
@@ -235,15 +288,27 @@
         ring = Ring(n)
         acts = encode_on_ring(residual, enc_weight, enc_bias, threshold, ring)
         acts_twin = lax.ppermute(acts, "tok", swap)
-        early, *late = ring.gather(acts, lambda *blocks: blocks)
-        got = choose(by_slot, (0, 1, n - 1, 2, n - 2, 3, n - 3, 4, n), [*early, *late])
-    else:
-        acts = encode_gathered(residual, enc_weight, enc_bias, threshold)
-        acts_twin = lax.ppermute(acts, "tok", swap)
-        slices = lax.all_to_all(acts.reshape(n, tok_rows // n, width), "lat", 0, 0)
-        outgoing = jnp.take(slices, jnp.minimum(partners[:, 1:], n - 1), axis=0)
-        got = lax.all_to_all(outgoing, "lat", 0, 0)
-        got = got.transpose(1, 0, 2, 3).reshape(slots - 1, tok_rows, width)
+
+        def add_tiles(before, hops, blocks):
+            twins = [lax.ppermute(block, "tok", swap) for block in blocks]
+            return tiles_of(
+                by_slot, acts, acts_twin, hops, blocks, twins, before, tok_scale, halves, n
+            )
+
+        def beside_second(ahead, behind):
+            return add_tiles(None, (1, n - 1), (ahead, behind))
+
+        def beside_third(ahead, behind, ahead_2, behind_2, corner, before):
+            return add_tiles(before, (2, n - 2, n // 2), (ahead_2, behind_2, corner))
+
+        out, ahead, behind, _, middle = ring.gather(acts, beside_second, beside_third)
+        return add_tiles(out, (3, n - 3, n), (ahead, behind, middle))
+    acts = encode_gathered(residual, enc_weight, enc_bias, threshold)
+    acts_twin = lax.ppermute(acts, "tok", swap)
+    slices = lax.all_to_all(acts.reshape(n, tok_rows // n, width), "lat", 0, 0)
+    outgoing = jnp.take(slices, jnp.minimum(partners[:, 1:], n - 1), axis=0)
+    got = lax.all_to_all(outgoing, "lat", 0, 0)
+    got = got.transpose(1, 0, 2, 3).reshape(slots - 1, tok_rows, width)
     got_twin = lax.ppermute(got, "tok", swap)
     return gram(by_slot, acts, acts_twin, got, got_twin, tok_scale, halves, n)
 

time: 45.1 us -> 43.8 us (0.971)
  waiting for transfers between devices: 14 us -> 11.5 us
  Pallas kernels: 3.55 us -> 5.03 us
  local copies, waits for them, and re-layouts: 2.9 us -> 2.25 us
    ppermute x2, starting transfers between devices: 3.8 us -> 0.22 us  [gather(): behind = lax.ppermute(x, 'lat', self.backward)]
    ppermute x2, starting transfers between devices: 1.42 us -> 4.94 us  [gather(): ahead = lax.ppermute(x, 'lat', self.forward)]
    ppermute x2, waiting for transfers between devices: 6.11 us -> 2.61 us  [gather(): corner = lax.ppermute(x, 'lat', self.across)]
    ppermute x2, starting transfers between devices: 3.5 us -> 1.01 us  [gather(): ahead_2 = lax.ppermute(ahead, 'lat', self.forward)]
    ppermute x2, starting transfers between devices: 1.1 us -> 2.88 us  [gather(): behind_2 = lax.ppermute(behind, 'lat', self.backward)]
    pallas_call x3 -> x4, Pallas kernels: 3.06 us -> 4.54 us  [the longest x3 4.07 us: tiles_of(): pl.pallas_call(functools.partial(tiles_kernel, tok_scale, n, hops, first)...]
    ppermute x1, waiting for transfers between devices: 1.4 us -> 0.01 us  [body(): acts_twin = lax.ppermute(acts, 'tok', swap)]
    ppermute x2, starting transfers between devices: 3.45 us -> 2.2 us  [gather(): behind_3 = lax.ppermute(behind_2, 'lat', self.backward)]
  transfers between devices with their start and end apart: 18 -> 25, of which waited for: 10 -> 9; matrix products, arithmetic and copies ran while one was open for 0% -> 0% of each run, Pallas kernels for 1% -> 9%
where the time goes in v6:
time: 43.8 us; the launch traced here: 43 us
  starting transfers between devices  24.1 us (55%)
  waiting for transfers between devices  11.5 us (26%)
  Pallas kernels  5.03 us (11%)
  local copies, waits for them, and re-layouts  2.25 us (5%)
    ppermute x2, starting transfers between devices, gather(): corner = lax.ppermute(x, 'lat', self.across)  8.6 us
    ppermute x2, starting transfers between devices, gather(): ahead = lax.ppermute(x, 'lat', self.forward)  4.94 us
    pallas_call x3, Pallas kernels, tiles_of(): pl.pallas_call(functools.partial(tiles_kernel, tok_scale, n, hops, first)...  4.07 us
    ppermute x2, waiting for transfers between devices, gather(): ahead_2 = lax.ppermute(ahead, 'lat', self.forward)  3.53 us
    ppermute x2, waiting for transfers between devices, gather(): ahead_3 = lax.ppermute(ahead_2, 'lat', self.forward)  3.48 us
    ppermute x2, starting transfers between devices, gather(): behind_2 = lax.ppermute(behind, 'lat', self.backward)  2.88 us
    ppermute x2, waiting for transfers between devices, gather(): corner = lax.ppermute(x, 'lat', self.across)  2.61 us
    unnamed x12, local copies, waits for them, and re-layouts  2.25 us
  transfers between devices with their start and end apart: 25, of which 9 were waited for; matrix products, arithmetic and copies ran while one was open for 0% of the time, Pallas kernels for 9%

profile of v6, /device:TPU:0, one launch (start us, length us, event | category | flops | bytes accessed | tf_op | source)
XLA Modules:
  0.0 43.0 jit_solution(4959882410211587219)
XLA Ops:
  0.0 3.1 %collective-permute-start = (bf16[448,128]{1,0:T(8,128)(2,1)}, bf16[448,128]{1,0:T(8,128)(2,1)S(1)}, u32[]{:S(2)}, u32[]{:S(2)}) collective-permute-start(bf16[448,128]{1,0:T(8,128)(2,1)} %bitcast.7), channel_id=1, source_target_pairs={{0,4},{4,8},{8,12},{12,14},{14,10},{10,6},{6,2},{2,0},{1,5},{5,9},... | collective-permute-start | bytes 344072 | tf_op jit(solution)/shard_map/ppermute | solution.py:89
  3.1 5.0 %collective-permute-start.4 = (bf16[448,128]{1,0:T(8,128)(2,1)}, bf16[448,128]{1,0:T(8,128)(2,1)S(1)}, u32[]{:S(2)}, u32[]{:S(2)}) collective-permute-start(bf16[448,128]{1,0:T(8,128)(2,1)} %bitcast.9), channel_id=1, source_target_pairs={{0,14},{12,2},{14,0},{2,12},{4,6},{8,10},{10,8},{6,4},{1,15},{13,3... | collective-permute-start | bytes 344072 | tf_op jit(solution)/shard_map/ppermute | solution.py:91
  8.1 0.1 collective-permute-start.1
  8.2 0.0 collective-permute-done.2.refs_1_
  8.2 1.9 %collective-permute-start.3 = (bf16[448,128]{1,0:T(8,128)(2,1)S(1)}, bf16[448,128]{1,0:T(8,128)(2,1)S(1)}, u32[]{:S(2)}, u32[]{:S(2)}) collective-permute-start(bf16[448,128]{1,0:T(8,128)(2,1)S(1)} %collective-permute-done.2.refs_1_), channel_id=1, source_target_pairs={{4,0},{8,4},{12,8},{14,12},{10,14},{6,10},{2,6},{0,2},{5,1},{9,5},... | collective-permute-start | bytes 344072 | tf_op jit(solution)/shard_map/ppermute | solution.py:93
  10.1 0.7 %collective-permute-start.7 = (bf16[448,128]{1,0:T(8,128)(2,1)S(1)}, bf16[448,128]{1,0:T(8,128)(2,1)S(1)}, u32[]{:S(2)}, u32[]{:S(2)}) collective-permute-start(bf16[448,128]{1,0:T(8,128)(2,1)S(1)} %broadcast_select_fusion.1), channel_id=1, source_target_pairs={{4,6},{8,10},{10,8},{6,4},{5,7},{9,11},{11,9},{7,5},{20,22},{24,26... | collective-permute-start | bytes 344072 | tf_op jit(solution)/shard_map/ppermute | solution.py:95
  10.8 2.1 %collective-permute-done.4.x_corner = bf16[448,128]{1,0:T(8,128)(2,1)S(1)} collective-permute-done((bf16[448,128]{1,0:T(8,128)(2,1)}, bf16[448,128]{1,0:T(8,128)(2,1)S(1)}, u32[]{:S(2)}, u32[]{:S(2)}) %collective-permute-start.4) | collective-permute-done | bytes 114720 | tf_op jit(solution)/shard_map/ppermute | solution.py:91
  12.9 1.1 %collective-permute-done.1.refs_2_ = bf16[448,128]{1,0:T(8,128)(2,1)S(1)} collective-permute-done((bf16[448,128]{1,0:T(8,128)(2,1)S(1)}, bf16[448,128]{1,0:T(8,128)(2,1)S(1)}, u32[]{:S(2)}, u32[]{:S(2)}) %collective-permute-start.1) | collective-permute-done | bytes 114720 | tf_op jit(solution)/shard_map/ppermute | solution.py:92
  14.0 0.0 collective-permute-done.3.refs_3_
  14.0 1.1 %collective-permute-start.5 = (bf16[448,128]{1,0:T(8,128)(2,1)S(1)}, bf16[448,128]{1,0:T(8,128)(2,1)S(1)}, u32[]{:S(2)}, u32[]{:S(2)}) collective-permute-start(bf16[448,128]{1,0:T(8,128)(2,1)S(1)} %collective-permute-done.1.refs_2_), channel_id=1, source_target_pairs={{0,4},{4,8},{8,12},{12,14},{14,10},{10,6},{6,2},{2,0},{1,5},{5,9},... | collective-permute-start | bytes 344072 | tf_op jit(solution)/shard_map/ppermute | solution.py:100
  15.1 0.9 %collective-permute-start.6 = (bf16[448,128]{1,0:T(8,128)(2,1)S(1)}, bf16[448,128]{1,0:T(8,128)(2,1)S(1)}, u32[]{:S(2)}, u32[]{:S(2)}) collective-permute-start(bf16[448,128]{1,0:T(8,128)(2,1)S(1)} %collective-permute-done.3.refs_3_), channel_id=1, source_target_pairs={{4,0},{8,4},{12,8},{14,12},{10,14},{6,10},{2,6},{0,2},{5,1},{9,5},... | collective-permute-start | bytes 344072 | tf_op jit(solution)/shard_map/ppermute | solution.py:101
  16.0 2.0 %copy-done = bf16[3584,512]{1,0:T(8,128)(2,1)S(1)} copy-done((bf16[3584,512]{1,0:T(8,128)(2,1)S(1)}, bf16[3584,512]{1,0:T(8,128)(2,1)}, u32[]{:S(2)}) %copy-start) | copy-done | bytes 3670040
  18.1 0.5 %shard_map.55.before = f32[128,512]{1,0:T(8,128)S(1)} custom-call(bf16[448,128]{1,0:T(8,128)(2,1)S(1)} %collective-permute-done.refs_0_, bf16[448,128]{1,0:T(8,128)(2,1)S(1)} %collective-permute-done.2.refs_1_, bf16[448,128]{1,0:T(8,128)(2,1)S(1)} %collective-permute-done.1.refs_2_, bf16[448,128]{1,0:T(8,128)(2,1)S(1)} %collective-permute-done.3.refs_3_, ...), custom_call_target="tpu_custom_call" | custom-call | flops 234881024 | bytes 2818048 | tf_op jit(solution)/shard_map/pallas_call | solution.py:114
  18.6 0.0 collective-permute-done.7.x_middle
  18.6 0.2 collective-permute-done.5.x_f
  18.8 1.1 %collective-permute-done.6.x_b = bf16[448,128]{1,0:T(8,128)(2,1)S(1)} collective-permute-done((bf16[448,128]{1,0:T(8,128)(2,1)S(1)}, bf16[448,128]{1,0:T(8,128)(2,1)S(1)}, u32[]{:S(2)}, u32[]{:S(2)}) %collective-permute-start.6) | collective-permute-done | bytes 114720 | tf_op jit(solution)/shard_map/ppermute | solution.py:101
  19.9 0.2 copy-done.1
  20.1 0.5 %shard_map.56.own = bf16[128,512]{1,0:T(8,128)(2,1)S(1)} custom-call(bf16[448,128]{1,0:T(8,128)(2,1)S(1)} %bitcast.10, bf16[448,128]{1,0:T(8,128)(2,1)S(1)} %collective-permute-done.5.x_f, bf16[448,128]{1,0:T(8,128)(2,1)S(1)} %collective-permute-done.6.x_b, bf16[448,128]{1,0:T(8,128)(2,1)S(1)} %collective-permute-done.4.x_corner, ...), custom_call_target="tpu_custom_call" | custom-call | flops 234881024 | bytes 2818048 | tf_op jit(solution)/shard_map/pallas_call | solution.py:125
  20.6 1.9 %collective-permute-start.9 = (bf16[128,512]{1,0:T(8,128)(2,1)S(1)}, bf16[128,512]{1,0:T(8,128)(2,1)S(1)}, u32[]{:S(2)}, u32[]{:S(2)}) collective-permute-start(bf16[128,512]{1,0:T(8,128)(2,1)S(1)} %shard_map.56.own), channel_id=1, source_target_pairs={{0,4},{4,8},{8,12},{12,14},{14,10},{10,6},{6,2},{2,0},{1,5},{5,9},... | collective-permute-start | bytes 393224 | tf_op jit(solution)/shard_map/ppermute | solution.py:89
  22.5 0.2 collective-permute-start.11
  22.7 3.6 %collective-permute-start.13 = (bf16[128,512]{1,0:T(8,128)(2,1)S(1)}, bf16[128,512]{1,0:T(8,128)(2,1)S(1)}, u32[]{:S(2)}, u32[]{:S(2)}) collective-permute-start(bf16[128,512]{1,0:T(8,128)(2,1)S(1)} %shard_map.56.own), channel_id=1, source_target_pairs={{0,14},{12,2},{14,0},{2,12},{4,6},{8,10},{10,8},{6,4},{1,15},{13,3... | collective-permute-start | bytes 393224 | tf_op jit(solution)/shard_map/ppermute | solution.py:91
  26.3 0.2 collective-permute-start.14
  26.5 0.9 %collective-permute-start.10 = (bf16[128,512]{1,0:T(8,128)(2,1)S(1)}, bf16[128,512]{1,0:T(8,128)(2,1)S(1)}, u32[]{:S(2)}, u32[]{:S(2)}) collective-permute-start(bf16[128,512]{1,0:T(8,128)(2,1)S(1)} %collective-permute-done.9.refs_0_), channel_id=1, source_target_pairs={{0,4},{4,8},{8,12},{12,14},{14,10},{10,6},{6,2},{2,0},{1,5},{5,9},... | collective-permute-start | bytes 393224 | tf_op jit(solution)/shard_map/ppermute | solution.py:92
  27.4 0.0 collective-permute-done.11.refs_1_
  27.4 0.2 collective-permute-start.15
  27.7 0.0 collective-permute-done.8.own_twin
  27.7 1.0 %collective-permute-start.12 = (bf16[128,512]{1,0:T(8,128)(2,1)S(1)}, bf16[128,512]{1,0:T(8,128)(2,1)S(1)}, u32[]{:S(2)}, u32[]{:S(2)}) collective-permute-start(bf16[128,512]{1,0:T(8,128)(2,1)S(1)} %collective-permute-done.11.refs_1_), channel_id=1, source_target_pairs={{4,0},{8,4},{12,8},{14,12},{10,14},{6,10},{2,6},{0,2},{5,1},{9,5},... | collective-permute-start | bytes 393224 | tf_op jit(solution)/shard_map/ppermute | solution.py:93
  28.7 0.0 collective-permute-done.14.refs_2_
  28.7 0.7 %collective-permute-start.18 = (bf16[128,512]{1,0:T(8,128)(2,1)S(1)}, bf16[128,512]{1,0:T(8,128)(2,1)S(1)}, u32[]{:S(2)}, u32[]{:S(2)}) collective-permute-start(bf16[128,512]{1,0:T(8,128)(2,1)S(1)} %broadcast_select_fusion), channel_id=1, source_target_pairs={{4,6},{8,10},{10,8},{6,4},{5,7},{9,11},{11,9},{7,5},{20,22},{24,26... | collective-permute-start | bytes 393224 | tf_op jit(solution)/shard_map/ppermute | solution.py:95
  29.4 1.8 %shard_map.57.refs_6_ = bf16[1,4,256,512]{3,2,1,0:T(8,128)(2,1)} custom-call(s32[4,8]{1,0:T(4,128)S(1)} %bitcast.11, bf16[128,512]{1,0:T(8,128)(2,1)S(1)} %shard_map.56.own, bf16[128,512]{1,0:T(8,128)(2,1)S(1)} %collective-permute-done.8.own_twin, bf16[128,512]{1,0:T(8,128)(2,1)S(1)} %collective-permute-done.9.refs_0_, ...), custom_call_target="tpu_custom_call" | custom-call | flops 134217728 | bytes 1048576 | tf_op jit(solution)/shard_map/pallas_call | solution.py:259
  31.1 0.6 %collective-permute-done.13.refs_2_ = bf16[128,512]{1,0:T(8,128)(2,1)S(1)} collective-permute-done((bf16[128,512]{1,0:T(8,128)(2,1)S(1)}, bf16[128,512]{1,0:T(8,128)(2,1)S(1)}, u32[]{:S(2)}, u32[]{:S(2)}) %collective-permute-start.13) | collective-permute-done | bytes 131104 | tf_op jit(solution)/shard_map/ppermute | solution.py:91
  31.7 2.4 %collective-permute-done.10.refs_0_ = bf16[128,512]{1,0:T(8,128)(2,1)S(1)} collective-permute-done((bf16[128,512]{1,0:T(8,128)(2,1)S(1)}, bf16[128,512]{1,0:T(8,128)(2,1)S(1)}, u32[]{:S(2)}, u32[]{:S(2)}) %collective-permute-start.10) | collective-permute-done | bytes 131104 | tf_op jit(solution)/shard_map/ppermute | solution.py:92
  34.1 0.1 collective-permute-done.12.refs_1_
  34.2 0.0 collective-permute-start.22
  34.3 0.7 %collective-permute-start.16 = (bf16[128,512]{1,0:T(8,128)(2,1)S(1)}, bf16[128,512]{1,0:T(8,128)(2,1)S(1)}, u32[]{:S(2)}, u32[]{:S(2)}) collective-permute-start(bf16[128,512]{1,0:T(8,128)(2,1)S(1)} %collective-permute-done.10.refs_0_), channel_id=1, source_target_pairs={{0,4},{4,8},{8,12},{12,14},{14,10},{10,6},{6,2},{2,0},{1,5},{5,9},... | collective-permute-start | bytes 393224 | tf_op jit(solution)/shard_map/ppermute | solution.py:100
  35.0 1.3 %collective-permute-start.17 = (bf16[128,512]{1,0:T(8,128)(2,1)S(1)}, bf16[128,512]{1,0:T(8,128)(2,1)S(1)}, u32[]{:S(2)}, u32[]{:S(2)}) collective-permute-start(bf16[128,512]{1,0:T(8,128)(2,1)S(1)} %collective-permute-done.12.refs_1_), channel_id=1, source_target_pairs={{4,0},{8,4},{12,8},{14,12},{10,14},{6,10},{2,6},{0,2},{5,1},{9,5},... | collective-permute-start | bytes 393224 | tf_op jit(solution)/shard_map/ppermute | solution.py:101
  36.3 0.0 collective-permute-start.23
  36.3 0.0 collective-permute-done.18.refs_2_
  36.3 0.5 %collective-permute-start.24 = (bf16[128,512]{1,0:T(8,128)(2,1)S(1)}, bf16[128,512]{1,0:T(8,128)(2,1)S(1)}, u32[]{:S(2)}, u32[]{:S(2)}) collective-permute-start(bf16[128,512]{1,0:T(8,128)(2,1)S(1)} %collective-permute-done.13.refs_2_), channel_id=1, source_target_pairs={{0,1},{1,0},{2,3},{3,2},{4,5},{5,4},{6,7},{7,6},{8,9},{9,8},{10,11... | collective-permute-start | bytes 393224 | tf_op jit(solution)/shard_map/ppermute | solution.py:293
  36.8 0.1 collective-permute-start.21
  36.9 3.2 %collective-permute-done.16.refs_0_ = bf16[128,512]{1,0:T(8,128)(2,1)S(1)} collective-permute-done((bf16[128,512]{1,0:T(8,128)(2,1)S(1)}, bf16[128,512]{1,0:T(8,128)(2,1)S(1)}, u32[]{:S(2)}, u32[]{:S(2)}) %collective-permute-start.16) | collective-permute-done | bytes 131104 | tf_op jit(solution)/shard_map/ppermute | solution.py:100
  40.2 0.5 %collective-permute-done.17.refs_1_ = bf16[128,512]{1,0:T(8,128)(2,1)S(1)} collective-permute-done((bf16[128,512]{1,0:T(8,128)(2,1)S(1)}, bf16[128,512]{1,0:T(8,128)(2,1)S(1)}, u32[]{:S(2)}, u32[]{:S(2)}) %collective-permute-start.17) | collective-permute-done | bytes 131104 | tf_op jit(solution)/shard_map/ppermute | solution.py:101
  40.7 0.0 collective-permute-start.20
  40.7 0.0 collective-permute-done.23.refs_4_
  40.7 0.0 collective-permute-done.24.refs_5_
  40.7 1.6 %shard_map.58.refs_6_ = bf16[1,4,256,512]{3,2,1,0:T(8,128)(2,1)} custom-call(s32[4,8]{1,0:T(4,128)S(1)} %bitcast.12, bf16[128,512]{1,0:T(8,128)(2,1)S(1)} %shard_map.56.own, bf16[128,512]{1,0:T(8,128)(2,1)S(1)} %collective-permute-done.8.own_twin, bf16[128,512]{1,0:T(8,128)(2,1)S(1)} %collective-permute-done.10.refs_0_, ...), custom_call_target="tpu_custom_call", output_to_operand_aliasing={{}: (9, {})} | custom-call | flops 201326592 | bytes 1572864 | tf_op jit(solution)/shard_map/pallas_call | solution.py:259
  42.3 0.0 collective-permute-done.21.refs_5_
  42.3 0.7 %shard_map.59 = bf16[1,4,256,512]{3,2,1,0:T(8,128)(2,1)} custom-call(s32[4,8]{1,0:T(4,128)S(1)} %bitcast.13, bf16[128,512]{1,0:T(8,128)(2,1)S(1)} %shard_map.56.own, bf16[128,512]{1,0:T(8,128)(2,1)S(1)} %collective-permute-done.8.own_twin, bf16[128,512]{1,0:T(8,128)(2,1)S(1)} %collective-permute-done.16.refs_0_, ...), custom_call_target="tpu_custom_call", output_to_operand_aliasing={{}: (9, {})} | custom-call | flops 201326592 | bytes 1572864 | tf_op jit(solution)/shard_map/pallas_call | solution.py:259
  (21 shorter events, 0.1 us)
Async XLA Ops:
  0.0 19.9 %copy-start.2 = (bf16[128,448]{0,1:T(8,128)(2,1)S(1)}, bf16[128,448]{0,1:T(8,128)(2,1)}, u32[]{:S(2)}) copy-start(bf16[128,448]{0,1:T(8,128)(2,1)} %param.5) | copy-start | bytes 344068
  0.0 19.9 %copy-start.4 = (f32[512]{0:T(512)S(1)}, f32[512]{0:T(512)}, u32[]{:S(2)}) copy-start(f32[512]{0:T(512)} %param.7) | copy-start | bytes 6148
  0.0 19.9 %copy-start.5 = (f32[512]{0:T(512)S(1)}, f32[512]{0:T(512)}, u32[]{:S(2)}) copy-start(f32[512]{0:T(512)} %param.8) | copy-start | bytes 6148
  0.0 8.1 %collective-permute-start = (bf16[448,128]{1,0:T(8,128)(2,1)}, bf16[448,128]{1,0:T(8,128)(2,1)S(1)}, u32[]{:S(2)}, u32[]{:S(2)}) collective-permute-start(bf16[448,128]{1,0:T(8,128)(2,1)} %bitcast.7), channel_id=1, source_target_pairs={{0,4},{4,8},{8,12},{12,14},{14,10},{10,6},{6,2},{2,0},{1,5},{5,9},... | collective-permute-start | bytes 344072 | tf_op jit(solution)/shard_map/ppermute | solution.py:89
  3.1 5.1 %collective-permute-start.2 = (bf16[448,128]{1,0:T(8,128)(2,1)}, bf16[448,128]{1,0:T(8,128)(2,1)S(1)}, u32[]{:S(2)}, u32[]{:S(2)}) collective-permute-start(bf16[448,128]{1,0:T(8,128)(2,1)} %bitcast.8), channel_id=1, source_target_pairs={{4,0},{8,4},{12,8},{14,12},{10,14},{6,10},{2,6},{0,2},{5,1},{9,5},... | collective-permute-start | bytes 344072 | tf_op jit(solution)/shard_map/ppermute | solution.py:90
  3.1 9.8 %collective-permute-start.4 = (bf16[448,128]{1,0:T(8,128)(2,1)}, bf16[448,128]{1,0:T(8,128)(2,1)S(1)}, u32[]{:S(2)}, u32[]{:S(2)}) collective-permute-start(bf16[448,128]{1,0:T(8,128)(2,1)} %bitcast.9), channel_id=1, source_target_pairs={{0,14},{12,2},{14,0},{2,12},{4,6},{8,10},{10,8},{6,4},{1,15},{13,3... | collective-permute-start | bytes 344072 | tf_op jit(solution)/shard_map/ppermute | solution.py:91
  8.1 5.9 %collective-permute-start.1 = (bf16[448,128]{1,0:T(8,128)(2,1)S(1)}, bf16[448,128]{1,0:T(8,128)(2,1)S(1)}, u32[]{:S(2)}, u32[]{:S(2)}) collective-permute-start(bf16[448,128]{1,0:T(8,128)(2,1)S(1)} %collective-permute-done.refs_0_), channel_id=1, source_target_pairs={{0,4},{4,8},{8,12},{12,14},{14,10},{10,6},{6,2},{2,0},{1,5},{5,9},... | collective-permute-start | bytes 344072 | tf_op jit(solution)/shard_map/ppermute | solution.py:92
  8.2 5.8 %collective-permute-start.3 = (bf16[448,128]{1,0:T(8,128)(2,1)S(1)}, bf16[448,128]{1,0:T(8,128)(2,1)S(1)}, u32[]{:S(2)}, u32[]{:S(2)}) collective-permute-start(bf16[448,128]{1,0:T(8,128)(2,1)S(1)} %collective-permute-done.2.refs_1_), channel_id=1, source_target_pairs={{4,0},{8,4},{12,8},{14,12},{10,14},{6,10},{2,6},{0,2},{5,1},{9,5},... | collective-permute-start | bytes 344072 | tf_op jit(solution)/shard_map/ppermute | solution.py:93
  10.1 8.4 %collective-permute-start.7 = (bf16[448,128]{1,0:T(8,128)(2,1)S(1)}, bf16[448,128]{1,0:T(8,128)(2,1)S(1)}, u32[]{:S(2)}, u32[]{:S(2)}) collective-permute-start(bf16[448,128]{1,0:T(8,128)(2,1)S(1)} %broadcast_select_fusion.1), channel_id=1, source_target_pairs={{4,6},{8,10},{10,8},{6,4},{5,7},{9,11},{11,9},{7,5},{20,22},{24,26... | collective-permute-start | bytes 344072 | tf_op jit(solution)/shard_map/ppermute | solution.py:95
  14.0 4.8 %collective-permute-start.5 = (bf16[448,128]{1,0:T(8,128)(2,1)S(1)}, bf16[448,128]{1,0:T(8,128)(2,1)S(1)}, u32[]{:S(2)}, u32[]{:S(2)}) collective-permute-start(bf16[448,128]{1,0:T(8,128)(2,1)S(1)} %collective-permute-done.1.refs_2_), channel_id=1, source_target_pairs={{0,4},{4,8},{8,12},{12,14},{14,10},{10,6},{6,2},{2,0},{1,5},{5,9},... | collective-permute-start | bytes 344072 | tf_op jit(solution)/shard_map/ppermute | solution.py:100
  15.1 4.8 %collective-permute-start.6 = (bf16[448,128]{1,0:T(8,128)(2,1)S(1)}, bf16[448,128]{1,0:T(8,128)(2,1)S(1)}, u32[]{:S(2)}, u32[]{:S(2)}) collective-permute-start(bf16[448,128]{1,0:T(8,128)(2,1)S(1)} %collective-permute-done.3.refs_3_), channel_id=1, source_target_pairs={{4,0},{8,4},{12,8},{14,12},{10,14},{6,10},{2,6},{0,2},{5,1},{9,5},... | collective-permute-start | bytes 344072 | tf_op jit(solution)/shard_map/ppermute | solution.py:101
  16.0 2.0 %copy-start = (bf16[3584,512]{1,0:T(8,128)(2,1)S(1)}, bf16[3584,512]{1,0:T(8,128)(2,1)}, u32[]{:S(2)}) copy-start(bf16[3584,512]{1,0:T(8,128)(2,1)} %param.6) | copy-start | bytes 11010052
  18.1 2.0 %copy-start.1 = (bf16[3584,512]{1,0:T(8,128)(2,1)S(1)}, bf16[3584,512]{1,0:T(8,128)(2,1)}, u32[]{:S(2)}) copy-start(bf16[3584,512]{1,0:T(8,128)(2,1)} %param.6) | copy-start | bytes 11010052
  18.1 11.3 %copy-start.3 = (s32[8,4]{0,1:T(4,128)S(1)}, s32[8,4]{0,1:T(4,128)}, u32[]{:S(2)}) copy-start(s32[8,4]{0,1:T(4,128)} %param.9) | copy-start | bytes 388
  20.6 5.7 %collective-permute-start.9 = (bf16[128,512]{1,0:T(8,128)(2,1)S(1)}, bf16[128,512]{1,0:T(8,128)(2,1)S(1)}, u32[]{:S(2)}, u32[]{:S(2)}) collective-permute-start(bf16[128,512]{1,0:T(8,128)(2,1)S(1)} %shard_map.56.own), channel_id=1, source_target_pairs={{0,4},{4,8},{8,12},{12,14},{14,10},{10,6},{6,2},{2,0},{1,5},{5,9},... | collective-permute-start | bytes 393224 | tf_op jit(solution)/shard_map/ppermute | solution.py:89
  22.5 5.0 %collective-permute-start.11 = (bf16[128,512]{1,0:T(8,128)(2,1)S(1)}, bf16[128,512]{1,0:T(8,128)(2,1)S(1)}, u32[]{:S(2)}, u32[]{:S(2)}) collective-permute-start(bf16[128,512]{1,0:T(8,128)(2,1)S(1)} %shard_map.56.own), channel_id=1, source_target_pairs={{4,0},{8,4},{12,8},{14,12},{10,14},{6,10},{2,6},{0,2},{5,1},{9,5},... | collective-permute-start | bytes 393224 | tf_op jit(solution)/shard_map/ppermute | solution.py:90
  22.7 5.0 %collective-permute-start.8 = (bf16[128,512]{1,0:T(8,128)(2,1)S(1)}, bf16[128,512]{1,0:T(8,128)(2,1)S(1)}, u32[]{:S(2)}, u32[]{:S(2)}) collective-permute-start(bf16[128,512]{1,0:T(8,128)(2,1)S(1)} %shard_map.56.own), channel_id=1, source_target_pairs={{0,1},{1,0},{2,3},{3,2},{4,5},{5,4},{6,7},{7,6},{8,9},{9,8},{10,11... | collective-permute-start | bytes 393224 | tf_op jit(solution)/shard_map/ppermute | solution.py:290
  22.7 9.0 %collective-permute-start.13 = (bf16[128,512]{1,0:T(8,128)(2,1)S(1)}, bf16[128,512]{1,0:T(8,128)(2,1)S(1)}, u32[]{:S(2)}, u32[]{:S(2)}) collective-permute-start(bf16[128,512]{1,0:T(8,128)(2,1)S(1)} %shard_map.56.own), channel_id=1, source_target_pairs={{0,14},{12,2},{14,0},{2,12},{4,6},{8,10},{10,8},{6,4},{1,15},{13,3... | collective-permute-start | bytes 393224 | tf_op jit(solution)/shard_map/ppermute | solution.py:91
  26.3 2.3 %collective-permute-start.14 = (bf16[128,512]{1,0:T(8,128)(2,1)S(1)}, bf16[128,512]{1,0:T(8,128)(2,1)S(1)}, u32[]{:S(2)}, u32[]{:S(2)}) collective-permute-start(bf16[128,512]{1,0:T(8,128)(2,1)S(1)} %collective-permute-done.9.refs_0_), channel_id=1, source_target_pairs={{0,1},{1,0},{2,3},{3,2},{4,5},{5,4},{6,7},{7,6},{8,9},{9,8},{10,11... | collective-permute-start | bytes 393224 | tf_op jit(solution)/shard_map/ppermute | solution.py:293
  26.5 7.6 %collective-permute-start.10 = (bf16[128,512]{1,0:T(8,128)(2,1)S(1)}, bf16[128,512]{1,0:T(8,128)(2,1)S(1)}, u32[]{:S(2)}, u32[]{:S(2)}) collective-permute-start(bf16[128,512]{1,0:T(8,128)(2,1)S(1)} %collective-permute-done.9.refs_0_), channel_id=1, source_target_pairs={{0,4},{4,8},{8,12},{12,14},{14,10},{10,6},{6,2},{2,0},{1,5},{5,9},... | collective-permute-start | bytes 393224 | tf_op jit(solution)/shard_map/ppermute | solution.py:92
  27.4 1.9 %collective-permute-start.15 = (bf16[128,512]{1,0:T(8,128)(2,1)S(1)}, bf16[128,512]{1,0:T(8,128)(2,1)S(1)}, u32[]{:S(2)}, u32[]{:S(2)}) collective-permute-start(bf16[128,512]{1,0:T(8,128)(2,1)S(1)} %collective-permute-done.11.refs_1_), channel_id=1, source_target_pairs={{0,1},{1,0},{2,3},{3,2},{4,5},{5,4},{6,7},{7,6},{8,9},{9,8},{10,11... | collective-permute-start | bytes 393224 | tf_op jit(solution)/shard_map/ppermute | solution.py:293
  27.7 6.6 %collective-permute-start.12 = (bf16[128,512]{1,0:T(8,128)(2,1)S(1)}, bf16[128,512]{1,0:T(8,128)(2,1)S(1)}, u32[]{:S(2)}, u32[]{:S(2)}) collective-permute-start(bf16[128,512]{1,0:T(8,128)(2,1)S(1)} %collective-permute-done.11.refs_1_), channel_id=1, source_target_pairs={{4,0},{8,4},{12,8},{14,12},{10,14},{6,10},{2,6},{0,2},{5,1},{9,5},... | collective-permute-start | bytes 393224 | tf_op jit(solution)/shard_map/ppermute | solution.py:93
  28.7 7.7 %collective-permute-start.18 = (bf16[128,512]{1,0:T(8,128)(2,1)S(1)}, bf16[128,512]{1,0:T(8,128)(2,1)S(1)}, u32[]{:S(2)}, u32[]{:S(2)}) collective-permute-start(bf16[128,512]{1,0:T(8,128)(2,1)S(1)} %broadcast_select_fusion), channel_id=1, source_target_pairs={{4,6},{8,10},{10,8},{6,4},{5,7},{9,11},{11,9},{7,5},{20,22},{24,26... | collective-permute-start | bytes 393224 | tf_op jit(solution)/shard_map/ppermute | solution.py:95
  34.2 2.6 %collective-permute-start.22 = (bf16[128,512]{1,0:T(8,128)(2,1)S(1)}, bf16[128,512]{1,0:T(8,128)(2,1)S(1)}, u32[]{:S(2)}, u32[]{:S(2)}) collective-permute-start(bf16[128,512]{1,0:T(8,128)(2,1)S(1)} %collective-permute-done.10.refs_0_), channel_id=1, source_target_pairs={{0,1},{1,0},{2,3},{3,2},{4,5},{5,4},{6,7},{7,6},{8,9},{9,8},{10,11... | collective-permute-start | bytes 393224 | tf_op jit(solution)/shard_map/ppermute | solution.py:293
  34.3 5.9 %collective-permute-start.16 = (bf16[128,512]{1,0:T(8,128)(2,1)S(1)}, bf16[128,512]{1,0:T(8,128)(2,1)S(1)}, u32[]{:S(2)}, u32[]{:S(2)}) collective-permute-start(bf16[128,512]{1,0:T(8,128)(2,1)S(1)} %collective-permute-done.10.refs_0_), channel_id=1, source_target_pairs={{0,4},{4,8},{8,12},{12,14},{14,10},{10,6},{6,2},{2,0},{1,5},{5,9},... | collective-permute-start | bytes 393224 | tf_op jit(solution)/shard_map/ppermute | solution.py:100
  35.0 5.6 %collective-permute-start.17 = (bf16[128,512]{1,0:T(8,128)(2,1)S(1)}, bf16[128,512]{1,0:T(8,128)(2,1)S(1)}, u32[]{:S(2)}, u32[]{:S(2)}) collective-permute-start(bf16[128,512]{1,0:T(8,128)(2,1)S(1)} %collective-permute-done.12.refs_1_), channel_id=1, source_target_pairs={{4,0},{8,4},{12,8},{14,12},{10,14},{6,10},{2,6},{0,2},{5,1},{9,5},... | collective-permute-start | bytes 393224 | tf_op jit(solution)/shard_map/ppermute | solution.py:101
  36.3 4.4 %collective-permute-start.23 = (bf16[128,512]{1,0:T(8,128)(2,1)S(1)}, bf16[128,512]{1,0:T(8,128)(2,1)S(1)}, u32[]{:S(2)}, u32[]{:S(2)}) collective-permute-start(bf16[128,512]{1,0:T(8,128)(2,1)S(1)} %collective-permute-done.12.refs_1_), channel_id=1, source_target_pairs={{0,1},{1,0},{2,3},{3,2},{4,5},{5,4},{6,7},{7,6},{8,9},{9,8},{10,11... | collective-permute-start | bytes 393224 | tf_op jit(solution)/shard_map/ppermute | solution.py:293
  36.3 4.4 %collective-permute-start.24 = (bf16[128,512]{1,0:T(8,128)(2,1)S(1)}, bf16[128,512]{1,0:T(8,128)(2,1)S(1)}, u32[]{:S(2)}, u32[]{:S(2)}) collective-permute-start(bf16[128,512]{1,0:T(8,128)(2,1)S(1)} %collective-permute-done.13.refs_2_), channel_id=1, source_target_pairs={{0,1},{1,0},{2,3},{3,2},{4,5},{5,4},{6,7},{7,6},{8,9},{9,8},{10,11... | collective-permute-start | bytes 393224 | tf_op jit(solution)/shard_map/ppermute | solution.py:293
  36.8 5.5 %collective-permute-start.21 = (bf16[128,512]{1,0:T(8,128)(2,1)S(1)}, bf16[128,512]{1,0:T(8,128)(2,1)S(1)}, u32[]{:S(2)}, u32[]{:S(2)}) collective-permute-start(bf16[128,512]{1,0:T(8,128)(2,1)S(1)} %collective-permute-done.18.refs_2_), channel_id=1, source_target_pairs={{0,1},{1,0},{2,3},{3,2},{4,5},{5,4},{6,7},{7,6},{8,9},{9,8},{10,11... | collective-permute-start | bytes 393224 | tf_op jit(solution)/shard_map/ppermute | solution.py:293
  40.2 2.2 %collective-permute-start.19 = (bf16[128,512]{1,0:T(8,128)(2,1)S(1)}, bf16[128,512]{1,0:T(8,128)(2,1)S(1)}, u32[]{:S(2)}, u32[]{:S(2)}) collective-permute-start(bf16[128,512]{1,0:T(8,128)(2,1)S(1)} %collective-permute-done.16.refs_0_), channel_id=1, source_target_pairs={{0,1},{1,0},{2,3},{3,2},{4,5},{5,4},{6,7},{7,6},{8,9},{9,8},{10,11... | collective-permute-start | bytes 393224 | tf_op jit(solution)/shard_map/ppermute | solution.py:293
  40.7 1.7 %collective-permute-start.20 = (bf16[128,512]{1,0:T(8,128)(2,1)S(1)}, bf16[128,512]{1,0:T(8,128)(2,1)S(1)}, u32[]{:S(2)}, u32[]{:S(2)}) collective-permute-start(bf16[128,512]{1,0:T(8,128)(2,1)S(1)} %collective-permute-done.17.refs_1_), channel_id=1, source_target_pairs={{0,1},{1,0},{2,3},{3,2},{4,5},{5,4},{6,7},{7,6},{8,9},{9,8},{10,11... | collective-permute-start | bytes 393224 | tf_op jit(solution)/shard_map/ppermute | solution.py:293

commit v7 on v6

--- a/solution.py
+++ b/solution.py
@@ -44,10 +44,6 @@
     return lax.dot_general(x, w, rows_by_rows, preferred_element_type=jnp.float32)
 
 
-def on_corner(n):
-    return place_on_ring(lax.axis_index("lat"), n) % (n // 2) % (n // 2 - 1) == 0
-
-
 def first_step(hops, *refs):
     xs, weights, total = refs[:-2], refs[-2], refs[-1]
     n = weights.shape[0]
@@ -56,13 +52,12 @@
         total[...] += project(x[...], weights[origin(hop, n)])
 
 
-def last_step(x, x_f, x_b, x_corner, x_middle, before, weights, bias, threshold, acts):
+def last_step(x, x_f, x_b, x_far, before, weights, bias, threshold, acts):
     n = weights.shape[0]
     hops = n // 2 - 1
-    x_far = jnp.where(on_corner(n), x_corner[...], x_middle[...])
     pre_acts = before[...] + bias[...]
-    for hop, part in ((0, x[...]), (hops, x_f[...]), (-hops, x_b[...]), (n // 2, x_far)):
-        pre_acts = pre_acts + project(part, weights[origin(hop, n)])
+    for hop, part in ((0, x), (hops, x_f), (-hops, x_b), (n // 2, x_far)):
+        pre_acts = pre_acts + project(part[...], weights[origin(hop, n)])
     acts[...] = activate(pre_acts, threshold[...])
 
 
@@ -80,27 +75,21 @@
         self.n = n
         self.forward = [(walk[i], walk[(i + 1) % n]) for i in range(n)]
         self.backward = [(d, s) for s, d in self.forward]
-        beside = [(i, n - 1 - i) for i in range(n) if i % 4 in (1, 2)]
-        across = [(i, (i + 4) % n) for i in range(n) if i % 4 in (0, 3)]
-        self.beside = [(walk[i], walk[j]) for i, j in beside]
-        self.across = [(walk[i], walk[j]) for i, j in across + beside]
+        self.aslant = [(walk[i], walk[(i + (-2 if i % 4 < 2 else 2)) % n]) for i in range(n)]
 
     def gather(self, x, beside_second=None, beside_third=None):
         ahead = lax.ppermute(x, "lat", self.forward)
         behind = lax.ppermute(x, "lat", self.backward)
-        corner = lax.ppermute(x, "lat", self.across)
         ahead_2 = lax.ppermute(ahead, "lat", self.forward)
         behind_2 = lax.ppermute(behind, "lat", self.backward)
-        odd = place_on_ring(lax.axis_index("lat"), self.n) % 2 == 1
-        middle = lax.ppermute(jnp.where(odd, behind, ahead), "lat", self.beside)
         done = beside_second(ahead, behind) if beside_second else ()
-        ahead_2, behind_2, corner, done = lax.optimization_barrier(
-            (ahead_2, behind_2, corner, done)
-        )
+        ahead_2, behind_2, done = lax.optimization_barrier((ahead_2, behind_2, done))
         ahead_3 = lax.ppermute(ahead_2, "lat", self.forward)
         behind_3 = lax.ppermute(behind_2, "lat", self.backward)
-        done = beside_third(ahead, behind, ahead_2, behind_2, corner, done)
-        return done, ahead_3, behind_3, corner, middle
+        low = place_on_ring(lax.axis_index("lat"), self.n) % 4 < 2
+        far = lax.ppermute(jnp.where(low, behind_2, ahead_2), "lat", self.aslant)
+        done = beside_third(ahead, behind, ahead_2, behind_2, done)
+        return done, ahead_3, behind_3, far
 
 
 def encode_on_ring(residual, enc_weight, enc_bias, threshold, ring):
@@ -121,11 +110,11 @@
         )(*blocks, weights)
 
     x = residual.T
-    total, ahead, behind, corner, middle = ring.gather(x, beside_third=beside_third)
+    total, ahead, behind, far = ring.gather(x, beside_third=beside_third)
     return pl.pallas_call(
         last_step,
         out_shape=jax.ShapeDtypeStruct((tok_rows, width), jnp.bfloat16),
-        in_specs=[in_vmem] * 9,
+        in_specs=[in_vmem] * 8,
         out_specs=in_vmem,
         compiler_params=params,
         cost_estimate=cost(tok_rows, depth, width, 4),
@@ -133,8 +122,7 @@
         x,
         ahead,
         behind,
-        corner,
-        middle,
+        far,
         total,
         weights,
         enc_bias.reshape(1, width),
@@ -204,7 +192,6 @@
     me = lax.axis_index("lat")
     listed = partners[k, me]
     hop = lax.rem(place_on_ring(me, n) + n - place_on_ring(jnp.minimum(listed, n - 1), n), n)
-    hop = jnp.where((hop == n // 2) & jnp.logical_not(on_corner(n)), n, hop)
     return jnp.where(listed < n, hop, -1)
 
 
@@ -298,11 +285,11 @@
         def beside_second(ahead, behind):
             return add_tiles(None, (1, n - 1), (ahead, behind))
 
-        def beside_third(ahead, behind, ahead_2, behind_2, corner, before):
-            return add_tiles(before, (2, n - 2, n // 2), (ahead_2, behind_2, corner))
-
-        out, ahead, behind, _, middle = ring.gather(acts, beside_second, beside_third)
-        return add_tiles(out, (3, n - 3, n), (ahead, behind, middle))
+        def beside_third(ahead, behind, ahead_2, behind_2, before):
+            return add_tiles(before, (2, n - 2), (ahead_2, behind_2))
+
+        out, ahead, behind, far = ring.gather(acts, beside_second, beside_third)
+        return add_tiles(out, (3, n - 3, n // 2), (ahead, behind, far))
     acts = encode_gathered(residual, enc_weight, enc_bias, threshold)
     acts_twin = lax.ppermute(acts, "tok", swap)
     slices = lax.all_to_all(acts.reshape(n, tok_rows // n, width), "lat", 0, 0)

time: 43.8 us -> 46.8 us (1.068); the launches traced: 43 us -> 46.5 us
  waiting for transfers between devices: 11.5 us -> 20 us
  starting transfers between devices: 24.1 us -> 18.1 us
  Pallas kernels: 5.03 us -> 6.03 us
    ppermute x2, waiting for transfers between devices: 0.01 us -> 6.21 us  [gather(): ahead = lax.ppermute(x, 'lat', self.forward)]
    ppermute x4 -> x2, starting transfers between devices: 9.93 us -> 3.81 us  [gather(): far = lax.ppermute(jnp.where(low, behind_2, ahead_2), 'lat', self.aslant)]
    ppermute x2, waiting for transfers between devices: 0.18 us -> 3.82 us  [gather(): behind_2 = lax.ppermute(behind, 'lat', self.backward)]
    ppermute x2, starting transfers between devices: 1.01 us -> 3.52 us  [gather(): ahead_2 = lax.ppermute(ahead, 'lat', self.forward)]
    ppermute x2, starting transfers between devices: 2.88 us -> 0.53 us  [gather(): behind_2 = lax.ppermute(behind, 'lat', self.backward)]
    ppermute x2, waiting for transfers between devices: 0.01 us -> 1.85 us  [gather(): behind = lax.ppermute(x, 'lat', self.backward)]
    ppermute x2, waiting for transfers between devices: 1.61 us -> 0.38 us  [gather(): behind_3 = lax.ppermute(behind_2, 'lat', self.backward)]
    pallas_call x3, Pallas kernels: 4.07 us -> 5.07 us  [tiles_of(): pl.pallas_call(functools.partial(tiles_kernel, tok_scale, n, hops, first)...]
  transfers between devices with their start and end apart: 25 -> 22, of which waited for: 9 -> 10; matrix products, arithmetic and copies ran while one was open for 0% -> 0% of each run, Pallas kernels for 9% -> 8%
where the time goes in v7:
time: 46.8 us; the launch traced here: 46.5 us
  waiting for transfers between devices  20 us (43%)
  starting transfers between devices  18.1 us (39%)
  Pallas kernels  6.03 us (13%)
  local copies, waits for them, and re-layouts  2.22 us (5%)
    ppermute x2, waiting for transfers between devices, gather(): ahead = lax.ppermute(x, 'lat', self.forward)  6.21 us
    pallas_call x3, Pallas kernels, tiles_of(): pl.pallas_call(functools.partial(tiles_kernel, tok_scale, n, hops, first)...  5.07 us
    ppermute x2, starting transfers between devices, gather(): ahead = lax.ppermute(x, 'lat', self.forward)  4.98 us
    ppermute x2, waiting for transfers between devices, gather(): behind_2 = lax.ppermute(behind, 'lat', self.backward)  3.82 us
    ppermute x2, starting transfers between devices, gather(): far = lax.ppermute(jnp.where(low, behind_2, ahead_2), 'lat', self.aslant)  3.81 us
    ppermute x2, starting transfers between devices, gather(): ahead_2 = lax.ppermute(ahead, 'lat', self.forward)  3.52 us
    ppermute x2, starting transfers between devices, gather(): behind_3 = lax.ppermute(behind_2, 'lat', self.backward)  3.06 us
    ppermute x2, waiting for transfers between devices, gather(): ahead_2 = lax.ppermute(ahead, 'lat', self.forward)  2.76 us
  transfers between devices with their start and end apart: 22, of which 10 were waited for; matrix products, arithmetic and copies ran while one was open for 0% of the time, Pallas kernels for 8%

profile of v7, /device:TPU:0, one launch (start us, length us, event | category | flops | bytes accessed | tf_op | source)
XLA Modules:
  0.0 46.5 jit_solution(8316721808065524018)
XLA Ops:
  0.0 3.1 %collective-permute-start = (bf16[448,128]{1,0:T(8,128)(2,1)}, bf16[448,128]{1,0:T(8,128)(2,1)S(1)}, u32[]{:S(2)}, u32[]{:S(2)}) collective-permute-start(bf16[448,128]{1,0:T(8,128)(2,1)} %bitcast.7), channel_id=1, source_target_pairs={{0,4},{4,8},{8,12},{12,14},{14,10},{10,6},{6,2},{2,0},{1,5},{5,9},... | collective-permute-start | bytes 344072 | tf_op jit(solution)/shard_map/ppermute | solution.py:81
  3.1 0.0 collective-permute-start.2
  3.1 3.3 %collective-permute-done.refs_0_ = bf16[448,128]{1,0:T(8,128)(2,1)S(1)} collective-permute-done((bf16[448,128]{1,0:T(8,128)(2,1)}, bf16[448,128]{1,0:T(8,128)(2,1)S(1)}, u32[]{:S(2)}, u32[]{:S(2)}) %collective-permute-start) | collective-permute-done | bytes 114720 | tf_op jit(solution)/shard_map/ppermute | solution.py:81
  6.4 1.8 %collective-permute-start.1 = (bf16[448,128]{1,0:T(8,128)(2,1)S(1)}, bf16[448,128]{1,0:T(8,128)(2,1)S(1)}, u32[]{:S(2)}, u32[]{:S(2)}) collective-permute-start(bf16[448,128]{1,0:T(8,128)(2,1)S(1)} %collective-permute-done.refs_0_), channel_id=1, source_target_pairs={{0,4},{4,8},{8,12},{12,14},{14,10},{10,6},{6,2},{2,0},{1,5},{5,9},... | collective-permute-start | bytes 344072 | tf_op jit(solution)/shard_map/ppermute | solution.py:83
  8.2 0.0 collective-permute-done.2.refs_1_
  8.2 0.2 collective-permute-start.3
  8.4 2.8 %collective-permute-done.1.refs_2_ = bf16[448,128]{1,0:T(8,128)(2,1)S(1)} collective-permute-done((bf16[448,128]{1,0:T(8,128)(2,1)S(1)}, bf16[448,128]{1,0:T(8,128)(2,1)S(1)}, u32[]{:S(2)}, u32[]{:S(2)}) %collective-permute-start.1) | collective-permute-done | bytes 114720 | tf_op jit(solution)/shard_map/ppermute | solution.py:83
  11.2 1.8 %collective-permute-done.3.refs_3_ = bf16[448,128]{1,0:T(8,128)(2,1)S(1)} collective-permute-done((bf16[448,128]{1,0:T(8,128)(2,1)S(1)}, bf16[448,128]{1,0:T(8,128)(2,1)S(1)}, u32[]{:S(2)}, u32[]{:S(2)}) %collective-permute-start.3) | collective-permute-done | bytes 114720 | tf_op jit(solution)/shard_map/ppermute | solution.py:84
  13.0 1.4 %collective-permute-start.6 = (bf16[448,128]{1,0:T(8,128)(2,1)S(1)}, bf16[448,128]{1,0:T(8,128)(2,1)S(1)}, u32[]{:S(2)}, u32[]{:S(2)}) collective-permute-start(bf16[448,128]{1,0:T(8,128)(2,1)S(1)} %broadcast_select_fusion.1), channel_id=1, source_target_pairs={{0,6},{4,2},{8,14},{12,10},{14,8},{10,12},{6,0},{2,4},{1,7},{5,3},... | collective-permute-start | bytes 344072 | tf_op jit(solution)/shard_map/ppermute | solution.py:90
  14.4 0.3 collective-permute-start.4
  14.7 1.7 %collective-permute-start.5 = (bf16[448,128]{1,0:T(8,128)(2,1)S(1)}, bf16[448,128]{1,0:T(8,128)(2,1)S(1)}, u32[]{:S(2)}, u32[]{:S(2)}) collective-permute-start(bf16[448,128]{1,0:T(8,128)(2,1)S(1)} %collective-permute-done.3.refs_3_), channel_id=1, source_target_pairs={{4,0},{8,4},{12,8},{14,12},{10,14},{6,10},{2,6},{0,2},{5,1},{9,5},... | collective-permute-start | bytes 344072 | tf_op jit(solution)/shard_map/ppermute | solution.py:88
  16.5 2.0 %copy-done = bf16[3584,512]{1,0:T(8,128)(2,1)S(1)} copy-done((bf16[3584,512]{1,0:T(8,128)(2,1)S(1)}, bf16[3584,512]{1,0:T(8,128)(2,1)}, u32[]{:S(2)}) %copy-start) | copy-done | bytes 3670040
  18.5 0.5 shard_map.55.before
  19.0 0.0 collective-permute-done.6.x_far
  19.0 1.0 %collective-permute-done.4.x_f = bf16[448,128]{1,0:T(8,128)(2,1)S(1)} collective-permute-done((bf16[448,128]{1,0:T(8,128)(2,1)S(1)}, bf16[448,128]{1,0:T(8,128)(2,1)S(1)}, u32[]{:S(2)}, u32[]{:S(2)}) %collective-permute-start.4) | collective-permute-done | bytes 114720 | tf_op jit(solution)/shard_map/ppermute | solution.py:87
  20.0 0.4 collective-permute-done.5.x_b
  20.4 0.2 copy-done.1
  20.5 0.5 %shard_map.56.own = bf16[128,512]{1,0:T(8,128)(2,1)S(1)} custom-call(bf16[448,128]{1,0:T(8,128)(2,1)S(1)} %bitcast.9, bf16[448,128]{1,0:T(8,128)(2,1)S(1)} %collective-permute-done.4.x_f, bf16[448,128]{1,0:T(8,128)(2,1)S(1)} %collective-permute-done.5.x_b, bf16[448,128]{1,0:T(8,128)(2,1)S(1)} %collective-permute-done.6.x_far, ...), custom_call_target="tpu_custom_call" | custom-call | flops 234881024 | bytes 2818048 | tf_op jit(solution)/shard_map/pallas_call | solution.py:114
  21.1 1.9 %collective-permute-start.8 = (bf16[128,512]{1,0:T(8,128)(2,1)S(1)}, bf16[128,512]{1,0:T(8,128)(2,1)S(1)}, u32[]{:S(2)}, u32[]{:S(2)}) collective-permute-start(bf16[128,512]{1,0:T(8,128)(2,1)S(1)} %shard_map.56.own), channel_id=1, source_target_pairs={{0,4},{4,8},{8,12},{12,14},{14,10},{10,6},{6,2},{2,0},{1,5},{5,9},... | collective-permute-start | bytes 393224 | tf_op jit(solution)/shard_map/ppermute | solution.py:81
  23.0 0.2 collective-permute-start.10
  23.1 0.0 collective-permute-start.7
  23.1 2.9 %collective-permute-done.8.refs_0_ = bf16[128,512]{1,0:T(8,128)(2,1)S(1)} collective-permute-done((bf16[128,512]{1,0:T(8,128)(2,1)S(1)}, bf16[128,512]{1,0:T(8,128)(2,1)S(1)}, u32[]{:S(2)}, u32[]{:S(2)}) %collective-permute-start.8) | collective-permute-done | bytes 131104 | tf_op jit(solution)/shard_map/ppermute | solution.py:81
  26.1 0.0 collective-permute-start.12
  26.1 1.9 %collective-permute-done.10.refs_1_ = bf16[128,512]{1,0:T(8,128)(2,1)S(1)} collective-permute-done((bf16[128,512]{1,0:T(8,128)(2,1)S(1)}, bf16[128,512]{1,0:T(8,128)(2,1)S(1)}, u32[]{:S(2)}, u32[]{:S(2)}) %collective-permute-start.10) | collective-permute-done | bytes 131104 | tf_op jit(solution)/shard_map/ppermute | solution.py:82
  27.9 0.0 collective-permute-start.13
  27.9 0.3 collective-permute-start.11
  28.3 1.7 %collective-permute-start.9 = (bf16[128,512]{1,0:T(8,128)(2,1)S(1)}, bf16[128,512]{1,0:T(8,128)(2,1)S(1)}, u32[]{:S(2)}, u32[]{:S(2)}) collective-permute-start(bf16[128,512]{1,0:T(8,128)(2,1)S(1)} %collective-permute-done.8.refs_0_), channel_id=1, source_target_pairs={{0,4},{4,8},{8,12},{12,14},{14,10},{10,6},{6,2},{2,0},{1,5},{5,9},... | collective-permute-start | bytes 393224 | tf_op jit(solution)/shard_map/ppermute | solution.py:83
  30.0 0.0 collective-permute-done.7.own_twin
  30.0 0.0 collective-permute-done.12.refs_2_
  30.0 0.0 collective-permute-done.13.refs_3_
  30.0 1.9 %shard_map.57.refs_4_ = bf16[1,4,256,512]{3,2,1,0:T(8,128)(2,1)} custom-call(s32[4,8]{1,0:T(4,128)S(1)} %bitcast.10, bf16[128,512]{1,0:T(8,128)(2,1)S(1)} %shard_map.56.own, bf16[128,512]{1,0:T(8,128)(2,1)S(1)} %collective-permute-done.7.own_twin, bf16[128,512]{1,0:T(8,128)(2,1)S(1)} %collective-permute-done.8.refs_0_, ...), custom_call_target="tpu_custom_call" | custom-call | flops 134217728 | bytes 1048576 | tf_op jit(solution)/shard_map/pallas_call | solution.py:246
  31.8 2.0 %collective-permute-done.11.refs_1_ = bf16[128,512]{1,0:T(8,128)(2,1)S(1)} collective-permute-done((bf16[128,512]{1,0:T(8,128)(2,1)S(1)}, bf16[128,512]{1,0:T(8,128)(2,1)S(1)}, u32[]{:S(2)}, u32[]{:S(2)}) %collective-permute-start.11) | collective-permute-done | bytes 131104 | tf_op jit(solution)/shard_map/ppermute | solution.py:84
  33.8 0.0 collective-permute-done.9.refs_0_
  33.9 2.4 %collective-permute-start.16 = (bf16[128,512]{1,0:T(8,128)(2,1)S(1)}, bf16[128,512]{1,0:T(8,128)(2,1)S(1)}, u32[]{:S(2)}, u32[]{:S(2)}) collective-permute-start(bf16[128,512]{1,0:T(8,128)(2,1)S(1)} %broadcast_select_fusion), channel_id=1, source_target_pairs={{0,6},{4,2},{8,14},{12,10},{14,8},{10,12},{6,0},{2,4},{1,7},{5,3},... | collective-permute-start | bytes 393224 | tf_op jit(solution)/shard_map/ppermute | solution.py:90
  36.2 0.7 %collective-permute-start.14 = (bf16[128,512]{1,0:T(8,128)(2,1)S(1)}, bf16[128,512]{1,0:T(8,128)(2,1)S(1)}, u32[]{:S(2)}, u32[]{:S(2)}) collective-permute-start(bf16[128,512]{1,0:T(8,128)(2,1)S(1)} %collective-permute-done.9.refs_0_), channel_id=1, source_target_pairs={{0,4},{4,8},{8,12},{12,14},{14,10},{10,6},{6,2},{2,0},{1,5},{5,9},... | collective-permute-start | bytes 393224 | tf_op jit(solution)/shard_map/ppermute | solution.py:87
  36.9 1.3 %collective-permute-start.15 = (bf16[128,512]{1,0:T(8,128)(2,1)S(1)}, bf16[128,512]{1,0:T(8,128)(2,1)S(1)}, u32[]{:S(2)}, u32[]{:S(2)}) collective-permute-start(bf16[128,512]{1,0:T(8,128)(2,1)S(1)} %collective-permute-done.11.refs_1_), channel_id=1, source_target_pairs={{4,0},{8,4},{12,8},{14,12},{10,14},{6,10},{2,6},{0,2},{5,1},{9,5},... | collective-permute-start | bytes 393224 | tf_op jit(solution)/shard_map/ppermute | solution.py:88
  38.3 0.5 %collective-permute-start.21 = (bf16[128,512]{1,0:T(8,128)(2,1)S(1)}, bf16[128,512]{1,0:T(8,128)(2,1)S(1)}, u32[]{:S(2)}, u32[]{:S(2)}) collective-permute-start(bf16[128,512]{1,0:T(8,128)(2,1)S(1)} %collective-permute-done.11.refs_1_), channel_id=1, source_target_pairs={{0,1},{1,0},{2,3},{3,2},{4,5},{5,4},{6,7},{7,6},{8,9},{9,8},{10,11... | collective-permute-start | bytes 393224 | tf_op jit(solution)/shard_map/ppermute | solution.py:280
  38.8 2.5 %collective-permute-done.16.refs_2_ = bf16[128,512]{1,0:T(8,128)(2,1)S(1)} collective-permute-done((bf16[128,512]{1,0:T(8,128)(2,1)S(1)}, bf16[128,512]{1,0:T(8,128)(2,1)S(1)}, u32[]{:S(2)}, u32[]{:S(2)}) %collective-permute-start.16) | collective-permute-done | bytes 131104 | tf_op jit(solution)/shard_map/ppermute | solution.py:90
  41.2 1.5 %collective-permute-done.14.refs_0_ = bf16[128,512]{1,0:T(8,128)(2,1)S(1)} collective-permute-done((bf16[128,512]{1,0:T(8,128)(2,1)S(1)}, bf16[128,512]{1,0:T(8,128)(2,1)S(1)}, u32[]{:S(2)}, u32[]{:S(2)}) %collective-permute-start.14) | collective-permute-done | bytes 131104 | tf_op jit(solution)/shard_map/ppermute | solution.py:87
  42.8 0.0 collective-permute-start.17
  42.8 0.0 collective-permute-done.15.refs_1_
  42.8 0.5 %collective-permute-start.18 = (bf16[128,512]{1,0:T(8,128)(2,1)S(1)}, bf16[128,512]{1,0:T(8,128)(2,1)S(1)}, u32[]{:S(2)}, u32[]{:S(2)}) collective-permute-start(bf16[128,512]{1,0:T(8,128)(2,1)S(1)} %collective-permute-done.15.refs_1_), channel_id=1, source_target_pairs={{0,1},{1,0},{2,3},{3,2},{4,5},{5,4},{6,7},{7,6},{8,9},{9,8},{10,11... | collective-permute-start | bytes 393224 | tf_op jit(solution)/shard_map/ppermute | solution.py:280
  43.3 0.0 collective-permute-done.20.refs_2_
  43.3 0.0 collective-permute-done.21.refs_3_
  43.3 1.6 %shard_map.58.refs_6_ = bf16[1,4,256,512]{3,2,1,0:T(8,128)(2,1)} custom-call(s32[4,8]{1,0:T(4,128)S(1)} %bitcast.11, bf16[128,512]{1,0:T(8,128)(2,1)S(1)} %shard_map.56.own, bf16[128,512]{1,0:T(8,128)(2,1)S(1)} %collective-permute-done.7.own_twin, bf16[128,512]{1,0:T(8,128)(2,1)S(1)} %collective-permute-done.9.refs_0_, ...), custom_call_target="tpu_custom_call", output_to_operand_aliasing={{}: (7, {})} | custom-call | flops 134217728 | bytes 1048576 | tf_op jit(solution)/shard_map/pallas_call | solution.py:246
  44.9 0.0 collective-permute-done.19.refs_5_
  44.9 0.0 collective-permute-done.17.refs_3_
  44.9 1.6 %shard_map.59 = bf16[1,4,256,512]{3,2,1,0:T(8,128)(2,1)} custom-call(s32[4,8]{1,0:T(4,128)S(1)} %bitcast.12, bf16[128,512]{1,0:T(8,128)(2,1)S(1)} %shard_map.56.own, bf16[128,512]{1,0:T(8,128)(2,1)S(1)} %collective-permute-done.7.own_twin, bf16[128,512]{1,0:T(8,128)(2,1)S(1)} %collective-permute-done.14.refs_0_, ...), custom_call_target="tpu_custom_call", output_to_operand_aliasing={{}: (9, {})} | custom-call | flops 201326592 | bytes 1572864 | tf_op jit(solution)/shard_map/pallas_call | solution.py:246
  (15 shorter events, 0.1 us)
Async XLA Ops:
  0.0 20.4 %copy-start.2 = (bf16[128,448]{0,1:T(8,128)(2,1)S(1)}, bf16[128,448]{0,1:T(8,128)(2,1)}, u32[]{:S(2)}) copy-start(bf16[128,448]{0,1:T(8,128)(2,1)} %param.5) | copy-start | bytes 344068
  0.0 20.4 %copy-start.4 = (f32[512]{0:T(512)S(1)}, f32[512]{0:T(512)}, u32[]{:S(2)}) copy-start(f32[512]{0:T(512)} %param.7) | copy-start | bytes 6148
  0.0 20.4 %copy-start.5 = (f32[512]{0:T(512)S(1)}, f32[512]{0:T(512)}, u32[]{:S(2)}) copy-start(f32[512]{0:T(512)} %param.8) | copy-start | bytes 6148
  0.0 6.4 %collective-permute-start = (bf16[448,128]{1,0:T(8,128)(2,1)}, bf16[448,128]{1,0:T(8,128)(2,1)S(1)}, u32[]{:S(2)}, u32[]{:S(2)}) collective-permute-start(bf16[448,128]{1,0:T(8,128)(2,1)} %bitcast.7), channel_id=1, source_target_pairs={{0,4},{4,8},{8,12},{12,14},{14,10},{10,6},{6,2},{2,0},{1,5},{5,9},... | collective-permute-start | bytes 344072 | tf_op jit(solution)/shard_map/ppermute | solution.py:81
  3.1 5.1 %collective-permute-start.2 = (bf16[448,128]{1,0:T(8,128)(2,1)}, bf16[448,128]{1,0:T(8,128)(2,1)S(1)}, u32[]{:S(2)}, u32[]{:S(2)}) collective-permute-start(bf16[448,128]{1,0:T(8,128)(2,1)} %bitcast.8), channel_id=1, source_target_pairs={{4,0},{8,4},{12,8},{14,12},{10,14},{6,10},{2,6},{0,2},{5,1},{9,5},... | collective-permute-start | bytes 344072 | tf_op jit(solution)/shard_map/ppermute | solution.py:82
  6.4 4.8 %collective-permute-start.1 = (bf16[448,128]{1,0:T(8,128)(2,1)S(1)}, bf16[448,128]{1,0:T(8,128)(2,1)S(1)}, u32[]{:S(2)}, u32[]{:S(2)}) collective-permute-start(bf16[448,128]{1,0:T(8,128)(2,1)S(1)} %collective-permute-done.refs_0_), channel_id=1, source_target_pairs={{0,4},{4,8},{8,12},{12,14},{14,10},{10,6},{6,2},{2,0},{1,5},{5,9},... | collective-permute-start | bytes 344072 | tf_op jit(solution)/shard_map/ppermute | solution.py:83
  8.2 4.8 %collective-permute-start.3 = (bf16[448,128]{1,0:T(8,128)(2,1)S(1)}, bf16[448,128]{1,0:T(8,128)(2,1)S(1)}, u32[]{:S(2)}, u32[]{:S(2)}) collective-permute-start(bf16[448,128]{1,0:T(8,128)(2,1)S(1)} %collective-permute-done.2.refs_1_), channel_id=1, source_target_pairs={{4,0},{8,4},{12,8},{14,12},{10,14},{6,10},{2,6},{0,2},{5,1},{9,5},... | collective-permute-start | bytes 344072 | tf_op jit(solution)/shard_map/ppermute | solution.py:84
  13.0 6.0 %collective-permute-start.6 = (bf16[448,128]{1,0:T(8,128)(2,1)S(1)}, bf16[448,128]{1,0:T(8,128)(2,1)S(1)}, u32[]{:S(2)}, u32[]{:S(2)}) collective-permute-start(bf16[448,128]{1,0:T(8,128)(2,1)S(1)} %broadcast_select_fusion.1), channel_id=1, source_target_pairs={{0,6},{4,2},{8,14},{12,10},{14,8},{10,12},{6,0},{2,4},{1,7},{5,3},... | collective-permute-start | bytes 344072 | tf_op jit(solution)/shard_map/ppermute | solution.py:90
  14.4 5.5 %collective-permute-start.4 = (bf16[448,128]{1,0:T(8,128)(2,1)S(1)}, bf16[448,128]{1,0:T(8,128)(2,1)S(1)}, u32[]{:S(2)}, u32[]{:S(2)}) collective-permute-start(bf16[448,128]{1,0:T(8,128)(2,1)S(1)} %collective-permute-done.1.refs_2_), channel_id=1, source_target_pairs={{0,4},{4,8},{8,12},{12,14},{14,10},{10,6},{6,2},{2,0},{1,5},{5,9},... | collective-permute-start | bytes 344072 | tf_op jit(solution)/shard_map/ppermute | solution.py:87
  14.7 5.6 %collective-permute-start.5 = (bf16[448,128]{1,0:T(8,128)(2,1)S(1)}, bf16[448,128]{1,0:T(8,128)(2,1)S(1)}, u32[]{:S(2)}, u32[]{:S(2)}) collective-permute-start(bf16[448,128]{1,0:T(8,128)(2,1)S(1)} %collective-permute-done.3.refs_3_), channel_id=1, source_target_pairs={{4,0},{8,4},{12,8},{14,12},{10,14},{6,10},{2,6},{0,2},{5,1},{9,5},... | collective-permute-start | bytes 344072 | tf_op jit(solution)/shard_map/ppermute | solution.py:88
  16.5 2.0 %copy-start = (bf16[3584,512]{1,0:T(8,128)(2,1)S(1)}, bf16[3584,512]{1,0:T(8,128)(2,1)}, u32[]{:S(2)}) copy-start(bf16[3584,512]{1,0:T(8,128)(2,1)} %param.6) | copy-start | bytes 11010052
  18.5 2.0 %copy-start.1 = (bf16[3584,512]{1,0:T(8,128)(2,1)S(1)}, bf16[3584,512]{1,0:T(8,128)(2,1)}, u32[]{:S(2)}) copy-start(bf16[3584,512]{1,0:T(8,128)(2,1)} %param.6) | copy-start | bytes 11010052
  18.5 11.5 %copy-start.3 = (s32[8,4]{0,1:T(4,128)S(1)}, s32[8,4]{0,1:T(4,128)}, u32[]{:S(2)}) copy-start(s32[8,4]{0,1:T(4,128)} %param.9) | copy-start | bytes 388
  21.1 5.0 %collective-permute-start.8 = (bf16[128,512]{1,0:T(8,128)(2,1)S(1)}, bf16[128,512]{1,0:T(8,128)(2,1)S(1)}, u32[]{:S(2)}, u32[]{:S(2)}) collective-permute-start(bf16[128,512]{1,0:T(8,128)(2,1)S(1)} %shard_map.56.own), channel_id=1, source_target_pairs={{0,4},{4,8},{8,12},{12,14},{14,10},{10,6},{6,2},{2,0},{1,5},{5,9},... | collective-permute-start | bytes 393224 | tf_op jit(solution)/shard_map/ppermute | solution.py:81
  23.0 5.0 %collective-permute-start.10 = (bf16[128,512]{1,0:T(8,128)(2,1)S(1)}, bf16[128,512]{1,0:T(8,128)(2,1)S(1)}, u32[]{:S(2)}, u32[]{:S(2)}) collective-permute-start(bf16[128,512]{1,0:T(8,128)(2,1)S(1)} %shard_map.56.own), channel_id=1, source_target_pairs={{4,0},{8,4},{12,8},{14,12},{10,14},{6,10},{2,6},{0,2},{5,1},{9,5},... | collective-permute-start | bytes 393224 | tf_op jit(solution)/shard_map/ppermute | solution.py:82
  23.1 6.8 %collective-permute-start.7 = (bf16[128,512]{1,0:T(8,128)(2,1)S(1)}, bf16[128,512]{1,0:T(8,128)(2,1)S(1)}, u32[]{:S(2)}, u32[]{:S(2)}) collective-permute-start(bf16[128,512]{1,0:T(8,128)(2,1)S(1)} %shard_map.56.own), channel_id=1, source_target_pairs={{0,1},{1,0},{2,3},{3,2},{4,5},{5,4},{6,7},{7,6},{8,9},{9,8},{10,11... | collective-permute-start | bytes 393224 | tf_op jit(solution)/shard_map/ppermute | solution.py:277
  26.1 3.9 %collective-permute-start.12 = (bf16[128,512]{1,0:T(8,128)(2,1)S(1)}, bf16[128,512]{1,0:T(8,128)(2,1)S(1)}, u32[]{:S(2)}, u32[]{:S(2)}) collective-permute-start(bf16[128,512]{1,0:T(8,128)(2,1)S(1)} %collective-permute-done.8.refs_0_), channel_id=1, source_target_pairs={{0,1},{1,0},{2,3},{3,2},{4,5},{5,4},{6,7},{7,6},{8,9},{9,8},{10,11... | collective-permute-start | bytes 393224 | tf_op jit(solution)/shard_map/ppermute | solution.py:280
  27.9 2.0 %collective-permute-start.13 = (bf16[128,512]{1,0:T(8,128)(2,1)S(1)}, bf16[128,512]{1,0:T(8,128)(2,1)S(1)}, u32[]{:S(2)}, u32[]{:S(2)}) collective-permute-start(bf16[128,512]{1,0:T(8,128)(2,1)S(1)} %collective-permute-done.10.refs_1_), channel_id=1, source_target_pairs={{0,1},{1,0},{2,3},{3,2},{4,5},{5,4},{6,7},{7,6},{8,9},{9,8},{10,11... | collective-permute-start | bytes 393224 | tf_op jit(solution)/shard_map/ppermute | solution.py:280
  27.9 5.9 %collective-permute-start.11 = (bf16[128,512]{1,0:T(8,128)(2,1)S(1)}, bf16[128,512]{1,0:T(8,128)(2,1)S(1)}, u32[]{:S(2)}, u32[]{:S(2)}) collective-permute-start(bf16[128,512]{1,0:T(8,128)(2,1)S(1)} %collective-permute-done.10.refs_1_), channel_id=1, source_target_pairs={{4,0},{8,4},{12,8},{14,12},{10,14},{6,10},{2,6},{0,2},{5,1},{9,5},... | collective-permute-start | bytes 393224 | tf_op jit(solution)/shard_map/ppermute | solution.py:84
  28.3 5.6 %collective-permute-start.9 = (bf16[128,512]{1,0:T(8,128)(2,1)S(1)}, bf16[128,512]{1,0:T(8,128)(2,1)S(1)}, u32[]{:S(2)}, u32[]{:S(2)}) collective-permute-start(bf16[128,512]{1,0:T(8,128)(2,1)S(1)} %collective-permute-done.8.refs_0_), channel_id=1, source_target_pairs={{0,4},{4,8},{8,12},{12,14},{14,10},{10,6},{6,2},{2,0},{1,5},{5,9},... | collective-permute-start | bytes 393224 | tf_op jit(solution)/shard_map/ppermute | solution.py:83
  33.9 7.4 %collective-permute-start.16 = (bf16[128,512]{1,0:T(8,128)(2,1)S(1)}, bf16[128,512]{1,0:T(8,128)(2,1)S(1)}, u32[]{:S(2)}, u32[]{:S(2)}) collective-permute-start(bf16[128,512]{1,0:T(8,128)(2,1)S(1)} %broadcast_select_fusion), channel_id=1, source_target_pairs={{0,6},{4,2},{8,14},{12,10},{14,8},{10,12},{6,0},{2,4},{1,7},{5,3},... | collective-permute-start | bytes 393224 | tf_op jit(solution)/shard_map/ppermute | solution.py:90
  36.2 6.5 %collective-permute-start.14 = (bf16[128,512]{1,0:T(8,128)(2,1)S(1)}, bf16[128,512]{1,0:T(8,128)(2,1)S(1)}, u32[]{:S(2)}, u32[]{:S(2)}) collective-permute-start(bf16[128,512]{1,0:T(8,128)(2,1)S(1)} %collective-permute-done.9.refs_0_), channel_id=1, source_target_pairs={{0,4},{4,8},{8,12},{12,14},{14,10},{10,6},{6,2},{2,0},{1,5},{5,9},... | collective-permute-start | bytes 393224 | tf_op jit(solution)/shard_map/ppermute | solution.py:87
  36.9 5.8 %collective-permute-start.15 = (bf16[128,512]{1,0:T(8,128)(2,1)S(1)}, bf16[128,512]{1,0:T(8,128)(2,1)S(1)}, u32[]{:S(2)}, u32[]{:S(2)}) collective-permute-start(bf16[128,512]{1,0:T(8,128)(2,1)S(1)} %collective-permute-done.11.refs_1_), channel_id=1, source_target_pairs={{4,0},{8,4},{12,8},{14,12},{10,14},{6,10},{2,6},{0,2},{5,1},{9,5},... | collective-permute-start | bytes 393224 | tf_op jit(solution)/shard_map/ppermute | solution.py:88
  38.3 5.0 %collective-permute-start.20 = (bf16[128,512]{1,0:T(8,128)(2,1)S(1)}, bf16[128,512]{1,0:T(8,128)(2,1)S(1)}, u32[]{:S(2)}, u32[]{:S(2)}) collective-permute-start(bf16[128,512]{1,0:T(8,128)(2,1)S(1)} %collective-permute-done.9.refs_0_), channel_id=1, source_target_pairs={{0,1},{1,0},{2,3},{3,2},{4,5},{5,4},{6,7},{7,6},{8,9},{9,8},{10,11... | collective-permute-start | bytes 393224 | tf_op jit(solution)/shard_map/ppermute | solution.py:280
  38.3 5.0 %collective-permute-start.21 = (bf16[128,512]{1,0:T(8,128)(2,1)S(1)}, bf16[128,512]{1,0:T(8,128)(2,1)S(1)}, u32[]{:S(2)}, u32[]{:S(2)}) collective-permute-start(bf16[128,512]{1,0:T(8,128)(2,1)S(1)} %collective-permute-done.11.refs_1_), channel_id=1, source_target_pairs={{0,1},{1,0},{2,3},{3,2},{4,5},{5,4},{6,7},{7,6},{8,9},{9,8},{10,11... | collective-permute-start | bytes 393224 | tf_op jit(solution)/shard_map/ppermute | solution.py:280
  41.2 3.7 %collective-permute-start.19 = (bf16[128,512]{1,0:T(8,128)(2,1)S(1)}, bf16[128,512]{1,0:T(8,128)(2,1)S(1)}, u32[]{:S(2)}, u32[]{:S(2)}) collective-permute-start(bf16[128,512]{1,0:T(8,128)(2,1)S(1)} %collective-permute-done.16.refs_2_), channel_id=1, source_target_pairs={{0,1},{1,0},{2,3},{3,2},{4,5},{5,4},{6,7},{7,6},{8,9},{9,8},{10,11... | collective-permute-start | bytes 393224 | tf_op jit(solution)/shard_map/ppermute | solution.py:280
  42.8 2.1 %collective-permute-start.17 = (bf16[128,512]{1,0:T(8,128)(2,1)S(1)}, bf16[128,512]{1,0:T(8,128)(2,1)S(1)}, u32[]{:S(2)}, u32[]{:S(2)}) collective-permute-start(bf16[128,512]{1,0:T(8,128)(2,1)S(1)} %collective-permute-done.14.refs_0_), channel_id=1, source_target_pairs={{0,1},{1,0},{2,3},{3,2},{4,5},{5,4},{6,7},{7,6},{8,9},{9,8},{10,11... | collective-permute-start | bytes 393224 | tf_op jit(solution)/shard_map/ppermute | solution.py:280
  42.8 2.1 %collective-permute-start.18 = (bf16[128,512]{1,0:T(8,128)(2,1)S(1)}, bf16[128,512]{1,0:T(8,128)(2,1)S(1)}, u32[]{:S(2)}, u32[]{:S(2)}) collective-permute-start(bf16[128,512]{1,0:T(8,128)(2,1)S(1)} %collective-permute-done.15.refs_1_), channel_id=1, source_target_pairs={{0,1},{1,0},{2,3},{3,2},{4,5},{5,4},{6,7},{7,6},{8,9},{9,8},{10,11... | collective-permute-start | bytes 393224 | tf_op jit(solution)/shard_map/ppermute | solution.py:280

commit v8 on v6

--- a/solution.py
+++ b/solution.py
@@ -14,6 +14,7 @@
 in_smem = pl.BlockSpec(memory_space=pltpu.SMEM)
 in_hbm = pl.BlockSpec(memory_space=pltpu.HBM)
 params = pltpu.CompilerParams(vmem_limit_bytes=24 * 1024 * 1024)
+streaming_params = pltpu.CompilerParams(vmem_limit_bytes=53000000)
 
 rows_by_rows = (((0,), (0,)), ((), ()))
 
@@ -48,21 +49,29 @@
     return place_on_ring(lax.axis_index("lat"), n) % (n // 2) % (n // 2 - 1) == 0
 
 
-def first_step(hops, *refs):
-    xs, weights, total = refs[:-2], refs[-2], refs[-1]
+def first_step(hops, later, *refs):
+    xs, (weights, total, kept, blocks, sems) = refs[:-5], refs[-5:]
     n = weights.shape[0]
-    total[...] = project(xs[0][...], weights[origin(hops[0], n)])
-    for hop, x in zip(hops[1:], xs[1:]):
-        total[...] += project(x[...], weights[origin(hop, n)])
-
-
-def last_step(x, x_f, x_b, x_corner, x_middle, before, weights, bias, threshold, acts):
-    n = weights.shape[0]
-    hops = n // 2 - 1
-    x_far = jnp.where(on_corner(n), x_corner[...], x_middle[...])
+    copies = [
+        pltpu.make_async_copy(weights.at[origin(hop, n)], into.at[j], sems.at[j + base])
+        for into, base, some in ((blocks, 0, hops), (kept, len(hops), later))
+        for j, hop in enumerate(some)
+    ]
+    for copy in copies:
+        copy.start()
+    for j, x in enumerate(xs):
+        copies[j].wait()
+        part = project(x[...], blocks[j])
+        total[...] = part if j == 0 else total[...] + part
+    for copy in copies[len(hops) :]:
+        copy.wait()
+
+
+def last_step(x, x_f, x_b, x_corner, x_middle, before, blocks, bias, threshold, acts):
+    x_far = jnp.where(on_corner(2 * blocks.shape[0]), x_corner[...], x_middle[...])
     pre_acts = before[...] + bias[...]
-    for hop, part in ((0, x[...]), (hops, x_f[...]), (-hops, x_b[...]), (n // 2, x_far)):
-        pre_acts = pre_acts + project(part, weights[origin(hop, n)])
+    for j, part in enumerate((x[...], x_f[...], x_b[...], x_far)):
+        pre_acts = pre_acts + project(part, blocks[j])
     acts[...] = activate(pre_acts, threshold[...])
 
 
@@ -111,17 +120,23 @@
 
     def beside_third(*blocks):
         blocks = blocks[:4]
+        hops, later = (1, -1, 2, -2), (0, 3, -3, n // 2)
+        kept = jax.ShapeDtypeStruct((len(later),) + weights.shape[1:], weights.dtype)
         return pl.pallas_call(
-            functools.partial(first_step, (1, -1, 2, -2)),
-            out_shape=jax.ShapeDtypeStruct((tok_rows, width), jnp.float32),
-            in_specs=[in_vmem] * (len(blocks) + 1),
-            out_specs=in_vmem,
-            compiler_params=params,
+            functools.partial(first_step, hops, later),
+            out_shape=(jax.ShapeDtypeStruct((tok_rows, width), jnp.float32), kept),
+            in_specs=[in_vmem] * len(blocks) + [in_hbm],
+            out_specs=(in_vmem, in_vmem),
+            scratch_shapes=[
+                pltpu.VMEM((len(hops),) + weights.shape[1:], weights.dtype),
+                pltpu.SemaphoreType.DMA((len(hops) + len(later),)),
+            ],
+            compiler_params=streaming_params,
             cost_estimate=cost(tok_rows, depth, width, 4),
         )(*blocks, weights)
 
     x = residual.T
-    total, ahead, behind, corner, middle = ring.gather(x, beside_third=beside_third)
+    (total, kept), ahead, behind, corner, middle = ring.gather(x, beside_third=beside_third)
     return pl.pallas_call(
         last_step,
         out_shape=jax.ShapeDtypeStruct((tok_rows, width), jnp.bfloat16),
@@ -136,7 +151,7 @@
         corner,
         middle,
         total,
-        weights,
+        kept,
         enc_bias.reshape(1, width),
         threshold.reshape(1, width),
     )
@@ -302,6 +317,7 @@
             return add_tiles(before, (2, n - 2, n // 2), (ahead_2, behind_2, corner))
 
         out, ahead, behind, _, middle = ring.gather(acts, beside_second, beside_third)
+        out, ahead, behind = lax.optimization_barrier((out, ahead, behind))
         return add_tiles(out, (3, n - 3, n), (ahead, behind, middle))
     acts = encode_gathered(residual, enc_weight, enc_bias, threshold)
     acts_twin = lax.ppermute(acts, "tok", swap)

time: 43.8 us -> 44.4 us (1.014); the launches traced: 43 us -> 44.2 us
  waiting for transfers between devices: 11.5 us -> 13.9 us
  local copies, waits for them, and re-layouts: 2.25 us -> 0.02 us
  Pallas kernels: 5.03 us -> 6.76 us
  starting transfers between devices: 24.1 us -> 23.4 us
    unnamed x12 -> x8, local copies, waits for them, and re-layouts: 2.25 us -> 0.02 us
    pallas_call x1, Pallas kernels: 0.47 us -> 2.05 us  [beside_third(): pl.pallas_call(functools.partial(first_step, hops, later), out_shape=(jax...]
    ppermute x8, waiting for transfers between devices: 0.02 us -> 1.38 us  [add_tiles(): twins = [lax.ppermute(block, 'tok', swap) for block in blocks]]
    ppermute x2, starting transfers between devices: 1.01 us -> 2.08 us  [gather(): ahead_2 = lax.ppermute(ahead, 'lat', self.forward)]
    ppermute x2, starting transfers between devices: 8.6 us -> 7.54 us  [gather(): corner = lax.ppermute(x, 'lat', self.across)]
    ppermute x2, starting transfers between devices: 2.88 us -> 1.98 us  [gather(): behind_2 = lax.ppermute(behind, 'lat', self.backward)]
    ppermute x2, waiting for transfers between devices: 2.61 us -> 3.1 us  [gather(): corner = lax.ppermute(x, 'lat', self.across)]
  transfers between devices with their start and end apart: 25 -> 25, of which waited for: 9 -> 13; matrix products, arithmetic and copies ran while one was open for 0% -> 0% of each run, Pallas kernels for 9% -> 10%
where the time goes in v8:
time: 44.4 us; the launch traced here: 44.2 us
  starting transfers between devices  23.4 us (53%)
  waiting for transfers between devices  13.9 us (31%)
  Pallas kernels  6.76 us (15%)
    ppermute x2, starting transfers between devices, gather(): corner = lax.ppermute(x, 'lat', self.across)  7.54 us
    ppermute x2, starting transfers between devices, gather(): ahead = lax.ppermute(x, 'lat', self.forward)  5.1 us
    pallas_call x3, Pallas kernels, tiles_of(): pl.pallas_call(functools.partial(tiles_kernel, tok_scale, n, hops, first)...  4.21 us
    ppermute x2, waiting for transfers between devices, gather(): ahead_3 = lax.ppermute(ahead_2, 'lat', self.forward)  3.81 us
    ppermute x2, waiting for transfers between devices, gather(): ahead_2 = lax.ppermute(ahead, 'lat', self.forward)  3.53 us
    ppermute x2, waiting for transfers between devices, gather(): corner = lax.ppermute(x, 'lat', self.across)  3.1 us
    ppermute x2, starting transfers between devices, gather(): behind_3 = lax.ppermute(behind_2, 'lat', self.backward)  2.43 us
    ppermute x2, starting transfers between devices, gather(): ahead_2 = lax.ppermute(ahead, 'lat', self.forward)  2.08 us
  transfers between devices with their start and end apart: 25, of which 13 were waited for; matrix products, arithmetic and copies ran while one was open for 0% of the time, Pallas kernels for 10%

profile of v8, /device:TPU:0, one launch (start us, length us, event | category | flops | bytes accessed | tf_op | source)
XLA Modules:
  0.0 44.2 jit_solution(18103011932938190250)
XLA Ops:
  0.0 3.1 %collective-permute-start = (bf16[448,128]{1,0:T(8,128)(2,1)}, bf16[448,128]{1,0:T(8,128)(2,1)S(1)}, u32[]{:S(2)}, u32[]{:S(2)}) collective-permute-start(bf16[448,128]{1,0:T(8,128)(2,1)} %bitcast.5), channel_id=1, source_target_pairs={{0,4},{4,8},{8,12},{12,14},{14,10},{10,6},{6,2},{2,0},{1,5},{5,9},... | collective-permute-start | bytes 344072 | tf_op jit(solution)/shard_map/ppermute | solution.py:98
  3.1 0.0 collective-permute-start.2
  3.1 5.0 %collective-permute-start.4 = (bf16[448,128]{1,0:T(8,128)(2,1)}, bf16[448,128]{1,0:T(8,128)(2,1)S(1)}, u32[]{:S(2)}, u32[]{:S(2)}) collective-permute-start(bf16[448,128]{1,0:T(8,128)(2,1)} %bitcast.7), channel_id=1, source_target_pairs={{0,14},{12,2},{14,0},{2,12},{4,6},{8,10},{10,8},{6,4},{1,15},{13,3... | collective-permute-start | bytes 344072 | tf_op jit(solution)/shard_map/ppermute | solution.py:100
  8.1 0.0 collective-permute-done.refs_0_
  8.1 0.1 collective-permute-start.1
  8.2 0.0 collective-permute-done.2.refs_1_
  8.2 1.9 %collective-permute-start.3 = (bf16[448,128]{1,0:T(8,128)(2,1)S(1)}, bf16[448,128]{1,0:T(8,128)(2,1)S(1)}, u32[]{:S(2)}, u32[]{:S(2)}) collective-permute-start(bf16[448,128]{1,0:T(8,128)(2,1)S(1)} %collective-permute-done.2.refs_1_), channel_id=1, source_target_pairs={{4,0},{8,4},{12,8},{14,12},{10,14},{6,10},{2,6},{0,2},{5,1},{9,5},... | collective-permute-start | bytes 344072 | tf_op jit(solution)/shard_map/ppermute | solution.py:102
  10.1 0.0 copy-start.1
  10.1 0.7 %collective-permute-start.7 = (bf16[448,128]{1,0:T(8,128)(2,1)S(1)}, bf16[448,128]{1,0:T(8,128)(2,1)S(1)}, u32[]{:S(2)}, u32[]{:S(2)}) collective-permute-start(bf16[448,128]{1,0:T(8,128)(2,1)S(1)} %broadcast_select_fusion.1), channel_id=1, source_target_pairs={{4,6},{8,10},{10,8},{6,4},{5,7},{9,11},{11,9},{7,5},{20,22},{24,26... | collective-permute-start | bytes 344072 | tf_op jit(solution)/shard_map/ppermute | solution.py:104
  10.8 2.0 %collective-permute-done.4.x_corner = bf16[448,128]{1,0:T(8,128)(2,1)S(1)} collective-permute-done((bf16[448,128]{1,0:T(8,128)(2,1)}, bf16[448,128]{1,0:T(8,128)(2,1)S(1)}, u32[]{:S(2)}, u32[]{:S(2)}) %collective-permute-start.4) | collective-permute-done | bytes 114720 | tf_op jit(solution)/shard_map/ppermute | solution.py:100
  12.9 1.1 %collective-permute-done.1.refs_2_ = bf16[448,128]{1,0:T(8,128)(2,1)S(1)} collective-permute-done((bf16[448,128]{1,0:T(8,128)(2,1)S(1)}, bf16[448,128]{1,0:T(8,128)(2,1)S(1)}, u32[]{:S(2)}, u32[]{:S(2)}) %collective-permute-start.1) | collective-permute-done | bytes 114720 | tf_op jit(solution)/shard_map/ppermute | solution.py:101
  14.0 0.0 collective-permute-done.3.refs_3_
  14.0 1.1 %collective-permute-start.5 = (bf16[448,128]{1,0:T(8,128)(2,1)S(1)}, bf16[448,128]{1,0:T(8,128)(2,1)S(1)}, u32[]{:S(2)}, u32[]{:S(2)}) collective-permute-start(bf16[448,128]{1,0:T(8,128)(2,1)S(1)} %collective-permute-done.1.refs_2_), channel_id=1, source_target_pairs={{0,4},{4,8},{8,12},{12,14},{14,10},{10,6},{6,2},{2,0},{1,5},{5,9},... | collective-permute-start | bytes 344072 | tf_op jit(solution)/shard_map/ppermute | solution.py:109
  15.1 0.9 %collective-permute-start.6 = (bf16[448,128]{1,0:T(8,128)(2,1)S(1)}, bf16[448,128]{1,0:T(8,128)(2,1)S(1)}, u32[]{:S(2)}, u32[]{:S(2)}) collective-permute-start(bf16[448,128]{1,0:T(8,128)(2,1)S(1)} %collective-permute-done.3.refs_3_), channel_id=1, source_target_pairs={{4,0},{8,4},{12,8},{14,12},{10,14},{6,10},{2,6},{0,2},{5,1},{9,5},... | collective-permute-start | bytes 344072 | tf_op jit(solution)/shard_map/ppermute | solution.py:110
  16.0 2.1 %shard_map.55 = (f32[128,512]{1,0:T(8,128)S(1)}, bf16[4,448,512]{2,1,0:T(8,128)(2,1)S(1)}) custom-call(bf16[448,128]{1,0:T(8,128)(2,1)S(1)} %collective-permute-done.refs_0_, bf16[448,128]{1,0:T(8,128)(2,1)S(1)} %collective-permute-done.2.refs_1_, bf16[448,128]{1,0:T(8,128)(2,1)S(1)} %collective-permute-done.1.refs_2_, ...), custom_call_target="tpu_custom_call" | custom-call | flops 234881024 | bytes 2818048 | tf_op jit(solution)/shard_map/pallas_call | solution.py:125
  18.1 0.0 collective-permute-done.7.x_middle
  18.1 0.7 %collective-permute-done.5.x_f = bf16[448,128]{1,0:T(8,128)(2,1)S(1)} collective-permute-done((bf16[448,128]{1,0:T(8,128)(2,1)S(1)}, bf16[448,128]{1,0:T(8,128)(2,1)S(1)}, u32[]{:S(2)}, u32[]{:S(2)}) %collective-permute-start.5) | collective-permute-done | bytes 114720 | tf_op jit(solution)/shard_map/ppermute | solution.py:109
  18.8 1.1 %collective-permute-done.6.x_b = bf16[448,128]{1,0:T(8,128)(2,1)S(1)} collective-permute-done((bf16[448,128]{1,0:T(8,128)(2,1)S(1)}, bf16[448,128]{1,0:T(8,128)(2,1)S(1)}, u32[]{:S(2)}, u32[]{:S(2)}) %collective-permute-start.6) | collective-permute-done | bytes 114720 | tf_op jit(solution)/shard_map/ppermute | solution.py:110
  19.9 0.5 %shard_map.56.own = bf16[128,512]{1,0:T(8,128)(2,1)S(1)} custom-call(bf16[448,128]{1,0:T(8,128)(2,1)S(1)} %bitcast.8, bf16[448,128]{1,0:T(8,128)(2,1)S(1)} %collective-permute-done.5.x_f, bf16[448,128]{1,0:T(8,128)(2,1)S(1)} %collective-permute-done.6.x_b, bf16[448,128]{1,0:T(8,128)(2,1)S(1)} %collective-permute-done.4.x_corner, ...), custom_call_target="tpu_custom_call" | custom-call | flops 234881024 | bytes 2818048 | tf_op jit(solution)/shard_map/pallas_call | solution.py:140
  20.4 2.0 %collective-permute-start.9 = (bf16[128,512]{1,0:T(8,128)(2,1)S(1)}, bf16[128,512]{1,0:T(8,128)(2,1)S(1)}, u32[]{:S(2)}, u32[]{:S(2)}) collective-permute-start(bf16[128,512]{1,0:T(8,128)(2,1)S(1)} %shard_map.56.own), channel_id=1, source_target_pairs={{0,4},{4,8},{8,12},{12,14},{14,10},{10,6},{6,2},{2,0},{1,5},{5,9},... | collective-permute-start | bytes 393224 | tf_op jit(solution)/shard_map/ppermute | solution.py:98
  22.4 0.1 collective-permute-start.11
  22.5 2.6 %collective-permute-start.13 = (bf16[128,512]{1,0:T(8,128)(2,1)S(1)}, bf16[128,512]{1,0:T(8,128)(2,1)S(1)}, u32[]{:S(2)}, u32[]{:S(2)}) collective-permute-start(bf16[128,512]{1,0:T(8,128)(2,1)S(1)} %shard_map.56.own), channel_id=1, source_target_pairs={{0,14},{12,2},{14,0},{2,12},{4,6},{8,10},{10,8},{6,4},{1,15},{13,3... | collective-permute-start | bytes 393224 | tf_op jit(solution)/shard_map/ppermute | solution.py:100
  25.1 0.4 collective-permute-done.9.refs_0_
  25.4 2.0 %collective-permute-start.10 = (bf16[128,512]{1,0:T(8,128)(2,1)S(1)}, bf16[128,512]{1,0:T(8,128)(2,1)S(1)}, u32[]{:S(2)}, u32[]{:S(2)}) collective-permute-start(bf16[128,512]{1,0:T(8,128)(2,1)S(1)} %collective-permute-done.9.refs_0_), channel_id=1, source_target_pairs={{0,4},{4,8},{8,12},{12,14},{14,10},{10,6},{6,2},{2,0},{1,5},{5,9},... | collective-permute-start | bytes 393224 | tf_op jit(solution)/shard_map/ppermute | solution.py:101
  27.4 0.0 collective-permute-done.11.refs_1_
  27.4 0.2 collective-permute-start.15
  27.6 0.1 collective-permute-start.12
  27.7 0.7 %collective-permute-start.21 = (bf16[128,512]{1,0:T(8,128)(2,1)S(1)}, bf16[128,512]{1,0:T(8,128)(2,1)S(1)}, u32[]{:S(2)}, u32[]{:S(2)}) collective-permute-start(bf16[128,512]{1,0:T(8,128)(2,1)S(1)} %broadcast_select_fusion), channel_id=1, source_target_pairs={{4,6},{8,10},{10,8},{6,4},{5,7},{9,11},{11,9},{7,5},{20,22},{24,26... | collective-permute-start | bytes 393224 | tf_op jit(solution)/shard_map/ppermute | solution.py:104
  28.4 0.3 collective-permute-done.15.refs_3_
  28.8 1.7 %shard_map.57.refs_6_ = bf16[1,4,256,512]{3,2,1,0:T(8,128)(2,1)} custom-call(s32[4,8]{1,0:T(4,128)S(1)} %bitcast.9, bf16[128,512]{1,0:T(8,128)(2,1)S(1)} %shard_map.56.own, bf16[128,512]{1,0:T(8,128)(2,1)S(1)} %collective-permute-done.8.own_twin, bf16[128,512]{1,0:T(8,128)(2,1)S(1)} %collective-permute-done.9.refs_0_, ...), custom_call_target="tpu_custom_call" | custom-call | flops 134217728 | bytes 1048576 | tf_op jit(solution)/shard_map/pallas_call | solution.py:274
  30.4 1.1 %collective-permute-done.13.refs_2_ = bf16[128,512]{1,0:T(8,128)(2,1)S(1)} collective-permute-done((bf16[128,512]{1,0:T(8,128)(2,1)S(1)}, bf16[128,512]{1,0:T(8,128)(2,1)S(1)}, u32[]{:S(2)}, u32[]{:S(2)}) %collective-permute-start.13) | collective-permute-done | bytes 131104 | tf_op jit(solution)/shard_map/ppermute | solution.py:100
  31.5 2.4 %collective-permute-done.10.refs_0_ = bf16[128,512]{1,0:T(8,128)(2,1)S(1)} collective-permute-done((bf16[128,512]{1,0:T(8,128)(2,1)S(1)}, bf16[128,512]{1,0:T(8,128)(2,1)S(1)}, u32[]{:S(2)}, u32[]{:S(2)}) %collective-permute-start.10) | collective-permute-done | bytes 131104 | tf_op jit(solution)/shard_map/ppermute | solution.py:101
  33.9 0.2 collective-permute-done.12.refs_1_
  34.1 0.0 collective-permute-start.16
  34.2 0.5 %collective-permute-start.17 = (bf16[128,512]{1,0:T(8,128)(2,1)S(1)}, bf16[128,512]{1,0:T(8,128)(2,1)S(1)}, u32[]{:S(2)}, u32[]{:S(2)}) collective-permute-start(bf16[128,512]{1,0:T(8,128)(2,1)S(1)} %collective-permute-done.12.refs_1_), channel_id=1, source_target_pairs={{0,1},{1,0},{2,3},{3,2},{4,5},{5,4},{6,7},{7,6},{8,9},{9,8},{10,11... | collective-permute-start | bytes 393224 | tf_op jit(solution)/shard_map/ppermute | solution.py:308
  34.6 0.0 collective-permute-start.18
  34.7 0.5 %collective-permute-start.19 = (bf16[128,512]{1,0:T(8,128)(2,1)S(1)}, bf16[128,512]{1,0:T(8,128)(2,1)S(1)}, u32[]{:S(2)}, u32[]{:S(2)}) collective-permute-start(bf16[128,512]{1,0:T(8,128)(2,1)S(1)} %collective-permute-done.10.refs_0_), channel_id=1, source_target_pairs={{0,4},{4,8},{8,12},{12,14},{14,10},{10,6},{6,2},{2,0},{1,5},{5,9},... | collective-permute-start | bytes 393224 | tf_op jit(solution)/shard_map/ppermute | solution.py:109
  35.2 0.0 collective-permute-done.21.refs_2_
  35.2 1.5 %collective-permute-start.20 = (bf16[128,512]{1,0:T(8,128)(2,1)S(1)}, bf16[128,512]{1,0:T(8,128)(2,1)S(1)}, u32[]{:S(2)}, u32[]{:S(2)}) collective-permute-start(bf16[128,512]{1,0:T(8,128)(2,1)S(1)} %collective-permute-done.12.refs_1_), channel_id=1, source_target_pairs={{4,0},{8,4},{12,8},{14,12},{10,14},{6,10},{2,6},{0,2},{5,1},{9,5},... | collective-permute-start | bytes 393224 | tf_op jit(solution)/shard_map/ppermute | solution.py:110
  36.7 0.0 collective-permute-done.16.refs_3_
  36.7 0.0 collective-permute-start.24
  36.7 0.7 %shard_map.58.refs_6_ = bf16[1,4,256,512]{3,2,1,0:T(8,128)(2,1)} custom-call(s32[4,8]{1,0:T(4,128)S(1)} %bitcast.10, bf16[128,512]{1,0:T(8,128)(2,1)S(1)} %shard_map.56.own, bf16[128,512]{1,0:T(8,128)(2,1)S(1)} %collective-permute-done.8.own_twin, bf16[128,512]{1,0:T(8,128)(2,1)S(1)} %collective-permute-done.10.refs_0_, ...), custom_call_target="tpu_custom_call", output_to_operand_aliasing={{}: (9, {})} | custom-call | flops 201326592 | bytes 1572864 | tf_op jit(solution)/shard_map/pallas_call | solution.py:274
  37.4 3.1 %collective-permute-done.19.refs_0_ = bf16[128,512]{1,0:T(8,128)(2,1)S(1)} collective-permute-done((bf16[128,512]{1,0:T(8,128)(2,1)S(1)}, bf16[128,512]{1,0:T(8,128)(2,1)S(1)}, u32[]{:S(2)}, u32[]{:S(2)}) %collective-permute-start.19) | collective-permute-done | bytes 131104 | tf_op jit(solution)/shard_map/ppermute | solution.py:109
  40.5 0.3 collective-permute-done.20.refs_1_
  40.8 0.5 %collective-permute-start.23 = (bf16[128,512]{1,0:T(8,128)(2,1)S(1)}, bf16[128,512]{1,0:T(8,128)(2,1)S(1)}, u32[]{:S(2)}, u32[]{:S(2)}) collective-permute-start(bf16[128,512]{1,0:T(8,128)(2,1)S(1)} %collective-permute-done.20.refs_1_), channel_id=1, source_target_pairs={{0,1},{1,0},{2,3},{3,2},{4,5},{5,4},{6,7},{7,6},{8,9},{9,8},{10,11... | collective-permute-start | bytes 393224 | tf_op jit(solution)/shard_map/ppermute | solution.py:308
  41.3 0.8 %collective-permute-done.22.refs_3_ = bf16[128,512]{1,0:T(8,128)(2,1)S(1)} collective-permute-done((bf16[128,512]{1,0:T(8,128)(2,1)S(1)}, bf16[128,512]{1,0:T(8,128)(2,1)S(1)}, u32[]{:S(2)}, u32[]{:S(2)}) %collective-permute-start.22) | collective-permute-done | bytes 131104 | tf_op jit(solution)/shard_map/ppermute | solution.py:308
  42.2 0.2 collective-permute-done.23.refs_4_
  42.4 1.9 %shard_map.59 = bf16[1,4,256,512]{3,2,1,0:T(8,128)(2,1)} custom-call(s32[4,8]{1,0:T(4,128)S(1)} %bitcast.11, bf16[128,512]{1,0:T(8,128)(2,1)S(1)} %shard_map.56.own, bf16[128,512]{1,0:T(8,128)(2,1)S(1)} %collective-permute-done.8.own_twin, bf16[128,512]{1,0:T(8,128)(2,1)S(1)} %collective-permute-done.19.refs_0_, ...), custom_call_target="tpu_custom_call", output_to_operand_aliasing={{}: (9, {})} | custom-call | flops 201326592 | bytes 1572864 | tf_op jit(solution)/shard_map/pallas_call | solution.py:274
  (17 shorter events, 0.1 us)
Async XLA Ops:
  0.0 19.9 %copy-start = (bf16[128,448]{0,1:T(8,128)(2,1)S(1)}, bf16[128,448]{0,1:T(8,128)(2,1)}, u32[]{:S(2)}) copy-start(bf16[128,448]{0,1:T(8,128)(2,1)} %param.5) | copy-start | bytes 344068
  0.0 19.9 %copy-start.2 = (f32[512]{0:T(512)S(1)}, f32[512]{0:T(512)}, u32[]{:S(2)}) copy-start(f32[512]{0:T(512)} %param.7) | copy-start | bytes 6148
  0.0 19.9 %copy-start.3 = (f32[512]{0:T(512)S(1)}, f32[512]{0:T(512)}, u32[]{:S(2)}) copy-start(f32[512]{0:T(512)} %param.8) | copy-start | bytes 6148
  0.0 8.1 %collective-permute-start = (bf16[448,128]{1,0:T(8,128)(2,1)}, bf16[448,128]{1,0:T(8,128)(2,1)S(1)}, u32[]{:S(2)}, u32[]{:S(2)}) collective-permute-start(bf16[448,128]{1,0:T(8,128)(2,1)} %bitcast.5), channel_id=1, source_target_pairs={{0,4},{4,8},{8,12},{12,14},{14,10},{10,6},{6,2},{2,0},{1,5},{5,9},... | collective-permute-start | bytes 344072 | tf_op jit(solution)/shard_map/ppermute | solution.py:98
  3.1 5.1 %collective-permute-start.2 = (bf16[448,128]{1,0:T(8,128)(2,1)}, bf16[448,128]{1,0:T(8,128)(2,1)S(1)}, u32[]{:S(2)}, u32[]{:S(2)}) collective-permute-start(bf16[448,128]{1,0:T(8,128)(2,1)} %bitcast.6), channel_id=1, source_target_pairs={{4,0},{8,4},{12,8},{14,12},{10,14},{6,10},{2,6},{0,2},{5,1},{9,5},... | collective-permute-start | bytes 344072 | tf_op jit(solution)/shard_map/ppermute | solution.py:99
  3.1 9.8 %collective-permute-start.4 = (bf16[448,128]{1,0:T(8,128)(2,1)}, bf16[448,128]{1,0:T(8,128)(2,1)S(1)}, u32[]{:S(2)}, u32[]{:S(2)}) collective-permute-start(bf16[448,128]{1,0:T(8,128)(2,1)} %bitcast.7), channel_id=1, source_target_pairs={{0,14},{12,2},{14,0},{2,12},{4,6},{8,10},{10,8},{6,4},{1,15},{13,3... | collective-permute-start | bytes 344072 | tf_op jit(solution)/shard_map/ppermute | solution.py:100
  8.1 5.9 %collective-permute-start.1 = (bf16[448,128]{1,0:T(8,128)(2,1)S(1)}, bf16[448,128]{1,0:T(8,128)(2,1)S(1)}, u32[]{:S(2)}, u32[]{:S(2)}) collective-permute-start(bf16[448,128]{1,0:T(8,128)(2,1)S(1)} %collective-permute-done.refs_0_), channel_id=1, source_target_pairs={{0,4},{4,8},{8,12},{12,14},{14,10},{10,6},{6,2},{2,0},{1,5},{5,9},... | collective-permute-start | bytes 344072 | tf_op jit(solution)/shard_map/ppermute | solution.py:101
  8.2 5.8 %collective-permute-start.3 = (bf16[448,128]{1,0:T(8,128)(2,1)S(1)}, bf16[448,128]{1,0:T(8,128)(2,1)S(1)}, u32[]{:S(2)}, u32[]{:S(2)}) collective-permute-start(bf16[448,128]{1,0:T(8,128)(2,1)S(1)} %collective-permute-done.2.refs_1_), channel_id=1, source_target_pairs={{4,0},{8,4},{12,8},{14,12},{10,14},{6,10},{2,6},{0,2},{5,1},{9,5},... | collective-permute-start | bytes 344072 | tf_op jit(solution)/shard_map/ppermute | solution.py:102
  10.1 18.6 %copy-start.1 = (s32[8,4]{0,1:T(4,128)S(1)}, s32[8,4]{0,1:T(4,128)}, u32[]{:S(2)}) copy-start(s32[8,4]{0,1:T(4,128)} %param.9) | copy-start | bytes 388
  10.1 8.0 %collective-permute-start.7 = (bf16[448,128]{1,0:T(8,128)(2,1)S(1)}, bf16[448,128]{1,0:T(8,128)(2,1)S(1)}, u32[]{:S(2)}, u32[]{:S(2)}) collective-permute-start(bf16[448,128]{1,0:T(8,128)(2,1)S(1)} %broadcast_select_fusion.1), channel_id=1, source_target_pairs={{4,6},{8,10},{10,8},{6,4},{5,7},{9,11},{11,9},{7,5},{20,22},{24,26... | collective-permute-start | bytes 344072 | tf_op jit(solution)/shard_map/ppermute | solution.py:104
  14.0 4.8 %collective-permute-start.5 = (bf16[448,128]{1,0:T(8,128)(2,1)S(1)}, bf16[448,128]{1,0:T(8,128)(2,1)S(1)}, u32[]{:S(2)}, u32[]{:S(2)}) collective-permute-start(bf16[448,128]{1,0:T(8,128)(2,1)S(1)} %collective-permute-done.1.refs_2_), channel_id=1, source_target_pairs={{0,4},{4,8},{8,12},{12,14},{14,10},{10,6},{6,2},{2,0},{1,5},{5,9},... | collective-permute-start | bytes 344072 | tf_op jit(solution)/shard_map/ppermute | solution.py:109
  15.1 4.8 %collective-permute-start.6 = (bf16[448,128]{1,0:T(8,128)(2,1)S(1)}, bf16[448,128]{1,0:T(8,128)(2,1)S(1)}, u32[]{:S(2)}, u32[]{:S(2)}) collective-permute-start(bf16[448,128]{1,0:T(8,128)(2,1)S(1)} %collective-permute-done.3.refs_3_), channel_id=1, source_target_pairs={{4,0},{8,4},{12,8},{14,12},{10,14},{6,10},{2,6},{0,2},{5,1},{9,5},... | collective-permute-start | bytes 344072 | tf_op jit(solution)/shard_map/ppermute | solution.py:110
  20.4 5.0 %collective-permute-start.9 = (bf16[128,512]{1,0:T(8,128)(2,1)S(1)}, bf16[128,512]{1,0:T(8,128)(2,1)S(1)}, u32[]{:S(2)}, u32[]{:S(2)}) collective-permute-start(bf16[128,512]{1,0:T(8,128)(2,1)S(1)} %shard_map.56.own), channel_id=1, source_target_pairs={{0,4},{4,8},{8,12},{12,14},{14,10},{10,6},{6,2},{2,0},{1,5},{5,9},... | collective-permute-start | bytes 393224 | tf_op jit(solution)/shard_map/ppermute | solution.py:98
  22.4 5.0 %collective-permute-start.11 = (bf16[128,512]{1,0:T(8,128)(2,1)S(1)}, bf16[128,512]{1,0:T(8,128)(2,1)S(1)}, u32[]{:S(2)}, u32[]{:S(2)}) collective-permute-start(bf16[128,512]{1,0:T(8,128)(2,1)S(1)} %shard_map.56.own), channel_id=1, source_target_pairs={{4,0},{8,4},{12,8},{14,12},{10,14},{6,10},{2,6},{0,2},{5,1},{9,5},... | collective-permute-start | bytes 393224 | tf_op jit(solution)/shard_map/ppermute | solution.py:99
  22.5 5.1 %collective-permute-start.8 = (bf16[128,512]{1,0:T(8,128)(2,1)S(1)}, bf16[128,512]{1,0:T(8,128)(2,1)S(1)}, u32[]{:S(2)}, u32[]{:S(2)}) collective-permute-start(bf16[128,512]{1,0:T(8,128)(2,1)S(1)} %shard_map.56.own), channel_id=1, source_target_pairs={{0,1},{1,0},{2,3},{3,2},{4,5},{5,4},{6,7},{7,6},{8,9},{9,8},{10,11... | collective-permute-start | bytes 393224 | tf_op jit(solution)/shard_map/ppermute | solution.py:305
  22.5 9.0 %collective-permute-start.13 = (bf16[128,512]{1,0:T(8,128)(2,1)S(1)}, bf16[128,512]{1,0:T(8,128)(2,1)S(1)}, u32[]{:S(2)}, u32[]{:S(2)}) collective-permute-start(bf16[128,512]{1,0:T(8,128)(2,1)S(1)} %shard_map.56.own), channel_id=1, source_target_pairs={{0,14},{12,2},{14,0},{2,12},{4,6},{8,10},{10,8},{6,4},{1,15},{13,3... | collective-permute-start | bytes 393224 | tf_op jit(solution)/shard_map/ppermute | solution.py:100
  25.4 2.3 %collective-permute-start.14 = (bf16[128,512]{1,0:T(8,128)(2,1)S(1)}, bf16[128,512]{1,0:T(8,128)(2,1)S(1)}, u32[]{:S(2)}, u32[]{:S(2)}) collective-permute-start(bf16[128,512]{1,0:T(8,128)(2,1)S(1)} %collective-permute-done.9.refs_0_), channel_id=1, source_target_pairs={{0,1},{1,0},{2,3},{3,2},{4,5},{5,4},{6,7},{7,6},{8,9},{9,8},{10,11... | collective-permute-start | bytes 393224 | tf_op jit(solution)/shard_map/ppermute | solution.py:308
  25.4 8.5 %collective-permute-start.10 = (bf16[128,512]{1,0:T(8,128)(2,1)S(1)}, bf16[128,512]{1,0:T(8,128)(2,1)S(1)}, u32[]{:S(2)}, u32[]{:S(2)}) collective-permute-start(bf16[128,512]{1,0:T(8,128)(2,1)S(1)} %collective-permute-done.9.refs_0_), channel_id=1, source_target_pairs={{0,4},{4,8},{8,12},{12,14},{14,10},{10,6},{6,2},{2,0},{1,5},{5,9},... | collective-permute-start | bytes 393224 | tf_op jit(solution)/shard_map/ppermute | solution.py:101
  27.4 1.3 %collective-permute-start.15 = (bf16[128,512]{1,0:T(8,128)(2,1)S(1)}, bf16[128,512]{1,0:T(8,128)(2,1)S(1)}, u32[]{:S(2)}, u32[]{:S(2)}) collective-permute-start(bf16[128,512]{1,0:T(8,128)(2,1)S(1)} %collective-permute-done.11.refs_1_), channel_id=1, source_target_pairs={{0,1},{1,0},{2,3},{3,2},{4,5},{5,4},{6,7},{7,6},{8,9},{9,8},{10,11... | collective-permute-start | bytes 393224 | tf_op jit(solution)/shard_map/ppermute | solution.py:308
  27.6 6.5 %collective-permute-start.12 = (bf16[128,512]{1,0:T(8,128)(2,1)S(1)}, bf16[128,512]{1,0:T(8,128)(2,1)S(1)}, u32[]{:S(2)}, u32[]{:S(2)}) collective-permute-start(bf16[128,512]{1,0:T(8,128)(2,1)S(1)} %collective-permute-done.11.refs_1_), channel_id=1, source_target_pairs={{4,0},{8,4},{12,8},{14,12},{10,14},{6,10},{2,6},{0,2},{5,1},{9,5},... | collective-permute-start | bytes 393224 | tf_op jit(solution)/shard_map/ppermute | solution.py:102
  27.7 7.5 %collective-permute-start.21 = (bf16[128,512]{1,0:T(8,128)(2,1)S(1)}, bf16[128,512]{1,0:T(8,128)(2,1)S(1)}, u32[]{:S(2)}, u32[]{:S(2)}) collective-permute-start(bf16[128,512]{1,0:T(8,128)(2,1)S(1)} %broadcast_select_fusion), channel_id=1, source_target_pairs={{4,6},{8,10},{10,8},{6,4},{5,7},{9,11},{11,9},{7,5},{20,22},{24,26... | collective-permute-start | bytes 393224 | tf_op jit(solution)/shard_map/ppermute | solution.py:104
  34.1 2.6 %collective-permute-start.16 = (bf16[128,512]{1,0:T(8,128)(2,1)S(1)}, bf16[128,512]{1,0:T(8,128)(2,1)S(1)}, u32[]{:S(2)}, u32[]{:S(2)}) collective-permute-start(bf16[128,512]{1,0:T(8,128)(2,1)S(1)} %collective-permute-done.10.refs_0_), channel_id=1, source_target_pairs={{0,1},{1,0},{2,3},{3,2},{4,5},{5,4},{6,7},{7,6},{8,9},{9,8},{10,11... | collective-permute-start | bytes 393224 | tf_op jit(solution)/shard_map/ppermute | solution.py:308
  34.2 2.6 %collective-permute-start.17 = (bf16[128,512]{1,0:T(8,128)(2,1)S(1)}, bf16[128,512]{1,0:T(8,128)(2,1)S(1)}, u32[]{:S(2)}, u32[]{:S(2)}) collective-permute-start(bf16[128,512]{1,0:T(8,128)(2,1)S(1)} %collective-permute-done.12.refs_1_), channel_id=1, source_target_pairs={{0,1},{1,0},{2,3},{3,2},{4,5},{5,4},{6,7},{7,6},{8,9},{9,8},{10,11... | collective-permute-start | bytes 393224 | tf_op jit(solution)/shard_map/ppermute | solution.py:308
  34.6 2.1 %collective-permute-start.18 = (bf16[128,512]{1,0:T(8,128)(2,1)S(1)}, bf16[128,512]{1,0:T(8,128)(2,1)S(1)}, u32[]{:S(2)}, u32[]{:S(2)}) collective-permute-start(bf16[128,512]{1,0:T(8,128)(2,1)S(1)} %collective-permute-done.13.refs_2_), channel_id=1, source_target_pairs={{0,1},{1,0},{2,3},{3,2},{4,5},{5,4},{6,7},{7,6},{8,9},{9,8},{10,11... | collective-permute-start | bytes 393224 | tf_op jit(solution)/shard_map/ppermute | solution.py:308
  34.7 5.9 %collective-permute-start.19 = (bf16[128,512]{1,0:T(8,128)(2,1)S(1)}, bf16[128,512]{1,0:T(8,128)(2,1)S(1)}, u32[]{:S(2)}, u32[]{:S(2)}) collective-permute-start(bf16[128,512]{1,0:T(8,128)(2,1)S(1)} %collective-permute-done.10.refs_0_), channel_id=1, source_target_pairs={{0,4},{4,8},{8,12},{12,14},{14,10},{10,6},{6,2},{2,0},{1,5},{5,9},... | collective-permute-start | bytes 393224 | tf_op jit(solution)/shard_map/ppermute | solution.py:109
  35.2 5.6 %collective-permute-start.20 = (bf16[128,512]{1,0:T(8,128)(2,1)S(1)}, bf16[128,512]{1,0:T(8,128)(2,1)S(1)}, u32[]{:S(2)}, u32[]{:S(2)}) collective-permute-start(bf16[128,512]{1,0:T(8,128)(2,1)S(1)} %collective-permute-done.12.refs_1_), channel_id=1, source_target_pairs={{4,0},{8,4},{12,8},{14,12},{10,14},{6,10},{2,6},{0,2},{5,1},{9,5},... | collective-permute-start | bytes 393224 | tf_op jit(solution)/shard_map/ppermute | solution.py:110
  36.7 4.6 %collective-permute-start.24 = (bf16[128,512]{1,0:T(8,128)(2,1)S(1)}, bf16[128,512]{1,0:T(8,128)(2,1)S(1)}, u32[]{:S(2)}, u32[]{:S(2)}) collective-permute-start(bf16[128,512]{1,0:T(8,128)(2,1)S(1)} %collective-permute-done.21.refs_2_), channel_id=1, source_target_pairs={{0,1},{1,0},{2,3},{3,2},{4,5},{5,4},{6,7},{7,6},{8,9},{9,8},{10,11... | collective-permute-start | bytes 393224 | tf_op jit(solution)/shard_map/ppermute | solution.py:308
  40.8 1.3 %collective-permute-start.22 = (bf16[128,512]{1,0:T(8,128)(2,1)S(1)}, bf16[128,512]{1,0:T(8,128)(2,1)S(1)}, u32[]{:S(2)}, u32[]{:S(2)}) collective-permute-start(bf16[128,512]{1,0:T(8,128)(2,1)S(1)} %collective-permute-done.19.refs_0_), channel_id=1, source_target_pairs={{0,1},{1,0},{2,3},{3,2},{4,5},{5,4},{6,7},{7,6},{8,9},{9,8},{10,11... | collective-permute-start | bytes 393224 | tf_op jit(solution)/shard_map/ppermute | solution.py:308
  40.8 1.5 %collective-permute-start.23 = (bf16[128,512]{1,0:T(8,128)(2,1)S(1)}, bf16[128,512]{1,0:T(8,128)(2,1)S(1)}, u32[]{:S(2)}, u32[]{:S(2)}) collective-permute-start(bf16[128,512]{1,0:T(8,128)(2,1)S(1)} %collective-permute-done.20.refs_1_), channel_id=1, source_target_pairs={{0,1},{1,0},{2,3},{3,2},{4,5},{5,4},{6,7},{7,6},{8,9},{9,8},{10,11... | collective-permute-start | bytes 393224 | tf_op jit(solution)/shard_map/ppermute | solution.py:308

commit v9 on v8

--- a/solution.py
+++ b/solution.py
@@ -223,35 +223,49 @@
     return jnp.where(listed < n, hop, -1)
 
 
-def tiles_kernel(tok_scale, n, hops, is_first, partners, own, own_twin, *refs):
+def tiles_kernel(tok_scale, n, hops, is_first, partners, *refs):
     count = len(hops)
+    if is_first:
+        own, own_twin, refs = refs[0], refs[1], refs[2:]
+        left, refs = refs[-4], refs[:-4] + refs[-3:]
+    else:
+        left, refs = refs[0], refs[1:]
     blocks, twins = refs[:count], refs[count : 2 * count]
     out, tiles, sems = refs[-3:]
     rows, width = tiles.shape[1:]
+    half = rows // 2
     slots = partners.shape[0]
-    columns = pl.ds(pl.multiple_of(lax.axis_index("tok") * rows, rows), rows)
-    left = jnp.concatenate([own[:, columns], own_twin[:, columns]], axis=0)
-
-    def tile_of(right, right_twin):
-        tile = project(left, jnp.concatenate([right[...], right_twin[...]], axis=0))
-        return (tile * tok_scale).astype(tiles.dtype)
+    if is_first:
+        columns = pl.ds(pl.multiple_of(lax.axis_index("tok") * rows, rows), rows)
+        left[...] = jnp.concatenate([own[:, columns], own_twin[:, columns]], axis=0).T
 
     slot_hops = [hop_of_slot(partners, k, n) for k in range(1, slots)]
     copies = []
 
-    def send(place, slot, when, value):
-        copy = pltpu.make_async_copy(tiles.at[place], out.at[0, slot], sems.at[len(copies)])
-        copies.append((copy, when))
+    def send(place, slot, when, pair):
+        both = []
+        for i in range(2):
+            part = pl.ds(i * half, half)
+            sem = sems.at[len(copies), i]
+            both.append(
+                pltpu.make_async_copy(tiles.at[place, part], out.at[0, slot, part], sem)
+            )
+        copies.append((both, when))
 
         @pl.when(when)
         def _():
-            if value is not None:
-                tiles[place] = value()
-            copy.start()
+            if pair is not None:
+                right = jnp.concatenate([pair[0][...], pair[1][...]], axis=0)
+            for i in range(2):
+                part = pl.ds(i * half, half)
+                if pair is not None:
+                    tile = jnp.dot(left[part, :], right, preferred_element_type=jnp.float32)
+                    tiles[place, part, :] = (tile * tok_scale).astype(tiles.dtype)
+                both[i].start()
 
     if is_first:
         always = lax.axis_index("lat") >= 0
-        send(count, 0, always, lambda: tile_of(own, own_twin))
+        send(count, 0, always, (own, own_twin))
         tiles[count + 1] = jnp.zeros((rows, width), tiles.dtype)
         for k, hop in enumerate(slot_hops):
             send(count + 1, k + 1, hop < 0, None)
@@ -259,35 +273,46 @@
         slot = jnp.int32(0)
         for k, h in enumerate(slot_hops):
             slot = jnp.where(h == hop, jnp.int32(k + 1), slot)
-        send(j, slot, slot > 0, functools.partial(tile_of, blocks[j], twins[j]))
-    for copy, when in copies:
-        pl.when(when)(copy.wait)
-
-
-def tiles_of(partners, own, own_twin, hops, blocks, twins, before, tok_scale, halves, n):
-    width = own.shape[1]
+        send(j, slot, slot > 0, (blocks[j], twins[j]))
+    for both, when in copies:
+
+        @pl.when(when)
+        def _():
+            for copy in both:
+                copy.wait()
+
+
+def tiles_of(partners, owns, before, hops, blocks, twins, tok_scale, halves, n):
+    tok_rows, width = blocks[0].shape
     slots = partners.shape[0]
     rows = width // halves
     first = before is None
-    operands = (partners, own, own_twin, *blocks, *twins) + (() if first else (before,))
-    specs = [in_smem] + [in_vmem] * (2 + 2 * len(hops)) + ([] if first else [in_hbm])
-    return pl.pallas_call(
+    dtype = blocks[0].dtype
+    out_shape = jax.ShapeDtypeStruct((1, slots, rows, width), dtype)
+    left_shape = jax.ShapeDtypeStruct((rows, tok_rows * halves), dtype)
+    if first:
+        operands = (partners, *owns, *blocks, *twins)
+    else:
+        operands = (partners, before[0], *blocks, *twins, before[1])
+    specs = [in_smem] + [in_vmem] * (len(operands) - 1)
+    done = pl.pallas_call(
         functools.partial(tiles_kernel, tok_scale, n, hops, first),
-        out_shape=jax.ShapeDtypeStruct((1, slots, rows, width), own.dtype),
-        in_specs=specs,
-        out_specs=in_hbm,
+        out_shape=(left_shape, out_shape) if first else out_shape,
+        in_specs=specs if first else specs[:-1] + [in_hbm],
+        out_specs=(in_vmem, in_hbm) if first else in_hbm,
         input_output_aliases={} if first else {len(operands) - 1: 0},
         scratch_shapes=[
-            pltpu.VMEM((len(hops) + (2 if first else 0), rows, width), own.dtype),
-            pltpu.SemaphoreType.DMA((len(hops) + (slots if first else 0),)),
+            pltpu.VMEM((len(hops) + (2 if first else 0), rows, width), dtype),
+            pltpu.SemaphoreType.DMA((len(hops) + (slots if first else 0), 2)),
         ],
         compiler_params=params,
         cost_estimate=pl.CostEstimate(
-            flops=4 * rows * width * own.shape[0] * len(hops),
+            flops=4 * rows * width * tok_rows * len(hops),
             bytes_accessed=4 * rows * width * len(hops),
             transcendentals=0,
         ),
     )(*operands)
+    return done if first else (before[0], done)
 
 
 def body(residual, enc_weight, enc_bias, threshold, partners):
@@ -306,9 +331,8 @@
 
         def add_tiles(before, hops, blocks):
             twins = [lax.ppermute(block, "tok", swap) for block in blocks]
-            return tiles_of(
-                by_slot, acts, acts_twin, hops, blocks, twins, before, tok_scale, halves, n
-            )
+            owns = (acts, acts_twin)
+            return tiles_of(by_slot, owns, before, hops, blocks, twins, tok_scale, halves, n)
 
         def beside_second(ahead, behind):
             return add_tiles(None, (1, n - 1), (ahead, behind))
@@ -318,7 +342,7 @@
 
         out, ahead, behind, _, middle = ring.gather(acts, beside_second, beside_third)
         out, ahead, behind = lax.optimization_barrier((out, ahead, behind))
-        return add_tiles(out, (3, n - 3, n), (ahead, behind, middle))
+        return add_tiles(out, (3, n - 3, n), (ahead, behind, middle))[1]
     acts = encode_gathered(residual, enc_weight, enc_bias, threshold)
     acts_twin = lax.ppermute(acts, "tok", swap)
     slices = lax.all_to_all(acts.reshape(n, tok_rows // n, width), "lat", 0, 0)

time: 44.4 us -> 43.6 us (0.982); the launches traced: 44.2 us -> 42.8 us
  Pallas kernels: 6.76 us -> 5.88 us
  waiting for transfers between devices: 13.9 us -> 13.2 us
    ppermute x2, waiting for transfers between devices: 3.53 us -> 1.69 us  [gather(): ahead_2 = lax.ppermute(ahead, 'lat', self.forward)]
    ppermute x2, waiting for transfers between devices: 0.25 us -> 2.09 us  [gather(): behind_2 = lax.ppermute(behind, 'lat', self.backward)]
    ppermute x2, starting transfers between devices: 1.98 us -> 3.73 us  [gather(): behind_2 = lax.ppermute(behind, 'lat', self.backward)]
    ppermute x2, starting transfers between devices: 2.08 us -> 0.77 us  [gather(): ahead_2 = lax.ppermute(ahead, 'lat', self.forward)]
    ppermute x2, waiting for transfers between devices: 3.1 us -> 2.15 us  [gather(): corner = lax.ppermute(x, 'lat', self.across)]
    ppermute x2, starting transfers between devices: 0.06 us -> 0.98 us  [gather(): behind = lax.ppermute(x, 'lat', self.backward)]
    ppermute x2, starting transfers between devices: 5.1 us -> 4.19 us  [gather(): ahead = lax.ppermute(x, 'lat', self.forward)]
    pallas_call x3, Pallas kernels: 4.21 us -> 3.34 us  [tiles_of(): pl.pallas_call(functools.partial(tiles_kernel, tok_scale, n, hops, first)...]
  transfers between devices with their start and end apart: 25 -> 25, of which waited for: 13 -> 13; matrix products, arithmetic and copies ran while one was open for 0% -> 0% of each run, Pallas kernels for 10% -> 11%
where the time goes in v9:
time: 43.6 us; the launch traced here: 42.8 us
  starting transfers between devices  23.6 us (54%)
  waiting for transfers between devices  13.2 us (30%)
  Pallas kernels  5.88 us (13%)
    ppermute x2, starting transfers between devices, gather(): corner = lax.ppermute(x, 'lat', self.across)  7.48 us
    ppermute x2, starting transfers between devices, gather(): ahead = lax.ppermute(x, 'lat', self.forward)  4.19 us
    ppermute x2, waiting for transfers between devices, gather(): ahead_3 = lax.ppermute(ahead_2, 'lat', self.forward)  3.83 us
    ppermute x2, starting transfers between devices, gather(): behind_2 = lax.ppermute(behind, 'lat', self.backward)  3.73 us
    pallas_call x3, Pallas kernels, tiles_of(): pl.pallas_call(functools.partial(tiles_kernel, tok_scale, n, hops, first)...  3.34 us
    ppermute x2, starting transfers between devices, gather(): behind_3 = lax.ppermute(behind_2, 'lat', self.backward)  2.39 us
    ppermute x2, waiting for transfers between devices, gather(): corner = lax.ppermute(x, 'lat', self.across)  2.15 us
    ppermute x2, waiting for transfers between devices, gather(): behind_2 = lax.ppermute(behind, 'lat', self.backward)  2.09 us
  transfers between devices with their start and end apart: 25, of which 13 were waited for; matrix products, arithmetic and copies ran while one was open for 0% of the time, Pallas kernels for 11%

profile of v9, /device:TPU:0, one launch (start us, length us, event | category | flops | bytes accessed | tf_op | source)
XLA Modules:
  0.0 42.8 jit_solution(4315362129853740514)
XLA Ops:
  0.0 3.1 %collective-permute-start = (bf16[448,128]{1,0:T(8,128)(2,1)}, bf16[448,128]{1,0:T(8,128)(2,1)S(1)}, u32[]{:S(2)}, u32[]{:S(2)}) collective-permute-start(bf16[448,128]{1,0:T(8,128)(2,1)} %bitcast.5), channel_id=1, source_target_pairs={{0,4},{4,8},{8,12},{12,14},{14,10},{10,6},{6,2},{2,0},{1,5},{5,9},... | collective-permute-start | bytes 344072 | tf_op jit(solution)/shard_map/ppermute | solution.py:98
  3.1 5.0 %collective-permute-start.4 = (bf16[448,128]{1,0:T(8,128)(2,1)}, bf16[448,128]{1,0:T(8,128)(2,1)S(1)}, u32[]{:S(2)}, u32[]{:S(2)}) collective-permute-start(bf16[448,128]{1,0:T(8,128)(2,1)} %bitcast.7), channel_id=1, source_target_pairs={{0,14},{12,2},{14,0},{2,12},{4,6},{8,10},{10,8},{6,4},{1,15},{13,3... | collective-permute-start | bytes 344072 | tf_op jit(solution)/shard_map/ppermute | solution.py:100
  8.1 0.1 collective-permute-start.1
  8.2 1.9 %collective-permute-start.3 = (bf16[448,128]{1,0:T(8,128)(2,1)S(1)}, bf16[448,128]{1,0:T(8,128)(2,1)S(1)}, u32[]{:S(2)}, u32[]{:S(2)}) collective-permute-start(bf16[448,128]{1,0:T(8,128)(2,1)S(1)} %collective-permute-done.2.refs_1_), channel_id=1, source_target_pairs={{4,0},{8,4},{12,8},{14,12},{10,14},{6,10},{2,6},{0,2},{5,1},{9,5},... | collective-permute-start | bytes 344072 | tf_op jit(solution)/shard_map/ppermute | solution.py:102
  10.1 0.0 copy-start.1
  10.1 0.7 %collective-permute-start.7 = (bf16[448,128]{1,0:T(8,128)(2,1)S(1)}, bf16[448,128]{1,0:T(8,128)(2,1)S(1)}, u32[]{:S(2)}, u32[]{:S(2)}) collective-permute-start(bf16[448,128]{1,0:T(8,128)(2,1)S(1)} %broadcast_select_fusion.1), channel_id=1, source_target_pairs={{4,6},{8,10},{10,8},{6,4},{5,7},{9,11},{11,9},{7,5},{20,22},{24,26... | collective-permute-start | bytes 344072 | tf_op jit(solution)/shard_map/ppermute | solution.py:104
  10.8 2.0 %collective-permute-done.4.x_corner = bf16[448,128]{1,0:T(8,128)(2,1)S(1)} collective-permute-done((bf16[448,128]{1,0:T(8,128)(2,1)}, bf16[448,128]{1,0:T(8,128)(2,1)S(1)}, u32[]{:S(2)}, u32[]{:S(2)}) %collective-permute-start.4) | collective-permute-done | bytes 114720 | tf_op jit(solution)/shard_map/ppermute | solution.py:100
  12.9 1.1 %collective-permute-done.1.refs_2_ = bf16[448,128]{1,0:T(8,128)(2,1)S(1)} collective-permute-done((bf16[448,128]{1,0:T(8,128)(2,1)S(1)}, bf16[448,128]{1,0:T(8,128)(2,1)S(1)}, u32[]{:S(2)}, u32[]{:S(2)}) %collective-permute-start.1) | collective-permute-done | bytes 114720 | tf_op jit(solution)/shard_map/ppermute | solution.py:101
  14.0 0.0 collective-permute-done.3.refs_3_
  14.0 1.1 %collective-permute-start.5 = (bf16[448,128]{1,0:T(8,128)(2,1)S(1)}, bf16[448,128]{1,0:T(8,128)(2,1)S(1)}, u32[]{:S(2)}, u32[]{:S(2)}) collective-permute-start(bf16[448,128]{1,0:T(8,128)(2,1)S(1)} %collective-permute-done.1.refs_2_), channel_id=1, source_target_pairs={{0,4},{4,8},{8,12},{12,14},{14,10},{10,6},{6,2},{2,0},{1,5},{5,9},... | collective-permute-start | bytes 344072 | tf_op jit(solution)/shard_map/ppermute | solution.py:109
  15.1 0.9 %collective-permute-start.6 = (bf16[448,128]{1,0:T(8,128)(2,1)S(1)}, bf16[448,128]{1,0:T(8,128)(2,1)S(1)}, u32[]{:S(2)}, u32[]{:S(2)}) collective-permute-start(bf16[448,128]{1,0:T(8,128)(2,1)S(1)} %collective-permute-done.3.refs_3_), channel_id=1, source_target_pairs={{4,0},{8,4},{12,8},{14,12},{10,14},{6,10},{2,6},{0,2},{5,1},{9,5},... | collective-permute-start | bytes 344072 | tf_op jit(solution)/shard_map/ppermute | solution.py:110
  16.0 2.1 %shard_map.55 = (f32[128,512]{1,0:T(8,128)S(1)}, bf16[4,448,512]{2,1,0:T(8,128)(2,1)S(1)}) custom-call(bf16[448,128]{1,0:T(8,128)(2,1)S(1)} %collective-permute-done.refs_0_, bf16[448,128]{1,0:T(8,128)(2,1)S(1)} %collective-permute-done.2.refs_1_, bf16[448,128]{1,0:T(8,128)(2,1)S(1)} %collective-permute-done.1.refs_2_, ...), custom_call_target="tpu_custom_call" | custom-call | flops 234881024 | bytes 2818048 | tf_op jit(solution)/shard_map/pallas_call | solution.py:125
  18.1 0.7 %collective-permute-done.5.x_f = bf16[448,128]{1,0:T(8,128)(2,1)S(1)} collective-permute-done((bf16[448,128]{1,0:T(8,128)(2,1)S(1)}, bf16[448,128]{1,0:T(8,128)(2,1)S(1)}, u32[]{:S(2)}, u32[]{:S(2)}) %collective-permute-start.5) | collective-permute-done | bytes 114720 | tf_op jit(solution)/shard_map/ppermute | solution.py:109
  18.8 1.1 %collective-permute-done.6.x_b = bf16[448,128]{1,0:T(8,128)(2,1)S(1)} collective-permute-done((bf16[448,128]{1,0:T(8,128)(2,1)S(1)}, bf16[448,128]{1,0:T(8,128)(2,1)S(1)}, u32[]{:S(2)}, u32[]{:S(2)}) %collective-permute-start.6) | collective-permute-done | bytes 114720 | tf_op jit(solution)/shard_map/ppermute | solution.py:110
  19.9 0.5 %shard_map.56.refs_0_ = bf16[128,512]{1,0:T(8,128)(2,1)S(1)} custom-call(bf16[448,128]{1,0:T(8,128)(2,1)S(1)} %bitcast.8, bf16[448,128]{1,0:T(8,128)(2,1)S(1)} %collective-permute-done.5.x_f, bf16[448,128]{1,0:T(8,128)(2,1)S(1)} %collective-permute-done.6.x_b, bf16[448,128]{1,0:T(8,128)(2,1)S(1)} %collective-permute-done.4.x_corner, ...), custom_call_target="tpu_custom_call" | custom-call | flops 234881024 | bytes 2818048 | tf_op jit(solution)/shard_map/pallas_call | solution.py:140
  20.4 1.0 %collective-permute-start.10 = (bf16[128,512]{1,0:T(8,128)(2,1)S(1)}, bf16[128,512]{1,0:T(8,128)(2,1)S(1)}, u32[]{:S(2)}, u32[]{:S(2)}) collective-permute-start(bf16[128,512]{1,0:T(8,128)(2,1)S(1)} %shard_map.56.refs_0_), channel_id=1, source_target_pairs={{4,0},{8,4},{12,8},{14,12},{10,14},{6,10},{2,6},{0,2},{5,1},{9,5},... | collective-permute-start | bytes 393224 | tf_op jit(solution)/shard_map/ppermute | solution.py:99
  21.4 1.1 %collective-permute-start.8 = (bf16[128,512]{1,0:T(8,128)(2,1)S(1)}, bf16[128,512]{1,0:T(8,128)(2,1)S(1)}, u32[]{:S(2)}, u32[]{:S(2)}) collective-permute-start(bf16[128,512]{1,0:T(8,128)(2,1)S(1)} %shard_map.56.refs_0_), channel_id=1, source_target_pairs={{0,4},{4,8},{8,12},{12,14},{14,10},{10,6},{6,2},{2,0},{1,5},{5,9},... | collective-permute-start | bytes 393224 | tf_op jit(solution)/shard_map/ppermute | solution.py:98
  22.5 2.5 %collective-permute-start.12 = (bf16[128,512]{1,0:T(8,128)(2,1)S(1)}, bf16[128,512]{1,0:T(8,128)(2,1)S(1)}, u32[]{:S(2)}, u32[]{:S(2)}) collective-permute-start(bf16[128,512]{1,0:T(8,128)(2,1)S(1)} %shard_map.56.refs_0_), channel_id=1, source_target_pairs={{0,14},{12,2},{14,0},{2,12},{4,6},{8,10},{10,8},{6,4},{1,15},{13,3... | collective-permute-start | bytes 393224 | tf_op jit(solution)/shard_map/ppermute | solution.py:100
  25.0 0.4 collective-permute-done.10.refs_3_
  25.4 0.0 collective-permute-start.15
  25.4 1.8 %collective-permute-start.11 = (bf16[128,512]{1,0:T(8,128)(2,1)S(1)}, bf16[128,512]{1,0:T(8,128)(2,1)S(1)}, u32[]{:S(2)}, u32[]{:S(2)}) collective-permute-start(bf16[128,512]{1,0:T(8,128)(2,1)S(1)} %collective-permute-done.10.refs_3_), channel_id=1, source_target_pairs={{4,0},{8,4},{12,8},{14,12},{10,14},{6,10},{2,6},{0,2},{5,1},{9,5},... | collective-permute-start | bytes 393224 | tf_op jit(solution)/shard_map/ppermute | solution.py:102
  27.3 0.0 collective-permute-done.8.refs_2_
  27.3 0.0 collective-permute-start.14
  27.3 0.0 collective-permute-done.13.refs_1_
  27.3 0.7 %collective-permute-start.9 = (bf16[128,512]{1,0:T(8,128)(2,1)S(1)}, bf16[128,512]{1,0:T(8,128)(2,1)S(1)}, u32[]{:S(2)}, u32[]{:S(2)}) collective-permute-start(bf16[128,512]{1,0:T(8,128)(2,1)S(1)} %collective-permute-done.8.refs_2_), channel_id=1, source_target_pairs={{0,4},{4,8},{8,12},{12,14},{14,10},{10,6},{6,2},{2,0},{1,5},{5,9},... | collective-permute-start | bytes 393224 | tf_op jit(solution)/shard_map/ppermute | solution.py:101
  27.9 0.7 %collective-permute-done.14.refs_4_ = bf16[128,512]{1,0:T(8,128)(2,1)S(1)} collective-permute-done((bf16[128,512]{1,0:T(8,128)(2,1)S(1)}, bf16[128,512]{1,0:T(8,128)(2,1)S(1)}, u32[]{:S(2)}, u32[]{:S(2)}) %collective-permute-start.14) | collective-permute-done | bytes 131104 | tf_op jit(solution)/shard_map/ppermute | solution.py:333
  28.6 0.7 %collective-permute-start.21 = (bf16[128,512]{1,0:T(8,128)(2,1)S(1)}, bf16[128,512]{1,0:T(8,128)(2,1)S(1)}, u32[]{:S(2)}, u32[]{:S(2)}) collective-permute-start(bf16[128,512]{1,0:T(8,128)(2,1)S(1)} %broadcast_select_fusion), channel_id=1, source_target_pairs={{4,6},{8,10},{10,8},{6,4},{5,7},{9,11},{11,9},{7,5},{20,22},{24,26... | collective-permute-start | bytes 393224 | tf_op jit(solution)/shard_map/ppermute | solution.py:104
  29.3 0.0 collective-permute-done.15.refs_5_
  29.3 1.9 %shard_map.57 = (bf16[256,256]{1,0:T(8,128)(2,1)S(1)}, bf16[1,4,256,512]{3,2,1,0:T(8,128)(2,1)}) custom-call(s32[4,8]{1,0:T(4,128)S(1)} %bitcast.9, bf16[128,512]{1,0:T(8,128)(2,1)S(1)} %shard_map.56.refs_0_, bf16[128,512]{1,0:T(8,128)(2,1)S(1)} %collective-permute-done.13.refs_1_, bf16[128,512]{1,0:T(8,128)(2,1)S(1)} %collective-permute-done.8.refs_2_, ...), custom_call_target="tpu_custom_call" | custom-call | flops 134217728 | bytes 1048576 | tf_op jit(solution)/shard_map/pallas_call | solution.py:298
  31.2 0.1 collective-permute-done.12.refs_3_
  31.3 2.0 %collective-permute-done.11.refs_2_ = bf16[128,512]{1,0:T(8,128)(2,1)S(1)} collective-permute-done((bf16[128,512]{1,0:T(8,128)(2,1)S(1)}, bf16[128,512]{1,0:T(8,128)(2,1)S(1)}, u32[]{:S(2)}, u32[]{:S(2)}) %collective-permute-start.11) | collective-permute-done | bytes 131104 | tf_op jit(solution)/shard_map/ppermute | solution.py:102
  33.4 0.6 %collective-permute-done.9.refs_1_ = bf16[128,512]{1,0:T(8,128)(2,1)S(1)} collective-permute-done((bf16[128,512]{1,0:T(8,128)(2,1)S(1)}, bf16[128,512]{1,0:T(8,128)(2,1)S(1)}, u32[]{:S(2)}, u32[]{:S(2)}) %collective-permute-start.9) | collective-permute-done | bytes 131104 | tf_op jit(solution)/shard_map/ppermute | solution.py:101
  34.0 0.0 collective-permute-start.16
  34.0 0.5 %collective-permute-start.17 = (bf16[128,512]{1,0:T(8,128)(2,1)S(1)}, bf16[128,512]{1,0:T(8,128)(2,1)S(1)}, u32[]{:S(2)}, u32[]{:S(2)}) collective-permute-start(bf16[128,512]{1,0:T(8,128)(2,1)S(1)} %collective-permute-done.11.refs_2_), channel_id=1, source_target_pairs={{0,1},{1,0},{2,3},{3,2},{4,5},{5,4},{6,7},{7,6},{8,9},{9,8},{10,11... | collective-permute-start | bytes 393224 | tf_op jit(solution)/shard_map/ppermute | solution.py:333
  34.5 0.0 collective-permute-start.18
  34.5 0.6 %collective-permute-start.19 = (bf16[128,512]{1,0:T(8,128)(2,1)S(1)}, bf16[128,512]{1,0:T(8,128)(2,1)S(1)}, u32[]{:S(2)}, u32[]{:S(2)}) collective-permute-start(bf16[128,512]{1,0:T(8,128)(2,1)S(1)} %collective-permute-done.9.refs_1_), channel_id=1, source_target_pairs={{0,4},{4,8},{8,12},{12,14},{14,10},{10,6},{6,2},{2,0},{1,5},{5,9},... | collective-permute-start | bytes 393224 | tf_op jit(solution)/shard_map/ppermute | solution.py:109
  35.0 0.0 collective-permute-done.21.refs_3_
  35.0 1.5 %collective-permute-start.20 = (bf16[128,512]{1,0:T(8,128)(2,1)S(1)}, bf16[128,512]{1,0:T(8,128)(2,1)S(1)}, u32[]{:S(2)}, u32[]{:S(2)}) collective-permute-start(bf16[128,512]{1,0:T(8,128)(2,1)S(1)} %collective-permute-done.11.refs_2_), channel_id=1, source_target_pairs={{4,0},{8,4},{12,8},{14,12},{10,14},{6,10},{2,6},{0,2},{5,1},{9,5},... | collective-permute-start | bytes 393224 | tf_op jit(solution)/shard_map/ppermute | solution.py:110
  36.5 0.0 collective-permute-done.16.refs_4_
  36.5 0.0 collective-permute-start.24
  36.5 0.0 collective-permute-done.17.refs_5_
  36.5 0.7 %shard_map.58.refs_7_ = bf16[1,4,256,512]{3,2,1,0:T(8,128)(2,1)} custom-call(s32[4,8]{1,0:T(4,128)S(1)} %bitcast.10, bf16[256,256]{1,0:T(8,128)(2,1)S(1)} %get-tuple-element.33.refs_0_, bf16[128,512]{1,0:T(8,128)(2,1)S(1)} %collective-permute-done.9.refs_1_, bf16[128,512]{1,0:T(8,128)(2,1)S(1)} %collective-permute-done.11.refs_2_, ...), custom_call_target="tpu_custom_call", output_to_operand_aliasing={{}: (8, {})} | custom-call | flops 201326592 | bytes 1572864 | tf_op jit(solution)/shard_map/pallas_call | solution.py:298
  37.2 3.1 %collective-permute-done.19.refs_1_ = bf16[128,512]{1,0:T(8,128)(2,1)S(1)} collective-permute-done((bf16[128,512]{1,0:T(8,128)(2,1)S(1)}, bf16[128,512]{1,0:T(8,128)(2,1)S(1)}, u32[]{:S(2)}, u32[]{:S(2)}) %collective-permute-start.19) | collective-permute-done | bytes 131104 | tf_op jit(solution)/shard_map/ppermute | solution.py:109
  40.4 0.2 collective-permute-done.20.refs_2_
  40.6 0.5 %collective-permute-start.23 = (bf16[128,512]{1,0:T(8,128)(2,1)S(1)}, bf16[128,512]{1,0:T(8,128)(2,1)S(1)}, u32[]{:S(2)}, u32[]{:S(2)}) collective-permute-start(bf16[128,512]{1,0:T(8,128)(2,1)S(1)} %collective-permute-done.20.refs_2_), channel_id=1, source_target_pairs={{0,1},{1,0},{2,3},{3,2},{4,5},{5,4},{6,7},{7,6},{8,9},{9,8},{10,11... | collective-permute-start | bytes 393224 | tf_op jit(solution)/shard_map/ppermute | solution.py:333
  41.1 0.8 %collective-permute-done.22.refs_4_ = bf16[128,512]{1,0:T(8,128)(2,1)S(1)} collective-permute-done((bf16[128,512]{1,0:T(8,128)(2,1)S(1)}, bf16[128,512]{1,0:T(8,128)(2,1)S(1)}, u32[]{:S(2)}, u32[]{:S(2)}) %collective-permute-start.22) | collective-permute-done | bytes 131104 | tf_op jit(solution)/shard_map/ppermute | solution.py:333
  41.9 0.2 collective-permute-done.23.refs_5_
  42.1 0.7 %shard_map.59 = bf16[1,4,256,512]{3,2,1,0:T(8,128)(2,1)} custom-call(s32[4,8]{1,0:T(4,128)S(1)} %bitcast.11, bf16[256,256]{1,0:T(8,128)(2,1)S(1)} %get-tuple-element.33.refs_0_, bf16[128,512]{1,0:T(8,128)(2,1)S(1)} %collective-permute-done.19.refs_1_, bf16[128,512]{1,0:T(8,128)(2,1)S(1)} %collective-permute-done.20.refs_2_, ...), custom_call_target="tpu_custom_call", output_to_operand_aliasing={{}: (8, {})} | custom-call | flops 201326592 | bytes 1572864 | tf_op jit(solution)/shard_map/pallas_call | solution.py:298
  (17 shorter events, 0.1 us)
Async XLA Ops:
  0.0 19.9 %copy-start = (bf16[128,448]{0,1:T(8,128)(2,1)S(1)}, bf16[128,448]{0,1:T(8,128)(2,1)}, u32[]{:S(2)}) copy-start(bf16[128,448]{0,1:T(8,128)(2,1)} %param.5) | copy-start | bytes 344068
  0.0 19.9 %copy-start.2 = (f32[512]{0:T(512)S(1)}, f32[512]{0:T(512)}, u32[]{:S(2)}) copy-start(f32[512]{0:T(512)} %param.7) | copy-start | bytes 6148
  0.0 19.9 %copy-start.3 = (f32[512]{0:T(512)S(1)}, f32[512]{0:T(512)}, u32[]{:S(2)}) copy-start(f32[512]{0:T(512)} %param.8) | copy-start | bytes 6148
  0.0 8.1 %collective-permute-start = (bf16[448,128]{1,0:T(8,128)(2,1)}, bf16[448,128]{1,0:T(8,128)(2,1)S(1)}, u32[]{:S(2)}, u32[]{:S(2)}) collective-permute-start(bf16[448,128]{1,0:T(8,128)(2,1)} %bitcast.5), channel_id=1, source_target_pairs={{0,4},{4,8},{8,12},{12,14},{14,10},{10,6},{6,2},{2,0},{1,5},{5,9},... | collective-permute-start | bytes 344072 | tf_op jit(solution)/shard_map/ppermute | solution.py:98
  3.1 5.1 %collective-permute-start.2 = (bf16[448,128]{1,0:T(8,128)(2,1)}, bf16[448,128]{1,0:T(8,128)(2,1)S(1)}, u32[]{:S(2)}, u32[]{:S(2)}) collective-permute-start(bf16[448,128]{1,0:T(8,128)(2,1)} %bitcast.6), channel_id=1, source_target_pairs={{4,0},{8,4},{12,8},{14,12},{10,14},{6,10},{2,6},{0,2},{5,1},{9,5},... | collective-permute-start | bytes 344072 | tf_op jit(solution)/shard_map/ppermute | solution.py:99
  3.1 9.8 %collective-permute-start.4 = (bf16[448,128]{1,0:T(8,128)(2,1)}, bf16[448,128]{1,0:T(8,128)(2,1)S(1)}, u32[]{:S(2)}, u32[]{:S(2)}) collective-permute-start(bf16[448,128]{1,0:T(8,128)(2,1)} %bitcast.7), channel_id=1, source_target_pairs={{0,14},{12,2},{14,0},{2,12},{4,6},{8,10},{10,8},{6,4},{1,15},{13,3... | collective-permute-start | bytes 344072 | tf_op jit(solution)/shard_map/ppermute | solution.py:100
  8.1 5.9 %collective-permute-start.1 = (bf16[448,128]{1,0:T(8,128)(2,1)S(1)}, bf16[448,128]{1,0:T(8,128)(2,1)S(1)}, u32[]{:S(2)}, u32[]{:S(2)}) collective-permute-start(bf16[448,128]{1,0:T(8,128)(2,1)S(1)} %collective-permute-done.refs_0_), channel_id=1, source_target_pairs={{0,4},{4,8},{8,12},{12,14},{14,10},{10,6},{6,2},{2,0},{1,5},{5,9},... | collective-permute-start | bytes 344072 | tf_op jit(solution)/shard_map/ppermute | solution.py:101
  8.2 5.8 %collective-permute-start.3 = (bf16[448,128]{1,0:T(8,128)(2,1)S(1)}, bf16[448,128]{1,0:T(8,128)(2,1)S(1)}, u32[]{:S(2)}, u32[]{:S(2)}) collective-permute-start(bf16[448,128]{1,0:T(8,128)(2,1)S(1)} %collective-permute-done.2.refs_1_), channel_id=1, source_target_pairs={{4,0},{8,4},{12,8},{14,12},{10,14},{6,10},{2,6},{0,2},{5,1},{9,5},... | collective-permute-start | bytes 344072 | tf_op jit(solution)/shard_map/ppermute | solution.py:102
  10.1 19.2 %copy-start.1 = (s32[8,4]{0,1:T(4,128)S(1)}, s32[8,4]{0,1:T(4,128)}, u32[]{:S(2)}) copy-start(s32[8,4]{0,1:T(4,128)} %param.9) | copy-start | bytes 388
  10.1 8.0 %collective-permute-start.7 = (bf16[448,128]{1,0:T(8,128)(2,1)S(1)}, bf16[448,128]{1,0:T(8,128)(2,1)S(1)}, u32[]{:S(2)}, u32[]{:S(2)}) collective-permute-start(bf16[448,128]{1,0:T(8,128)(2,1)S(1)} %broadcast_select_fusion.1), channel_id=1, source_target_pairs={{4,6},{8,10},{10,8},{6,4},{5,7},{9,11},{11,9},{7,5},{20,22},{24,26... | collective-permute-start | bytes 344072 | tf_op jit(solution)/shard_map/ppermute | solution.py:104
  14.0 4.8 %collective-permute-start.5 = (bf16[448,128]{1,0:T(8,128)(2,1)S(1)}, bf16[448,128]{1,0:T(8,128)(2,1)S(1)}, u32[]{:S(2)}, u32[]{:S(2)}) collective-permute-start(bf16[448,128]{1,0:T(8,128)(2,1)S(1)} %collective-permute-done.1.refs_2_), channel_id=1, source_target_pairs={{0,4},{4,8},{8,12},{12,14},{14,10},{10,6},{6,2},{2,0},{1,5},{5,9},... | collective-permute-start | bytes 344072 | tf_op jit(solution)/shard_map/ppermute | solution.py:109
  15.1 4.8 %collective-permute-start.6 = (bf16[448,128]{1,0:T(8,128)(2,1)S(1)}, bf16[448,128]{1,0:T(8,128)(2,1)S(1)}, u32[]{:S(2)}, u32[]{:S(2)}) collective-permute-start(bf16[448,128]{1,0:T(8,128)(2,1)S(1)} %collective-permute-done.3.refs_3_), channel_id=1, source_target_pairs={{4,0},{8,4},{12,8},{14,12},{10,14},{6,10},{2,6},{0,2},{5,1},{9,5},... | collective-permute-start | bytes 344072 | tf_op jit(solution)/shard_map/ppermute | solution.py:110
  20.4 5.0 %collective-permute-start.10 = (bf16[128,512]{1,0:T(8,128)(2,1)S(1)}, bf16[128,512]{1,0:T(8,128)(2,1)S(1)}, u32[]{:S(2)}, u32[]{:S(2)}) collective-permute-start(bf16[128,512]{1,0:T(8,128)(2,1)S(1)} %shard_map.56.refs_0_), channel_id=1, source_target_pairs={{4,0},{8,4},{12,8},{14,12},{10,14},{6,10},{2,6},{0,2},{5,1},{9,5},... | collective-permute-start | bytes 393224 | tf_op jit(solution)/shard_map/ppermute | solution.py:99
  21.4 5.9 %collective-permute-start.8 = (bf16[128,512]{1,0:T(8,128)(2,1)S(1)}, bf16[128,512]{1,0:T(8,128)(2,1)S(1)}, u32[]{:S(2)}, u32[]{:S(2)}) collective-permute-start(bf16[128,512]{1,0:T(8,128)(2,1)S(1)} %shard_map.56.refs_0_), channel_id=1, source_target_pairs={{0,4},{4,8},{8,12},{12,14},{14,10},{10,6},{6,2},{2,0},{1,5},{5,9},... | collective-permute-start | bytes 393224 | tf_op jit(solution)/shard_map/ppermute | solution.py:98
  22.5 4.8 %collective-permute-start.13 = (bf16[128,512]{1,0:T(8,128)(2,1)S(1)}, bf16[128,512]{1,0:T(8,128)(2,1)S(1)}, u32[]{:S(2)}, u32[]{:S(2)}) collective-permute-start(bf16[128,512]{1,0:T(8,128)(2,1)S(1)} %shard_map.56.refs_0_), channel_id=1, source_target_pairs={{0,1},{1,0},{2,3},{3,2},{4,5},{5,4},{6,7},{7,6},{8,9},{9,8},{10,11... | collective-permute-start | bytes 393224 | tf_op jit(solution)/shard_map/ppermute | solution.py:330
  22.5 8.8 %collective-permute-start.12 = (bf16[128,512]{1,0:T(8,128)(2,1)S(1)}, bf16[128,512]{1,0:T(8,128)(2,1)S(1)}, u32[]{:S(2)}, u32[]{:S(2)}) collective-permute-start(bf16[128,512]{1,0:T(8,128)(2,1)S(1)} %shard_map.56.refs_0_), channel_id=1, source_target_pairs={{0,14},{12,2},{14,0},{2,12},{4,6},{8,10},{10,8},{6,4},{1,15},{13,3... | collective-permute-start | bytes 393224 | tf_op jit(solution)/shard_map/ppermute | solution.py:100
  25.4 3.8 %collective-permute-start.15 = (bf16[128,512]{1,0:T(8,128)(2,1)S(1)}, bf16[128,512]{1,0:T(8,128)(2,1)S(1)}, u32[]{:S(2)}, u32[]{:S(2)}) collective-permute-start(bf16[128,512]{1,0:T(8,128)(2,1)S(1)} %collective-permute-done.10.refs_3_), channel_id=1, source_target_pairs={{0,1},{1,0},{2,3},{3,2},{4,5},{5,4},{6,7},{7,6},{8,9},{9,8},{10,11... | collective-permute-start | bytes 393224 | tf_op jit(solution)/shard_map/ppermute | solution.py:333
  25.4 7.9 %collective-permute-start.11 = (bf16[128,512]{1,0:T(8,128)(2,1)S(1)}, bf16[128,512]{1,0:T(8,128)(2,1)S(1)}, u32[]{:S(2)}, u32[]{:S(2)}) collective-permute-start(bf16[128,512]{1,0:T(8,128)(2,1)S(1)} %collective-permute-done.10.refs_3_), channel_id=1, source_target_pairs={{4,0},{8,4},{12,8},{14,12},{10,14},{6,10},{2,6},{0,2},{5,1},{9,5},... | collective-permute-start | bytes 393224 | tf_op jit(solution)/shard_map/ppermute | solution.py:102
  27.3 1.3 %collective-permute-start.14 = (bf16[128,512]{1,0:T(8,128)(2,1)S(1)}, bf16[128,512]{1,0:T(8,128)(2,1)S(1)}, u32[]{:S(2)}, u32[]{:S(2)}) collective-permute-start(bf16[128,512]{1,0:T(8,128)(2,1)S(1)} %collective-permute-done.8.refs_2_), channel_id=1, source_target_pairs={{0,1},{1,0},{2,3},{3,2},{4,5},{5,4},{6,7},{7,6},{8,9},{9,8},{10,11... | collective-permute-start | bytes 393224 | tf_op jit(solution)/shard_map/ppermute | solution.py:333
  27.3 6.7 %collective-permute-start.9 = (bf16[128,512]{1,0:T(8,128)(2,1)S(1)}, bf16[128,512]{1,0:T(8,128)(2,1)S(1)}, u32[]{:S(2)}, u32[]{:S(2)}) collective-permute-start(bf16[128,512]{1,0:T(8,128)(2,1)S(1)} %collective-permute-done.8.refs_2_), channel_id=1, source_target_pairs={{0,4},{4,8},{8,12},{12,14},{14,10},{10,6},{6,2},{2,0},{1,5},{5,9},... | collective-permute-start | bytes 393224 | tf_op jit(solution)/shard_map/ppermute | solution.py:101
  28.6 6.4 %collective-permute-start.21 = (bf16[128,512]{1,0:T(8,128)(2,1)S(1)}, bf16[128,512]{1,0:T(8,128)(2,1)S(1)}, u32[]{:S(2)}, u32[]{:S(2)}) collective-permute-start(bf16[128,512]{1,0:T(8,128)(2,1)S(1)} %broadcast_select_fusion), channel_id=1, source_target_pairs={{4,6},{8,10},{10,8},{6,4},{5,7},{9,11},{11,9},{7,5},{20,22},{24,26... | collective-permute-start | bytes 393224 | tf_op jit(solution)/shard_map/ppermute | solution.py:104
  34.0 2.5 %collective-permute-start.16 = (bf16[128,512]{1,0:T(8,128)(2,1)S(1)}, bf16[128,512]{1,0:T(8,128)(2,1)S(1)}, u32[]{:S(2)}, u32[]{:S(2)}) collective-permute-start(bf16[128,512]{1,0:T(8,128)(2,1)S(1)} %collective-permute-done.9.refs_1_), channel_id=1, source_target_pairs={{0,1},{1,0},{2,3},{3,2},{4,5},{5,4},{6,7},{7,6},{8,9},{9,8},{10,11... | collective-permute-start | bytes 393224 | tf_op jit(solution)/shard_map/ppermute | solution.py:333
  34.0 2.6 %collective-permute-start.17 = (bf16[128,512]{1,0:T(8,128)(2,1)S(1)}, bf16[128,512]{1,0:T(8,128)(2,1)S(1)}, u32[]{:S(2)}, u32[]{:S(2)}) collective-permute-start(bf16[128,512]{1,0:T(8,128)(2,1)S(1)} %collective-permute-done.11.refs_2_), channel_id=1, source_target_pairs={{0,1},{1,0},{2,3},{3,2},{4,5},{5,4},{6,7},{7,6},{8,9},{9,8},{10,11... | collective-permute-start | bytes 393224 | tf_op jit(solution)/shard_map/ppermute | solution.py:333
  34.5 2.0 %collective-permute-start.18 = (bf16[128,512]{1,0:T(8,128)(2,1)S(1)}, bf16[128,512]{1,0:T(8,128)(2,1)S(1)}, u32[]{:S(2)}, u32[]{:S(2)}) collective-permute-start(bf16[128,512]{1,0:T(8,128)(2,1)S(1)} %collective-permute-done.12.refs_3_), channel_id=1, source_target_pairs={{0,1},{1,0},{2,3},{3,2},{4,5},{5,4},{6,7},{7,6},{8,9},{9,8},{10,11... | collective-permute-start | bytes 393224 | tf_op jit(solution)/shard_map/ppermute | solution.py:333
  34.5 5.9 %collective-permute-start.19 = (bf16[128,512]{1,0:T(8,128)(2,1)S(1)}, bf16[128,512]{1,0:T(8,128)(2,1)S(1)}, u32[]{:S(2)}, u32[]{:S(2)}) collective-permute-start(bf16[128,512]{1,0:T(8,128)(2,1)S(1)} %collective-permute-done.9.refs_1_), channel_id=1, source_target_pairs={{0,4},{4,8},{8,12},{12,14},{14,10},{10,6},{6,2},{2,0},{1,5},{5,9},... | collective-permute-start | bytes 393224 | tf_op jit(solution)/shard_map/ppermute | solution.py:109
  35.0 5.6 %collective-permute-start.20 = (bf16[128,512]{1,0:T(8,128)(2,1)S(1)}, bf16[128,512]{1,0:T(8,128)(2,1)S(1)}, u32[]{:S(2)}, u32[]{:S(2)}) collective-permute-start(bf16[128,512]{1,0:T(8,128)(2,1)S(1)} %collective-permute-done.11.refs_2_), channel_id=1, source_target_pairs={{4,0},{8,4},{12,8},{14,12},{10,14},{6,10},{2,6},{0,2},{5,1},{9,5},... | collective-permute-start | bytes 393224 | tf_op jit(solution)/shard_map/ppermute | solution.py:110
  36.5 4.6 %collective-permute-start.24 = (bf16[128,512]{1,0:T(8,128)(2,1)S(1)}, bf16[128,512]{1,0:T(8,128)(2,1)S(1)}, u32[]{:S(2)}, u32[]{:S(2)}) collective-permute-start(bf16[128,512]{1,0:T(8,128)(2,1)S(1)} %collective-permute-done.21.refs_3_), channel_id=1, source_target_pairs={{0,1},{1,0},{2,3},{3,2},{4,5},{5,4},{6,7},{7,6},{8,9},{9,8},{10,11... | collective-permute-start | bytes 393224 | tf_op jit(solution)/shard_map/ppermute | solution.py:333
  40.6 1.3 %collective-permute-start.22 = (bf16[128,512]{1,0:T(8,128)(2,1)S(1)}, bf16[128,512]{1,0:T(8,128)(2,1)S(1)}, u32[]{:S(2)}, u32[]{:S(2)}) collective-permute-start(bf16[128,512]{1,0:T(8,128)(2,1)S(1)} %collective-permute-done.19.refs_1_), channel_id=1, source_target_pairs={{0,1},{1,0},{2,3},{3,2},{4,5},{5,4},{6,7},{7,6},{8,9},{9,8},{10,11... | collective-permute-start | bytes 393224 | tf_op jit(solution)/shard_map/ppermute | solution.py:333
  40.6 1.5 %collective-permute-start.23 = (bf16[128,512]{1,0:T(8,128)(2,1)S(1)}, bf16[128,512]{1,0:T(8,128)(2,1)S(1)}, u32[]{:S(2)}, u32[]{:S(2)}) collective-permute-start(bf16[128,512]{1,0:T(8,128)(2,1)S(1)} %collective-permute-done.20.refs_2_), channel_id=1, source_target_pairs={{0,1},{1,0},{2,3},{3,2},{4,5},{5,4},{6,7},{7,6},{8,9},{9,8},{10,11... | collective-permute-start | bytes 393224 | tf_op jit(solution)/shard_map/ppermute | solution.py:333

commit v10 on v9

--- a/solution.py
+++ b/solution.py
@@ -91,7 +91,9 @@
         self.backward = [(d, s) for s, d in self.forward]
         beside = [(i, n - 1 - i) for i in range(n) if i % 4 in (1, 2)]
         across = [(i, (i + 4) % n) for i in range(n) if i % 4 in (0, 3)]
-        self.beside = [(walk[i], walk[j]) for i, j in beside]
+        aside = [(2 * walk[i] + t, 2 * walk[j] + t) for i, j in beside for t in range(2)]
+        stay = [(2 * walk[i] + t, 2 * walk[i] + 1 - t) for i, _ in across for t in range(2)]
+        self.beside = aside + stay
         self.across = [(walk[i], walk[j]) for i, j in across + beside]
 
     def gather(self, x, beside_second=None, beside_third=None):
@@ -101,13 +103,14 @@
         ahead_2 = lax.ppermute(ahead, "lat", self.forward)
         behind_2 = lax.ppermute(behind, "lat", self.backward)
         odd = place_on_ring(lax.axis_index("lat"), self.n) % 2 == 1
-        middle = lax.ppermute(jnp.where(odd, behind, ahead), "lat", self.beside)
+        middle = lax.ppermute(jnp.where(odd, behind, ahead), ("lat", "tok"), self.beside)
         done = beside_second(ahead, behind) if beside_second else ()
         ahead_2, behind_2, corner, done = lax.optimization_barrier(
             (ahead_2, behind_2, corner, done)
         )
         ahead_3 = lax.ppermute(ahead_2, "lat", self.forward)
         behind_3 = lax.ppermute(behind_2, "lat", self.backward)
+        done, middle = lax.optimization_barrier((done, middle))
         done = beside_third(ahead, behind, ahead_2, behind_2, corner, done)
         return done, ahead_3, behind_3, corner, middle
 
@@ -340,8 +343,8 @@
         def beside_third(ahead, behind, ahead_2, behind_2, corner, before):
             return add_tiles(before, (2, n - 2, n // 2), (ahead_2, behind_2, corner))
 
-        out, ahead, behind, _, middle = ring.gather(acts, beside_second, beside_third)
-        out, ahead, behind = lax.optimization_barrier((out, ahead, behind))
+        out, *late = ring.gather(acts, beside_second, beside_third)
+        out, (ahead, behind, _, middle) = lax.optimization_barrier((out, late))
         return add_tiles(out, (3, n - 3, n), (ahead, behind, middle))[1]
     acts = encode_gathered(residual, enc_weight, enc_bias, threshold)
     acts_twin = lax.ppermute(acts, "tok", swap)

time: 43.6 us -> 43.4 us (level)
  waiting for transfers between devices: 13.2 us -> 14.5 us
  starting transfers between devices: 23.6 us -> 22.4 us
    ppermute x2, waiting for transfers between devices: 2.15 us -> 3.28 us  [gather(): corner = lax.ppermute(x, 'lat', self.across)]
    ppermute x2, starting transfers between devices: 1.33 us -> 0.22 us  [gather(): lax.ppermute(jnp.where(odd, behind, ahead), ('lat', 'tok'), self.beside)]
    ppermute x2, starting transfers between devices: 1.66 us -> 1.16 us  [gather(): ahead_3 = lax.ppermute(ahead_2, 'lat', self.forward)]
    ppermute x2, starting transfers between devices: 2.39 us -> 2.89 us  [gather(): behind_3 = lax.ppermute(behind_2, 'lat', self.backward)]
where the time goes in v10:
time: 43.4 us; the launch traced here: 42.9 us
  starting transfers between devices  22.4 us (52%)
  waiting for transfers between devices  14.5 us (33%)
  Pallas kernels  5.88 us (14%)
    ppermute x2, starting transfers between devices, gather(): corner = lax.ppermute(x, 'lat', self.across)  7.48 us
    ppermute x2, starting transfers between devices, gather(): ahead = lax.ppermute(x, 'lat', self.forward)  4.19 us
    ppermute x2, waiting for transfers between devices, gather(): ahead_3 = lax.ppermute(ahead_2, 'lat', self.forward)  3.85 us
    ppermute x2, starting transfers between devices, gather(): behind_2 = lax.ppermute(behind, 'lat', self.backward)  3.73 us
    pallas_call x3, Pallas kernels, tiles_of(): pl.pallas_call(functools.partial(tiles_kernel, tok_scale, n, hops, first)...  3.34 us
    ppermute x2, waiting for transfers between devices, gather(): corner = lax.ppermute(x, 'lat', self.across)  3.28 us
    ppermute x2, starting transfers between devices, gather(): behind_3 = lax.ppermute(behind_2, 'lat', self.backward)  2.89 us
    ppermute x2, waiting for transfers between devices, gather(): behind_2 = lax.ppermute(behind, 'lat', self.backward)  2.09 us
  transfers between devices with their start and end apart: 25, of which 13 were waited for; matrix products, arithmetic and copies ran while one was open for 0% of the time, Pallas kernels for 11%

profile of v10, /device:TPU:0, one launch (start us, length us, event | category | flops | bytes accessed | tf_op | source)
XLA Modules:
  0.0 42.9 jit_solution(6615114097967288785)
XLA Ops:
  0.0 3.1 %collective-permute-start = (bf16[448,128]{1,0:T(8,128)(2,1)}, bf16[448,128]{1,0:T(8,128)(2,1)S(1)}, u32[]{:S(2)}, u32[]{:S(2)}) collective-permute-start(bf16[448,128]{1,0:T(8,128)(2,1)} %bitcast.5), channel_id=1, source_target_pairs={{0,4},{4,8},{8,12},{12,14},{14,10},{10,6},{6,2},{2,0},{1,5},{5,9},... | collective-permute-start | bytes 344072 | tf_op jit(solution)/shard_map/ppermute | solution.py:100
  3.1 5.0 %collective-permute-start.4 = (bf16[448,128]{1,0:T(8,128)(2,1)}, bf16[448,128]{1,0:T(8,128)(2,1)S(1)}, u32[]{:S(2)}, u32[]{:S(2)}) collective-permute-start(bf16[448,128]{1,0:T(8,128)(2,1)} %bitcast.7), channel_id=1, source_target_pairs={{0,14},{12,2},{14,0},{2,12},{4,6},{8,10},{10,8},{6,4},{1,15},{13,3... | collective-permute-start | bytes 344072 | tf_op jit(solution)/shard_map/ppermute | solution.py:102
  8.1 0.1 collective-permute-start.1
  8.2 1.9 %collective-permute-start.3 = (bf16[448,128]{1,0:T(8,128)(2,1)S(1)}, bf16[448,128]{1,0:T(8,128)(2,1)S(1)}, u32[]{:S(2)}, u32[]{:S(2)}) collective-permute-start(bf16[448,128]{1,0:T(8,128)(2,1)S(1)} %collective-permute-done.2.refs_1_), channel_id=1, source_target_pairs={{4,0},{8,4},{12,8},{14,12},{10,14},{6,10},{2,6},{0,2},{5,1},{9,5},... | collective-permute-start | bytes 344072 | tf_op jit(solution)/shard_map/ppermute | solution.py:104
  10.1 0.0 copy-start.1
  10.1 0.1 collective-permute-start.7
  10.2 2.6 %collective-permute-done.4.x_corner = bf16[448,128]{1,0:T(8,128)(2,1)S(1)} collective-permute-done((bf16[448,128]{1,0:T(8,128)(2,1)}, bf16[448,128]{1,0:T(8,128)(2,1)S(1)}, u32[]{:S(2)}, u32[]{:S(2)}) %collective-permute-start.4) | collective-permute-done | bytes 114720 | tf_op jit(solution)/shard_map/ppermute | solution.py:102
  12.9 1.1 %collective-permute-done.1.refs_2_ = bf16[448,128]{1,0:T(8,128)(2,1)S(1)} collective-permute-done((bf16[448,128]{1,0:T(8,128)(2,1)S(1)}, bf16[448,128]{1,0:T(8,128)(2,1)S(1)}, u32[]{:S(2)}, u32[]{:S(2)}) %collective-permute-start.1) | collective-permute-done | bytes 114720 | tf_op jit(solution)/shard_map/ppermute | solution.py:103
  14.0 0.0 collective-permute-done.3.refs_3_
  14.0 1.1 %collective-permute-start.5 = (bf16[448,128]{1,0:T(8,128)(2,1)S(1)}, bf16[448,128]{1,0:T(8,128)(2,1)S(1)}, u32[]{:S(2)}, u32[]{:S(2)}) collective-permute-start(bf16[448,128]{1,0:T(8,128)(2,1)S(1)} %collective-permute-done.1.refs_2_), channel_id=1, source_target_pairs={{0,4},{4,8},{8,12},{12,14},{14,10},{10,6},{6,2},{2,0},{1,5},{5,9},... | collective-permute-start | bytes 344072 | tf_op jit(solution)/shard_map/ppermute | solution.py:111
  15.1 0.9 %collective-permute-start.6 = (bf16[448,128]{1,0:T(8,128)(2,1)S(1)}, bf16[448,128]{1,0:T(8,128)(2,1)S(1)}, u32[]{:S(2)}, u32[]{:S(2)}) collective-permute-start(bf16[448,128]{1,0:T(8,128)(2,1)S(1)} %collective-permute-done.3.refs_3_), channel_id=1, source_target_pairs={{4,0},{8,4},{12,8},{14,12},{10,14},{6,10},{2,6},{0,2},{5,1},{9,5},... | collective-permute-start | bytes 344072 | tf_op jit(solution)/shard_map/ppermute | solution.py:112
  16.0 2.1 %shard_map.55 = (f32[128,512]{1,0:T(8,128)S(1)}, bf16[4,448,512]{2,1,0:T(8,128)(2,1)S(1)}) custom-call(bf16[448,128]{1,0:T(8,128)(2,1)S(1)} %collective-permute-done.refs_0_, bf16[448,128]{1,0:T(8,128)(2,1)S(1)} %collective-permute-done.2.refs_1_, bf16[448,128]{1,0:T(8,128)(2,1)S(1)} %collective-permute-done.1.refs_2_, ...), custom_call_target="tpu_custom_call" | custom-call | flops 234881024 | bytes 2818048 | tf_op jit(solution)/shard_map/pallas_call | solution.py:128
  18.1 0.7 %collective-permute-done.5.x_f = bf16[448,128]{1,0:T(8,128)(2,1)S(1)} collective-permute-done((bf16[448,128]{1,0:T(8,128)(2,1)S(1)}, bf16[448,128]{1,0:T(8,128)(2,1)S(1)}, u32[]{:S(2)}, u32[]{:S(2)}) %collective-permute-start.5) | collective-permute-done | bytes 114720 | tf_op jit(solution)/shard_map/ppermute | solution.py:111
  18.8 1.1 %collective-permute-done.6.x_b = bf16[448,128]{1,0:T(8,128)(2,1)S(1)} collective-permute-done((bf16[448,128]{1,0:T(8,128)(2,1)S(1)}, bf16[448,128]{1,0:T(8,128)(2,1)S(1)}, u32[]{:S(2)}, u32[]{:S(2)}) %collective-permute-start.6) | collective-permute-done | bytes 114720 | tf_op jit(solution)/shard_map/ppermute | solution.py:112
  19.9 0.5 %shard_map.56.refs_0_ = bf16[128,512]{1,0:T(8,128)(2,1)S(1)} custom-call(bf16[448,128]{1,0:T(8,128)(2,1)S(1)} %bitcast.8, bf16[448,128]{1,0:T(8,128)(2,1)S(1)} %collective-permute-done.5.x_f, bf16[448,128]{1,0:T(8,128)(2,1)S(1)} %collective-permute-done.6.x_b, bf16[448,128]{1,0:T(8,128)(2,1)S(1)} %collective-permute-done.4.x_corner, ...), custom_call_target="tpu_custom_call" | custom-call | flops 234881024 | bytes 2818048 | tf_op jit(solution)/shard_map/pallas_call | solution.py:143
  20.4 1.0 %collective-permute-start.10 = (bf16[128,512]{1,0:T(8,128)(2,1)S(1)}, bf16[128,512]{1,0:T(8,128)(2,1)S(1)}, u32[]{:S(2)}, u32[]{:S(2)}) collective-permute-start(bf16[128,512]{1,0:T(8,128)(2,1)S(1)} %shard_map.56.refs_0_), channel_id=1, source_target_pairs={{4,0},{8,4},{12,8},{14,12},{10,14},{6,10},{2,6},{0,2},{5,1},{9,5},... | collective-permute-start | bytes 393224 | tf_op jit(solution)/shard_map/ppermute | solution.py:101
  21.4 1.1 %collective-permute-start.8 = (bf16[128,512]{1,0:T(8,128)(2,1)S(1)}, bf16[128,512]{1,0:T(8,128)(2,1)S(1)}, u32[]{:S(2)}, u32[]{:S(2)}) collective-permute-start(bf16[128,512]{1,0:T(8,128)(2,1)S(1)} %shard_map.56.refs_0_), channel_id=1, source_target_pairs={{0,4},{4,8},{8,12},{12,14},{14,10},{10,6},{6,2},{2,0},{1,5},{5,9},... | collective-permute-start | bytes 393224 | tf_op jit(solution)/shard_map/ppermute | solution.py:100
  22.5 0.0 collective-permute-start.13
  22.5 2.5 %collective-permute-start.12 = (bf16[128,512]{1,0:T(8,128)(2,1)S(1)}, bf16[128,512]{1,0:T(8,128)(2,1)S(1)}, u32[]{:S(2)}, u32[]{:S(2)}) collective-permute-start(bf16[128,512]{1,0:T(8,128)(2,1)S(1)} %shard_map.56.refs_0_), channel_id=1, source_target_pairs={{0,14},{12,2},{14,0},{2,12},{4,6},{8,10},{10,8},{6,4},{1,15},{13,3... | collective-permute-start | bytes 393224 | tf_op jit(solution)/shard_map/ppermute | solution.py:102
  25.0 0.4 collective-permute-done.10.refs_3_
  25.4 0.0 collective-permute-start.15
  25.4 1.8 %collective-permute-start.11 = (bf16[128,512]{1,0:T(8,128)(2,1)S(1)}, bf16[128,512]{1,0:T(8,128)(2,1)S(1)}, u32[]{:S(2)}, u32[]{:S(2)}) collective-permute-start(bf16[128,512]{1,0:T(8,128)(2,1)S(1)} %collective-permute-done.10.refs_3_), channel_id=1, source_target_pairs={{4,0},{8,4},{12,8},{14,12},{10,14},{6,10},{2,6},{0,2},{5,1},{9,5},... | collective-permute-start | bytes 393224 | tf_op jit(solution)/shard_map/ppermute | solution.py:104
  27.3 0.0 collective-permute-done.8.refs_2_
  27.3 0.0 collective-permute-start.14
  27.3 0.7 %collective-permute-start.9 = (bf16[128,512]{1,0:T(8,128)(2,1)S(1)}, bf16[128,512]{1,0:T(8,128)(2,1)S(1)}, u32[]{:S(2)}, u32[]{:S(2)}) collective-permute-start(bf16[128,512]{1,0:T(8,128)(2,1)S(1)} %collective-permute-done.8.refs_2_), channel_id=1, source_target_pairs={{0,4},{4,8},{8,12},{12,14},{14,10},{10,6},{6,2},{2,0},{1,5},{5,9},... | collective-permute-start | bytes 393224 | tf_op jit(solution)/shard_map/ppermute | solution.py:103
  27.9 0.7 %collective-permute-done.14.refs_4_ = bf16[128,512]{1,0:T(8,128)(2,1)S(1)} collective-permute-done((bf16[128,512]{1,0:T(8,128)(2,1)S(1)}, bf16[128,512]{1,0:T(8,128)(2,1)S(1)}, u32[]{:S(2)}, u32[]{:S(2)}) %collective-permute-start.14) | collective-permute-done | bytes 131104 | tf_op jit(solution)/shard_map/ppermute | solution.py:336
  28.6 0.1 collective-permute-start.16
  28.8 0.0 collective-permute-done.15.refs_5_
  28.8 1.9 %shard_map.57 = (bf16[256,256]{1,0:T(8,128)(2,1)S(1)}, bf16[1,4,256,512]{3,2,1,0:T(8,128)(2,1)}) custom-call(s32[4,8]{1,0:T(4,128)S(1)} %bitcast.9, bf16[128,512]{1,0:T(8,128)(2,1)S(1)} %shard_map.56.refs_0_, bf16[128,512]{1,0:T(8,128)(2,1)S(1)} %collective-permute-done.13.refs_1_, bf16[128,512]{1,0:T(8,128)(2,1)S(1)} %collective-permute-done.8.refs_2_, ...), custom_call_target="tpu_custom_call" | custom-call | flops 134217728 | bytes 1048576 | tf_op jit(solution)/shard_map/pallas_call | solution.py:301
  30.7 0.6 %collective-permute-done.12.refs_3_ = bf16[128,512]{1,0:T(8,128)(2,1)S(1)} collective-permute-done((bf16[128,512]{1,0:T(8,128)(2,1)S(1)}, bf16[128,512]{1,0:T(8,128)(2,1)S(1)}, u32[]{:S(2)}, u32[]{:S(2)}) %collective-permute-start.12) | collective-permute-done | bytes 131104 | tf_op jit(solution)/shard_map/ppermute | solution.py:102
  31.3 2.0 %collective-permute-done.11.refs_2_ = bf16[128,512]{1,0:T(8,128)(2,1)S(1)} collective-permute-done((bf16[128,512]{1,0:T(8,128)(2,1)S(1)}, bf16[128,512]{1,0:T(8,128)(2,1)S(1)}, u32[]{:S(2)}, u32[]{:S(2)}) %collective-permute-start.11) | collective-permute-done | bytes 131104 | tf_op jit(solution)/shard_map/ppermute | solution.py:104
  33.4 0.6 %collective-permute-done.9.refs_1_ = bf16[128,512]{1,0:T(8,128)(2,1)S(1)} collective-permute-done((bf16[128,512]{1,0:T(8,128)(2,1)S(1)}, bf16[128,512]{1,0:T(8,128)(2,1)S(1)}, u32[]{:S(2)}, u32[]{:S(2)}) %collective-permute-start.9) | collective-permute-done | bytes 131104 | tf_op jit(solution)/shard_map/ppermute | solution.py:103
  34.0 0.0 collective-permute-start.17
  34.0 0.5 %collective-permute-start.18 = (bf16[128,512]{1,0:T(8,128)(2,1)S(1)}, bf16[128,512]{1,0:T(8,128)(2,1)S(1)}, u32[]{:S(2)}, u32[]{:S(2)}) collective-permute-start(bf16[128,512]{1,0:T(8,128)(2,1)S(1)} %collective-permute-done.11.refs_2_), channel_id=1, source_target_pairs={{0,1},{1,0},{2,3},{3,2},{4,5},{5,4},{6,7},{7,6},{8,9},{9,8},{10,11... | collective-permute-start | bytes 393224 | tf_op jit(solution)/shard_map/ppermute | solution.py:336
  34.5 0.0 collective-permute-start.19
  34.5 0.1 collective-permute-start.20
  34.5 2.0 %collective-permute-start.21 = (bf16[128,512]{1,0:T(8,128)(2,1)S(1)}, bf16[128,512]{1,0:T(8,128)(2,1)S(1)}, u32[]{:S(2)}, u32[]{:S(2)}) collective-permute-start(bf16[128,512]{1,0:T(8,128)(2,1)S(1)} %collective-permute-done.11.refs_2_), channel_id=1, source_target_pairs={{4,0},{8,4},{12,8},{14,12},{10,14},{6,10},{2,6},{0,2},{5,1},{9,5},... | collective-permute-start | bytes 393224 | tf_op jit(solution)/shard_map/ppermute | solution.py:112
  36.5 0.0 collective-permute-done.17.refs_4_
  36.5 0.0 collective-permute-done.18.refs_5_
  36.5 0.7 %shard_map.58.refs_7_ = bf16[1,4,256,512]{3,2,1,0:T(8,128)(2,1)} custom-call(s32[4,8]{1,0:T(4,128)S(1)} %bitcast.10, bf16[256,256]{1,0:T(8,128)(2,1)S(1)} %get-tuple-element.40.refs_0_, bf16[128,512]{1,0:T(8,128)(2,1)S(1)} %collective-permute-done.9.refs_1_, bf16[128,512]{1,0:T(8,128)(2,1)S(1)} %collective-permute-done.11.refs_2_, ...), custom_call_target="tpu_custom_call", output_to_operand_aliasing={{}: (8, {})} | custom-call | flops 201326592 | bytes 1572864 | tf_op jit(solution)/shard_map/pallas_call | solution.py:301
  37.2 3.1 %collective-permute-done.20.refs_1_ = bf16[128,512]{1,0:T(8,128)(2,1)S(1)} collective-permute-done((bf16[128,512]{1,0:T(8,128)(2,1)S(1)}, bf16[128,512]{1,0:T(8,128)(2,1)S(1)}, u32[]{:S(2)}, u32[]{:S(2)}) %collective-permute-start.20) | collective-permute-done | bytes 131104 | tf_op jit(solution)/shard_map/ppermute | solution.py:111
  40.4 0.0 collective-permute-done.21.refs_2_
  40.4 0.5 %collective-permute-start.23 = (bf16[128,512]{1,0:T(8,128)(2,1)S(1)}, bf16[128,512]{1,0:T(8,128)(2,1)S(1)}, u32[]{:S(2)}, u32[]{:S(2)}) collective-permute-start(bf16[128,512]{1,0:T(8,128)(2,1)S(1)} %collective-permute-done.21.refs_2_), channel_id=1, source_target_pairs={{0,1},{1,0},{2,3},{3,2},{4,5},{5,4},{6,7},{7,6},{8,9},{9,8},{10,11... | collective-permute-start | bytes 393224 | tf_op jit(solution)/shard_map/ppermute | solution.py:336
  40.9 0.0 collective-permute-start.24
  40.9 0.8 %collective-permute-done.22.refs_4_ = bf16[128,512]{1,0:T(8,128)(2,1)S(1)} collective-permute-done((bf16[128,512]{1,0:T(8,128)(2,1)S(1)}, bf16[128,512]{1,0:T(8,128)(2,1)S(1)}, u32[]{:S(2)}, u32[]{:S(2)}) %collective-permute-start.22) | collective-permute-done | bytes 131104 | tf_op jit(solution)/shard_map/ppermute | solution.py:336
  41.7 0.2 collective-permute-done.23.refs_5_
  41.9 0.3 collective-permute-done.24.refs_6_
  42.2 0.7 %shard_map.59 = bf16[1,4,256,512]{3,2,1,0:T(8,128)(2,1)} custom-call(s32[4,8]{1,0:T(4,128)S(1)} %bitcast.11, bf16[256,256]{1,0:T(8,128)(2,1)S(1)} %get-tuple-element.40.refs_0_, bf16[128,512]{1,0:T(8,128)(2,1)S(1)} %collective-permute-done.20.refs_1_, bf16[128,512]{1,0:T(8,128)(2,1)S(1)} %collective-permute-done.21.refs_2_, ...), custom_call_target="tpu_custom_call", output_to_operand_aliasing={{}: (8, {})} | custom-call | flops 201326592 | bytes 1572864 | tf_op jit(solution)/shard_map/pallas_call | solution.py:301
  (17 shorter events, 0.1 us)
Async XLA Ops:
  0.0 19.9 %copy-start = (bf16[128,448]{0,1:T(8,128)(2,1)S(1)}, bf16[128,448]{0,1:T(8,128)(2,1)}, u32[]{:S(2)}) copy-start(bf16[128,448]{0,1:T(8,128)(2,1)} %param.5) | copy-start | bytes 344068
  0.0 19.9 %copy-start.2 = (f32[512]{0:T(512)S(1)}, f32[512]{0:T(512)}, u32[]{:S(2)}) copy-start(f32[512]{0:T(512)} %param.7) | copy-start | bytes 6148
  0.0 19.9 %copy-start.3 = (f32[512]{0:T(512)S(1)}, f32[512]{0:T(512)}, u32[]{:S(2)}) copy-start(f32[512]{0:T(512)} %param.8) | copy-start | bytes 6148
  0.0 8.1 %collective-permute-start = (bf16[448,128]{1,0:T(8,128)(2,1)}, bf16[448,128]{1,0:T(8,128)(2,1)S(1)}, u32[]{:S(2)}, u32[]{:S(2)}) collective-permute-start(bf16[448,128]{1,0:T(8,128)(2,1)} %bitcast.5), channel_id=1, source_target_pairs={{0,4},{4,8},{8,12},{12,14},{14,10},{10,6},{6,2},{2,0},{1,5},{5,9},... | collective-permute-start | bytes 344072 | tf_op jit(solution)/shard_map/ppermute | solution.py:100
  3.1 5.1 %collective-permute-start.2 = (bf16[448,128]{1,0:T(8,128)(2,1)}, bf16[448,128]{1,0:T(8,128)(2,1)S(1)}, u32[]{:S(2)}, u32[]{:S(2)}) collective-permute-start(bf16[448,128]{1,0:T(8,128)(2,1)} %bitcast.6), channel_id=1, source_target_pairs={{4,0},{8,4},{12,8},{14,12},{10,14},{6,10},{2,6},{0,2},{5,1},{9,5},... | collective-permute-start | bytes 344072 | tf_op jit(solution)/shard_map/ppermute | solution.py:101
  3.1 9.8 %collective-permute-start.4 = (bf16[448,128]{1,0:T(8,128)(2,1)}, bf16[448,128]{1,0:T(8,128)(2,1)S(1)}, u32[]{:S(2)}, u32[]{:S(2)}) collective-permute-start(bf16[448,128]{1,0:T(8,128)(2,1)} %bitcast.7), channel_id=1, source_target_pairs={{0,14},{12,2},{14,0},{2,12},{4,6},{8,10},{10,8},{6,4},{1,15},{13,3... | collective-permute-start | bytes 344072 | tf_op jit(solution)/shard_map/ppermute | solution.py:102
  8.1 5.9 %collective-permute-start.1 = (bf16[448,128]{1,0:T(8,128)(2,1)S(1)}, bf16[448,128]{1,0:T(8,128)(2,1)S(1)}, u32[]{:S(2)}, u32[]{:S(2)}) collective-permute-start(bf16[448,128]{1,0:T(8,128)(2,1)S(1)} %collective-permute-done.refs_0_), channel_id=1, source_target_pairs={{0,4},{4,8},{8,12},{12,14},{14,10},{10,6},{6,2},{2,0},{1,5},{5,9},... | collective-permute-start | bytes 344072 | tf_op jit(solution)/shard_map/ppermute | solution.py:103
  8.2 5.8 %collective-permute-start.3 = (bf16[448,128]{1,0:T(8,128)(2,1)S(1)}, bf16[448,128]{1,0:T(8,128)(2,1)S(1)}, u32[]{:S(2)}, u32[]{:S(2)}) collective-permute-start(bf16[448,128]{1,0:T(8,128)(2,1)S(1)} %collective-permute-done.2.refs_1_), channel_id=1, source_target_pairs={{4,0},{8,4},{12,8},{14,12},{10,14},{6,10},{2,6},{0,2},{5,1},{9,5},... | collective-permute-start | bytes 344072 | tf_op jit(solution)/shard_map/ppermute | solution.py:104
  10.1 18.6 %copy-start.1 = (s32[8,4]{0,1:T(4,128)S(1)}, s32[8,4]{0,1:T(4,128)}, u32[]{:S(2)}) copy-start(s32[8,4]{0,1:T(4,128)} %param.9) | copy-start | bytes 388
  10.1 5.9 %collective-permute-start.7 = (bf16[448,128]{1,0:T(8,128)(2,1)S(1)}, bf16[448,128]{1,0:T(8,128)(2,1)S(1)}, u32[]{:S(2)}, u32[]{:S(2)}) collective-permute-start(bf16[448,128]{1,0:T(8,128)(2,1)S(1)} %broadcast_select_fusion.1), channel_id=1, source_target_pairs={{4,6},{5,7},{8,10},{9,11},{10,8},{11,9},{6,4},{7,5},{0,1},{1,0},{1... | collective-permute-start | bytes 344072 | tf_op jit(solution)/shard_map/ppermute | solution.py:106
  14.0 4.8 %collective-permute-start.5 = (bf16[448,128]{1,0:T(8,128)(2,1)S(1)}, bf16[448,128]{1,0:T(8,128)(2,1)S(1)}, u32[]{:S(2)}, u32[]{:S(2)}) collective-permute-start(bf16[448,128]{1,0:T(8,128)(2,1)S(1)} %collective-permute-done.1.refs_2_), channel_id=1, source_target_pairs={{0,4},{4,8},{8,12},{12,14},{14,10},{10,6},{6,2},{2,0},{1,5},{5,9},... | collective-permute-start | bytes 344072 | tf_op jit(solution)/shard_map/ppermute | solution.py:111
  15.1 4.8 %collective-permute-start.6 = (bf16[448,128]{1,0:T(8,128)(2,1)S(1)}, bf16[448,128]{1,0:T(8,128)(2,1)S(1)}, u32[]{:S(2)}, u32[]{:S(2)}) collective-permute-start(bf16[448,128]{1,0:T(8,128)(2,1)S(1)} %collective-permute-done.3.refs_3_), channel_id=1, source_target_pairs={{4,0},{8,4},{12,8},{14,12},{10,14},{6,10},{2,6},{0,2},{5,1},{9,5},... | collective-permute-start | bytes 344072 | tf_op jit(solution)/shard_map/ppermute | solution.py:112
  20.4 5.0 %collective-permute-start.10 = (bf16[128,512]{1,0:T(8,128)(2,1)S(1)}, bf16[128,512]{1,0:T(8,128)(2,1)S(1)}, u32[]{:S(2)}, u32[]{:S(2)}) collective-permute-start(bf16[128,512]{1,0:T(8,128)(2,1)S(1)} %shard_map.56.refs_0_), channel_id=1, source_target_pairs={{4,0},{8,4},{12,8},{14,12},{10,14},{6,10},{2,6},{0,2},{5,1},{9,5},... | collective-permute-start | bytes 393224 | tf_op jit(solution)/shard_map/ppermute | solution.py:101
  21.4 5.9 %collective-permute-start.8 = (bf16[128,512]{1,0:T(8,128)(2,1)S(1)}, bf16[128,512]{1,0:T(8,128)(2,1)S(1)}, u32[]{:S(2)}, u32[]{:S(2)}) collective-permute-start(bf16[128,512]{1,0:T(8,128)(2,1)S(1)} %shard_map.56.refs_0_), channel_id=1, source_target_pairs={{0,4},{4,8},{8,12},{12,14},{14,10},{10,6},{6,2},{2,0},{1,5},{5,9},... | collective-permute-start | bytes 393224 | tf_op jit(solution)/shard_map/ppermute | solution.py:100
  22.5 4.8 %collective-permute-start.13 = (bf16[128,512]{1,0:T(8,128)(2,1)S(1)}, bf16[128,512]{1,0:T(8,128)(2,1)S(1)}, u32[]{:S(2)}, u32[]{:S(2)}) collective-permute-start(bf16[128,512]{1,0:T(8,128)(2,1)S(1)} %shard_map.56.refs_0_), channel_id=1, source_target_pairs={{0,1},{1,0},{2,3},{3,2},{4,5},{5,4},{6,7},{7,6},{8,9},{9,8},{10,11... | collective-permute-start | bytes 393224 | tf_op jit(solution)/shard_map/ppermute | solution.py:333
  22.5 8.8 %collective-permute-start.12 = (bf16[128,512]{1,0:T(8,128)(2,1)S(1)}, bf16[128,512]{1,0:T(8,128)(2,1)S(1)}, u32[]{:S(2)}, u32[]{:S(2)}) collective-permute-start(bf16[128,512]{1,0:T(8,128)(2,1)S(1)} %shard_map.56.refs_0_), channel_id=1, source_target_pairs={{0,14},{12,2},{14,0},{2,12},{4,6},{8,10},{10,8},{6,4},{1,15},{13,3... | collective-permute-start | bytes 393224 | tf_op jit(solution)/shard_map/ppermute | solution.py:102
  25.4 3.3 %collective-permute-start.15 = (bf16[128,512]{1,0:T(8,128)(2,1)S(1)}, bf16[128,512]{1,0:T(8,128)(2,1)S(1)}, u32[]{:S(2)}, u32[]{:S(2)}) collective-permute-start(bf16[128,512]{1,0:T(8,128)(2,1)S(1)} %collective-permute-done.10.refs_3_), channel_id=1, source_target_pairs={{0,1},{1,0},{2,3},{3,2},{4,5},{5,4},{6,7},{7,6},{8,9},{9,8},{10,11... | collective-permute-start | bytes 393224 | tf_op jit(solution)/shard_map/ppermute | solution.py:336
  25.4 7.9 %collective-permute-start.11 = (bf16[128,512]{1,0:T(8,128)(2,1)S(1)}, bf16[128,512]{1,0:T(8,128)(2,1)S(1)}, u32[]{:S(2)}, u32[]{:S(2)}) collective-permute-start(bf16[128,512]{1,0:T(8,128)(2,1)S(1)} %collective-permute-done.10.refs_3_), channel_id=1, source_target_pairs={{4,0},{8,4},{12,8},{14,12},{10,14},{6,10},{2,6},{0,2},{5,1},{9,5},... | collective-permute-start | bytes 393224 | tf_op jit(solution)/shard_map/ppermute | solution.py:104
  27.3 1.3 %collective-permute-start.14 = (bf16[128,512]{1,0:T(8,128)(2,1)S(1)}, bf16[128,512]{1,0:T(8,128)(2,1)S(1)}, u32[]{:S(2)}, u32[]{:S(2)}) collective-permute-start(bf16[128,512]{1,0:T(8,128)(2,1)S(1)} %collective-permute-done.8.refs_2_), channel_id=1, source_target_pairs={{0,1},{1,0},{2,3},{3,2},{4,5},{5,4},{6,7},{7,6},{8,9},{9,8},{10,11... | collective-permute-start | bytes 393224 | tf_op jit(solution)/shard_map/ppermute | solution.py:336
  27.3 6.7 %collective-permute-start.9 = (bf16[128,512]{1,0:T(8,128)(2,1)S(1)}, bf16[128,512]{1,0:T(8,128)(2,1)S(1)}, u32[]{:S(2)}, u32[]{:S(2)}) collective-permute-start(bf16[128,512]{1,0:T(8,128)(2,1)S(1)} %collective-permute-done.8.refs_2_), channel_id=1, source_target_pairs={{0,4},{4,8},{8,12},{12,14},{14,10},{10,6},{6,2},{2,0},{1,5},{5,9},... | collective-permute-start | bytes 393224 | tf_op jit(solution)/shard_map/ppermute | solution.py:103
  28.6 5.9 %collective-permute-start.16 = (bf16[128,512]{1,0:T(8,128)(2,1)S(1)}, bf16[128,512]{1,0:T(8,128)(2,1)S(1)}, u32[]{:S(2)}, u32[]{:S(2)}) collective-permute-start(bf16[128,512]{1,0:T(8,128)(2,1)S(1)} %broadcast_select_fusion), channel_id=1, source_target_pairs={{4,6},{5,7},{8,10},{9,11},{10,8},{11,9},{6,4},{7,5},{0,1},{1,0},{1... | collective-permute-start | bytes 393224 | tf_op jit(solution)/shard_map/ppermute | solution.py:106
  34.0 2.5 %collective-permute-start.17 = (bf16[128,512]{1,0:T(8,128)(2,1)S(1)}, bf16[128,512]{1,0:T(8,128)(2,1)S(1)}, u32[]{:S(2)}, u32[]{:S(2)}) collective-permute-start(bf16[128,512]{1,0:T(8,128)(2,1)S(1)} %collective-permute-done.9.refs_1_), channel_id=1, source_target_pairs={{0,1},{1,0},{2,3},{3,2},{4,5},{5,4},{6,7},{7,6},{8,9},{9,8},{10,11... | collective-permute-start | bytes 393224 | tf_op jit(solution)/shard_map/ppermute | solution.py:336
  34.0 2.5 %collective-permute-start.18 = (bf16[128,512]{1,0:T(8,128)(2,1)S(1)}, bf16[128,512]{1,0:T(8,128)(2,1)S(1)}, u32[]{:S(2)}, u32[]{:S(2)}) collective-permute-start(bf16[128,512]{1,0:T(8,128)(2,1)S(1)} %collective-permute-done.11.refs_2_), channel_id=1, source_target_pairs={{0,1},{1,0},{2,3},{3,2},{4,5},{5,4},{6,7},{7,6},{8,9},{9,8},{10,11... | collective-permute-start | bytes 393224 | tf_op jit(solution)/shard_map/ppermute | solution.py:336
  34.5 2.0 %collective-permute-start.19 = (bf16[128,512]{1,0:T(8,128)(2,1)S(1)}, bf16[128,512]{1,0:T(8,128)(2,1)S(1)}, u32[]{:S(2)}, u32[]{:S(2)}) collective-permute-start(bf16[128,512]{1,0:T(8,128)(2,1)S(1)} %collective-permute-done.12.refs_3_), channel_id=1, source_target_pairs={{0,1},{1,0},{2,3},{3,2},{4,5},{5,4},{6,7},{7,6},{8,9},{9,8},{10,11... | collective-permute-start | bytes 393224 | tf_op jit(solution)/shard_map/ppermute | solution.py:336
  34.5 5.9 %collective-permute-start.20 = (bf16[128,512]{1,0:T(8,128)(2,1)S(1)}, bf16[128,512]{1,0:T(8,128)(2,1)S(1)}, u32[]{:S(2)}, u32[]{:S(2)}) collective-permute-start(bf16[128,512]{1,0:T(8,128)(2,1)S(1)} %collective-permute-done.9.refs_1_), channel_id=1, source_target_pairs={{0,4},{4,8},{8,12},{12,14},{14,10},{10,6},{6,2},{2,0},{1,5},{5,9},... | collective-permute-start | bytes 393224 | tf_op jit(solution)/shard_map/ppermute | solution.py:111
  34.5 5.9 %collective-permute-start.21 = (bf16[128,512]{1,0:T(8,128)(2,1)S(1)}, bf16[128,512]{1,0:T(8,128)(2,1)S(1)}, u32[]{:S(2)}, u32[]{:S(2)}) collective-permute-start(bf16[128,512]{1,0:T(8,128)(2,1)S(1)} %collective-permute-done.11.refs_2_), channel_id=1, source_target_pairs={{4,0},{8,4},{12,8},{14,12},{10,14},{6,10},{2,6},{0,2},{5,1},{9,5},... | collective-permute-start | bytes 393224 | tf_op jit(solution)/shard_map/ppermute | solution.py:112
  40.4 1.3 %collective-permute-start.22 = (bf16[128,512]{1,0:T(8,128)(2,1)S(1)}, bf16[128,512]{1,0:T(8,128)(2,1)S(1)}, u32[]{:S(2)}, u32[]{:S(2)}) collective-permute-start(bf16[128,512]{1,0:T(8,128)(2,1)S(1)} %collective-permute-done.20.refs_1_), channel_id=1, source_target_pairs={{0,1},{1,0},{2,3},{3,2},{4,5},{5,4},{6,7},{7,6},{8,9},{9,8},{10,11... | collective-permute-start | bytes 393224 | tf_op jit(solution)/shard_map/ppermute | solution.py:336
  40.4 1.5 %collective-permute-start.23 = (bf16[128,512]{1,0:T(8,128)(2,1)S(1)}, bf16[128,512]{1,0:T(8,128)(2,1)S(1)}, u32[]{:S(2)}, u32[]{:S(2)}) collective-permute-start(bf16[128,512]{1,0:T(8,128)(2,1)S(1)} %collective-permute-done.21.refs_2_), channel_id=1, source_target_pairs={{0,1},{1,0},{2,3},{3,2},{4,5},{5,4},{6,7},{7,6},{8,9},{9,8},{10,11... | collective-permute-start | bytes 393224 | tf_op jit(solution)/shard_map/ppermute | solution.py:336
  40.9 1.3 %collective-permute-start.24 = (bf16[128,512]{1,0:T(8,128)(2,1)S(1)}, bf16[128,512]{1,0:T(8,128)(2,1)S(1)}, u32[]{:S(2)}, u32[]{:S(2)}) collective-permute-start(bf16[128,512]{1,0:T(8,128)(2,1)S(1)} %collective-permute-done.16.refs_3_), channel_id=1, source_target_pairs={{0,1},{1,0},{2,3},{3,2},{4,5},{5,4},{6,7},{7,6},{8,9},{9,8},{10,11... | collective-permute-start | bytes 393224 | tf_op jit(solution)/shard_map/ppermute | solution.py:336

commit v11 on v10

--- a/solution.py
+++ b/solution.py
@@ -222,7 +222,6 @@
     me = lax.axis_index("lat")
     listed = partners[k, me]
     hop = lax.rem(place_on_ring(me, n) + n - place_on_ring(jnp.minimum(listed, n - 1), n), n)
-    hop = jnp.where((hop == n // 2) & jnp.logical_not(on_corner(n)), n, hop)
     return jnp.where(listed < n, hop, -1)
 
 
@@ -340,12 +339,14 @@
         def beside_second(ahead, behind):
             return add_tiles(None, (1, n - 1), (ahead, behind))
 
-        def beside_third(ahead, behind, ahead_2, behind_2, corner, before):
-            return add_tiles(before, (2, n - 2, n // 2), (ahead_2, behind_2, corner))
+        def beside_third(ahead, behind, ahead_2, behind_2, _, before):
+            return add_tiles(before, (2, n - 2), (ahead_2, behind_2))
 
         out, *late = ring.gather(acts, beside_second, beside_third)
-        out, (ahead, behind, _, middle) = lax.optimization_barrier((out, late))
-        return add_tiles(out, (3, n - 3, n), (ahead, behind, middle))[1]
+        ahead, behind, corner, middle = late
+        far = jnp.where(on_corner(n), corner, middle)
+        out, ahead, behind = lax.optimization_barrier((out, ahead, behind))
+        return add_tiles(out, (3, n - 3, n // 2), (ahead, behind, far))[1]
     acts = encode_gathered(residual, enc_weight, enc_bias, threshold)
     acts_twin = lax.ppermute(acts, "tok", swap)
     slices = lax.all_to_all(acts.reshape(n, tok_rows // n, width), "lat", 0, 0)

time: 43.4 us -> 43.3 us (level)
  the two profiles are of different devices: /device:TPU:0 before, /device:TPU:21 now
where the time goes in v11:
time: 43.3 us; the launch traced here: 43.2 us
  starting transfers between devices  21.4 us (49%)
  waiting for transfers between devices  14.9 us (34%)
  Pallas kernels  6.72 us (16%)
    ppermute x7, starting transfers between devices, add_tiles(): twins = [lax.ppermute(block, 'tok', swap) for block in blocks]  5.78 us
    ppermute x2, waiting for transfers between devices, gather(): ahead_2 = lax.ppermute(ahead, 'lat', self.forward)  4.44 us
    pallas_call x3, Pallas kernels, tiles_of(): pl.pallas_call(functools.partial(tiles_kernel, tok_scale, n, hops, first)...  4.16 us
    ppermute x2, waiting for transfers between devices, gather(): behind_3 = lax.ppermute(behind_2, 'lat', self.backward)  4.15 us
    ppermute x2, starting transfers between devices, gather(): ahead_3 = lax.ppermute(ahead_2, 'lat', self.forward)  4 us
    ppermute x1, starting transfers between devices, body(): acts_twin = lax.ppermute(acts, 'tok', swap)  3.16 us
    ppermute x2, starting transfers between devices, gather(): ahead = lax.ppermute(x, 'lat', self.forward)  2.77 us
    ppermute x7, waiting for transfers between devices, add_tiles(): twins = [lax.ppermute(block, 'tok', swap) for block in blocks]  2.42 us
  transfers between devices with their start and end apart: 24, of which 12 were waited for; matrix products, arithmetic and copies ran while one was open for 0% of the time, Pallas kernels for 11%

profile of v11, /device:TPU:21, one launch (start us, length us, event | category | flops | bytes accessed | tf_op | source)
XLA Modules:
  0.0 43.2 jit_solution(16401111194266057199)
XLA Ops:
  0.0 1.3 %collective-permute-start = (bf16[448,128]{1,0:T(8,128)(2,1)}, bf16[448,128]{1,0:T(8,128)(2,1)S(1)}, u32[]{:S(2)}, u32[]{:S(2)}) collective-permute-start(bf16[448,128]{1,0:T(8,128)(2,1)} %bitcast.5), channel_id=1, source_target_pairs={{0,4},{4,8},{8,12},{12,14},{14,10},{10,6},{6,2},{2,0},{1,5},{5,9},... | collective-permute-start | bytes 344072 | tf_op jit(solution)/shard_map/ppermute | solution.py:100
  1.4 0.2 collective-permute-start.2
  1.5 1.2 %collective-permute-start.4 = (bf16[448,128]{1,0:T(8,128)(2,1)}, bf16[448,128]{1,0:T(8,128)(2,1)S(1)}, u32[]{:S(2)}, u32[]{:S(2)}) collective-permute-start(bf16[448,128]{1,0:T(8,128)(2,1)} %bitcast.7), channel_id=1, source_target_pairs={{0,14},{12,2},{14,0},{2,12},{4,6},{8,10},{10,8},{6,4},{1,15},{13,3... | collective-permute-start | bytes 344072 | tf_op jit(solution)/shard_map/ppermute | solution.py:102
  2.7 1.5 %collective-permute-done.refs_0_ = bf16[448,128]{1,0:T(8,128)(2,1)S(1)} collective-permute-done((bf16[448,128]{1,0:T(8,128)(2,1)}, bf16[448,128]{1,0:T(8,128)(2,1)S(1)}, u32[]{:S(2)}, u32[]{:S(2)}) %collective-permute-start) | collective-permute-done | bytes 114720 | tf_op jit(solution)/shard_map/ppermute | solution.py:100
  4.3 1.3 %collective-permute-start.1 = (bf16[448,128]{1,0:T(8,128)(2,1)S(1)}, bf16[448,128]{1,0:T(8,128)(2,1)S(1)}, u32[]{:S(2)}, u32[]{:S(2)}) collective-permute-start(bf16[448,128]{1,0:T(8,128)(2,1)S(1)} %collective-permute-done.refs_0_), channel_id=1, source_target_pairs={{0,4},{4,8},{8,12},{12,14},{14,10},{10,6},{6,2},{2,0},{1,5},{5,9},... | collective-permute-start | bytes 344072 | tf_op jit(solution)/shard_map/ppermute | solution.py:103
  5.6 0.0 collective-permute-done.2.refs_1_
  5.6 0.2 collective-permute-start.3
  5.8 1.3 %collective-permute-start.7 = (bf16[448,128]{1,0:T(8,128)(2,1)S(1)}, bf16[448,128]{1,0:T(8,128)(2,1)S(1)}, u32[]{:S(2)}, u32[]{:S(2)}) collective-permute-start(bf16[448,128]{1,0:T(8,128)(2,1)S(1)} %broadcast_select_fusion.2), channel_id=1, source_target_pairs={{4,6},{5,7},{8,10},{9,11},{10,8},{11,9},{6,4},{7,5},{0,1},{1,0},{1... | collective-permute-start | bytes 344072 | tf_op jit(solution)/shard_map/ppermute | solution.py:106
  7.1 0.0 collective-permute-done.4.x_corner
  7.1 3.9 %collective-permute-done.1.refs_2_ = bf16[448,128]{1,0:T(8,128)(2,1)S(1)} collective-permute-done((bf16[448,128]{1,0:T(8,128)(2,1)S(1)}, bf16[448,128]{1,0:T(8,128)(2,1)S(1)}, u32[]{:S(2)}, u32[]{:S(2)}) %collective-permute-start.1) | collective-permute-done | bytes 114720 | tf_op jit(solution)/shard_map/ppermute | solution.py:103
  11.0 0.0 collective-permute-done.3.refs_3_
  11.0 1.4 %collective-permute-start.5 = (bf16[448,128]{1,0:T(8,128)(2,1)S(1)}, bf16[448,128]{1,0:T(8,128)(2,1)S(1)}, u32[]{:S(2)}, u32[]{:S(2)}) collective-permute-start(bf16[448,128]{1,0:T(8,128)(2,1)S(1)} %collective-permute-done.1.refs_2_), channel_id=1, source_target_pairs={{0,4},{4,8},{8,12},{12,14},{14,10},{10,6},{6,2},{2,0},{1,5},{5,9},... | collective-permute-start | bytes 344072 | tf_op jit(solution)/shard_map/ppermute | solution.py:111
  12.4 0.0 collective-permute-start.6
  12.4 0.0 collective-permute-done.7.x_middle
  12.5 2.1 %shard_map.55 = (f32[128,512]{1,0:T(8,128)S(1)}, bf16[4,448,512]{2,1,0:T(8,128)(2,1)S(1)}) custom-call(bf16[448,128]{1,0:T(8,128)(2,1)S(1)} %collective-permute-done.refs_0_, bf16[448,128]{1,0:T(8,128)(2,1)S(1)} %collective-permute-done.2.refs_1_, bf16[448,128]{1,0:T(8,128)(2,1)S(1)} %collective-permute-done.1.refs_2_, ...), custom_call_target="tpu_custom_call" | custom-call | flops 234881024 | bytes 2818048 | tf_op jit(solution)/shard_map/pallas_call | solution.py:128
  14.5 0.1 collective-permute-done.5.x_f
  14.6 1.7 %collective-permute-done.6.x_b = bf16[448,128]{1,0:T(8,128)(2,1)S(1)} collective-permute-done((bf16[448,128]{1,0:T(8,128)(2,1)S(1)}, bf16[448,128]{1,0:T(8,128)(2,1)S(1)}, u32[]{:S(2)}, u32[]{:S(2)}) %collective-permute-start.6) | collective-permute-done | bytes 114720 | tf_op jit(solution)/shard_map/ppermute | solution.py:112
  16.3 0.5 %shard_map.56.refs_0_ = bf16[128,512]{1,0:T(8,128)(2,1)S(1)} custom-call(bf16[448,128]{1,0:T(8,128)(2,1)S(1)} %bitcast.8, bf16[448,128]{1,0:T(8,128)(2,1)S(1)} %collective-permute-done.5.x_f, bf16[448,128]{1,0:T(8,128)(2,1)S(1)} %collective-permute-done.6.x_b, bf16[448,128]{1,0:T(8,128)(2,1)S(1)} %collective-permute-done.4.x_corner, ...), custom_call_target="tpu_custom_call" | custom-call | flops 234881024 | bytes 2818048 | tf_op jit(solution)/shard_map/pallas_call | solution.py:143
  16.8 0.1 collective-permute-start.10
  16.9 1.4 %collective-permute-start.8 = (bf16[128,512]{1,0:T(8,128)(2,1)S(1)}, bf16[128,512]{1,0:T(8,128)(2,1)S(1)}, u32[]{:S(2)}, u32[]{:S(2)}) collective-permute-start(bf16[128,512]{1,0:T(8,128)(2,1)S(1)} %shard_map.56.refs_0_), channel_id=1, source_target_pairs={{0,4},{4,8},{8,12},{12,14},{14,10},{10,6},{6,2},{2,0},{1,5},{5,9},... | collective-permute-start | bytes 393224 | tf_op jit(solution)/shard_map/ppermute | solution.py:100
  18.4 3.2 %collective-permute-start.13 = (bf16[128,512]{1,0:T(8,128)(2,1)S(1)}, bf16[128,512]{1,0:T(8,128)(2,1)S(1)}, u32[]{:S(2)}, u32[]{:S(2)}) collective-permute-start(bf16[128,512]{1,0:T(8,128)(2,1)S(1)} %shard_map.56.refs_0_), channel_id=1, source_target_pairs={{0,1},{1,0},{2,3},{3,2},{4,5},{5,4},{6,7},{7,6},{8,9},{9,8},{10,11... | collective-permute-start | bytes 393224 | tf_op jit(solution)/shard_map/ppermute | solution.py:332
  21.5 2.9 %collective-permute-start.15 = (bf16[128,512]{1,0:T(8,128)(2,1)S(1)}, bf16[128,512]{1,0:T(8,128)(2,1)S(1)}, u32[]{:S(2)}, u32[]{:S(2)}) collective-permute-start(bf16[128,512]{1,0:T(8,128)(2,1)S(1)} %collective-permute-done.10.refs_3_), channel_id=1, source_target_pairs={{0,1},{1,0},{2,3},{3,2},{4,5},{5,4},{6,7},{7,6},{8,9},{9,8},{10,11... | collective-permute-start | bytes 393224 | tf_op jit(solution)/shard_map/ppermute | solution.py:335
  24.5 0.8 %collective-permute-start.11 = (bf16[128,512]{1,0:T(8,128)(2,1)S(1)}, bf16[128,512]{1,0:T(8,128)(2,1)S(1)}, u32[]{:S(2)}, u32[]{:S(2)}) collective-permute-start(bf16[128,512]{1,0:T(8,128)(2,1)S(1)} %collective-permute-done.10.refs_3_), channel_id=1, source_target_pairs={{4,0},{8,4},{12,8},{14,12},{10,14},{6,10},{2,6},{0,2},{5,1},{9,5},... | collective-permute-start | bytes 393224 | tf_op jit(solution)/shard_map/ppermute | solution.py:104
  25.2 0.3 collective-permute-start.14
  25.5 0.0 collective-permute-done.13.refs_1_
  25.5 0.7 %collective-permute-start.9 = (bf16[128,512]{1,0:T(8,128)(2,1)S(1)}, bf16[128,512]{1,0:T(8,128)(2,1)S(1)}, u32[]{:S(2)}, u32[]{:S(2)}) collective-permute-start(bf16[128,512]{1,0:T(8,128)(2,1)S(1)} %collective-permute-done.8.refs_2_), channel_id=1, source_target_pairs={{0,4},{4,8},{8,12},{12,14},{14,10},{10,6},{6,2},{2,0},{1,5},{5,9},... | collective-permute-start | bytes 393224 | tf_op jit(solution)/shard_map/ppermute | solution.py:103
  26.2 0.3 collective-permute-done.14.refs_4_
  26.6 0.0 collective-permute-start.16
  26.6 0.0 collective-permute-done.15.refs_5_
  26.6 1.9 %shard_map.57 = (bf16[256,256]{1,0:T(8,128)(2,1)S(1)}, bf16[1,4,256,512]{3,2,1,0:T(8,128)(2,1)}) custom-call(s32[4,8]{1,0:T(4,128)S(1)} %bitcast.9, bf16[128,512]{1,0:T(8,128)(2,1)S(1)} %shard_map.56.refs_0_, bf16[128,512]{1,0:T(8,128)(2,1)S(1)} %collective-permute-done.13.refs_1_, bf16[128,512]{1,0:T(8,128)(2,1)S(1)} %collective-permute-done.8.refs_2_, ...), custom_call_target="tpu_custom_call" | custom-call | flops 134217728 | bytes 1048576 | tf_op jit(solution)/shard_map/pallas_call | solution.py:300
  28.5 1.4 %collective-permute-done.11.refs_2_ = bf16[128,512]{1,0:T(8,128)(2,1)S(1)} collective-permute-done((bf16[128,512]{1,0:T(8,128)(2,1)S(1)}, bf16[128,512]{1,0:T(8,128)(2,1)S(1)}, u32[]{:S(2)}, u32[]{:S(2)}) %collective-permute-start.11) | collective-permute-done | bytes 131104 | tf_op jit(solution)/shard_map/ppermute | solution.py:104
  29.9 0.5 %collective-permute-done.9.refs_1_ = bf16[128,512]{1,0:T(8,128)(2,1)S(1)} collective-permute-done((bf16[128,512]{1,0:T(8,128)(2,1)S(1)}, bf16[128,512]{1,0:T(8,128)(2,1)S(1)}, u32[]{:S(2)}, u32[]{:S(2)}) %collective-permute-start.9) | collective-permute-done | bytes 131104 | tf_op jit(solution)/shard_map/ppermute | solution.py:103
  30.4 1.0 %collective-permute-start.17 = (bf16[128,512]{1,0:T(8,128)(2,1)S(1)}, bf16[128,512]{1,0:T(8,128)(2,1)S(1)}, u32[]{:S(2)}, u32[]{:S(2)}) collective-permute-start(bf16[128,512]{1,0:T(8,128)(2,1)S(1)} %collective-permute-done.9.refs_1_), channel_id=1, source_target_pairs={{0,1},{1,0},{2,3},{3,2},{4,5},{5,4},{6,7},{7,6},{8,9},{9,8},{10,11... | collective-permute-start | bytes 393224 | tf_op jit(solution)/shard_map/ppermute | solution.py:335
  31.4 2.6 %collective-permute-start.19 = (bf16[128,512]{1,0:T(8,128)(2,1)S(1)}, bf16[128,512]{1,0:T(8,128)(2,1)S(1)}, u32[]{:S(2)}, u32[]{:S(2)}) collective-permute-start(bf16[128,512]{1,0:T(8,128)(2,1)S(1)} %collective-permute-done.9.refs_1_), channel_id=1, source_target_pairs={{0,4},{4,8},{8,12},{12,14},{14,10},{10,6},{6,2},{2,0},{1,5},{5,9},... | collective-permute-start | bytes 393224 | tf_op jit(solution)/shard_map/ppermute | solution.py:111
  34.0 0.3 collective-permute-start.18
  34.4 0.0 collective-permute-start.20
  34.4 0.0 collective-permute-done.16
  34.4 0.2 collective-permute-start.23
  34.6 0.0 collective-permute-done.17.refs_3_
  34.6 0.7 %collective-permute-done.18.refs_4_ = bf16[128,512]{1,0:T(8,128)(2,1)S(1)} collective-permute-done((bf16[128,512]{1,0:T(8,128)(2,1)S(1)}, bf16[128,512]{1,0:T(8,128)(2,1)S(1)}, u32[]{:S(2)}, u32[]{:S(2)}) %collective-permute-start.18) | collective-permute-done | bytes 131104 | tf_op jit(solution)/shard_map/ppermute | solution.py:335
  35.4 0.7 %shard_map.58.refs_7_ = bf16[1,4,256,512]{3,2,1,0:T(8,128)(2,1)} custom-call(s32[4,8]{1,0:T(4,128)S(1)} %bitcast.10, bf16[256,256]{1,0:T(8,128)(2,1)S(1)} %get-tuple-element.37.refs_0_, bf16[128,512]{1,0:T(8,128)(2,1)S(1)} %collective-permute-done.9.refs_1_, bf16[128,512]{1,0:T(8,128)(2,1)S(1)} %collective-permute-done.11.refs_2_, ...), custom_call_target="tpu_custom_call", output_to_operand_aliasing={{}: (6, {})} | custom-call | flops 134217728 | bytes 1048576 | tf_op jit(solution)/shard_map/pallas_call | solution.py:300
  36.0 0.8 %collective-permute-done.19.refs_1_ = bf16[128,512]{1,0:T(8,128)(2,1)S(1)} collective-permute-done((bf16[128,512]{1,0:T(8,128)(2,1)S(1)}, bf16[128,512]{1,0:T(8,128)(2,1)S(1)}, u32[]{:S(2)}, u32[]{:S(2)}) %collective-permute-start.19) | collective-permute-done | bytes 131104 | tf_op jit(solution)/shard_map/ppermute | solution.py:111
  36.9 2.4 %collective-permute-done.20.refs_2_ = bf16[128,512]{1,0:T(8,128)(2,1)S(1)} collective-permute-done((bf16[128,512]{1,0:T(8,128)(2,1)S(1)}, bf16[128,512]{1,0:T(8,128)(2,1)S(1)}, u32[]{:S(2)}, u32[]{:S(2)}) %collective-permute-start.20) | collective-permute-done | bytes 131104 | tf_op jit(solution)/shard_map/ppermute | solution.py:112
  39.3 1.0 %collective-permute-start.21 = (bf16[128,512]{1,0:T(8,128)(2,1)S(1)}, bf16[128,512]{1,0:T(8,128)(2,1)S(1)}, u32[]{:S(2)}, u32[]{:S(2)}) collective-permute-start(bf16[128,512]{1,0:T(8,128)(2,1)S(1)} %collective-permute-done.19.refs_1_), channel_id=1, source_target_pairs={{0,1},{1,0},{2,3},{3,2},{4,5},{5,4},{6,7},{7,6},{8,9},{9,8},{10,11... | collective-permute-start | bytes 393224 | tf_op jit(solution)/shard_map/ppermute | solution.py:335
  40.3 0.0 collective-permute-start.22
  40.3 1.0 %collective-permute-done.21.refs_4_ = bf16[128,512]{1,0:T(8,128)(2,1)S(1)} collective-permute-done((bf16[128,512]{1,0:T(8,128)(2,1)S(1)}, bf16[128,512]{1,0:T(8,128)(2,1)S(1)}, u32[]{:S(2)}, u32[]{:S(2)}) %collective-permute-start.21) | collective-permute-done | bytes 131104 | tf_op jit(solution)/shard_map/ppermute | solution.py:335
  41.3 0.4 collective-permute-done.22.refs_5_
  41.6 1.6 %shard_map.59 = bf16[1,4,256,512]{3,2,1,0:T(8,128)(2,1)} custom-call(s32[4,8]{1,0:T(4,128)S(1)} %bitcast.11, bf16[256,256]{1,0:T(8,128)(2,1)S(1)} %get-tuple-element.37.refs_0_, bf16[128,512]{1,0:T(8,128)(2,1)S(1)} %collective-permute-done.19.refs_1_, bf16[128,512]{1,0:T(8,128)(2,1)S(1)} %collective-permute-done.20.refs_2_, ...), custom_call_target="tpu_custom_call", output_to_operand_aliasing={{}: (8, {})} | custom-call | flops 201326592 | bytes 1572864 | tf_op jit(solution)/shard_map/pallas_call | solution.py:300
  (16 shorter events, 0.1 us)
Async XLA Ops:
  0.0 16.3 %copy-start = (bf16[128,448]{0,1:T(8,128)(2,1)S(1)}, bf16[128,448]{0,1:T(8,128)(2,1)}, u32[]{:S(2)}) copy-start(bf16[128,448]{0,1:T(8,128)(2,1)} %param.5) | copy-start | bytes 344068
  0.0 16.3 %copy-start.2 = (f32[512]{0:T(512)S(1)}, f32[512]{0:T(512)}, u32[]{:S(2)}) copy-start(f32[512]{0:T(512)} %param.7) | copy-start | bytes 6148
  0.0 16.3 %copy-start.3 = (f32[512]{0:T(512)S(1)}, f32[512]{0:T(512)}, u32[]{:S(2)}) copy-start(f32[512]{0:T(512)} %param.8) | copy-start | bytes 6148
  0.0 4.3 %collective-permute-start = (bf16[448,128]{1,0:T(8,128)(2,1)}, bf16[448,128]{1,0:T(8,128)(2,1)S(1)}, u32[]{:S(2)}, u32[]{:S(2)}) collective-permute-start(bf16[448,128]{1,0:T(8,128)(2,1)} %bitcast.5), channel_id=1, source_target_pairs={{0,4},{4,8},{8,12},{12,14},{14,10},{10,6},{6,2},{2,0},{1,5},{5,9},... | collective-permute-start | bytes 344072 | tf_op jit(solution)/shard_map/ppermute | solution.py:100
  1.4 4.2 %collective-permute-start.2 = (bf16[448,128]{1,0:T(8,128)(2,1)}, bf16[448,128]{1,0:T(8,128)(2,1)S(1)}, u32[]{:S(2)}, u32[]{:S(2)}) collective-permute-start(bf16[448,128]{1,0:T(8,128)(2,1)} %bitcast.6), channel_id=1, source_target_pairs={{4,0},{8,4},{12,8},{14,12},{10,14},{6,10},{2,6},{0,2},{5,1},{9,5},... | collective-permute-start | bytes 344072 | tf_op jit(solution)/shard_map/ppermute | solution.py:101
  1.5 5.5 %collective-permute-start.4 = (bf16[448,128]{1,0:T(8,128)(2,1)}, bf16[448,128]{1,0:T(8,128)(2,1)S(1)}, u32[]{:S(2)}, u32[]{:S(2)}) collective-permute-start(bf16[448,128]{1,0:T(8,128)(2,1)} %bitcast.7), channel_id=1, source_target_pairs={{0,14},{12,2},{14,0},{2,12},{4,6},{8,10},{10,8},{6,4},{1,15},{13,3... | collective-permute-start | bytes 344072 | tf_op jit(solution)/shard_map/ppermute | solution.py:102
  4.3 6.7 %collective-permute-start.1 = (bf16[448,128]{1,0:T(8,128)(2,1)S(1)}, bf16[448,128]{1,0:T(8,128)(2,1)S(1)}, u32[]{:S(2)}, u32[]{:S(2)}) collective-permute-start(bf16[448,128]{1,0:T(8,128)(2,1)S(1)} %collective-permute-done.refs_0_), channel_id=1, source_target_pairs={{0,4},{4,8},{8,12},{12,14},{14,10},{10,6},{6,2},{2,0},{1,5},{5,9},... | collective-permute-start | bytes 344072 | tf_op jit(solution)/shard_map/ppermute | solution.py:103
  5.6 5.4 %collective-permute-start.3 = (bf16[448,128]{1,0:T(8,128)(2,1)S(1)}, bf16[448,128]{1,0:T(8,128)(2,1)S(1)}, u32[]{:S(2)}, u32[]{:S(2)}) collective-permute-start(bf16[448,128]{1,0:T(8,128)(2,1)S(1)} %collective-permute-done.2.refs_1_), channel_id=1, source_target_pairs={{4,0},{8,4},{12,8},{14,12},{10,14},{6,10},{2,6},{0,2},{5,1},{9,5},... | collective-permute-start | bytes 344072 | tf_op jit(solution)/shard_map/ppermute | solution.py:104
  5.8 6.7 %collective-permute-start.7 = (bf16[448,128]{1,0:T(8,128)(2,1)S(1)}, bf16[448,128]{1,0:T(8,128)(2,1)S(1)}, u32[]{:S(2)}, u32[]{:S(2)}) collective-permute-start(bf16[448,128]{1,0:T(8,128)(2,1)S(1)} %broadcast_select_fusion.2), channel_id=1, source_target_pairs={{4,6},{5,7},{8,10},{9,11},{10,8},{11,9},{6,4},{7,5},{0,1},{1,0},{1... | collective-permute-start | bytes 344072 | tf_op jit(solution)/shard_map/ppermute | solution.py:106
  11.0 3.6 %collective-permute-start.5 = (bf16[448,128]{1,0:T(8,128)(2,1)S(1)}, bf16[448,128]{1,0:T(8,128)(2,1)S(1)}, u32[]{:S(2)}, u32[]{:S(2)}) collective-permute-start(bf16[448,128]{1,0:T(8,128)(2,1)S(1)} %collective-permute-done.1.refs_2_), channel_id=1, source_target_pairs={{0,4},{4,8},{8,12},{12,14},{14,10},{10,6},{6,2},{2,0},{1,5},{5,9},... | collective-permute-start | bytes 344072 | tf_op jit(solution)/shard_map/ppermute | solution.py:111
  12.4 3.9 %collective-permute-start.6 = (bf16[448,128]{1,0:T(8,128)(2,1)S(1)}, bf16[448,128]{1,0:T(8,128)(2,1)S(1)}, u32[]{:S(2)}, u32[]{:S(2)}) collective-permute-start(bf16[448,128]{1,0:T(8,128)(2,1)S(1)} %collective-permute-done.3.refs_3_), channel_id=1, source_target_pairs={{4,0},{8,4},{12,8},{14,12},{10,14},{6,10},{2,6},{0,2},{5,1},{9,5},... | collective-permute-start | bytes 344072 | tf_op jit(solution)/shard_map/ppermute | solution.py:112
  12.4 14.1 %copy-start.1 = (s32[8,4]{0,1:T(4,128)S(1)}, s32[8,4]{0,1:T(4,128)}, u32[]{:S(2)}) copy-start(s32[8,4]{0,1:T(4,128)} %param.9) | copy-start | bytes 388
  16.8 4.7 %collective-permute-start.10 = (bf16[128,512]{1,0:T(8,128)(2,1)S(1)}, bf16[128,512]{1,0:T(8,128)(2,1)S(1)}, u32[]{:S(2)}, u32[]{:S(2)}) collective-permute-start(bf16[128,512]{1,0:T(8,128)(2,1)S(1)} %shard_map.56.refs_0_), channel_id=1, source_target_pairs={{4,0},{8,4},{12,8},{14,12},{10,14},{6,10},{2,6},{0,2},{5,1},{9,5},... | collective-permute-start | bytes 393224 | tf_op jit(solution)/shard_map/ppermute | solution.py:101
  16.9 8.3 %collective-permute-start.8 = (bf16[128,512]{1,0:T(8,128)(2,1)S(1)}, bf16[128,512]{1,0:T(8,128)(2,1)S(1)}, u32[]{:S(2)}, u32[]{:S(2)}) collective-permute-start(bf16[128,512]{1,0:T(8,128)(2,1)S(1)} %shard_map.56.refs_0_), channel_id=1, source_target_pairs={{0,4},{4,8},{8,12},{12,14},{14,10},{10,6},{6,2},{2,0},{1,5},{5,9},... | collective-permute-start | bytes 393224 | tf_op jit(solution)/shard_map/ppermute | solution.py:100
  18.4 7.1 %collective-permute-start.13 = (bf16[128,512]{1,0:T(8,128)(2,1)S(1)}, bf16[128,512]{1,0:T(8,128)(2,1)S(1)}, u32[]{:S(2)}, u32[]{:S(2)}) collective-permute-start(bf16[128,512]{1,0:T(8,128)(2,1)S(1)} %shard_map.56.refs_0_), channel_id=1, source_target_pairs={{0,1},{1,0},{2,3},{3,2},{4,5},{5,4},{6,7},{7,6},{8,9},{9,8},{10,11... | collective-permute-start | bytes 393224 | tf_op jit(solution)/shard_map/ppermute | solution.py:332
  21.5 7.0 %collective-permute-start.12 = (bf16[128,512]{1,0:T(8,128)(2,1)S(1)}, bf16[128,512]{1,0:T(8,128)(2,1)S(1)}, u32[]{:S(2)}, u32[]{:S(2)}) collective-permute-start(bf16[128,512]{1,0:T(8,128)(2,1)S(1)} %shard_map.56.refs_0_), channel_id=1, source_target_pairs={{0,14},{12,2},{14,0},{2,12},{4,6},{8,10},{10,8},{6,4},{1,15},{13,3... | collective-permute-start | bytes 393224 | tf_op jit(solution)/shard_map/ppermute | solution.py:102
  21.5 5.0 %collective-permute-start.15 = (bf16[128,512]{1,0:T(8,128)(2,1)S(1)}, bf16[128,512]{1,0:T(8,128)(2,1)S(1)}, u32[]{:S(2)}, u32[]{:S(2)}) collective-permute-start(bf16[128,512]{1,0:T(8,128)(2,1)S(1)} %collective-permute-done.10.refs_3_), channel_id=1, source_target_pairs={{0,1},{1,0},{2,3},{3,2},{4,5},{5,4},{6,7},{7,6},{8,9},{9,8},{10,11... | collective-permute-start | bytes 393224 | tf_op jit(solution)/shard_map/ppermute | solution.py:335
  24.5 5.4 %collective-permute-start.11 = (bf16[128,512]{1,0:T(8,128)(2,1)S(1)}, bf16[128,512]{1,0:T(8,128)(2,1)S(1)}, u32[]{:S(2)}, u32[]{:S(2)}) collective-permute-start(bf16[128,512]{1,0:T(8,128)(2,1)S(1)} %collective-permute-done.10.refs_3_), channel_id=1, source_target_pairs={{4,0},{8,4},{12,8},{14,12},{10,14},{6,10},{2,6},{0,2},{5,1},{9,5},... | collective-permute-start | bytes 393224 | tf_op jit(solution)/shard_map/ppermute | solution.py:104
  25.2 1.3 %collective-permute-start.14 = (bf16[128,512]{1,0:T(8,128)(2,1)S(1)}, bf16[128,512]{1,0:T(8,128)(2,1)S(1)}, u32[]{:S(2)}, u32[]{:S(2)}) collective-permute-start(bf16[128,512]{1,0:T(8,128)(2,1)S(1)} %collective-permute-done.8.refs_2_), channel_id=1, source_target_pairs={{0,1},{1,0},{2,3},{3,2},{4,5},{5,4},{6,7},{7,6},{8,9},{9,8},{10,11... | collective-permute-start | bytes 393224 | tf_op jit(solution)/shard_map/ppermute | solution.py:335
  25.5 4.9 %collective-permute-start.9 = (bf16[128,512]{1,0:T(8,128)(2,1)S(1)}, bf16[128,512]{1,0:T(8,128)(2,1)S(1)}, u32[]{:S(2)}, u32[]{:S(2)}) collective-permute-start(bf16[128,512]{1,0:T(8,128)(2,1)S(1)} %collective-permute-done.8.refs_2_), channel_id=1, source_target_pairs={{0,4},{4,8},{8,12},{12,14},{14,10},{10,6},{6,2},{2,0},{1,5},{5,9},... | collective-permute-start | bytes 393224 | tf_op jit(solution)/shard_map/ppermute | solution.py:103
  26.6 7.8 %collective-permute-start.16 = (bf16[128,512]{1,0:T(8,128)(2,1)S(1)}, bf16[128,512]{1,0:T(8,128)(2,1)S(1)}, u32[]{:S(2)}, u32[]{:S(2)}) collective-permute-start(bf16[128,512]{1,0:T(8,128)(2,1)S(1)} %broadcast_select_fusion.1), channel_id=1, source_target_pairs={{4,6},{5,7},{8,10},{9,11},{10,8},{11,9},{6,4},{7,5},{0,1},{1,0},{1... | collective-permute-start | bytes 393224 | tf_op jit(solution)/shard_map/ppermute | solution.py:106
  30.4 4.2 %collective-permute-start.17 = (bf16[128,512]{1,0:T(8,128)(2,1)S(1)}, bf16[128,512]{1,0:T(8,128)(2,1)S(1)}, u32[]{:S(2)}, u32[]{:S(2)}) collective-permute-start(bf16[128,512]{1,0:T(8,128)(2,1)S(1)} %collective-permute-done.9.refs_1_), channel_id=1, source_target_pairs={{0,1},{1,0},{2,3},{3,2},{4,5},{5,4},{6,7},{7,6},{8,9},{9,8},{10,11... | collective-permute-start | bytes 393224 | tf_op jit(solution)/shard_map/ppermute | solution.py:335
  31.4 5.4 %collective-permute-start.19 = (bf16[128,512]{1,0:T(8,128)(2,1)S(1)}, bf16[128,512]{1,0:T(8,128)(2,1)S(1)}, u32[]{:S(2)}, u32[]{:S(2)}) collective-permute-start(bf16[128,512]{1,0:T(8,128)(2,1)S(1)} %collective-permute-done.9.refs_1_), channel_id=1, source_target_pairs={{0,4},{4,8},{8,12},{12,14},{14,10},{10,6},{6,2},{2,0},{1,5},{5,9},... | collective-permute-start | bytes 393224 | tf_op jit(solution)/shard_map/ppermute | solution.py:111
  34.0 1.3 %collective-permute-start.18 = (bf16[128,512]{1,0:T(8,128)(2,1)S(1)}, bf16[128,512]{1,0:T(8,128)(2,1)S(1)}, u32[]{:S(2)}, u32[]{:S(2)}) collective-permute-start(bf16[128,512]{1,0:T(8,128)(2,1)S(1)} %collective-permute-done.11.refs_2_), channel_id=1, source_target_pairs={{0,1},{1,0},{2,3},{3,2},{4,5},{5,4},{6,7},{7,6},{8,9},{9,8},{10,11... | collective-permute-start | bytes 393224 | tf_op jit(solution)/shard_map/ppermute | solution.py:335
  34.4 4.9 %collective-permute-start.20 = (bf16[128,512]{1,0:T(8,128)(2,1)S(1)}, bf16[128,512]{1,0:T(8,128)(2,1)S(1)}, u32[]{:S(2)}, u32[]{:S(2)}) collective-permute-start(bf16[128,512]{1,0:T(8,128)(2,1)S(1)} %collective-permute-done.11.refs_2_), channel_id=1, source_target_pairs={{4,0},{8,4},{12,8},{14,12},{10,14},{6,10},{2,6},{0,2},{5,1},{9,5},... | collective-permute-start | bytes 393224 | tf_op jit(solution)/shard_map/ppermute | solution.py:112
  34.4 5.9 %collective-permute-start.23 = (bf16[128,512]{1,0:T(8,128)(2,1)S(1)}, bf16[128,512]{1,0:T(8,128)(2,1)S(1)}, u32[]{:S(2)}, u32[]{:S(2)}) collective-permute-start(bf16[128,512]{1,0:T(8,128)(2,1)S(1)} %broadcast_select_fusion.refs_3_), channel_id=1, source_target_pairs={{0,1},{1,0},{2,3},{3,2},{4,5},{5,4},{6,7},{7,6},{8,9},{9,8},{10,11... | collective-permute-start | bytes 393224 | tf_op jit(solution)/shard_map/ppermute | solution.py:335
  39.3 2.0 %collective-permute-start.21 = (bf16[128,512]{1,0:T(8,128)(2,1)S(1)}, bf16[128,512]{1,0:T(8,128)(2,1)S(1)}, u32[]{:S(2)}, u32[]{:S(2)}) collective-permute-start(bf16[128,512]{1,0:T(8,128)(2,1)S(1)} %collective-permute-done.19.refs_1_), channel_id=1, source_target_pairs={{0,1},{1,0},{2,3},{3,2},{4,5},{5,4},{6,7},{7,6},{8,9},{9,8},{10,11... | collective-permute-start | bytes 393224 | tf_op jit(solution)/shard_map/ppermute | solution.py:335
  40.3 1.3 %collective-permute-start.22 = (bf16[128,512]{1,0:T(8,128)(2,1)S(1)}, bf16[128,512]{1,0:T(8,128)(2,1)S(1)}, u32[]{:S(2)}, u32[]{:S(2)}) collective-permute-start(bf16[128,512]{1,0:T(8,128)(2,1)S(1)} %collective-permute-done.20.refs_2_), channel_id=1, source_target_pairs={{0,1},{1,0},{2,3},{3,2},{4,5},{5,4},{6,7},{7,6},{8,9},{9,8},{10,11... | collective-permute-start | bytes 393224 | tf_op jit(solution)/shard_map/ppermute | solution.py:335

commit v12 on v11

--- a/solution.py
+++ b/solution.py
@@ -220,7 +220,9 @@
 
 def hop_of_slot(partners, k, n):
     me = lax.axis_index("lat")
-    listed = partners[k, me]
+    row = partners[k : k + 1, :]
+    mine = lax.broadcasted_iota(jnp.int32, row.shape, 1) == me
+    listed = jnp.sum(jnp.where(mine, row, 0))
     hop = lax.rem(place_on_ring(me, n) + n - place_on_ring(jnp.minimum(listed, n - 1), n), n)
     return jnp.where(listed < n, hop, -1)
 
@@ -296,7 +298,7 @@
         operands = (partners, *owns, *blocks, *twins)
     else:
         operands = (partners, before[0], *blocks, *twins, before[1])
-    specs = [in_smem] + [in_vmem] * (len(operands) - 1)
+    specs = [in_vmem] * len(operands)
     done = pl.pallas_call(
         functools.partial(tiles_kernel, tok_scale, n, hops, first),
         out_shape=(left_shape, out_shape) if first else out_shape,

time: 43.3 us -> 42.8 us (0.988)
  the two profiles are of different devices: /device:TPU:21 before, /device:TPU:0 now
where the time goes in v12:
time: 42.8 us; the launch traced here: 42.6 us
  starting transfers between devices  22.2 us (52%)
  waiting for transfers between devices  14 us (33%)
  Pallas kernels  6.2 us (14%)
    ppermute x2, starting transfers between devices, gather(): corner = lax.ppermute(x, 'lat', self.across)  7.48 us
    ppermute x2, starting transfers between devices, gather(): ahead = lax.ppermute(x, 'lat', self.forward)  4.19 us
    ppermute x2, waiting for transfers between devices, gather(): corner = lax.ppermute(x, 'lat', self.across)  3.79 us
    ppermute x2, starting transfers between devices, gather(): behind_2 = lax.ppermute(behind, 'lat', self.backward)  3.73 us
    pallas_call x3, Pallas kernels, tiles_of(): pl.pallas_call(functools.partial(tiles_kernel, tok_scale, n, hops, first)...  3.64 us
    ppermute x2, waiting for transfers between devices, gather(): ahead_3 = lax.ppermute(ahead_2, 'lat', self.forward)  3.1 us
    ppermute x2, starting transfers between devices, gather(): behind_3 = lax.ppermute(behind_2, 'lat', self.backward)  2.66 us
    ppermute x2, waiting for transfers between devices, gather(): behind_2 = lax.ppermute(behind, 'lat', self.backward)  2.09 us
  transfers between devices with their start and end apart: 24, of which 13 were waited for; matrix products, arithmetic and copies ran while one was open for 0% of the time, Pallas kernels for 11%

profile of v12, /device:TPU:0, one launch (start us, length us, event | category | flops | bytes accessed | tf_op | source)
XLA Modules:
  0.0 42.6 jit_solution(3962347308370303122)
XLA Ops:
  0.0 3.1 %collective-permute-start = (bf16[448,128]{1,0:T(8,128)(2,1)}, bf16[448,128]{1,0:T(8,128)(2,1)S(1)}, u32[]{:S(2)}, u32[]{:S(2)}) collective-permute-start(bf16[448,128]{1,0:T(8,128)(2,1)} %bitcast.5), channel_id=1, source_target_pairs={{0,4},{4,8},{8,12},{12,14},{14,10},{10,6},{6,2},{2,0},{1,5},{5,9},... | collective-permute-start | bytes 344072 | tf_op jit(solution)/shard_map/ppermute | solution.py:100
  3.1 0.0 collective-permute-start.2
  3.1 5.0 %collective-permute-start.4 = (bf16[448,128]{1,0:T(8,128)(2,1)}, bf16[448,128]{1,0:T(8,128)(2,1)S(1)}, u32[]{:S(2)}, u32[]{:S(2)}) collective-permute-start(bf16[448,128]{1,0:T(8,128)(2,1)} %bitcast.7), channel_id=1, source_target_pairs={{0,14},{12,2},{14,0},{2,12},{4,6},{8,10},{10,8},{6,4},{1,15},{13,3... | collective-permute-start | bytes 344072 | tf_op jit(solution)/shard_map/ppermute | solution.py:102
  8.1 0.0 collective-permute-done.refs_0_
  8.1 0.1 collective-permute-start.1
  8.2 0.0 collective-permute-done.2.refs_1_
  8.2 1.9 %collective-permute-start.3 = (bf16[448,128]{1,0:T(8,128)(2,1)S(1)}, bf16[448,128]{1,0:T(8,128)(2,1)S(1)}, u32[]{:S(2)}, u32[]{:S(2)}) collective-permute-start(bf16[448,128]{1,0:T(8,128)(2,1)S(1)} %collective-permute-done.2.refs_1_), channel_id=1, source_target_pairs={{4,0},{8,4},{12,8},{14,12},{10,14},{6,10},{2,6},{0,2},{5,1},{9,5},... | collective-permute-start | bytes 344072 | tf_op jit(solution)/shard_map/ppermute | solution.py:104
  10.1 0.1 collective-permute-start.7
  10.2 2.7 %collective-permute-done.4.x_corner = bf16[448,128]{1,0:T(8,128)(2,1)S(1)} collective-permute-done((bf16[448,128]{1,0:T(8,128)(2,1)}, bf16[448,128]{1,0:T(8,128)(2,1)S(1)}, u32[]{:S(2)}, u32[]{:S(2)}) %collective-permute-start.4) | collective-permute-done | bytes 114720 | tf_op jit(solution)/shard_map/ppermute | solution.py:102
  12.9 1.1 %collective-permute-done.1.refs_2_ = bf16[448,128]{1,0:T(8,128)(2,1)S(1)} collective-permute-done((bf16[448,128]{1,0:T(8,128)(2,1)S(1)}, bf16[448,128]{1,0:T(8,128)(2,1)S(1)}, u32[]{:S(2)}, u32[]{:S(2)}) %collective-permute-start.1) | collective-permute-done | bytes 114720 | tf_op jit(solution)/shard_map/ppermute | solution.py:103
  14.0 0.0 collective-permute-done.3.refs_3_
  14.0 1.1 %collective-permute-start.5 = (bf16[448,128]{1,0:T(8,128)(2,1)S(1)}, bf16[448,128]{1,0:T(8,128)(2,1)S(1)}, u32[]{:S(2)}, u32[]{:S(2)}) collective-permute-start(bf16[448,128]{1,0:T(8,128)(2,1)S(1)} %collective-permute-done.1.refs_2_), channel_id=1, source_target_pairs={{0,4},{4,8},{8,12},{12,14},{14,10},{10,6},{6,2},{2,0},{1,5},{5,9},... | collective-permute-start | bytes 344072 | tf_op jit(solution)/shard_map/ppermute | solution.py:111
  15.1 0.9 %collective-permute-start.6 = (bf16[448,128]{1,0:T(8,128)(2,1)S(1)}, bf16[448,128]{1,0:T(8,128)(2,1)S(1)}, u32[]{:S(2)}, u32[]{:S(2)}) collective-permute-start(bf16[448,128]{1,0:T(8,128)(2,1)S(1)} %collective-permute-done.3.refs_3_), channel_id=1, source_target_pairs={{4,0},{8,4},{12,8},{14,12},{10,14},{6,10},{2,6},{0,2},{5,1},{9,5},... | collective-permute-start | bytes 344072 | tf_op jit(solution)/shard_map/ppermute | solution.py:112
  16.0 0.0 collective-permute-done.7.x_middle
  16.0 2.1 %shard_map.55 = (f32[128,512]{1,0:T(8,128)S(1)}, bf16[4,448,512]{2,1,0:T(8,128)(2,1)S(1)}) custom-call(bf16[448,128]{1,0:T(8,128)(2,1)S(1)} %collective-permute-done.refs_0_, bf16[448,128]{1,0:T(8,128)(2,1)S(1)} %collective-permute-done.2.refs_1_, bf16[448,128]{1,0:T(8,128)(2,1)S(1)} %collective-permute-done.1.refs_2_, ...), custom_call_target="tpu_custom_call" | custom-call | flops 234881024 | bytes 2818048 | tf_op jit(solution)/shard_map/pallas_call | solution.py:128
  18.1 0.7 %collective-permute-done.5.x_f = bf16[448,128]{1,0:T(8,128)(2,1)S(1)} collective-permute-done((bf16[448,128]{1,0:T(8,128)(2,1)S(1)}, bf16[448,128]{1,0:T(8,128)(2,1)S(1)}, u32[]{:S(2)}, u32[]{:S(2)}) %collective-permute-start.5) | collective-permute-done | bytes 114720 | tf_op jit(solution)/shard_map/ppermute | solution.py:111
  18.8 1.1 %collective-permute-done.6.x_b = bf16[448,128]{1,0:T(8,128)(2,1)S(1)} collective-permute-done((bf16[448,128]{1,0:T(8,128)(2,1)S(1)}, bf16[448,128]{1,0:T(8,128)(2,1)S(1)}, u32[]{:S(2)}, u32[]{:S(2)}) %collective-permute-start.6) | collective-permute-done | bytes 114720 | tf_op jit(solution)/shard_map/ppermute | solution.py:112
  19.9 0.5 %shard_map.56.refs_0_ = bf16[128,512]{1,0:T(8,128)(2,1)S(1)} custom-call(bf16[448,128]{1,0:T(8,128)(2,1)S(1)} %bitcast.8, bf16[448,128]{1,0:T(8,128)(2,1)S(1)} %collective-permute-done.5.x_f, bf16[448,128]{1,0:T(8,128)(2,1)S(1)} %collective-permute-done.6.x_b, bf16[448,128]{1,0:T(8,128)(2,1)S(1)} %collective-permute-done.4.x_corner, ...), custom_call_target="tpu_custom_call" | custom-call | flops 234881024 | bytes 2818048 | tf_op jit(solution)/shard_map/pallas_call | solution.py:143
  20.4 1.0 %collective-permute-start.10 = (bf16[128,512]{1,0:T(8,128)(2,1)S(1)}, bf16[128,512]{1,0:T(8,128)(2,1)S(1)}, u32[]{:S(2)}, u32[]{:S(2)}) collective-permute-start(bf16[128,512]{1,0:T(8,128)(2,1)S(1)} %shard_map.56.refs_0_), channel_id=1, source_target_pairs={{4,0},{8,4},{12,8},{14,12},{10,14},{6,10},{2,6},{0,2},{5,1},{9,5},... | collective-permute-start | bytes 393224 | tf_op jit(solution)/shard_map/ppermute | solution.py:101
  21.4 1.1 %collective-permute-start.8 = (bf16[128,512]{1,0:T(8,128)(2,1)S(1)}, bf16[128,512]{1,0:T(8,128)(2,1)S(1)}, u32[]{:S(2)}, u32[]{:S(2)}) collective-permute-start(bf16[128,512]{1,0:T(8,128)(2,1)S(1)} %shard_map.56.refs_0_), channel_id=1, source_target_pairs={{0,4},{4,8},{8,12},{12,14},{14,10},{10,6},{6,2},{2,0},{1,5},{5,9},... | collective-permute-start | bytes 393224 | tf_op jit(solution)/shard_map/ppermute | solution.py:100
  22.5 0.0 collective-permute-start.13
  22.5 2.5 %collective-permute-start.12 = (bf16[128,512]{1,0:T(8,128)(2,1)S(1)}, bf16[128,512]{1,0:T(8,128)(2,1)S(1)}, u32[]{:S(2)}, u32[]{:S(2)}) collective-permute-start(bf16[128,512]{1,0:T(8,128)(2,1)S(1)} %shard_map.56.refs_0_), channel_id=1, source_target_pairs={{0,14},{12,2},{14,0},{2,12},{4,6},{8,10},{10,8},{6,4},{1,15},{13,3... | collective-permute-start | bytes 393224 | tf_op jit(solution)/shard_map/ppermute | solution.py:102
  25.0 0.4 %collective-permute-done.10.refs_3_ = bf16[128,512]{1,0:T(8,128)(2,1)S(1)} collective-permute-done((bf16[128,512]{1,0:T(8,128)(2,1)S(1)}, bf16[128,512]{1,0:T(8,128)(2,1)S(1)}, u32[]{:S(2)}, u32[]{:S(2)}) %collective-permute-start.10) | collective-permute-done | bytes 131104 | tf_op jit(solution)/shard_map/ppermute | solution.py:101
  25.4 0.0 collective-permute-start.15
  25.4 1.8 %collective-permute-start.11 = (bf16[128,512]{1,0:T(8,128)(2,1)S(1)}, bf16[128,512]{1,0:T(8,128)(2,1)S(1)}, u32[]{:S(2)}, u32[]{:S(2)}) collective-permute-start(bf16[128,512]{1,0:T(8,128)(2,1)S(1)} %collective-permute-done.10.refs_3_), channel_id=1, source_target_pairs={{4,0},{8,4},{12,8},{14,12},{10,14},{6,10},{2,6},{0,2},{5,1},{9,5},... | collective-permute-start | bytes 393224 | tf_op jit(solution)/shard_map/ppermute | solution.py:104
  27.3 0.0 collective-permute-start.14
  27.3 0.7 %collective-permute-start.9 = (bf16[128,512]{1,0:T(8,128)(2,1)S(1)}, bf16[128,512]{1,0:T(8,128)(2,1)S(1)}, u32[]{:S(2)}, u32[]{:S(2)}) collective-permute-start(bf16[128,512]{1,0:T(8,128)(2,1)S(1)} %collective-permute-done.8.refs_2_), channel_id=1, source_target_pairs={{0,4},{4,8},{8,12},{12,14},{14,10},{10,6},{6,2},{2,0},{1,5},{5,9},... | collective-permute-start | bytes 393224 | tf_op jit(solution)/shard_map/ppermute | solution.py:103
  27.9 0.7 %collective-permute-done.14.refs_4_ = bf16[128,512]{1,0:T(8,128)(2,1)S(1)} collective-permute-done((bf16[128,512]{1,0:T(8,128)(2,1)S(1)}, bf16[128,512]{1,0:T(8,128)(2,1)S(1)}, u32[]{:S(2)}, u32[]{:S(2)}) %collective-permute-start.14) | collective-permute-done | bytes 131104 | tf_op jit(solution)/shard_map/ppermute | solution.py:337
  28.6 0.1 collective-permute-start.16
  28.8 1.4 %shard_map.57 = (bf16[256,256]{1,0:T(8,128)(2,1)S(1)}, bf16[1,4,256,512]{3,2,1,0:T(8,128)(2,1)}) custom-call(s32[4,8]{1,0:T(4,128)S(1)} %bitcast.9, bf16[128,512]{1,0:T(8,128)(2,1)S(1)} %shard_map.56.refs_0_, bf16[128,512]{1,0:T(8,128)(2,1)S(1)} %collective-permute-done.13.refs_1_, bf16[128,512]{1,0:T(8,128)(2,1)S(1)} %collective-permute-done.8.refs_2_, ...), custom_call_target="tpu_custom_call" | custom-call | flops 134217728 | bytes 1048576 | tf_op jit(solution)/shard_map/pallas_call | solution.py:302
  30.2 1.1 %collective-permute-done.12 = bf16[128,512]{1,0:T(8,128)(2,1)S(1)} collective-permute-done((bf16[128,512]{1,0:T(8,128)(2,1)S(1)}, bf16[128,512]{1,0:T(8,128)(2,1)S(1)}, u32[]{:S(2)}, u32[]{:S(2)}) %collective-permute-start.12) | collective-permute-done | bytes 131104 | tf_op jit(solution)/shard_map/ppermute | solution.py:102
  31.3 2.0 %collective-permute-done.11.refs_2_ = bf16[128,512]{1,0:T(8,128)(2,1)S(1)} collective-permute-done((bf16[128,512]{1,0:T(8,128)(2,1)S(1)}, bf16[128,512]{1,0:T(8,128)(2,1)S(1)}, u32[]{:S(2)}, u32[]{:S(2)}) %collective-permute-start.11) | collective-permute-done | bytes 131104 | tf_op jit(solution)/shard_map/ppermute | solution.py:104
  33.4 0.6 %collective-permute-done.9.refs_1_ = bf16[128,512]{1,0:T(8,128)(2,1)S(1)} collective-permute-done((bf16[128,512]{1,0:T(8,128)(2,1)S(1)}, bf16[128,512]{1,0:T(8,128)(2,1)S(1)}, u32[]{:S(2)}, u32[]{:S(2)}) %collective-permute-start.9) | collective-permute-done | bytes 131104 | tf_op jit(solution)/shard_map/ppermute | solution.py:103
  34.0 0.1 collective-permute-start.19
  34.0 0.5 %collective-permute-start.18 = (bf16[128,512]{1,0:T(8,128)(2,1)S(1)}, bf16[128,512]{1,0:T(8,128)(2,1)S(1)}, u32[]{:S(2)}, u32[]{:S(2)}) collective-permute-start(bf16[128,512]{1,0:T(8,128)(2,1)S(1)} %collective-permute-done.11.refs_2_), channel_id=1, source_target_pairs={{0,1},{1,0},{2,3},{3,2},{4,5},{5,4},{6,7},{7,6},{8,9},{9,8},{10,11... | collective-permute-start | bytes 393224 | tf_op jit(solution)/shard_map/ppermute | solution.py:337
  34.5 1.7 %collective-permute-start.20 = (bf16[128,512]{1,0:T(8,128)(2,1)S(1)}, bf16[128,512]{1,0:T(8,128)(2,1)S(1)}, u32[]{:S(2)}, u32[]{:S(2)}) collective-permute-start(bf16[128,512]{1,0:T(8,128)(2,1)S(1)} %collective-permute-done.11.refs_2_), channel_id=1, source_target_pairs={{4,0},{8,4},{12,8},{14,12},{10,14},{6,10},{2,6},{0,2},{5,1},{9,5},... | collective-permute-start | bytes 393224 | tf_op jit(solution)/shard_map/ppermute | solution.py:112
  36.2 0.0 collective-permute-done.16
  36.2 0.1 collective-permute-start.23
  36.3 0.0 collective-permute-done.17.refs_3_
  36.3 1.1 %shard_map.58.refs_7_ = bf16[1,4,256,512]{3,2,1,0:T(8,128)(2,1)} custom-call(s32[4,8]{1,0:T(4,128)S(1)} %bitcast.10, bf16[256,256]{1,0:T(8,128)(2,1)S(1)} %get-tuple-element.37.refs_0_, bf16[128,512]{1,0:T(8,128)(2,1)S(1)} %collective-permute-done.9.refs_1_, bf16[128,512]{1,0:T(8,128)(2,1)S(1)} %collective-permute-done.11.refs_2_, ...), custom_call_target="tpu_custom_call", output_to_operand_aliasing={{}: (6, {})} | custom-call | flops 134217728 | bytes 1048576 | tf_op jit(solution)/shard_map/pallas_call | solution.py:302
  37.4 2.4 %collective-permute-done.19.refs_1_ = bf16[128,512]{1,0:T(8,128)(2,1)S(1)} collective-permute-done((bf16[128,512]{1,0:T(8,128)(2,1)S(1)}, bf16[128,512]{1,0:T(8,128)(2,1)S(1)}, u32[]{:S(2)}, u32[]{:S(2)}) %collective-permute-start.19) | collective-permute-done | bytes 131104 | tf_op jit(solution)/shard_map/ppermute | solution.py:111
  39.9 0.1 collective-permute-done.20.refs_2_
  39.9 0.0 collective-permute-start.21
  39.9 0.5 %collective-permute-start.22 = (bf16[128,512]{1,0:T(8,128)(2,1)S(1)}, bf16[128,512]{1,0:T(8,128)(2,1)S(1)}, u32[]{:S(2)}, u32[]{:S(2)}) collective-permute-start(bf16[128,512]{1,0:T(8,128)(2,1)S(1)} %collective-permute-done.20.refs_2_), channel_id=1, source_target_pairs={{0,1},{1,0},{2,3},{3,2},{4,5},{5,4},{6,7},{7,6},{8,9},{9,8},{10,11... | collective-permute-start | bytes 393224 | tf_op jit(solution)/shard_map/ppermute | solution.py:337
  40.4 0.0 collective-permute-done.23.refs_6_
  40.4 0.8 %collective-permute-done.21.refs_4_ = bf16[128,512]{1,0:T(8,128)(2,1)S(1)} collective-permute-done((bf16[128,512]{1,0:T(8,128)(2,1)S(1)}, bf16[128,512]{1,0:T(8,128)(2,1)S(1)}, u32[]{:S(2)}, u32[]{:S(2)}) %collective-permute-start.21) | collective-permute-done | bytes 131104 | tf_op jit(solution)/shard_map/ppermute | solution.py:337
  41.3 0.2 collective-permute-done.22.refs_5_
  41.5 1.1 %shard_map.59 = bf16[1,4,256,512]{3,2,1,0:T(8,128)(2,1)} custom-call(s32[4,8]{1,0:T(4,128)S(1)} %bitcast.11, bf16[256,256]{1,0:T(8,128)(2,1)S(1)} %get-tuple-element.37.refs_0_, bf16[128,512]{1,0:T(8,128)(2,1)S(1)} %collective-permute-done.19.refs_1_, bf16[128,512]{1,0:T(8,128)(2,1)S(1)} %collective-permute-done.20.refs_2_, ...), custom_call_target="tpu_custom_call", output_to_operand_aliasing={{}: (8, {})} | custom-call | flops 201326592 | bytes 1572864 | tf_op jit(solution)/shard_map/pallas_call | solution.py:302
  (16 shorter events, 0.1 us)
Async XLA Ops:
  0.0 19.9 %copy-start = (bf16[128,448]{0,1:T(8,128)(2,1)S(1)}, bf16[128,448]{0,1:T(8,128)(2,1)}, u32[]{:S(2)}) copy-start(bf16[128,448]{0,1:T(8,128)(2,1)} %param.5) | copy-start | bytes 344068
  0.0 19.9 %copy-start.2 = (f32[512]{0:T(512)S(1)}, f32[512]{0:T(512)}, u32[]{:S(2)}) copy-start(f32[512]{0:T(512)} %param.7) | copy-start | bytes 6148
  0.0 19.9 %copy-start.3 = (f32[512]{0:T(512)S(1)}, f32[512]{0:T(512)}, u32[]{:S(2)}) copy-start(f32[512]{0:T(512)} %param.8) | copy-start | bytes 6148
  0.0 8.1 %collective-permute-start = (bf16[448,128]{1,0:T(8,128)(2,1)}, bf16[448,128]{1,0:T(8,128)(2,1)S(1)}, u32[]{:S(2)}, u32[]{:S(2)}) collective-permute-start(bf16[448,128]{1,0:T(8,128)(2,1)} %bitcast.5), channel_id=1, source_target_pairs={{0,4},{4,8},{8,12},{12,14},{14,10},{10,6},{6,2},{2,0},{1,5},{5,9},... | collective-permute-start | bytes 344072 | tf_op jit(solution)/shard_map/ppermute | solution.py:100
  3.1 5.1 %collective-permute-start.2 = (bf16[448,128]{1,0:T(8,128)(2,1)}, bf16[448,128]{1,0:T(8,128)(2,1)S(1)}, u32[]{:S(2)}, u32[]{:S(2)}) collective-permute-start(bf16[448,128]{1,0:T(8,128)(2,1)} %bitcast.6), channel_id=1, source_target_pairs={{4,0},{8,4},{12,8},{14,12},{10,14},{6,10},{2,6},{0,2},{5,1},{9,5},... | collective-permute-start | bytes 344072 | tf_op jit(solution)/shard_map/ppermute | solution.py:101
  3.1 9.8 %collective-permute-start.4 = (bf16[448,128]{1,0:T(8,128)(2,1)}, bf16[448,128]{1,0:T(8,128)(2,1)S(1)}, u32[]{:S(2)}, u32[]{:S(2)}) collective-permute-start(bf16[448,128]{1,0:T(8,128)(2,1)} %bitcast.7), channel_id=1, source_target_pairs={{0,14},{12,2},{14,0},{2,12},{4,6},{8,10},{10,8},{6,4},{1,15},{13,3... | collective-permute-start | bytes 344072 | tf_op jit(solution)/shard_map/ppermute | solution.py:102
  8.1 5.9 %collective-permute-start.1 = (bf16[448,128]{1,0:T(8,128)(2,1)S(1)}, bf16[448,128]{1,0:T(8,128)(2,1)S(1)}, u32[]{:S(2)}, u32[]{:S(2)}) collective-permute-start(bf16[448,128]{1,0:T(8,128)(2,1)S(1)} %collective-permute-done.refs_0_), channel_id=1, source_target_pairs={{0,4},{4,8},{8,12},{12,14},{14,10},{10,6},{6,2},{2,0},{1,5},{5,9},... | collective-permute-start | bytes 344072 | tf_op jit(solution)/shard_map/ppermute | solution.py:103
  8.2 5.8 %collective-permute-start.3 = (bf16[448,128]{1,0:T(8,128)(2,1)S(1)}, bf16[448,128]{1,0:T(8,128)(2,1)S(1)}, u32[]{:S(2)}, u32[]{:S(2)}) collective-permute-start(bf16[448,128]{1,0:T(8,128)(2,1)S(1)} %collective-permute-done.2.refs_1_), channel_id=1, source_target_pairs={{4,0},{8,4},{12,8},{14,12},{10,14},{6,10},{2,6},{0,2},{5,1},{9,5},... | collective-permute-start | bytes 344072 | tf_op jit(solution)/shard_map/ppermute | solution.py:104
  10.1 5.9 %collective-permute-start.7 = (bf16[448,128]{1,0:T(8,128)(2,1)S(1)}, bf16[448,128]{1,0:T(8,128)(2,1)S(1)}, u32[]{:S(2)}, u32[]{:S(2)}) collective-permute-start(bf16[448,128]{1,0:T(8,128)(2,1)S(1)} %broadcast_select_fusion.2), channel_id=1, source_target_pairs={{4,6},{5,7},{8,10},{9,11},{10,8},{11,9},{6,4},{7,5},{0,1},{1,0},{1... | collective-permute-start | bytes 344072 | tf_op jit(solution)/shard_map/ppermute | solution.py:106
  14.0 4.8 %collective-permute-start.5 = (bf16[448,128]{1,0:T(8,128)(2,1)S(1)}, bf16[448,128]{1,0:T(8,128)(2,1)S(1)}, u32[]{:S(2)}, u32[]{:S(2)}) collective-permute-start(bf16[448,128]{1,0:T(8,128)(2,1)S(1)} %collective-permute-done.1.refs_2_), channel_id=1, source_target_pairs={{0,4},{4,8},{8,12},{12,14},{14,10},{10,6},{6,2},{2,0},{1,5},{5,9},... | collective-permute-start | bytes 344072 | tf_op jit(solution)/shard_map/ppermute | solution.py:111
  15.1 4.8 %collective-permute-start.6 = (bf16[448,128]{1,0:T(8,128)(2,1)S(1)}, bf16[448,128]{1,0:T(8,128)(2,1)S(1)}, u32[]{:S(2)}, u32[]{:S(2)}) collective-permute-start(bf16[448,128]{1,0:T(8,128)(2,1)S(1)} %collective-permute-done.3.refs_3_), channel_id=1, source_target_pairs={{4,0},{8,4},{12,8},{14,12},{10,14},{6,10},{2,6},{0,2},{5,1},{9,5},... | collective-permute-start | bytes 344072 | tf_op jit(solution)/shard_map/ppermute | solution.py:112
  16.0 12.7 %copy-start.1 = (s32[8,4]{0,1:T(4,128)S(1)}, s32[8,4]{0,1:T(4,128)}, u32[]{:S(2)}) copy-start(s32[8,4]{0,1:T(4,128)} %param.9) | copy-start | bytes 388
  20.4 5.0 %collective-permute-start.10 = (bf16[128,512]{1,0:T(8,128)(2,1)S(1)}, bf16[128,512]{1,0:T(8,128)(2,1)S(1)}, u32[]{:S(2)}, u32[]{:S(2)}) collective-permute-start(bf16[128,512]{1,0:T(8,128)(2,1)S(1)} %shard_map.56.refs_0_), channel_id=1, source_target_pairs={{4,0},{8,4},{12,8},{14,12},{10,14},{6,10},{2,6},{0,2},{5,1},{9,5},... | collective-permute-start | bytes 393224 | tf_op jit(solution)/shard_map/ppermute | solution.py:101
  21.4 5.9 %collective-permute-start.8 = (bf16[128,512]{1,0:T(8,128)(2,1)S(1)}, bf16[128,512]{1,0:T(8,128)(2,1)S(1)}, u32[]{:S(2)}, u32[]{:S(2)}) collective-permute-start(bf16[128,512]{1,0:T(8,128)(2,1)S(1)} %shard_map.56.refs_0_), channel_id=1, source_target_pairs={{0,4},{4,8},{8,12},{12,14},{14,10},{10,6},{6,2},{2,0},{1,5},{5,9},... | collective-permute-start | bytes 393224 | tf_op jit(solution)/shard_map/ppermute | solution.py:100
  22.5 4.8 %collective-permute-start.13 = (bf16[128,512]{1,0:T(8,128)(2,1)S(1)}, bf16[128,512]{1,0:T(8,128)(2,1)S(1)}, u32[]{:S(2)}, u32[]{:S(2)}) collective-permute-start(bf16[128,512]{1,0:T(8,128)(2,1)S(1)} %shard_map.56.refs_0_), channel_id=1, source_target_pairs={{0,1},{1,0},{2,3},{3,2},{4,5},{5,4},{6,7},{7,6},{8,9},{9,8},{10,11... | collective-permute-start | bytes 393224 | tf_op jit(solution)/shard_map/ppermute | solution.py:334
  22.5 8.8 %collective-permute-start.12 = (bf16[128,512]{1,0:T(8,128)(2,1)S(1)}, bf16[128,512]{1,0:T(8,128)(2,1)S(1)}, u32[]{:S(2)}, u32[]{:S(2)}) collective-permute-start(bf16[128,512]{1,0:T(8,128)(2,1)S(1)} %shard_map.56.refs_0_), channel_id=1, source_target_pairs={{0,14},{12,2},{14,0},{2,12},{4,6},{8,10},{10,8},{6,4},{1,15},{13,3... | collective-permute-start | bytes 393224 | tf_op jit(solution)/shard_map/ppermute | solution.py:102
  25.4 3.3 %collective-permute-start.15 = (bf16[128,512]{1,0:T(8,128)(2,1)S(1)}, bf16[128,512]{1,0:T(8,128)(2,1)S(1)}, u32[]{:S(2)}, u32[]{:S(2)}) collective-permute-start(bf16[128,512]{1,0:T(8,128)(2,1)S(1)} %collective-permute-done.10.refs_3_), channel_id=1, source_target_pairs={{0,1},{1,0},{2,3},{3,2},{4,5},{5,4},{6,7},{7,6},{8,9},{9,8},{10,11... | collective-permute-start | bytes 393224 | tf_op jit(solution)/shard_map/ppermute | solution.py:337
  25.4 7.9 %collective-permute-start.11 = (bf16[128,512]{1,0:T(8,128)(2,1)S(1)}, bf16[128,512]{1,0:T(8,128)(2,1)S(1)}, u32[]{:S(2)}, u32[]{:S(2)}) collective-permute-start(bf16[128,512]{1,0:T(8,128)(2,1)S(1)} %collective-permute-done.10.refs_3_), channel_id=1, source_target_pairs={{4,0},{8,4},{12,8},{14,12},{10,14},{6,10},{2,6},{0,2},{5,1},{9,5},... | collective-permute-start | bytes 393224 | tf_op jit(solution)/shard_map/ppermute | solution.py:104
  27.3 1.3 %collective-permute-start.14 = (bf16[128,512]{1,0:T(8,128)(2,1)S(1)}, bf16[128,512]{1,0:T(8,128)(2,1)S(1)}, u32[]{:S(2)}, u32[]{:S(2)}) collective-permute-start(bf16[128,512]{1,0:T(8,128)(2,1)S(1)} %collective-permute-done.8.refs_2_), channel_id=1, source_target_pairs={{0,1},{1,0},{2,3},{3,2},{4,5},{5,4},{6,7},{7,6},{8,9},{9,8},{10,11... | collective-permute-start | bytes 393224 | tf_op jit(solution)/shard_map/ppermute | solution.py:337
  27.3 6.7 %collective-permute-start.9 = (bf16[128,512]{1,0:T(8,128)(2,1)S(1)}, bf16[128,512]{1,0:T(8,128)(2,1)S(1)}, u32[]{:S(2)}, u32[]{:S(2)}) collective-permute-start(bf16[128,512]{1,0:T(8,128)(2,1)S(1)} %collective-permute-done.8.refs_2_), channel_id=1, source_target_pairs={{0,4},{4,8},{8,12},{12,14},{14,10},{10,6},{6,2},{2,0},{1,5},{5,9},... | collective-permute-start | bytes 393224 | tf_op jit(solution)/shard_map/ppermute | solution.py:103
  28.6 7.6 %collective-permute-start.16 = (bf16[128,512]{1,0:T(8,128)(2,1)S(1)}, bf16[128,512]{1,0:T(8,128)(2,1)S(1)}, u32[]{:S(2)}, u32[]{:S(2)}) collective-permute-start(bf16[128,512]{1,0:T(8,128)(2,1)S(1)} %broadcast_select_fusion.1), channel_id=1, source_target_pairs={{4,6},{5,7},{8,10},{9,11},{10,8},{11,9},{6,4},{7,5},{0,1},{1,0},{1... | collective-permute-start | bytes 393224 | tf_op jit(solution)/shard_map/ppermute | solution.py:106
  34.0 2.4 %collective-permute-start.17 = (bf16[128,512]{1,0:T(8,128)(2,1)S(1)}, bf16[128,512]{1,0:T(8,128)(2,1)S(1)}, u32[]{:S(2)}, u32[]{:S(2)}) collective-permute-start(bf16[128,512]{1,0:T(8,128)(2,1)S(1)} %collective-permute-done.9.refs_1_), channel_id=1, source_target_pairs={{0,1},{1,0},{2,3},{3,2},{4,5},{5,4},{6,7},{7,6},{8,9},{9,8},{10,11... | collective-permute-start | bytes 393224 | tf_op jit(solution)/shard_map/ppermute | solution.py:337
  34.0 5.9 %collective-permute-start.19 = (bf16[128,512]{1,0:T(8,128)(2,1)S(1)}, bf16[128,512]{1,0:T(8,128)(2,1)S(1)}, u32[]{:S(2)}, u32[]{:S(2)}) collective-permute-start(bf16[128,512]{1,0:T(8,128)(2,1)S(1)} %collective-permute-done.9.refs_1_), channel_id=1, source_target_pairs={{0,4},{4,8},{8,12},{12,14},{14,10},{10,6},{6,2},{2,0},{1,5},{5,9},... | collective-permute-start | bytes 393224 | tf_op jit(solution)/shard_map/ppermute | solution.py:111
  34.0 2.3 %collective-permute-start.18 = (bf16[128,512]{1,0:T(8,128)(2,1)S(1)}, bf16[128,512]{1,0:T(8,128)(2,1)S(1)}, u32[]{:S(2)}, u32[]{:S(2)}) collective-permute-start(bf16[128,512]{1,0:T(8,128)(2,1)S(1)} %collective-permute-done.11.refs_2_), channel_id=1, source_target_pairs={{0,1},{1,0},{2,3},{3,2},{4,5},{5,4},{6,7},{7,6},{8,9},{9,8},{10,11... | collective-permute-start | bytes 393224 | tf_op jit(solution)/shard_map/ppermute | solution.py:337
  34.5 5.5 %collective-permute-start.20 = (bf16[128,512]{1,0:T(8,128)(2,1)S(1)}, bf16[128,512]{1,0:T(8,128)(2,1)S(1)}, u32[]{:S(2)}, u32[]{:S(2)}) collective-permute-start(bf16[128,512]{1,0:T(8,128)(2,1)S(1)} %collective-permute-done.11.refs_2_), channel_id=1, source_target_pairs={{4,0},{8,4},{12,8},{14,12},{10,14},{6,10},{2,6},{0,2},{5,1},{9,5},... | collective-permute-start | bytes 393224 | tf_op jit(solution)/shard_map/ppermute | solution.py:112
  36.2 4.2 %collective-permute-start.23 = (bf16[128,512]{1,0:T(8,128)(2,1)S(1)}, bf16[128,512]{1,0:T(8,128)(2,1)S(1)}, u32[]{:S(2)}, u32[]{:S(2)}) collective-permute-start(bf16[128,512]{1,0:T(8,128)(2,1)S(1)} %broadcast_select_fusion.refs_3_), channel_id=1, source_target_pairs={{0,1},{1,0},{2,3},{3,2},{4,5},{5,4},{6,7},{7,6},{8,9},{9,8},{10,11... | collective-permute-start | bytes 393224 | tf_op jit(solution)/shard_map/ppermute | solution.py:337
  39.9 1.3 %collective-permute-start.21 = (bf16[128,512]{1,0:T(8,128)(2,1)S(1)}, bf16[128,512]{1,0:T(8,128)(2,1)S(1)}, u32[]{:S(2)}, u32[]{:S(2)}) collective-permute-start(bf16[128,512]{1,0:T(8,128)(2,1)S(1)} %collective-permute-done.19.refs_1_), channel_id=1, source_target_pairs={{0,1},{1,0},{2,3},{3,2},{4,5},{5,4},{6,7},{7,6},{8,9},{9,8},{10,11... | collective-permute-start | bytes 393224 | tf_op jit(solution)/shard_map/ppermute | solution.py:337
  39.9 1.5 %collective-permute-start.22 = (bf16[128,512]{1,0:T(8,128)(2,1)S(1)}, bf16[128,512]{1,0:T(8,128)(2,1)S(1)}, u32[]{:S(2)}, u32[]{:S(2)}) collective-permute-start(bf16[128,512]{1,0:T(8,128)(2,1)S(1)} %collective-permute-done.20.refs_2_), channel_id=1, source_target_pairs={{0,1},{1,0},{2,3},{3,2},{4,5},{5,4},{6,7},{7,6},{8,9},{9,8},{10,11... | collective-permute-start | bytes 393224 | tf_op jit(solution)/shard_map/ppermute | solution.py:337

commit v13 on v12

--- a/solution.py
+++ b/solution.py
@@ -96,7 +96,7 @@
         self.beside = aside + stay
         self.across = [(walk[i], walk[j]) for i, j in across + beside]
 
-    def gather(self, x, beside_second=None, beside_third=None):
+    def gather(self, x, beside_third):
         ahead = lax.ppermute(x, "lat", self.forward)
         behind = lax.ppermute(x, "lat", self.backward)
         corner = lax.ppermute(x, "lat", self.across)
@@ -104,14 +104,11 @@
         behind_2 = lax.ppermute(behind, "lat", self.backward)
         odd = place_on_ring(lax.axis_index("lat"), self.n) % 2 == 1
         middle = lax.ppermute(jnp.where(odd, behind, ahead), ("lat", "tok"), self.beside)
-        done = beside_second(ahead, behind) if beside_second else ()
-        ahead_2, behind_2, corner, done = lax.optimization_barrier(
-            (ahead_2, behind_2, corner, done)
-        )
+        ahead_2, behind_2, corner = lax.optimization_barrier((ahead_2, behind_2, corner))
         ahead_3 = lax.ppermute(ahead_2, "lat", self.forward)
         behind_3 = lax.ppermute(behind_2, "lat", self.backward)
-        done, middle = lax.optimization_barrier((done, middle))
-        done = beside_third(ahead, behind, ahead_2, behind_2, corner, done)
+        ahead, middle = lax.optimization_barrier((ahead, middle))
+        done = beside_third(ahead, behind, ahead_2, behind_2)
         return done, ahead_3, behind_3, corner, middle
 
 
@@ -139,7 +136,7 @@
         )(*blocks, weights)
 
     x = residual.T
-    (total, kept), ahead, behind, corner, middle = ring.gather(x, beside_third=beside_third)
+    (total, kept), ahead, behind, corner, middle = ring.gather(x, beside_third)
     return pl.pallas_call(
         last_step,
         out_shape=jax.ShapeDtypeStruct((tok_rows, width), jnp.bfloat16),
@@ -338,13 +335,10 @@
             owns = (acts, acts_twin)
             return tiles_of(by_slot, owns, before, hops, blocks, twins, tok_scale, halves, n)
 
-        def beside_second(ahead, behind):
-            return add_tiles(None, (1, n - 1), (ahead, behind))
-
-        def beside_third(ahead, behind, ahead_2, behind_2, _, before):
-            return add_tiles(before, (2, n - 2), (ahead_2, behind_2))
-
-        out, *late = ring.gather(acts, beside_second, beside_third)
+        def beside_third(ahead, behind, ahead_2, behind_2):
+            return add_tiles(None, (1, n - 1, 2, n - 2), (ahead, behind, ahead_2, behind_2))
+
+        out, *late = ring.gather(acts, beside_third)
         ahead, behind, corner, middle = late
         far = jnp.where(on_corner(n), corner, middle)
         out, ahead, behind = lax.optimization_barrier((out, ahead, behind))

time: 42.8 us -> 45 us (1.051); the launches traced: 42.6 us -> 45.3 us
  waiting for transfers between devices: 14 us -> 17.8 us
  Pallas kernels: 6.2 us -> 5.12 us
    ppermute x2, waiting for transfers between devices: 0.01 us -> 2.34 us  [gather(): ahead = lax.ppermute(x, 'lat', self.forward)]
    ppermute x2, starting transfers between devices: 3.73 us -> 1.92 us  [gather(): behind_2 = lax.ppermute(behind, 'lat', self.backward)]
    ppermute x2, waiting for transfers between devices: 1.17 us -> 2.82 us  [gather(): behind_3 = lax.ppermute(behind_2, 'lat', self.backward)]
    ppermute x2, starting transfers between devices: 1.16 us -> 2.81 us  [gather(): ahead_3 = lax.ppermute(ahead_2, 'lat', self.forward)]
    ppermute x2, waiting for transfers between devices: 3.1 us -> 1.52 us  [gather(): ahead_3 = lax.ppermute(ahead_2, 'lat', self.forward)]
    ppermute x2, starting transfers between devices: 2.66 us -> 1.24 us  [gather(): behind_3 = lax.ppermute(behind_2, 'lat', self.backward)]
    ppermute x2, waiting for transfers between devices: 3.79 us -> 2.66 us  [gather(): corner = lax.ppermute(x, 'lat', self.across)]
    pallas_call x3 -> x2, Pallas kernels: 3.64 us -> 2.57 us  [tiles_of(): pl.pallas_call(functools.partial(tiles_kernel, tok_scale, n, hops, first)...]
  transfers between devices with their start and end apart: 24 -> 24, of which waited for: 13 -> 14; matrix products, arithmetic and copies ran while one was open for 0% -> 0% of each run, Pallas kernels for 11% -> 8%
where the time goes in v13:
time: 45 us; the launch traced here: 45.3 us
  starting transfers between devices  22.2 us (49%)
  waiting for transfers between devices  17.8 us (40%)
  Pallas kernels  5.12 us (11%)
    ppermute x2, starting transfers between devices, gather(): corner = lax.ppermute(x, 'lat', self.across)  7.54 us
    ppermute x2, starting transfers between devices, gather(): ahead = lax.ppermute(x, 'lat', self.forward)  5.1 us
    ppermute x2, waiting for transfers between devices, gather(): behind_3 = lax.ppermute(behind_2, 'lat', self.backward)  2.82 us
    ppermute x2, starting transfers between devices, gather(): ahead_3 = lax.ppermute(ahead_2, 'lat', self.forward)  2.81 us
    ppermute x2, waiting for transfers between devices, gather(): behind_2 = lax.ppermute(behind, 'lat', self.backward)  2.73 us
    ppermute x2, waiting for transfers between devices, gather(): ahead_2 = lax.ppermute(ahead, 'lat', self.forward)  2.7 us
    ppermute x2, waiting for transfers between devices, gather(): corner = lax.ppermute(x, 'lat', self.across)  2.66 us
    pallas_call x2, Pallas kernels, tiles_of(): pl.pallas_call(functools.partial(tiles_kernel, tok_scale, n, hops, first)...  2.57 us
  transfers between devices with their start and end apart: 24, of which 14 were waited for; matrix products, arithmetic and copies ran while one was open for 0% of the time, Pallas kernels for 8%

profile of v13, /device:TPU:0, one launch (start us, length us, event | category | flops | bytes accessed | tf_op | source)
XLA Modules:
  0.0 45.3 jit_solution(1805049989489775015)
XLA Ops:
  0.0 3.1 %collective-permute-start = (bf16[448,128]{1,0:T(8,128)(2,1)}, bf16[448,128]{1,0:T(8,128)(2,1)S(1)}, u32[]{:S(2)}, u32[]{:S(2)}) collective-permute-start(bf16[448,128]{1,0:T(8,128)(2,1)} %bitcast.5), channel_id=1, source_target_pairs={{0,4},{4,8},{8,12},{12,14},{14,10},{10,6},{6,2},{2,0},{1,5},{5,9},... | collective-permute-start | bytes 344072 | tf_op jit(solution)/shard_map/ppermute | solution.py:100
  3.1 0.0 collective-permute-start.2
  3.1 5.0 %collective-permute-start.4 = (bf16[448,128]{1,0:T(8,128)(2,1)}, bf16[448,128]{1,0:T(8,128)(2,1)S(1)}, u32[]{:S(2)}, u32[]{:S(2)}) collective-permute-start(bf16[448,128]{1,0:T(8,128)(2,1)} %bitcast.7), channel_id=1, source_target_pairs={{0,14},{12,2},{14,0},{2,12},{4,6},{8,10},{10,8},{6,4},{1,15},{13,3... | collective-permute-start | bytes 344072 | tf_op jit(solution)/shard_map/ppermute | solution.py:102
  8.1 0.0 collective-permute-done.refs_0_
  8.1 0.1 collective-permute-start.1
  8.2 0.0 collective-permute-done.2.refs_1_
  8.2 1.9 %collective-permute-start.3 = (bf16[448,128]{1,0:T(8,128)(2,1)S(1)}, bf16[448,128]{1,0:T(8,128)(2,1)S(1)}, u32[]{:S(2)}, u32[]{:S(2)}) collective-permute-start(bf16[448,128]{1,0:T(8,128)(2,1)S(1)} %collective-permute-done.2.refs_1_), channel_id=1, source_target_pairs={{4,0},{8,4},{12,8},{14,12},{10,14},{6,10},{2,6},{0,2},{5,1},{9,5},... | collective-permute-start | bytes 344072 | tf_op jit(solution)/shard_map/ppermute | solution.py:104
  10.1 0.1 collective-permute-start.7
  10.2 2.7 %collective-permute-done.4.x_corner = bf16[448,128]{1,0:T(8,128)(2,1)S(1)} collective-permute-done((bf16[448,128]{1,0:T(8,128)(2,1)}, bf16[448,128]{1,0:T(8,128)(2,1)S(1)}, u32[]{:S(2)}, u32[]{:S(2)}) %collective-permute-start.4) | collective-permute-done | bytes 114720 | tf_op jit(solution)/shard_map/ppermute | solution.py:102
  12.9 1.1 %collective-permute-done.1.refs_2_ = bf16[448,128]{1,0:T(8,128)(2,1)S(1)} collective-permute-done((bf16[448,128]{1,0:T(8,128)(2,1)S(1)}, bf16[448,128]{1,0:T(8,128)(2,1)S(1)}, u32[]{:S(2)}, u32[]{:S(2)}) %collective-permute-start.1) | collective-permute-done | bytes 114720 | tf_op jit(solution)/shard_map/ppermute | solution.py:103
  14.0 0.0 collective-permute-done.3.refs_3_
  14.0 1.1 %collective-permute-start.5 = (bf16[448,128]{1,0:T(8,128)(2,1)S(1)}, bf16[448,128]{1,0:T(8,128)(2,1)S(1)}, u32[]{:S(2)}, u32[]{:S(2)}) collective-permute-start(bf16[448,128]{1,0:T(8,128)(2,1)S(1)} %collective-permute-done.1.refs_2_), channel_id=1, source_target_pairs={{0,4},{4,8},{8,12},{12,14},{14,10},{10,6},{6,2},{2,0},{1,5},{5,9},... | collective-permute-start | bytes 344072 | tf_op jit(solution)/shard_map/ppermute | solution.py:108
  15.1 0.9 %collective-permute-start.6 = (bf16[448,128]{1,0:T(8,128)(2,1)S(1)}, bf16[448,128]{1,0:T(8,128)(2,1)S(1)}, u32[]{:S(2)}, u32[]{:S(2)}) collective-permute-start(bf16[448,128]{1,0:T(8,128)(2,1)S(1)} %collective-permute-done.3.refs_3_), channel_id=1, source_target_pairs={{4,0},{8,4},{12,8},{14,12},{10,14},{6,10},{2,6},{0,2},{5,1},{9,5},... | collective-permute-start | bytes 344072 | tf_op jit(solution)/shard_map/ppermute | solution.py:109
  16.0 0.0 collective-permute-done.7.x_middle
  16.0 2.1 %shard_map.55 = (f32[128,512]{1,0:T(8,128)S(1)}, bf16[4,448,512]{2,1,0:T(8,128)(2,1)S(1)}) custom-call(bf16[448,128]{1,0:T(8,128)(2,1)S(1)} %collective-permute-done.refs_0_, bf16[448,128]{1,0:T(8,128)(2,1)S(1)} %collective-permute-done.2.refs_1_, bf16[448,128]{1,0:T(8,128)(2,1)S(1)} %collective-permute-done.1.refs_2_, ...), custom_call_target="tpu_custom_call" | custom-call | flops 234881024 | bytes 2818048 | tf_op jit(solution)/shard_map/pallas_call | solution.py:125
  18.1 0.7 %collective-permute-done.5.x_f = bf16[448,128]{1,0:T(8,128)(2,1)S(1)} collective-permute-done((bf16[448,128]{1,0:T(8,128)(2,1)S(1)}, bf16[448,128]{1,0:T(8,128)(2,1)S(1)}, u32[]{:S(2)}, u32[]{:S(2)}) %collective-permute-start.5) | collective-permute-done | bytes 114720 | tf_op jit(solution)/shard_map/ppermute | solution.py:108
  18.8 1.1 %collective-permute-done.6.x_b = bf16[448,128]{1,0:T(8,128)(2,1)S(1)} collective-permute-done((bf16[448,128]{1,0:T(8,128)(2,1)S(1)}, bf16[448,128]{1,0:T(8,128)(2,1)S(1)}, u32[]{:S(2)}, u32[]{:S(2)}) %collective-permute-start.6) | collective-permute-done | bytes 114720 | tf_op jit(solution)/shard_map/ppermute | solution.py:109
  19.9 0.5 %shard_map.56.refs_0_ = bf16[128,512]{1,0:T(8,128)(2,1)S(1)} custom-call(bf16[448,128]{1,0:T(8,128)(2,1)S(1)} %bitcast.8, bf16[448,128]{1,0:T(8,128)(2,1)S(1)} %collective-permute-done.5.x_f, bf16[448,128]{1,0:T(8,128)(2,1)S(1)} %collective-permute-done.6.x_b, bf16[448,128]{1,0:T(8,128)(2,1)S(1)} %collective-permute-done.4.x_corner, ...), custom_call_target="tpu_custom_call" | custom-call | flops 234881024 | bytes 2818048 | tf_op jit(solution)/shard_map/pallas_call | solution.py:140
  20.4 2.0 %collective-permute-start.9 = (bf16[128,512]{1,0:T(8,128)(2,1)S(1)}, bf16[128,512]{1,0:T(8,128)(2,1)S(1)}, u32[]{:S(2)}, u32[]{:S(2)}) collective-permute-start(bf16[128,512]{1,0:T(8,128)(2,1)S(1)} %shard_map.56.refs_0_), channel_id=1, source_target_pairs={{0,4},{4,8},{8,12},{12,14},{14,10},{10,6},{6,2},{2,0},{1,5},{5,9},... | collective-permute-start | bytes 393224 | tf_op jit(solution)/shard_map/ppermute | solution.py:100
  22.4 0.1 collective-permute-start.10
  22.5 2.6 %collective-permute-start.14 = (bf16[128,512]{1,0:T(8,128)(2,1)S(1)}, bf16[128,512]{1,0:T(8,128)(2,1)S(1)}, u32[]{:S(2)}, u32[]{:S(2)}) collective-permute-start(bf16[128,512]{1,0:T(8,128)(2,1)S(1)} %shard_map.56.refs_0_), channel_id=1, source_target_pairs={{0,14},{12,2},{14,0},{2,12},{4,6},{8,10},{10,8},{6,4},{1,15},{13,3... | collective-permute-start | bytes 393224 | tf_op jit(solution)/shard_map/ppermute | solution.py:102
  25.1 2.3 %collective-permute-done.9.refs_2_ = bf16[128,512]{1,0:T(8,128)(2,1)S(1)} collective-permute-done((bf16[128,512]{1,0:T(8,128)(2,1)S(1)}, bf16[128,512]{1,0:T(8,128)(2,1)S(1)}, u32[]{:S(2)}, u32[]{:S(2)}) %collective-permute-start.9) | collective-permute-done | bytes 131104 | tf_op jit(solution)/shard_map/ppermute | solution.py:100
  27.4 1.4 %collective-permute-start.12 = (bf16[128,512]{1,0:T(8,128)(2,1)S(1)}, bf16[128,512]{1,0:T(8,128)(2,1)S(1)}, u32[]{:S(2)}, u32[]{:S(2)}) collective-permute-start(bf16[128,512]{1,0:T(8,128)(2,1)S(1)} %collective-permute-done.9.refs_2_), channel_id=1, source_target_pairs={{0,4},{4,8},{8,12},{12,14},{14,10},{10,6},{6,2},{2,0},{1,5},{5,9},... | collective-permute-start | bytes 393224 | tf_op jit(solution)/shard_map/ppermute | solution.py:103
  28.8 1.3 %collective-permute-done.10.refs_3_ = bf16[128,512]{1,0:T(8,128)(2,1)S(1)} collective-permute-done((bf16[128,512]{1,0:T(8,128)(2,1)S(1)}, bf16[128,512]{1,0:T(8,128)(2,1)S(1)}, u32[]{:S(2)}, u32[]{:S(2)}) %collective-permute-start.10) | collective-permute-done | bytes 131104 | tf_op jit(solution)/shard_map/ppermute | solution.py:101
  30.1 0.1 collective-permute-start.11
  30.2 0.5 %collective-permute-start.8 = (bf16[128,512]{1,0:T(8,128)(2,1)S(1)}, bf16[128,512]{1,0:T(8,128)(2,1)S(1)}, u32[]{:S(2)}, u32[]{:S(2)}) collective-permute-start(bf16[128,512]{1,0:T(8,128)(2,1)S(1)} %shard_map.56.refs_0_), channel_id=1, source_target_pairs={{0,1},{1,0},{2,3},{3,2},{4,5},{5,4},{6,7},{7,6},{8,9},{9,8},{10,11... | collective-permute-start | bytes 393224 | tf_op jit(solution)/shard_map/ppermute | solution.py:331
  30.7 0.0 collective-permute-done.14
  30.7 0.1 collective-permute-start.16
  30.8 1.6 %collective-permute-done.12.refs_4_ = bf16[128,512]{1,0:T(8,128)(2,1)S(1)} collective-permute-done((bf16[128,512]{1,0:T(8,128)(2,1)S(1)}, bf16[128,512]{1,0:T(8,128)(2,1)S(1)}, u32[]{:S(2)}, u32[]{:S(2)}) %collective-permute-start.12) | collective-permute-done | bytes 131104 | tf_op jit(solution)/shard_map/ppermute | solution.py:103
  32.4 2.7 %collective-permute-done.13.refs_5_ = bf16[128,512]{1,0:T(8,128)(2,1)S(1)} collective-permute-done((bf16[128,512]{1,0:T(8,128)(2,1)S(1)}, bf16[128,512]{1,0:T(8,128)(2,1)S(1)}, u32[]{:S(2)}, u32[]{:S(2)}) %collective-permute-start.13) | collective-permute-done | bytes 131104 | tf_op jit(solution)/shard_map/ppermute | solution.py:104
  35.1 0.0 collective-permute-start.17
  35.1 1.7 %collective-permute-start.19 = (bf16[128,512]{1,0:T(8,128)(2,1)S(1)}, bf16[128,512]{1,0:T(8,128)(2,1)S(1)}, u32[]{:S(2)}, u32[]{:S(2)}) collective-permute-start(bf16[128,512]{1,0:T(8,128)(2,1)S(1)} %collective-permute-done.12.refs_4_), channel_id=1, source_target_pairs={{0,4},{4,8},{8,12},{12,14},{14,10},{10,6},{6,2},{2,0},{1,5},{5,9},... | collective-permute-start | bytes 393224 | tf_op jit(solution)/shard_map/ppermute | solution.py:108
  36.8 0.2 collective-permute-start.18
  37.0 0.3 collective-permute-start.20
  37.3 0.0 collective-permute-done.16.refs_7_
  37.3 0.0 collective-permute-start.15
  37.4 0.0 collective-permute-done.17.refs_8_
  37.4 0.5 %collective-permute-start.23 = (bf16[128,512]{1,0:T(8,128)(2,1)S(1)}, bf16[128,512]{1,0:T(8,128)(2,1)S(1)}, u32[]{:S(2)}, u32[]{:S(2)}) collective-permute-start(bf16[128,512]{1,0:T(8,128)(2,1)S(1)} %broadcast_select_fusion.refs_3_), channel_id=1, source_target_pairs={{0,1},{1,0},{2,3},{3,2},{4,5},{5,4},{6,7},{7,6},{8,9},{9,8},{10,11... | collective-permute-start | bytes 393224 | tf_op jit(solution)/shard_map/ppermute | solution.py:334
  37.9 0.2 collective-permute-done.18.refs_9_
  38.1 0.6 %collective-permute-done.15.refs_6_ = bf16[128,512]{1,0:T(8,128)(2,1)S(1)} collective-permute-done((bf16[128,512]{1,0:T(8,128)(2,1)S(1)}, bf16[128,512]{1,0:T(8,128)(2,1)S(1)}, u32[]{:S(2)}, u32[]{:S(2)}) %collective-permute-start.15) | collective-permute-done | bytes 131104 | tf_op jit(solution)/shard_map/ppermute | solution.py:334
  38.7 1.4 %shard_map.57 = (bf16[256,256]{1,0:T(8,128)(2,1)S(1)}, bf16[1,4,256,512]{3,2,1,0:T(8,128)(2,1)}) custom-call(s32[4,8]{1,0:T(4,128)S(1)} %bitcast.9, bf16[128,512]{1,0:T(8,128)(2,1)S(1)} %shard_map.56.refs_0_, bf16[128,512]{1,0:T(8,128)(2,1)S(1)} %collective-permute-done.8.refs_1_, bf16[128,512]{1,0:T(8,128)(2,1)S(1)} %collective-permute-done.9.refs_2_, ...), custom_call_target="tpu_custom_call" | custom-call | flops 268435456 | bytes 2097152 | tf_op jit(solution)/shard_map/pallas_call | solution.py:299
  40.1 0.8 %collective-permute-done.19.refs_1_ = bf16[128,512]{1,0:T(8,128)(2,1)S(1)} collective-permute-done((bf16[128,512]{1,0:T(8,128)(2,1)S(1)}, bf16[128,512]{1,0:T(8,128)(2,1)S(1)}, u32[]{:S(2)}, u32[]{:S(2)}) %collective-permute-start.19) | collective-permute-done | bytes 131104 | tf_op jit(solution)/shard_map/ppermute | solution.py:108
  41.0 1.7 %collective-permute-done.20.refs_2_ = bf16[128,512]{1,0:T(8,128)(2,1)S(1)} collective-permute-done((bf16[128,512]{1,0:T(8,128)(2,1)S(1)}, bf16[128,512]{1,0:T(8,128)(2,1)S(1)}, u32[]{:S(2)}, u32[]{:S(2)}) %collective-permute-start.20) | collective-permute-done | bytes 131104 | tf_op jit(solution)/shard_map/ppermute | solution.py:109
  42.7 0.0 collective-permute-start.21
  42.7 0.5 %collective-permute-start.22 = (bf16[128,512]{1,0:T(8,128)(2,1)S(1)}, bf16[128,512]{1,0:T(8,128)(2,1)S(1)}, u32[]{:S(2)}, u32[]{:S(2)}) collective-permute-start(bf16[128,512]{1,0:T(8,128)(2,1)S(1)} %collective-permute-done.20.refs_2_), channel_id=1, source_target_pairs={{0,1},{1,0},{2,3},{3,2},{4,5},{5,4},{6,7},{7,6},{8,9},{9,8},{10,11... | collective-permute-start | bytes 393224 | tf_op jit(solution)/shard_map/ppermute | solution.py:334
  43.2 0.8 %collective-permute-done.21.refs_4_ = bf16[128,512]{1,0:T(8,128)(2,1)S(1)} collective-permute-done((bf16[128,512]{1,0:T(8,128)(2,1)S(1)}, bf16[128,512]{1,0:T(8,128)(2,1)S(1)}, u32[]{:S(2)}, u32[]{:S(2)}) %collective-permute-start.21) | collective-permute-done | bytes 131104 | tf_op jit(solution)/shard_map/ppermute | solution.py:334
  44.0 0.2 collective-permute-done.22.refs_5_
  44.2 1.1 %shard_map.58 = bf16[1,4,256,512]{3,2,1,0:T(8,128)(2,1)} custom-call(s32[4,8]{1,0:T(4,128)S(1)} %bitcast.10, bf16[256,256]{1,0:T(8,128)(2,1)S(1)} %get-tuple-element.35.refs_0_, bf16[128,512]{1,0:T(8,128)(2,1)S(1)} %collective-permute-done.19.refs_1_, bf16[128,512]{1,0:T(8,128)(2,1)S(1)} %collective-permute-done.20.refs_2_, ...), custom_call_target="tpu_custom_call", output_to_operand_aliasing={{}: (8, {})} | custom-call | flops 201326592 | bytes 1572864 | tf_op jit(solution)/shard_map/pallas_call | solution.py:299
  (15 shorter events, 0.1 us)
Async XLA Ops:
  0.0 19.9 %copy-start = (bf16[128,448]{0,1:T(8,128)(2,1)S(1)}, bf16[128,448]{0,1:T(8,128)(2,1)}, u32[]{:S(2)}) copy-start(bf16[128,448]{0,1:T(8,128)(2,1)} %param.5) | copy-start | bytes 344068
  0.0 19.9 %copy-start.2 = (f32[512]{0:T(512)S(1)}, f32[512]{0:T(512)}, u32[]{:S(2)}) copy-start(f32[512]{0:T(512)} %param.7) | copy-start | bytes 6148
  0.0 19.9 %copy-start.3 = (f32[512]{0:T(512)S(1)}, f32[512]{0:T(512)}, u32[]{:S(2)}) copy-start(f32[512]{0:T(512)} %param.8) | copy-start | bytes 6148
  0.0 8.1 %collective-permute-start = (bf16[448,128]{1,0:T(8,128)(2,1)}, bf16[448,128]{1,0:T(8,128)(2,1)S(1)}, u32[]{:S(2)}, u32[]{:S(2)}) collective-permute-start(bf16[448,128]{1,0:T(8,128)(2,1)} %bitcast.5), channel_id=1, source_target_pairs={{0,4},{4,8},{8,12},{12,14},{14,10},{10,6},{6,2},{2,0},{1,5},{5,9},... | collective-permute-start | bytes 344072 | tf_op jit(solution)/shard_map/ppermute | solution.py:100
  3.1 5.1 %collective-permute-start.2 = (bf16[448,128]{1,0:T(8,128)(2,1)}, bf16[448,128]{1,0:T(8,128)(2,1)S(1)}, u32[]{:S(2)}, u32[]{:S(2)}) collective-permute-start(bf16[448,128]{1,0:T(8,128)(2,1)} %bitcast.6), channel_id=1, source_target_pairs={{4,0},{8,4},{12,8},{14,12},{10,14},{6,10},{2,6},{0,2},{5,1},{9,5},... | collective-permute-start | bytes 344072 | tf_op jit(solution)/shard_map/ppermute | solution.py:101
  3.1 9.8 %collective-permute-start.4 = (bf16[448,128]{1,0:T(8,128)(2,1)}, bf16[448,128]{1,0:T(8,128)(2,1)S(1)}, u32[]{:S(2)}, u32[]{:S(2)}) collective-permute-start(bf16[448,128]{1,0:T(8,128)(2,1)} %bitcast.7), channel_id=1, source_target_pairs={{0,14},{12,2},{14,0},{2,12},{4,6},{8,10},{10,8},{6,4},{1,15},{13,3... | collective-permute-start | bytes 344072 | tf_op jit(solution)/shard_map/ppermute | solution.py:102
  8.1 5.9 %collective-permute-start.1 = (bf16[448,128]{1,0:T(8,128)(2,1)S(1)}, bf16[448,128]{1,0:T(8,128)(2,1)S(1)}, u32[]{:S(2)}, u32[]{:S(2)}) collective-permute-start(bf16[448,128]{1,0:T(8,128)(2,1)S(1)} %collective-permute-done.refs_0_), channel_id=1, source_target_pairs={{0,4},{4,8},{8,12},{12,14},{14,10},{10,6},{6,2},{2,0},{1,5},{5,9},... | collective-permute-start | bytes 344072 | tf_op jit(solution)/shard_map/ppermute | solution.py:103
  8.2 5.8 %collective-permute-start.3 = (bf16[448,128]{1,0:T(8,128)(2,1)S(1)}, bf16[448,128]{1,0:T(8,128)(2,1)S(1)}, u32[]{:S(2)}, u32[]{:S(2)}) collective-permute-start(bf16[448,128]{1,0:T(8,128)(2,1)S(1)} %collective-permute-done.2.refs_1_), channel_id=1, source_target_pairs={{4,0},{8,4},{12,8},{14,12},{10,14},{6,10},{2,6},{0,2},{5,1},{9,5},... | collective-permute-start | bytes 344072 | tf_op jit(solution)/shard_map/ppermute | solution.py:104
  10.1 5.9 %collective-permute-start.7 = (bf16[448,128]{1,0:T(8,128)(2,1)S(1)}, bf16[448,128]{1,0:T(8,128)(2,1)S(1)}, u32[]{:S(2)}, u32[]{:S(2)}) collective-permute-start(bf16[448,128]{1,0:T(8,128)(2,1)S(1)} %broadcast_select_fusion.2), channel_id=1, source_target_pairs={{4,6},{5,7},{8,10},{9,11},{10,8},{11,9},{6,4},{7,5},{0,1},{1,0},{1... | collective-permute-start | bytes 344072 | tf_op jit(solution)/shard_map/ppermute | solution.py:106
  14.0 4.8 %collective-permute-start.5 = (bf16[448,128]{1,0:T(8,128)(2,1)S(1)}, bf16[448,128]{1,0:T(8,128)(2,1)S(1)}, u32[]{:S(2)}, u32[]{:S(2)}) collective-permute-start(bf16[448,128]{1,0:T(8,128)(2,1)S(1)} %collective-permute-done.1.refs_2_), channel_id=1, source_target_pairs={{0,4},{4,8},{8,12},{12,14},{14,10},{10,6},{6,2},{2,0},{1,5},{5,9},... | collective-permute-start | bytes 344072 | tf_op jit(solution)/shard_map/ppermute | solution.py:108
  15.1 4.8 %collective-permute-start.6 = (bf16[448,128]{1,0:T(8,128)(2,1)S(1)}, bf16[448,128]{1,0:T(8,128)(2,1)S(1)}, u32[]{:S(2)}, u32[]{:S(2)}) collective-permute-start(bf16[448,128]{1,0:T(8,128)(2,1)S(1)} %collective-permute-done.3.refs_3_), channel_id=1, source_target_pairs={{4,0},{8,4},{12,8},{14,12},{10,14},{6,10},{2,6},{0,2},{5,1},{9,5},... | collective-permute-start | bytes 344072 | tf_op jit(solution)/shard_map/ppermute | solution.py:109
  16.0 22.6 %copy-start.1 = (s32[8,4]{0,1:T(4,128)S(1)}, s32[8,4]{0,1:T(4,128)}, u32[]{:S(2)}) copy-start(s32[8,4]{0,1:T(4,128)} %param.9) | copy-start | bytes 388
  20.4 7.0 %collective-permute-start.9 = (bf16[128,512]{1,0:T(8,128)(2,1)S(1)}, bf16[128,512]{1,0:T(8,128)(2,1)S(1)}, u32[]{:S(2)}, u32[]{:S(2)}) collective-permute-start(bf16[128,512]{1,0:T(8,128)(2,1)S(1)} %shard_map.56.refs_0_), channel_id=1, source_target_pairs={{0,4},{4,8},{8,12},{12,14},{14,10},{10,6},{6,2},{2,0},{1,5},{5,9},... | collective-permute-start | bytes 393224 | tf_op jit(solution)/shard_map/ppermute | solution.py:100
  22.4 7.7 %collective-permute-start.10 = (bf16[128,512]{1,0:T(8,128)(2,1)S(1)}, bf16[128,512]{1,0:T(8,128)(2,1)S(1)}, u32[]{:S(2)}, u32[]{:S(2)}) collective-permute-start(bf16[128,512]{1,0:T(8,128)(2,1)S(1)} %shard_map.56.refs_0_), channel_id=1, source_target_pairs={{4,0},{8,4},{12,8},{14,12},{10,14},{6,10},{2,6},{0,2},{5,1},{9,5},... | collective-permute-start | bytes 393224 | tf_op jit(solution)/shard_map/ppermute | solution.py:101
  22.5 8.2 %collective-permute-start.14 = (bf16[128,512]{1,0:T(8,128)(2,1)S(1)}, bf16[128,512]{1,0:T(8,128)(2,1)S(1)}, u32[]{:S(2)}, u32[]{:S(2)}) collective-permute-start(bf16[128,512]{1,0:T(8,128)(2,1)S(1)} %shard_map.56.refs_0_), channel_id=1, source_target_pairs={{0,14},{12,2},{14,0},{2,12},{4,6},{8,10},{10,8},{6,4},{1,15},{13,3... | collective-permute-start | bytes 393224 | tf_op jit(solution)/shard_map/ppermute | solution.py:102
  27.4 5.0 %collective-permute-start.12 = (bf16[128,512]{1,0:T(8,128)(2,1)S(1)}, bf16[128,512]{1,0:T(8,128)(2,1)S(1)}, u32[]{:S(2)}, u32[]{:S(2)}) collective-permute-start(bf16[128,512]{1,0:T(8,128)(2,1)S(1)} %collective-permute-done.9.refs_2_), channel_id=1, source_target_pairs={{0,4},{4,8},{8,12},{12,14},{14,10},{10,6},{6,2},{2,0},{1,5},{5,9},... | collective-permute-start | bytes 393224 | tf_op jit(solution)/shard_map/ppermute | solution.py:103
  30.1 5.0 %collective-permute-start.13 = (bf16[128,512]{1,0:T(8,128)(2,1)S(1)}, bf16[128,512]{1,0:T(8,128)(2,1)S(1)}, u32[]{:S(2)}, u32[]{:S(2)}) collective-permute-start(bf16[128,512]{1,0:T(8,128)(2,1)S(1)} %collective-permute-done.10.refs_3_), channel_id=1, source_target_pairs={{4,0},{8,4},{12,8},{14,12},{10,14},{6,10},{2,6},{0,2},{5,1},{9,5},... | collective-permute-start | bytes 393224 | tf_op jit(solution)/shard_map/ppermute | solution.py:104
  30.1 6.7 %collective-permute-start.11 = (bf16[128,512]{1,0:T(8,128)(2,1)S(1)}, bf16[128,512]{1,0:T(8,128)(2,1)S(1)}, u32[]{:S(2)}, u32[]{:S(2)}) collective-permute-start(bf16[128,512]{1,0:T(8,128)(2,1)S(1)} %broadcast_select_fusion.1), channel_id=1, source_target_pairs={{4,6},{5,7},{8,10},{9,11},{10,8},{11,9},{6,4},{7,5},{0,1},{1,0},{1... | collective-permute-start | bytes 393224 | tf_op jit(solution)/shard_map/ppermute | solution.py:106
  30.2 6.8 %collective-permute-start.8 = (bf16[128,512]{1,0:T(8,128)(2,1)S(1)}, bf16[128,512]{1,0:T(8,128)(2,1)S(1)}, u32[]{:S(2)}, u32[]{:S(2)}) collective-permute-start(bf16[128,512]{1,0:T(8,128)(2,1)S(1)} %shard_map.56.refs_0_), channel_id=1, source_target_pairs={{0,1},{1,0},{2,3},{3,2},{4,5},{5,4},{6,7},{7,6},{8,9},{9,8},{10,11... | collective-permute-start | bytes 393224 | tf_op jit(solution)/shard_map/ppermute | solution.py:331
  30.7 6.6 %collective-permute-start.16 = (bf16[128,512]{1,0:T(8,128)(2,1)S(1)}, bf16[128,512]{1,0:T(8,128)(2,1)S(1)}, u32[]{:S(2)}, u32[]{:S(2)}) collective-permute-start(bf16[128,512]{1,0:T(8,128)(2,1)S(1)} %collective-permute-done.10.refs_3_), channel_id=1, source_target_pairs={{0,1},{1,0},{2,3},{3,2},{4,5},{5,4},{6,7},{7,6},{8,9},{9,8},{10,11... | collective-permute-start | bytes 393224 | tf_op jit(solution)/shard_map/ppermute | solution.py:334
  35.1 2.3 %collective-permute-start.17 = (bf16[128,512]{1,0:T(8,128)(2,1)S(1)}, bf16[128,512]{1,0:T(8,128)(2,1)S(1)}, u32[]{:S(2)}, u32[]{:S(2)}) collective-permute-start(bf16[128,512]{1,0:T(8,128)(2,1)S(1)} %collective-permute-done.12.refs_4_), channel_id=1, source_target_pairs={{0,1},{1,0},{2,3},{3,2},{4,5},{5,4},{6,7},{7,6},{8,9},{9,8},{10,11... | collective-permute-start | bytes 393224 | tf_op jit(solution)/shard_map/ppermute | solution.py:334
  35.1 5.9 %collective-permute-start.19 = (bf16[128,512]{1,0:T(8,128)(2,1)S(1)}, bf16[128,512]{1,0:T(8,128)(2,1)S(1)}, u32[]{:S(2)}, u32[]{:S(2)}) collective-permute-start(bf16[128,512]{1,0:T(8,128)(2,1)S(1)} %collective-permute-done.12.refs_4_), channel_id=1, source_target_pairs={{0,4},{4,8},{8,12},{12,14},{14,10},{10,6},{6,2},{2,0},{1,5},{5,9},... | collective-permute-start | bytes 393224 | tf_op jit(solution)/shard_map/ppermute | solution.py:108
  36.8 1.3 %collective-permute-start.18 = (bf16[128,512]{1,0:T(8,128)(2,1)S(1)}, bf16[128,512]{1,0:T(8,128)(2,1)S(1)}, u32[]{:S(2)}, u32[]{:S(2)}) collective-permute-start(bf16[128,512]{1,0:T(8,128)(2,1)S(1)} %collective-permute-done.13.refs_5_), channel_id=1, source_target_pairs={{0,1},{1,0},{2,3},{3,2},{4,5},{5,4},{6,7},{7,6},{8,9},{9,8},{10,11... | collective-permute-start | bytes 393224 | tf_op jit(solution)/shard_map/ppermute | solution.py:334
  37.0 5.7 %collective-permute-start.20 = (bf16[128,512]{1,0:T(8,128)(2,1)S(1)}, bf16[128,512]{1,0:T(8,128)(2,1)S(1)}, u32[]{:S(2)}, u32[]{:S(2)}) collective-permute-start(bf16[128,512]{1,0:T(8,128)(2,1)S(1)} %collective-permute-done.13.refs_5_), channel_id=1, source_target_pairs={{4,0},{8,4},{12,8},{14,12},{10,14},{6,10},{2,6},{0,2},{5,1},{9,5},... | collective-permute-start | bytes 393224 | tf_op jit(solution)/shard_map/ppermute | solution.py:109
  37.3 1.3 %collective-permute-start.15 = (bf16[128,512]{1,0:T(8,128)(2,1)S(1)}, bf16[128,512]{1,0:T(8,128)(2,1)S(1)}, u32[]{:S(2)}, u32[]{:S(2)}) collective-permute-start(bf16[128,512]{1,0:T(8,128)(2,1)S(1)} %collective-permute-done.9.refs_2_), channel_id=1, source_target_pairs={{0,1},{1,0},{2,3},{3,2},{4,5},{5,4},{6,7},{7,6},{8,9},{9,8},{10,11... | collective-permute-start | bytes 393224 | tf_op jit(solution)/shard_map/ppermute | solution.py:334
  37.4 5.8 %collective-permute-start.23 = (bf16[128,512]{1,0:T(8,128)(2,1)S(1)}, bf16[128,512]{1,0:T(8,128)(2,1)S(1)}, u32[]{:S(2)}, u32[]{:S(2)}) collective-permute-start(bf16[128,512]{1,0:T(8,128)(2,1)S(1)} %broadcast_select_fusion.refs_3_), channel_id=1, source_target_pairs={{0,1},{1,0},{2,3},{3,2},{4,5},{5,4},{6,7},{7,6},{8,9},{9,8},{10,11... | collective-permute-start | bytes 393224 | tf_op jit(solution)/shard_map/ppermute | solution.py:334
  42.7 1.3 %collective-permute-start.21 = (bf16[128,512]{1,0:T(8,128)(2,1)S(1)}, bf16[128,512]{1,0:T(8,128)(2,1)S(1)}, u32[]{:S(2)}, u32[]{:S(2)}) collective-permute-start(bf16[128,512]{1,0:T(8,128)(2,1)S(1)} %collective-permute-done.19.refs_1_), channel_id=1, source_target_pairs={{0,1},{1,0},{2,3},{3,2},{4,5},{5,4},{6,7},{7,6},{8,9},{9,8},{10,11... | collective-permute-start | bytes 393224 | tf_op jit(solution)/shard_map/ppermute | solution.py:334
  42.7 1.5 %collective-permute-start.22 = (bf16[128,512]{1,0:T(8,128)(2,1)S(1)}, bf16[128,512]{1,0:T(8,128)(2,1)S(1)}, u32[]{:S(2)}, u32[]{:S(2)}) collective-permute-start(bf16[128,512]{1,0:T(8,128)(2,1)S(1)} %collective-permute-done.20.refs_2_), channel_id=1, source_target_pairs={{0,1},{1,0},{2,3},{3,2},{4,5},{5,4},{6,7},{7,6},{8,9},{9,8},{10,11... | collective-permute-start | bytes 393224 | tf_op jit(solution)/shard_map/ppermute | solution.py:334

commit v14 on v12

--- a/solution.py
+++ b/solution.py
@@ -49,7 +49,8 @@
     return place_on_ring(lax.axis_index("lat"), n) % (n // 2) % (n // 2 - 1) == 0
 
 
-def first_step(hops, later, *refs):
+def first_step(hops, later, paces, *refs):
+    refs = refs[paces:]
     xs, (weights, total, kept, blocks, sems) = refs[:-5], refs[-5:]
     n = weights.shape[0]
     copies = [
@@ -96,10 +97,13 @@
         self.beside = aside + stay
         self.across = [(walk[i], walk[j]) for i, j in across + beside]
 
-    def gather(self, x, beside_second=None, beside_third=None):
+    def gather(self, x, beside_second=None, beside_third=None, in_pace=False):
         ahead = lax.ppermute(x, "lat", self.forward)
         behind = lax.ppermute(x, "lat", self.backward)
         corner = lax.ppermute(x, "lat", self.across)
+        if in_pace:
+            pace = lax.ppermute(x[:16], "tok", [(0, 1), (1, 0)])
+            ahead, behind, pace = lax.optimization_barrier((ahead, behind, pace))
         ahead_2 = lax.ppermute(ahead, "lat", self.forward)
         behind_2 = lax.ppermute(behind, "lat", self.backward)
         odd = place_on_ring(lax.axis_index("lat"), self.n) % 2 == 1
@@ -111,6 +115,8 @@
         ahead_3 = lax.ppermute(ahead_2, "lat", self.forward)
         behind_3 = lax.ppermute(behind_2, "lat", self.backward)
         done, middle = lax.optimization_barrier((done, middle))
+        if in_pace:
+            done = (pace, done)
         done = beside_third(ahead, behind, ahead_2, behind_2, corner, done)
         return done, ahead_3, behind_3, corner, middle
 
@@ -122,13 +128,13 @@
     weights = enc_weight.reshape(n, depth, width)
 
     def beside_third(*blocks):
-        blocks = blocks[:4]
+        blocks, paces = blocks[:4], jax.tree.leaves(blocks[5])
         hops, later = (1, -1, 2, -2), (0, 3, -3, n // 2)
         kept = jax.ShapeDtypeStruct((len(later),) + weights.shape[1:], weights.dtype)
         return pl.pallas_call(
-            functools.partial(first_step, hops, later),
+            functools.partial(first_step, hops, later, len(paces)),
             out_shape=(jax.ShapeDtypeStruct((tok_rows, width), jnp.float32), kept),
-            in_specs=[in_vmem] * len(blocks) + [in_hbm],
+            in_specs=[in_vmem] * (len(paces) + len(blocks)) + [in_hbm],
             out_specs=(in_vmem, in_vmem),
             scratch_shapes=[
                 pltpu.VMEM((len(hops),) + weights.shape[1:], weights.dtype),
@@ -136,10 +142,10 @@
             ],
             compiler_params=streaming_params,
             cost_estimate=cost(tok_rows, depth, width, 4),
-        )(*blocks, weights)
+        )(*paces, *blocks, weights)
 
     x = residual.T
-    (total, kept), ahead, behind, corner, middle = ring.gather(x, beside_third=beside_third)
+    (total, kept), ahead, behind, corner, middle = ring.gather(x, beside_third=beside_third, in_pace=True)
     return pl.pallas_call(
         last_step,
         out_shape=jax.ShapeDtypeStruct((tok_rows, width), jnp.bfloat16),

time: 42.8 us -> 44.8 us (1.047)
  waiting for transfers between devices: 14 us -> 16.4 us
  local copies, waits for them, and re-layouts: 0.01 us -> 0.77 us
  Pallas kernels: 6.2 us -> 5.55 us
    ppermute x2, waiting for transfers between devices: 1.69 us -> 4.73 us  [gather(): ahead_2 = lax.ppermute(ahead, 'lat', self.forward)]
    ppermute x2, waiting for transfers between devices: 2.09 us -> 0.01 us  [gather(): behind_2 = lax.ppermute(behind, 'lat', self.backward)]
    ppermute x2, waiting for transfers between devices: 3.1 us -> 4.25 us  [gather(): ahead_3 = lax.ppermute(ahead_2, 'lat', self.forward)]
    ppermute x2, starting transfers between devices: 3.73 us -> 2.78 us  [gather(): behind_2 = lax.ppermute(behind, 'lat', self.backward)]
    slice x0 -> x1, local copies, waits for them, and re-layouts: none -> 0.75 us  [gather(): pace = lax.ppermute(x[:16], 'tok', [(0, 1), (1, 0)])]
    ppermute x7, waiting for transfers between devices: 1.7 us -> 1.03 us  [add_tiles(): twins = [lax.ppermute(block, 'tok', swap) for block in blocks]]
    pallas_call x3, Pallas kernels: 3.64 us -> 2.99 us  [tiles_of(): pl.pallas_call(functools.partial(tiles_kernel, tok_scale, n, hops, first)...]
    ppermute x2, waiting for transfers between devices: 0.01 us -> 0.66 us  [gather(): ahead = lax.ppermute(x, 'lat', self.forward)]
  transfers between devices with their start and end apart: 24 -> 25, of which waited for: 13 -> 11; matrix products, arithmetic and copies ran while one was open for 0% -> 2% of each run, Pallas kernels for 11% -> 8%
where the time goes in v14:
time: 44.8 us
  starting transfers between devices  21.8 us (49%)
  waiting for transfers between devices  16.4 us (37%)
  Pallas kernels  5.55 us (12%)
  local copies, waits for them, and re-layouts  0.77 us (2%)
    ppermute x2, starting transfers between devices, gather(): corner = lax.ppermute(x, 'lat', self.across)  7.23 us
    ppermute x2, waiting for transfers between devices, gather(): ahead_2 = lax.ppermute(ahead, 'lat', self.forward)  4.73 us
    ppermute x2, waiting for transfers between devices, gather(): corner = lax.ppermute(x, 'lat', self.across)  4.28 us
    ppermute x2, waiting for transfers between devices, gather(): ahead_3 = lax.ppermute(ahead_2, 'lat', self.forward)  4.25 us
    ppermute x2, starting transfers between devices, gather(): ahead = lax.ppermute(x, 'lat', self.forward)  3.59 us
    pallas_call x3, Pallas kernels, tiles_of(): pl.pallas_call(functools.partial(tiles_kernel, tok_scale, n, hops, first)...  2.99 us
    ppermute x2, starting transfers between devices, gather(): behind_2 = lax.ppermute(behind, 'lat', self.backward)  2.78 us
    ppermute x2, starting transfers between devices, gather(): behind_3 = lax.ppermute(behind_2, 'lat', self.backward)  2.08 us
  transfers between devices with their start and end apart: 25, of which 11 were waited for; matrix products, arithmetic and copies ran while one was open for 2% of the time, Pallas kernels for 8%

profile of v14, /device:TPU:0, one launch (start us, length us, event | category | flops | bytes accessed | tf_op | source)
XLA Modules:
  0.0 44.8 jit_solution(4215187959781019425)
XLA Ops:
  0.0 3.1 %collective-permute-start = (bf16[448,128]{1,0:T(8,128)(2,1)}, bf16[448,128]{1,0:T(8,128)(2,1)S(1)}, u32[]{:S(2)}, u32[]{:S(2)}) collective-permute-start(bf16[448,128]{1,0:T(8,128)(2,1)} %bitcast.5), channel_id=1, source_target_pairs={{0,4},{4,8},{8,12},{12,14},{14,10},{10,6},{6,2},{2,0},{1,5},{5,9},... | collective-permute-start | bytes 344072 | tf_op jit(solution)/shard_map/ppermute | solution.py:101
  3.1 0.0 collective-permute-start.1
  3.1 0.8 %slice.4 = bf16[16,128]{1,0:T(8,128)(2,1)S(1)} slice(bf16[448,128]{1,0:T(8,128)(2,1)} %bitcast.7), slice={[0:16], [0:128]} | slice | bytes 8192 | tf_op jit(solution)/shard_map/slice | solution.py:105
  3.8 0.0 collective-permute-start.2
  3.8 4.9 %collective-permute-start.5 = (bf16[448,128]{1,0:T(8,128)(2,1)}, bf16[448,128]{1,0:T(8,128)(2,1)S(1)}, u32[]{:S(2)}, u32[]{:S(2)}) collective-permute-start(bf16[448,128]{1,0:T(8,128)(2,1)} %bitcast.8), channel_id=1, source_target_pairs={{0,14},{12,2},{14,0},{2,12},{4,6},{8,10},{10,8},{6,4},{1,15},{13,3... | collective-permute-start | bytes 344072 | tf_op jit(solution)/shard_map/ppermute | solution.py:103
  8.8 0.0 collective-permute-done.2.refs_0_
  8.8 0.0 collective-permute-done.refs_1_
  8.8 0.0 collective-permute-done.1.refs_2_
  8.8 0.9 %collective-permute-start.3 = (bf16[448,128]{1,0:T(8,128)(2,1)S(1)}, bf16[448,128]{1,0:T(8,128)(2,1)S(1)}, u32[]{:S(2)}, u32[]{:S(2)}) collective-permute-start(bf16[448,128]{1,0:T(8,128)(2,1)S(1)} %collective-permute-done.refs_1_), channel_id=1, source_target_pairs={{0,4},{4,8},{8,12},{12,14},{14,10},{10,6},{6,2},{2,0},{1,5},{5,9},... | collective-permute-start | bytes 344072 | tf_op jit(solution)/shard_map/ppermute | solution.py:107
  9.7 1.2 %collective-permute-start.4 = (bf16[448,128]{1,0:T(8,128)(2,1)S(1)}, bf16[448,128]{1,0:T(8,128)(2,1)S(1)}, u32[]{:S(2)}, u32[]{:S(2)}) collective-permute-start(bf16[448,128]{1,0:T(8,128)(2,1)S(1)} %collective-permute-done.1.refs_2_), channel_id=1, source_target_pairs={{4,0},{8,4},{12,8},{14,12},{10,14},{6,10},{2,6},{0,2},{5,1},{9,5},... | collective-permute-start | bytes 344072 | tf_op jit(solution)/shard_map/ppermute | solution.py:108
  10.9 0.1 collective-permute-start.8
  11.0 2.1 %collective-permute-done.5.x_corner = bf16[448,128]{1,0:T(8,128)(2,1)S(1)} collective-permute-done((bf16[448,128]{1,0:T(8,128)(2,1)}, bf16[448,128]{1,0:T(8,128)(2,1)S(1)}, u32[]{:S(2)}, u32[]{:S(2)}) %collective-permute-start.5) | collective-permute-done | bytes 114720 | tf_op jit(solution)/shard_map/ppermute | solution.py:103
  13.1 2.3 %collective-permute-done.3.refs_3_ = bf16[448,128]{1,0:T(8,128)(2,1)S(1)} collective-permute-done((bf16[448,128]{1,0:T(8,128)(2,1)S(1)}, bf16[448,128]{1,0:T(8,128)(2,1)S(1)}, u32[]{:S(2)}, u32[]{:S(2)}) %collective-permute-start.3) | collective-permute-done | bytes 114720 | tf_op jit(solution)/shard_map/ppermute | solution.py:107
  15.4 0.0 collective-permute-done.4.refs_4_
  15.4 1.7 %collective-permute-start.6 = (bf16[448,128]{1,0:T(8,128)(2,1)S(1)}, bf16[448,128]{1,0:T(8,128)(2,1)S(1)}, u32[]{:S(2)}, u32[]{:S(2)}) collective-permute-start(bf16[448,128]{1,0:T(8,128)(2,1)S(1)} %collective-permute-done.3.refs_3_), channel_id=1, source_target_pairs={{0,4},{4,8},{8,12},{12,14},{14,10},{10,6},{6,2},{2,0},{1,5},{5,9},... | collective-permute-start | bytes 344072 | tf_op jit(solution)/shard_map/ppermute | solution.py:115
  17.1 0.3 collective-permute-start.7
  17.4 0.0 collective-permute-done.8.x_middle
  17.4 2.1 %shard_map.55 = (f32[128,512]{1,0:T(8,128)S(1)}, bf16[4,448,512]{2,1,0:T(8,128)(2,1)S(1)}) custom-call(bf16[16,128]{1,0:T(8,128)(2,1)S(1)} %collective-permute-done.2.refs_0_, bf16[448,128]{1,0:T(8,128)(2,1)S(1)} %collective-permute-done.refs_1_, bf16[448,128]{1,0:T(8,128)(2,1)S(1)} %collective-permute-done.1.refs_2_, ...), custom_call_target="tpu_custom_call" | custom-call | flops 234881024 | bytes 2818048 | tf_op jit(solution)/shard_map/pallas_call | solution.py:134
  19.5 1.0 %collective-permute-done.6.x_f = bf16[448,128]{1,0:T(8,128)(2,1)S(1)} collective-permute-done((bf16[448,128]{1,0:T(8,128)(2,1)S(1)}, bf16[448,128]{1,0:T(8,128)(2,1)S(1)}, u32[]{:S(2)}, u32[]{:S(2)}) %collective-permute-start.6) | collective-permute-done | bytes 114720 | tf_op jit(solution)/shard_map/ppermute | solution.py:115
  20.5 1.4 %collective-permute-done.7.x_b = bf16[448,128]{1,0:T(8,128)(2,1)S(1)} collective-permute-done((bf16[448,128]{1,0:T(8,128)(2,1)S(1)}, bf16[448,128]{1,0:T(8,128)(2,1)S(1)}, u32[]{:S(2)}, u32[]{:S(2)}) %collective-permute-start.7) | collective-permute-done | bytes 114720 | tf_op jit(solution)/shard_map/ppermute | solution.py:116
  21.9 0.5 %shard_map.56.refs_0_ = bf16[128,512]{1,0:T(8,128)(2,1)S(1)} custom-call(bf16[448,128]{1,0:T(8,128)(2,1)S(1)} %bitcast.9, bf16[448,128]{1,0:T(8,128)(2,1)S(1)} %collective-permute-done.6.x_f, bf16[448,128]{1,0:T(8,128)(2,1)S(1)} %collective-permute-done.7.x_b, bf16[448,128]{1,0:T(8,128)(2,1)S(1)} %collective-permute-done.5.x_corner, ...), custom_call_target="tpu_custom_call" | custom-call | flops 234881024 | bytes 2818048 | tf_op jit(solution)/shard_map/pallas_call | solution.py:149
  22.4 0.5 %collective-permute-start.9 = (bf16[128,512]{1,0:T(8,128)(2,1)S(1)}, bf16[128,512]{1,0:T(8,128)(2,1)S(1)}, u32[]{:S(2)}, u32[]{:S(2)}) collective-permute-start(bf16[128,512]{1,0:T(8,128)(2,1)S(1)} %shard_map.56.refs_0_), channel_id=1, source_target_pairs={{0,4},{4,8},{8,12},{12,14},{14,10},{10,6},{6,2},{2,0},{1,5},{5,9},... | collective-permute-start | bytes 393224 | tf_op jit(solution)/shard_map/ppermute | solution.py:101
  22.9 1.6 %collective-permute-start.11 = (bf16[128,512]{1,0:T(8,128)(2,1)S(1)}, bf16[128,512]{1,0:T(8,128)(2,1)S(1)}, u32[]{:S(2)}, u32[]{:S(2)}) collective-permute-start(bf16[128,512]{1,0:T(8,128)(2,1)S(1)} %shard_map.56.refs_0_), channel_id=1, source_target_pairs={{4,0},{8,4},{12,8},{14,12},{10,14},{6,10},{2,6},{0,2},{5,1},{9,5},... | collective-permute-start | bytes 393224 | tf_op jit(solution)/shard_map/ppermute | solution.py:102
  24.5 2.3 %collective-permute-start.13 = (bf16[128,512]{1,0:T(8,128)(2,1)S(1)}, bf16[128,512]{1,0:T(8,128)(2,1)S(1)}, u32[]{:S(2)}, u32[]{:S(2)}) collective-permute-start(bf16[128,512]{1,0:T(8,128)(2,1)S(1)} %shard_map.56.refs_0_), channel_id=1, source_target_pairs={{0,14},{12,2},{14,0},{2,12},{4,6},{8,10},{10,8},{6,4},{1,15},{13,3... | collective-permute-start | bytes 393224 | tf_op jit(solution)/shard_map/ppermute | solution.py:103
  26.7 0.7 %collective-permute-done.9.refs_2_ = bf16[128,512]{1,0:T(8,128)(2,1)S(1)} collective-permute-done((bf16[128,512]{1,0:T(8,128)(2,1)S(1)}, bf16[128,512]{1,0:T(8,128)(2,1)S(1)}, u32[]{:S(2)}, u32[]{:S(2)}) %collective-permute-start.9) | collective-permute-done | bytes 131104 | tf_op jit(solution)/shard_map/ppermute | solution.py:101
  27.4 0.5 %collective-permute-start.10 = (bf16[128,512]{1,0:T(8,128)(2,1)S(1)}, bf16[128,512]{1,0:T(8,128)(2,1)S(1)}, u32[]{:S(2)}, u32[]{:S(2)}) collective-permute-start(bf16[128,512]{1,0:T(8,128)(2,1)S(1)} %collective-permute-done.9.refs_2_), channel_id=1, source_target_pairs={{0,4},{4,8},{8,12},{12,14},{14,10},{10,6},{6,2},{2,0},{1,5},{5,9},... | collective-permute-start | bytes 393224 | tf_op jit(solution)/shard_map/ppermute | solution.py:107
  27.9 0.2 collective-permute-start.16
  28.1 1.6 %collective-permute-start.12 = (bf16[128,512]{1,0:T(8,128)(2,1)S(1)}, bf16[128,512]{1,0:T(8,128)(2,1)S(1)}, u32[]{:S(2)}, u32[]{:S(2)}) collective-permute-start(bf16[128,512]{1,0:T(8,128)(2,1)S(1)} %collective-permute-done.11.refs_3_), channel_id=1, source_target_pairs={{4,0},{8,4},{12,8},{14,12},{10,14},{6,10},{2,6},{0,2},{5,1},{9,5},... | collective-permute-start | bytes 393224 | tf_op jit(solution)/shard_map/ppermute | solution.py:108
  29.7 0.1 collective-permute-start.17
  29.8 1.4 %shard_map.57 = (bf16[256,256]{1,0:T(8,128)(2,1)S(1)}, bf16[1,4,256,512]{3,2,1,0:T(8,128)(2,1)}) custom-call(s32[4,8]{1,0:T(4,128)S(1)} %bitcast.10, bf16[128,512]{1,0:T(8,128)(2,1)S(1)} %shard_map.56.refs_0_, bf16[128,512]{1,0:T(8,128)(2,1)S(1)} %collective-permute-done.14.refs_1_, bf16[128,512]{1,0:T(8,128)(2,1)S(1)} %collective-permute-done.9.refs_2_, ...), custom_call_target="tpu_custom_call" | custom-call | flops 134217728 | bytes 1048576 | tf_op jit(solution)/shard_map/pallas_call | solution.py:308
  31.3 2.2 %collective-permute-done.13 = bf16[128,512]{1,0:T(8,128)(2,1)S(1)} collective-permute-done((bf16[128,512]{1,0:T(8,128)(2,1)S(1)}, bf16[128,512]{1,0:T(8,128)(2,1)S(1)}, u32[]{:S(2)}, u32[]{:S(2)}) %collective-permute-start.13) | collective-permute-done | bytes 131104 | tf_op jit(solution)/shard_map/ppermute | solution.py:103
  33.5 2.4 %collective-permute-done.10.refs_1_ = bf16[128,512]{1,0:T(8,128)(2,1)S(1)} collective-permute-done((bf16[128,512]{1,0:T(8,128)(2,1)S(1)}, bf16[128,512]{1,0:T(8,128)(2,1)S(1)}, u32[]{:S(2)}, u32[]{:S(2)}) %collective-permute-start.10) | collective-permute-done | bytes 131104 | tf_op jit(solution)/shard_map/ppermute | solution.py:107
  35.9 0.0 collective-permute-done.12.refs_2_
  35.9 0.1 collective-permute-start.18
  36.0 0.4 collective-permute-start.19
  36.4 1.7 %collective-permute-start.21 = (bf16[128,512]{1,0:T(8,128)(2,1)S(1)}, bf16[128,512]{1,0:T(8,128)(2,1)S(1)}, u32[]{:S(2)}, u32[]{:S(2)}) collective-permute-start(bf16[128,512]{1,0:T(8,128)(2,1)S(1)} %collective-permute-done.12.refs_2_), channel_id=1, source_target_pairs={{4,0},{8,4},{12,8},{14,12},{10,14},{6,10},{2,6},{0,2},{5,1},{9,5},... | collective-permute-start | bytes 393224 | tf_op jit(solution)/shard_map/ppermute | solution.py:116
  38.1 0.0 collective-permute-done.17
  38.2 0.1 collective-permute-start.24
  38.3 0.0 collective-permute-done.18.refs_3_
  38.3 0.0 collective-permute-done.19.refs_4_
  38.3 0.2 shard_map.58.refs_7_
  38.5 3.3 %collective-permute-done.20.refs_1_ = bf16[128,512]{1,0:T(8,128)(2,1)S(1)} collective-permute-done((bf16[128,512]{1,0:T(8,128)(2,1)S(1)}, bf16[128,512]{1,0:T(8,128)(2,1)S(1)}, u32[]{:S(2)}, u32[]{:S(2)}) %collective-permute-start.20) | collective-permute-done | bytes 131104 | tf_op jit(solution)/shard_map/ppermute | solution.py:115
  41.8 0.1 collective-permute-done.21.refs_2_
  41.9 0.5 %collective-permute-start.23 = (bf16[128,512]{1,0:T(8,128)(2,1)S(1)}, bf16[128,512]{1,0:T(8,128)(2,1)S(1)}, u32[]{:S(2)}, u32[]{:S(2)}) collective-permute-start(bf16[128,512]{1,0:T(8,128)(2,1)S(1)} %collective-permute-done.21.refs_2_), channel_id=1, source_target_pairs={{0,1},{1,0},{2,3},{3,2},{4,5},{5,4},{6,7},{7,6},{8,9},{9,8},{10,11... | collective-permute-start | bytes 393224 | tf_op jit(solution)/shard_map/ppermute | solution.py:343
  42.4 0.0 collective-permute-done.24.refs_6_
  42.4 0.8 %collective-permute-done.22.refs_4_ = bf16[128,512]{1,0:T(8,128)(2,1)S(1)} collective-permute-done((bf16[128,512]{1,0:T(8,128)(2,1)S(1)}, bf16[128,512]{1,0:T(8,128)(2,1)S(1)}, u32[]{:S(2)}, u32[]{:S(2)}) %collective-permute-start.22) | collective-permute-done | bytes 131104 | tf_op jit(solution)/shard_map/ppermute | solution.py:343
  43.2 0.2 collective-permute-done.23.refs_5_
  43.4 1.3 %shard_map.59 = bf16[1,4,256,512]{3,2,1,0:T(8,128)(2,1)} custom-call(s32[4,8]{1,0:T(4,128)S(1)} %bitcast.12, bf16[256,256]{1,0:T(8,128)(2,1)S(1)} %get-tuple-element.43.refs_0_, bf16[128,512]{1,0:T(8,128)(2,1)S(1)} %collective-permute-done.20.refs_1_, bf16[128,512]{1,0:T(8,128)(2,1)S(1)} %collective-permute-done.21.refs_2_, ...), custom_call_target="tpu_custom_call", output_to_operand_aliasing={{}: (8, {})} | custom-call | flops 201326592 | bytes 1572864 | tf_op jit(solution)/shard_map/pallas_call | solution.py:308
  (19 shorter events, 0.1 us)
Async XLA Ops:
  0.0 21.9 %copy-start = (bf16[128,448]{0,1:T(8,128)(2,1)S(1)}, bf16[128,448]{0,1:T(8,128)(2,1)}, u32[]{:S(2)}) copy-start(bf16[128,448]{0,1:T(8,128)(2,1)} %param.5) | copy-start | bytes 344068
  0.0 21.9 %copy-start.2 = (f32[512]{0:T(512)S(1)}, f32[512]{0:T(512)}, u32[]{:S(2)}) copy-start(f32[512]{0:T(512)} %param.7) | copy-start | bytes 6148
  0.0 21.9 %copy-start.3 = (f32[512]{0:T(512)S(1)}, f32[512]{0:T(512)}, u32[]{:S(2)}) copy-start(f32[512]{0:T(512)} %param.8) | copy-start | bytes 6148
  0.0 8.8 %collective-permute-start = (bf16[448,128]{1,0:T(8,128)(2,1)}, bf16[448,128]{1,0:T(8,128)(2,1)S(1)}, u32[]{:S(2)}, u32[]{:S(2)}) collective-permute-start(bf16[448,128]{1,0:T(8,128)(2,1)} %bitcast.5), channel_id=1, source_target_pairs={{0,4},{4,8},{8,12},{12,14},{14,10},{10,6},{6,2},{2,0},{1,5},{5,9},... | collective-permute-start | bytes 344072 | tf_op jit(solution)/shard_map/ppermute | solution.py:101
  3.1 5.7 %collective-permute-start.1 = (bf16[448,128]{1,0:T(8,128)(2,1)}, bf16[448,128]{1,0:T(8,128)(2,1)S(1)}, u32[]{:S(2)}, u32[]{:S(2)}) collective-permute-start(bf16[448,128]{1,0:T(8,128)(2,1)} %bitcast.6), channel_id=1, source_target_pairs={{4,0},{8,4},{12,8},{14,12},{10,14},{6,10},{2,6},{0,2},{5,1},{9,5},... | collective-permute-start | bytes 344072 | tf_op jit(solution)/shard_map/ppermute | solution.py:102
  3.8 5.0 %collective-permute-start.2 = (bf16[16,128]{1,0:T(8,128)(2,1)S(1)}, bf16[16,128]{1,0:T(8,128)(2,1)S(1)}, u32[]{:S(2)}, u32[]{:S(2)}) collective-permute-start(bf16[16,128]{1,0:T(8,128)(2,1)S(1)} %slice.4), channel_id=1, source_target_pairs={{0,1},{1,0},{2,3},{3,2},{4,5},{5,4},{6,7},{7,6},{8,9},{9,8},{10,11... | collective-permute-start | bytes 12296 | tf_op jit(solution)/shard_map/ppermute | solution.py:105
  3.8 9.2 %collective-permute-start.5 = (bf16[448,128]{1,0:T(8,128)(2,1)}, bf16[448,128]{1,0:T(8,128)(2,1)S(1)}, u32[]{:S(2)}, u32[]{:S(2)}) collective-permute-start(bf16[448,128]{1,0:T(8,128)(2,1)} %bitcast.8), channel_id=1, source_target_pairs={{0,14},{12,2},{14,0},{2,12},{4,6},{8,10},{10,8},{6,4},{1,15},{13,3... | collective-permute-start | bytes 344072 | tf_op jit(solution)/shard_map/ppermute | solution.py:103
  8.8 6.6 %collective-permute-start.3 = (bf16[448,128]{1,0:T(8,128)(2,1)S(1)}, bf16[448,128]{1,0:T(8,128)(2,1)S(1)}, u32[]{:S(2)}, u32[]{:S(2)}) collective-permute-start(bf16[448,128]{1,0:T(8,128)(2,1)S(1)} %collective-permute-done.refs_1_), channel_id=1, source_target_pairs={{0,4},{4,8},{8,12},{12,14},{14,10},{10,6},{6,2},{2,0},{1,5},{5,9},... | collective-permute-start | bytes 344072 | tf_op jit(solution)/shard_map/ppermute | solution.py:107
  9.7 5.7 %collective-permute-start.4 = (bf16[448,128]{1,0:T(8,128)(2,1)S(1)}, bf16[448,128]{1,0:T(8,128)(2,1)S(1)}, u32[]{:S(2)}, u32[]{:S(2)}) collective-permute-start(bf16[448,128]{1,0:T(8,128)(2,1)S(1)} %collective-permute-done.1.refs_2_), channel_id=1, source_target_pairs={{4,0},{8,4},{12,8},{14,12},{10,14},{6,10},{2,6},{0,2},{5,1},{9,5},... | collective-permute-start | bytes 344072 | tf_op jit(solution)/shard_map/ppermute | solution.py:108
  10.9 6.5 %collective-permute-start.8 = (bf16[448,128]{1,0:T(8,128)(2,1)S(1)}, bf16[448,128]{1,0:T(8,128)(2,1)S(1)}, u32[]{:S(2)}, u32[]{:S(2)}) collective-permute-start(bf16[448,128]{1,0:T(8,128)(2,1)S(1)} %broadcast_select_fusion.2), channel_id=1, source_target_pairs={{4,6},{5,7},{8,10},{9,11},{10,8},{11,9},{6,4},{7,5},{0,1},{1,0},{1... | collective-permute-start | bytes 344072 | tf_op jit(solution)/shard_map/ppermute | solution.py:110
  15.4 5.1 %collective-permute-start.6 = (bf16[448,128]{1,0:T(8,128)(2,1)S(1)}, bf16[448,128]{1,0:T(8,128)(2,1)S(1)}, u32[]{:S(2)}, u32[]{:S(2)}) collective-permute-start(bf16[448,128]{1,0:T(8,128)(2,1)S(1)} %collective-permute-done.3.refs_3_), channel_id=1, source_target_pairs={{0,4},{4,8},{8,12},{12,14},{14,10},{10,6},{6,2},{2,0},{1,5},{5,9},... | collective-permute-start | bytes 344072 | tf_op jit(solution)/shard_map/ppermute | solution.py:115
  17.1 4.8 %collective-permute-start.7 = (bf16[448,128]{1,0:T(8,128)(2,1)S(1)}, bf16[448,128]{1,0:T(8,128)(2,1)S(1)}, u32[]{:S(2)}, u32[]{:S(2)}) collective-permute-start(bf16[448,128]{1,0:T(8,128)(2,1)S(1)} %collective-permute-done.4.refs_4_), channel_id=1, source_target_pairs={{4,0},{8,4},{12,8},{14,12},{10,14},{6,10},{2,6},{0,2},{5,1},{9,5},... | collective-permute-start | bytes 344072 | tf_op jit(solution)/shard_map/ppermute | solution.py:116
  17.4 12.4 %copy-start.1 = (s32[8,4]{0,1:T(4,128)S(1)}, s32[8,4]{0,1:T(4,128)}, u32[]{:S(2)}) copy-start(s32[8,4]{0,1:T(4,128)} %param.9) | copy-start | bytes 388
  22.4 5.0 %collective-permute-start.9 = (bf16[128,512]{1,0:T(8,128)(2,1)S(1)}, bf16[128,512]{1,0:T(8,128)(2,1)S(1)}, u32[]{:S(2)}, u32[]{:S(2)}) collective-permute-start(bf16[128,512]{1,0:T(8,128)(2,1)S(1)} %shard_map.56.refs_0_), channel_id=1, source_target_pairs={{0,4},{4,8},{8,12},{12,14},{14,10},{10,6},{6,2},{2,0},{1,5},{5,9},... | collective-permute-start | bytes 393224 | tf_op jit(solution)/shard_map/ppermute | solution.py:101
  22.9 5.0 %collective-permute-start.11 = (bf16[128,512]{1,0:T(8,128)(2,1)S(1)}, bf16[128,512]{1,0:T(8,128)(2,1)S(1)}, u32[]{:S(2)}, u32[]{:S(2)}) collective-permute-start(bf16[128,512]{1,0:T(8,128)(2,1)S(1)} %shard_map.56.refs_0_), channel_id=1, source_target_pairs={{4,0},{8,4},{12,8},{14,12},{10,14},{6,10},{2,6},{0,2},{5,1},{9,5},... | collective-permute-start | bytes 393224 | tf_op jit(solution)/shard_map/ppermute | solution.py:102
  24.5 3.6 %collective-permute-start.14 = (bf16[128,512]{1,0:T(8,128)(2,1)S(1)}, bf16[128,512]{1,0:T(8,128)(2,1)S(1)}, u32[]{:S(2)}, u32[]{:S(2)}) collective-permute-start(bf16[128,512]{1,0:T(8,128)(2,1)S(1)} %shard_map.56.refs_0_), channel_id=1, source_target_pairs={{0,1},{1,0},{2,3},{3,2},{4,5},{5,4},{6,7},{7,6},{8,9},{9,8},{10,11... | collective-permute-start | bytes 393224 | tf_op jit(solution)/shard_map/ppermute | solution.py:340
  24.5 9.0 %collective-permute-start.13 = (bf16[128,512]{1,0:T(8,128)(2,1)S(1)}, bf16[128,512]{1,0:T(8,128)(2,1)S(1)}, u32[]{:S(2)}, u32[]{:S(2)}) collective-permute-start(bf16[128,512]{1,0:T(8,128)(2,1)S(1)} %shard_map.56.refs_0_), channel_id=1, source_target_pairs={{0,14},{12,2},{14,0},{2,12},{4,6},{8,10},{10,8},{6,4},{1,15},{13,3... | collective-permute-start | bytes 393224 | tf_op jit(solution)/shard_map/ppermute | solution.py:103
  27.4 2.3 %collective-permute-start.15 = (bf16[128,512]{1,0:T(8,128)(2,1)S(1)}, bf16[128,512]{1,0:T(8,128)(2,1)S(1)}, u32[]{:S(2)}, u32[]{:S(2)}) collective-permute-start(bf16[128,512]{1,0:T(8,128)(2,1)S(1)} %collective-permute-done.9.refs_2_), channel_id=1, source_target_pairs={{0,1},{1,0},{2,3},{3,2},{4,5},{5,4},{6,7},{7,6},{8,9},{9,8},{10,11... | collective-permute-start | bytes 393224 | tf_op jit(solution)/shard_map/ppermute | solution.py:343
  27.4 8.5 %collective-permute-start.10 = (bf16[128,512]{1,0:T(8,128)(2,1)S(1)}, bf16[128,512]{1,0:T(8,128)(2,1)S(1)}, u32[]{:S(2)}, u32[]{:S(2)}) collective-permute-start(bf16[128,512]{1,0:T(8,128)(2,1)S(1)} %collective-permute-done.9.refs_2_), channel_id=1, source_target_pairs={{0,4},{4,8},{8,12},{12,14},{14,10},{10,6},{6,2},{2,0},{1,5},{5,9},... | collective-permute-start | bytes 393224 | tf_op jit(solution)/shard_map/ppermute | solution.py:107
  27.9 1.9 %collective-permute-start.16 = (bf16[128,512]{1,0:T(8,128)(2,1)S(1)}, bf16[128,512]{1,0:T(8,128)(2,1)S(1)}, u32[]{:S(2)}, u32[]{:S(2)}) collective-permute-start(bf16[128,512]{1,0:T(8,128)(2,1)S(1)} %collective-permute-done.11.refs_3_), channel_id=1, source_target_pairs={{0,1},{1,0},{2,3},{3,2},{4,5},{5,4},{6,7},{7,6},{8,9},{9,8},{10,11... | collective-permute-start | bytes 393224 | tf_op jit(solution)/shard_map/ppermute | solution.py:343
  28.1 7.8 %collective-permute-start.12 = (bf16[128,512]{1,0:T(8,128)(2,1)S(1)}, bf16[128,512]{1,0:T(8,128)(2,1)S(1)}, u32[]{:S(2)}, u32[]{:S(2)}) collective-permute-start(bf16[128,512]{1,0:T(8,128)(2,1)S(1)} %collective-permute-done.11.refs_3_), channel_id=1, source_target_pairs={{4,0},{8,4},{12,8},{14,12},{10,14},{6,10},{2,6},{0,2},{5,1},{9,5},... | collective-permute-start | bytes 393224 | tf_op jit(solution)/shard_map/ppermute | solution.py:108
  29.7 8.4 %collective-permute-start.17 = (bf16[128,512]{1,0:T(8,128)(2,1)S(1)}, bf16[128,512]{1,0:T(8,128)(2,1)S(1)}, u32[]{:S(2)}, u32[]{:S(2)}) collective-permute-start(bf16[128,512]{1,0:T(8,128)(2,1)S(1)} %broadcast_select_fusion.1), channel_id=1, source_target_pairs={{4,6},{5,7},{8,10},{9,11},{10,8},{11,9},{6,4},{7,5},{0,1},{1,0},{1... | collective-permute-start | bytes 393224 | tf_op jit(solution)/shard_map/ppermute | solution.py:110
  35.9 2.4 %collective-permute-start.18 = (bf16[128,512]{1,0:T(8,128)(2,1)S(1)}, bf16[128,512]{1,0:T(8,128)(2,1)S(1)}, u32[]{:S(2)}, u32[]{:S(2)}) collective-permute-start(bf16[128,512]{1,0:T(8,128)(2,1)S(1)} %collective-permute-done.10.refs_1_), channel_id=1, source_target_pairs={{0,1},{1,0},{2,3},{3,2},{4,5},{5,4},{6,7},{7,6},{8,9},{9,8},{10,11... | collective-permute-start | bytes 393224 | tf_op jit(solution)/shard_map/ppermute | solution.py:343
  36.0 5.8 %collective-permute-start.20 = (bf16[128,512]{1,0:T(8,128)(2,1)S(1)}, bf16[128,512]{1,0:T(8,128)(2,1)S(1)}, u32[]{:S(2)}, u32[]{:S(2)}) collective-permute-start(bf16[128,512]{1,0:T(8,128)(2,1)S(1)} %collective-permute-done.10.refs_1_), channel_id=1, source_target_pairs={{0,4},{4,8},{8,12},{12,14},{14,10},{10,6},{6,2},{2,0},{1,5},{5,9},... | collective-permute-start | bytes 393224 | tf_op jit(solution)/shard_map/ppermute | solution.py:115
  36.0 2.3 %collective-permute-start.19 = (bf16[128,512]{1,0:T(8,128)(2,1)S(1)}, bf16[128,512]{1,0:T(8,128)(2,1)S(1)}, u32[]{:S(2)}, u32[]{:S(2)}) collective-permute-start(bf16[128,512]{1,0:T(8,128)(2,1)S(1)} %collective-permute-done.12.refs_2_), channel_id=1, source_target_pairs={{0,1},{1,0},{2,3},{3,2},{4,5},{5,4},{6,7},{7,6},{8,9},{9,8},{10,11... | collective-permute-start | bytes 393224 | tf_op jit(solution)/shard_map/ppermute | solution.py:343
  36.4 5.5 %collective-permute-start.21 = (bf16[128,512]{1,0:T(8,128)(2,1)S(1)}, bf16[128,512]{1,0:T(8,128)(2,1)S(1)}, u32[]{:S(2)}, u32[]{:S(2)}) collective-permute-start(bf16[128,512]{1,0:T(8,128)(2,1)S(1)} %collective-permute-done.12.refs_2_), channel_id=1, source_target_pairs={{4,0},{8,4},{12,8},{14,12},{10,14},{6,10},{2,6},{0,2},{5,1},{9,5},... | collective-permute-start | bytes 393224 | tf_op jit(solution)/shard_map/ppermute | solution.py:116
  38.2 4.2 %collective-permute-start.24 = (bf16[128,512]{1,0:T(8,128)(2,1)S(1)}, bf16[128,512]{1,0:T(8,128)(2,1)S(1)}, u32[]{:S(2)}, u32[]{:S(2)}) collective-permute-start(bf16[128,512]{1,0:T(8,128)(2,1)S(1)} %broadcast_select_fusion.refs_3_), channel_id=1, source_target_pairs={{0,1},{1,0},{2,3},{3,2},{4,5},{5,4},{6,7},{7,6},{8,9},{9,8},{10,11... | collective-permute-start | bytes 393224 | tf_op jit(solution)/shard_map/ppermute | solution.py:343
  41.9 1.3 %collective-permute-start.22 = (bf16[128,512]{1,0:T(8,128)(2,1)S(1)}, bf16[128,512]{1,0:T(8,128)(2,1)S(1)}, u32[]{:S(2)}, u32[]{:S(2)}) collective-permute-start(bf16[128,512]{1,0:T(8,128)(2,1)S(1)} %collective-permute-done.20.refs_1_), channel_id=1, source_target_pairs={{0,1},{1,0},{2,3},{3,2},{4,5},{5,4},{6,7},{7,6},{8,9},{9,8},{10,11... | collective-permute-start | bytes 393224 | tf_op jit(solution)/shard_map/ppermute | solution.py:343
  41.9 1.5 %collective-permute-start.23 = (bf16[128,512]{1,0:T(8,128)(2,1)S(1)}, bf16[128,512]{1,0:T(8,128)(2,1)S(1)}, u32[]{:S(2)}, u32[]{:S(2)}) collective-permute-start(bf16[128,512]{1,0:T(8,128)(2,1)S(1)} %collective-permute-done.21.refs_2_), channel_id=1, source_target_pairs={{0,1},{1,0},{2,3},{3,2},{4,5},{5,4},{6,7},{7,6},{8,9},{9,8},{10,11... | collective-permute-start | bytes 393224 | tf_op jit(solution)/shard_map/ppermute | solution.py:343

commit v15 on v12

--- a/solution.py
+++ b/solution.py
@@ -287,11 +287,11 @@
 
 
 def tiles_of(partners, owns, before, hops, blocks, twins, tok_scale, halves, n):
-    tok_rows, width = blocks[0].shape
+    first = before is None
+    tok_rows, width = owns[0].shape
     slots = partners.shape[0]
     rows = width // halves
-    first = before is None
-    dtype = blocks[0].dtype
+    dtype = owns[0].dtype
     out_shape = jax.ShapeDtypeStruct((1, slots, rows, width), dtype)
     left_shape = jax.ShapeDtypeStruct((rows, tok_rows * halves), dtype)
     if first:
@@ -338,11 +338,12 @@
             owns = (acts, acts_twin)
             return tiles_of(by_slot, owns, before, hops, blocks, twins, tok_scale, halves, n)
 
-        def beside_second(ahead, behind):
-            return add_tiles(None, (1, n - 1), (ahead, behind))
+        def beside_second(*_):
+            return add_tiles(None, (), ())
 
         def beside_third(ahead, behind, ahead_2, behind_2, _, before):
-            return add_tiles(before, (2, n - 2), (ahead_2, behind_2))
+            blocks = (ahead, behind, ahead_2, behind_2)
+            return add_tiles(before, (1, n - 1, 2, n - 2), blocks)
 
         out, *late = ring.gather(acts, beside_second, beside_third)
         ahead, behind, corner, middle = late

time: 42.8 us -> 42.4 us (level); the launches traced: 42.6 us -> 42.7 us
    ppermute x2, waiting for transfers between devices: 3.79 us -> 4.99 us  [gather(): corner = lax.ppermute(x, 'lat', self.across)]
    ppermute x7, waiting for transfers between devices: 1.7 us -> 1.03 us  [add_tiles(): twins = [lax.ppermute(block, 'tok', swap) for block in blocks]]
    ppermute x7, starting transfers between devices: 1.04 us -> 1.6 us  [add_tiles(): twins = [lax.ppermute(block, 'tok', swap) for block in blocks]]
  transfers between devices with their start and end apart: 24 -> 24, of which waited for: 13 -> 12; matrix products, arithmetic and copies ran while one was open for 0% -> 0% of each run, Pallas kernels for 11% -> 11%
where the time goes in v15:
time: 42.4 us; the launch traced here: 42.7 us
  starting transfers between devices  22.2 us (52%)
  waiting for transfers between devices  14.1 us (33%)
  Pallas kernels  6.2 us (15%)
    ppermute x2, starting transfers between devices, gather(): corner = lax.ppermute(x, 'lat', self.across)  7.48 us
    ppermute x2, waiting for transfers between devices, gather(): corner = lax.ppermute(x, 'lat', self.across)  4.99 us
    ppermute x2, starting transfers between devices, gather(): ahead = lax.ppermute(x, 'lat', self.forward)  4.19 us
    pallas_call x3, Pallas kernels, tiles_of(): pl.pallas_call(functools.partial(tiles_kernel, tok_scale, n, hops, first)...  3.64 us
    ppermute x2, starting transfers between devices, gather(): behind_2 = lax.ppermute(behind, 'lat', self.backward)  3.51 us
    ppermute x2, waiting for transfers between devices, gather(): ahead_3 = lax.ppermute(ahead_2, 'lat', self.forward)  2.8 us
    ppermute x2, starting transfers between devices, gather(): behind_3 = lax.ppermute(behind_2, 'lat', self.backward)  2.66 us
    pallas_call x1, Pallas kernels, beside_third(): pl.pallas_call(functools.partial(first_step, hops, later), out_shape=(jax...  2.07 us
  transfers between devices with their start and end apart: 24, of which 12 were waited for; matrix products, arithmetic and copies ran while one was open for 0% of the time, Pallas kernels for 11%

profile of v15, /device:TPU:0, one launch (start us, length us, event | category | flops | bytes accessed | tf_op | source)
XLA Modules:
  0.0 42.7 jit_solution(7044216360273677278)
XLA Ops:
  0.0 3.1 %collective-permute-start = (bf16[448,128]{1,0:T(8,128)(2,1)}, bf16[448,128]{1,0:T(8,128)(2,1)S(1)}, u32[]{:S(2)}, u32[]{:S(2)}) collective-permute-start(bf16[448,128]{1,0:T(8,128)(2,1)} %bitcast.5), channel_id=1, source_target_pairs={{0,4},{4,8},{8,12},{12,14},{14,10},{10,6},{6,2},{2,0},{1,5},{5,9},... | collective-permute-start | bytes 344072 | tf_op jit(solution)/shard_map/ppermute | solution.py:100
  3.1 0.0 collective-permute-start.2
  3.1 5.0 %collective-permute-start.4 = (bf16[448,128]{1,0:T(8,128)(2,1)}, bf16[448,128]{1,0:T(8,128)(2,1)S(1)}, u32[]{:S(2)}, u32[]{:S(2)}) collective-permute-start(bf16[448,128]{1,0:T(8,128)(2,1)} %bitcast.7), channel_id=1, source_target_pairs={{0,14},{12,2},{14,0},{2,12},{4,6},{8,10},{10,8},{6,4},{1,15},{13,3... | collective-permute-start | bytes 344072 | tf_op jit(solution)/shard_map/ppermute | solution.py:102
  8.1 0.0 collective-permute-done.refs_0_
  8.1 0.1 collective-permute-start.1
  8.2 1.9 %collective-permute-start.3 = (bf16[448,128]{1,0:T(8,128)(2,1)S(1)}, bf16[448,128]{1,0:T(8,128)(2,1)S(1)}, u32[]{:S(2)}, u32[]{:S(2)}) collective-permute-start(bf16[448,128]{1,0:T(8,128)(2,1)S(1)} %collective-permute-done.2.refs_1_), channel_id=1, source_target_pairs={{4,0},{8,4},{12,8},{14,12},{10,14},{6,10},{2,6},{0,2},{5,1},{9,5},... | collective-permute-start | bytes 344072 | tf_op jit(solution)/shard_map/ppermute | solution.py:104
  10.1 0.1 collective-permute-start.7
  10.2 2.7 %collective-permute-done.4.x_corner = bf16[448,128]{1,0:T(8,128)(2,1)S(1)} collective-permute-done((bf16[448,128]{1,0:T(8,128)(2,1)}, bf16[448,128]{1,0:T(8,128)(2,1)S(1)}, u32[]{:S(2)}, u32[]{:S(2)}) %collective-permute-start.4) | collective-permute-done | bytes 114720 | tf_op jit(solution)/shard_map/ppermute | solution.py:102
  12.9 1.1 %collective-permute-done.1.refs_2_ = bf16[448,128]{1,0:T(8,128)(2,1)S(1)} collective-permute-done((bf16[448,128]{1,0:T(8,128)(2,1)S(1)}, bf16[448,128]{1,0:T(8,128)(2,1)S(1)}, u32[]{:S(2)}, u32[]{:S(2)}) %collective-permute-start.1) | collective-permute-done | bytes 114720 | tf_op jit(solution)/shard_map/ppermute | solution.py:103
  14.0 0.0 collective-permute-done.3.refs_3_
  14.0 1.1 %collective-permute-start.5 = (bf16[448,128]{1,0:T(8,128)(2,1)S(1)}, bf16[448,128]{1,0:T(8,128)(2,1)S(1)}, u32[]{:S(2)}, u32[]{:S(2)}) collective-permute-start(bf16[448,128]{1,0:T(8,128)(2,1)S(1)} %collective-permute-done.1.refs_2_), channel_id=1, source_target_pairs={{0,4},{4,8},{8,12},{12,14},{14,10},{10,6},{6,2},{2,0},{1,5},{5,9},... | collective-permute-start | bytes 344072 | tf_op jit(solution)/shard_map/ppermute | solution.py:111
  15.1 0.9 %collective-permute-start.6 = (bf16[448,128]{1,0:T(8,128)(2,1)S(1)}, bf16[448,128]{1,0:T(8,128)(2,1)S(1)}, u32[]{:S(2)}, u32[]{:S(2)}) collective-permute-start(bf16[448,128]{1,0:T(8,128)(2,1)S(1)} %collective-permute-done.3.refs_3_), channel_id=1, source_target_pairs={{4,0},{8,4},{12,8},{14,12},{10,14},{6,10},{2,6},{0,2},{5,1},{9,5},... | collective-permute-start | bytes 344072 | tf_op jit(solution)/shard_map/ppermute | solution.py:112
  16.0 0.0 collective-permute-done.7.x_middle
  16.0 2.1 %shard_map.55 = (f32[128,512]{1,0:T(8,128)S(1)}, bf16[4,448,512]{2,1,0:T(8,128)(2,1)S(1)}) custom-call(bf16[448,128]{1,0:T(8,128)(2,1)S(1)} %collective-permute-done.refs_0_, bf16[448,128]{1,0:T(8,128)(2,1)S(1)} %collective-permute-done.2.refs_1_, bf16[448,128]{1,0:T(8,128)(2,1)S(1)} %collective-permute-done.1.refs_2_, ...), custom_call_target="tpu_custom_call" | custom-call | flops 234881024 | bytes 2818048 | tf_op jit(solution)/shard_map/pallas_call | solution.py:128
  18.1 0.7 %collective-permute-done.5.x_f = bf16[448,128]{1,0:T(8,128)(2,1)S(1)} collective-permute-done((bf16[448,128]{1,0:T(8,128)(2,1)S(1)}, bf16[448,128]{1,0:T(8,128)(2,1)S(1)}, u32[]{:S(2)}, u32[]{:S(2)}) %collective-permute-start.5) | collective-permute-done | bytes 114720 | tf_op jit(solution)/shard_map/ppermute | solution.py:111
  18.8 1.1 %collective-permute-done.6.x_b = bf16[448,128]{1,0:T(8,128)(2,1)S(1)} collective-permute-done((bf16[448,128]{1,0:T(8,128)(2,1)S(1)}, bf16[448,128]{1,0:T(8,128)(2,1)S(1)}, u32[]{:S(2)}, u32[]{:S(2)}) %collective-permute-start.6) | collective-permute-done | bytes 114720 | tf_op jit(solution)/shard_map/ppermute | solution.py:112
  19.9 0.5 %shard_map.56.refs_0_ = bf16[128,512]{1,0:T(8,128)(2,1)S(1)} custom-call(bf16[448,128]{1,0:T(8,128)(2,1)S(1)} %bitcast.8, bf16[448,128]{1,0:T(8,128)(2,1)S(1)} %collective-permute-done.5.x_f, bf16[448,128]{1,0:T(8,128)(2,1)S(1)} %collective-permute-done.6.x_b, bf16[448,128]{1,0:T(8,128)(2,1)S(1)} %collective-permute-done.4.x_corner, ...), custom_call_target="tpu_custom_call" | custom-call | flops 234881024 | bytes 2818048 | tf_op jit(solution)/shard_map/pallas_call | solution.py:143
  20.4 1.0 %collective-permute-start.10 = (bf16[128,512]{1,0:T(8,128)(2,1)S(1)}, bf16[128,512]{1,0:T(8,128)(2,1)S(1)}, u32[]{:S(2)}, u32[]{:S(2)}) collective-permute-start(bf16[128,512]{1,0:T(8,128)(2,1)S(1)} %shard_map.56.refs_0_), channel_id=1, source_target_pairs={{4,0},{8,4},{12,8},{14,12},{10,14},{6,10},{2,6},{0,2},{5,1},{9,5},... | collective-permute-start | bytes 393224 | tf_op jit(solution)/shard_map/ppermute | solution.py:101
  21.4 1.1 %collective-permute-start.8 = (bf16[128,512]{1,0:T(8,128)(2,1)S(1)}, bf16[128,512]{1,0:T(8,128)(2,1)S(1)}, u32[]{:S(2)}, u32[]{:S(2)}) collective-permute-start(bf16[128,512]{1,0:T(8,128)(2,1)S(1)} %shard_map.56.refs_0_), channel_id=1, source_target_pairs={{0,4},{4,8},{8,12},{12,14},{14,10},{10,6},{6,2},{2,0},{1,5},{5,9},... | collective-permute-start | bytes 393224 | tf_op jit(solution)/shard_map/ppermute | solution.py:100
  22.5 2.5 %collective-permute-start.12 = (bf16[128,512]{1,0:T(8,128)(2,1)S(1)}, bf16[128,512]{1,0:T(8,128)(2,1)S(1)}, u32[]{:S(2)}, u32[]{:S(2)}) collective-permute-start(bf16[128,512]{1,0:T(8,128)(2,1)S(1)} %shard_map.56.refs_0_), channel_id=1, source_target_pairs={{0,14},{12,2},{14,0},{2,12},{4,6},{8,10},{10,8},{6,4},{1,15},{13,3... | collective-permute-start | bytes 393224 | tf_op jit(solution)/shard_map/ppermute | solution.py:102
  25.0 0.4 %collective-permute-done.10.refs_2_ = bf16[128,512]{1,0:T(8,128)(2,1)S(1)} collective-permute-done((bf16[128,512]{1,0:T(8,128)(2,1)S(1)}, bf16[128,512]{1,0:T(8,128)(2,1)S(1)}, u32[]{:S(2)}, u32[]{:S(2)}) %collective-permute-start.10) | collective-permute-done | bytes 131104 | tf_op jit(solution)/shard_map/ppermute | solution.py:101
  25.4 1.6 %collective-permute-start.11 = (bf16[128,512]{1,0:T(8,128)(2,1)S(1)}, bf16[128,512]{1,0:T(8,128)(2,1)S(1)}, u32[]{:S(2)}, u32[]{:S(2)}) collective-permute-start(bf16[128,512]{1,0:T(8,128)(2,1)S(1)} %collective-permute-done.10.refs_2_), channel_id=1, source_target_pairs={{4,0},{8,4},{12,8},{14,12},{10,14},{6,10},{2,6},{0,2},{5,1},{9,5},... | collective-permute-start | bytes 393224 | tf_op jit(solution)/shard_map/ppermute | solution.py:104
  27.0 0.0 collective-permute-done.8.refs_1_
  27.0 0.4 %collective-permute-start.9 = (bf16[128,512]{1,0:T(8,128)(2,1)S(1)}, bf16[128,512]{1,0:T(8,128)(2,1)S(1)}, u32[]{:S(2)}, u32[]{:S(2)}) collective-permute-start(bf16[128,512]{1,0:T(8,128)(2,1)S(1)} %collective-permute-done.8.refs_1_), channel_id=1, source_target_pairs={{0,4},{4,8},{8,12},{12,14},{14,10},{10,6},{6,2},{2,0},{1,5},{5,9},... | collective-permute-start | bytes 393224 | tf_op jit(solution)/shard_map/ppermute | solution.py:103
  27.5 0.1 collective-permute-start.14
  27.6 0.0 collective-permute-done.13.refs_1_
  27.6 0.5 %collective-permute-start.15 = (bf16[128,512]{1,0:T(8,128)(2,1)S(1)}, bf16[128,512]{1,0:T(8,128)(2,1)S(1)}, u32[]{:S(2)}, u32[]{:S(2)}) collective-permute-start(bf16[128,512]{1,0:T(8,128)(2,1)S(1)} %collective-permute-done.8.refs_1_), channel_id=1, source_target_pairs={{0,1},{1,0},{2,3},{3,2},{4,5},{5,4},{6,7},{7,6},{8,9},{9,8},{10,11... | collective-permute-start | bytes 393224 | tf_op jit(solution)/shard_map/ppermute | solution.py:337
  28.1 1.1 %shard_map.57 = (bf16[256,256]{1,0:T(8,128)(2,1)S(1)}, bf16[1,4,256,512]{3,2,1,0:T(8,128)(2,1)}) custom-call(s32[4,8]{1,0:T(4,128)S(1)} %bitcast.9, bf16[128,512]{1,0:T(8,128)(2,1)S(1)} %shard_map.56.refs_0_, bf16[128,512]{1,0:T(8,128)(2,1)S(1)} %collective-permute-done.13.refs_1_), custom_call_target="tpu_custom_call" | custom-call | tf_op jit(solution)/shard_map/pallas_call | solution.py:302
  29.2 2.3 %collective-permute-done.12 = bf16[128,512]{1,0:T(8,128)(2,1)S(1)} collective-permute-done((bf16[128,512]{1,0:T(8,128)(2,1)S(1)}, bf16[128,512]{1,0:T(8,128)(2,1)S(1)}, u32[]{:S(2)}, u32[]{:S(2)}) %collective-permute-start.12) | collective-permute-done | bytes 131104 | tf_op jit(solution)/shard_map/ppermute | solution.py:102
  31.5 0.0 collective-permute-start.16
  31.5 1.9 %collective-permute-done.11.refs_4_ = bf16[128,512]{1,0:T(8,128)(2,1)S(1)} collective-permute-done((bf16[128,512]{1,0:T(8,128)(2,1)S(1)}, bf16[128,512]{1,0:T(8,128)(2,1)S(1)}, u32[]{:S(2)}, u32[]{:S(2)}) %collective-permute-start.11) | collective-permute-done | bytes 131104 | tf_op jit(solution)/shard_map/ppermute | solution.py:104
  33.4 0.6 %collective-permute-done.9.refs_3_ = bf16[128,512]{1,0:T(8,128)(2,1)S(1)} collective-permute-done((bf16[128,512]{1,0:T(8,128)(2,1)S(1)}, bf16[128,512]{1,0:T(8,128)(2,1)S(1)}, u32[]{:S(2)}, u32[]{:S(2)}) %collective-permute-start.9) | collective-permute-done | bytes 131104 | tf_op jit(solution)/shard_map/ppermute | solution.py:103
  34.1 0.0 collective-permute-start.17
  34.1 0.0 collective-permute-start.19
  34.1 0.5 %collective-permute-start.18 = (bf16[128,512]{1,0:T(8,128)(2,1)S(1)}, bf16[128,512]{1,0:T(8,128)(2,1)S(1)}, u32[]{:S(2)}, u32[]{:S(2)}) collective-permute-start(bf16[128,512]{1,0:T(8,128)(2,1)S(1)} %collective-permute-done.11.refs_4_), channel_id=1, source_target_pairs={{0,1},{1,0},{2,3},{3,2},{4,5},{5,4},{6,7},{7,6},{8,9},{9,8},{10,11... | collective-permute-start | bytes 393224 | tf_op jit(solution)/shard_map/ppermute | solution.py:337
  34.6 1.7 %collective-permute-start.20 = (bf16[128,512]{1,0:T(8,128)(2,1)S(1)}, bf16[128,512]{1,0:T(8,128)(2,1)S(1)}, u32[]{:S(2)}, u32[]{:S(2)}) collective-permute-start(bf16[128,512]{1,0:T(8,128)(2,1)S(1)} %collective-permute-done.11.refs_4_), channel_id=1, source_target_pairs={{4,0},{8,4},{12,8},{14,12},{10,14},{6,10},{2,6},{0,2},{5,1},{9,5},... | collective-permute-start | bytes 393224 | tf_op jit(solution)/shard_map/ppermute | solution.py:112
  36.3 0.0 collective-permute-done.16.refs_6_
  36.4 0.1 collective-permute-start.23
  36.4 0.0 collective-permute-done.18.refs_8_
  36.5 1.4 %shard_map.58.refs_7_ = bf16[1,4,256,512]{3,2,1,0:T(8,128)(2,1)} custom-call(s32[4,8]{1,0:T(4,128)S(1)} %bitcast.10, bf16[256,256]{1,0:T(8,128)(2,1)S(1)} %get-tuple-element.37.refs_0_, bf16[128,512]{1,0:T(8,128)(2,1)S(1)} %collective-permute-done.8.refs_1_, bf16[128,512]{1,0:T(8,128)(2,1)S(1)} %collective-permute-done.10.refs_2_, ...), custom_call_target="tpu_custom_call", output_to_operand_aliasing={{}: (10, {})} | custom-call | flops 268435456 | bytes 2097152 | tf_op jit(solution)/shard_map/pallas_call | solution.py:302
  37.9 2.1 %collective-permute-done.19.refs_1_ = bf16[128,512]{1,0:T(8,128)(2,1)S(1)} collective-permute-done((bf16[128,512]{1,0:T(8,128)(2,1)S(1)}, bf16[128,512]{1,0:T(8,128)(2,1)S(1)}, u32[]{:S(2)}, u32[]{:S(2)}) %collective-permute-start.19) | collective-permute-done | bytes 131104 | tf_op jit(solution)/shard_map/ppermute | solution.py:111
  40.0 0.1 collective-permute-done.20.refs_2_
  40.1 0.0 collective-permute-start.21
  40.1 0.5 %collective-permute-start.22 = (bf16[128,512]{1,0:T(8,128)(2,1)S(1)}, bf16[128,512]{1,0:T(8,128)(2,1)S(1)}, u32[]{:S(2)}, u32[]{:S(2)}) collective-permute-start(bf16[128,512]{1,0:T(8,128)(2,1)S(1)} %collective-permute-done.20.refs_2_), channel_id=1, source_target_pairs={{0,1},{1,0},{2,3},{3,2},{4,5},{5,4},{6,7},{7,6},{8,9},{9,8},{10,11... | collective-permute-start | bytes 393224 | tf_op jit(solution)/shard_map/ppermute | solution.py:337
  40.6 0.0 collective-permute-done.23.refs_6_
  40.6 0.8 %collective-permute-done.21.refs_4_ = bf16[128,512]{1,0:T(8,128)(2,1)S(1)} collective-permute-done((bf16[128,512]{1,0:T(8,128)(2,1)S(1)}, bf16[128,512]{1,0:T(8,128)(2,1)S(1)}, u32[]{:S(2)}, u32[]{:S(2)}) %collective-permute-start.21) | collective-permute-done | bytes 131104 | tf_op jit(solution)/shard_map/ppermute | solution.py:337
  41.4 0.2 collective-permute-done.22.refs_5_
  41.6 1.1 %shard_map.59 = bf16[1,4,256,512]{3,2,1,0:T(8,128)(2,1)} custom-call(s32[4,8]{1,0:T(4,128)S(1)} %bitcast.11, bf16[256,256]{1,0:T(8,128)(2,1)S(1)} %get-tuple-element.37.refs_0_, bf16[128,512]{1,0:T(8,128)(2,1)S(1)} %collective-permute-done.19.refs_1_, bf16[128,512]{1,0:T(8,128)(2,1)S(1)} %collective-permute-done.20.refs_2_, ...), custom_call_target="tpu_custom_call", output_to_operand_aliasing={{}: (8, {})} | custom-call | flops 201326592 | bytes 1572864 | tf_op jit(solution)/shard_map/pallas_call | solution.py:302
  (16 shorter events, 0.1 us)
Async XLA Ops:
  0.0 19.9 %copy-start = (bf16[128,448]{0,1:T(8,128)(2,1)S(1)}, bf16[128,448]{0,1:T(8,128)(2,1)}, u32[]{:S(2)}) copy-start(bf16[128,448]{0,1:T(8,128)(2,1)} %param.5) | copy-start | bytes 344068
  0.0 19.9 %copy-start.2 = (f32[512]{0:T(512)S(1)}, f32[512]{0:T(512)}, u32[]{:S(2)}) copy-start(f32[512]{0:T(512)} %param.7) | copy-start | bytes 6148
  0.0 19.9 %copy-start.3 = (f32[512]{0:T(512)S(1)}, f32[512]{0:T(512)}, u32[]{:S(2)}) copy-start(f32[512]{0:T(512)} %param.8) | copy-start | bytes 6148
  0.0 8.1 %collective-permute-start = (bf16[448,128]{1,0:T(8,128)(2,1)}, bf16[448,128]{1,0:T(8,128)(2,1)S(1)}, u32[]{:S(2)}, u32[]{:S(2)}) collective-permute-start(bf16[448,128]{1,0:T(8,128)(2,1)} %bitcast.5), channel_id=1, source_target_pairs={{0,4},{4,8},{8,12},{12,14},{14,10},{10,6},{6,2},{2,0},{1,5},{5,9},... | collective-permute-start | bytes 344072 | tf_op jit(solution)/shard_map/ppermute | solution.py:100
  3.1 5.1 %collective-permute-start.2 = (bf16[448,128]{1,0:T(8,128)(2,1)}, bf16[448,128]{1,0:T(8,128)(2,1)S(1)}, u32[]{:S(2)}, u32[]{:S(2)}) collective-permute-start(bf16[448,128]{1,0:T(8,128)(2,1)} %bitcast.6), channel_id=1, source_target_pairs={{4,0},{8,4},{12,8},{14,12},{10,14},{6,10},{2,6},{0,2},{5,1},{9,5},... | collective-permute-start | bytes 344072 | tf_op jit(solution)/shard_map/ppermute | solution.py:101
  3.1 9.8 %collective-permute-start.4 = (bf16[448,128]{1,0:T(8,128)(2,1)}, bf16[448,128]{1,0:T(8,128)(2,1)S(1)}, u32[]{:S(2)}, u32[]{:S(2)}) collective-permute-start(bf16[448,128]{1,0:T(8,128)(2,1)} %bitcast.7), channel_id=1, source_target_pairs={{0,14},{12,2},{14,0},{2,12},{4,6},{8,10},{10,8},{6,4},{1,15},{13,3... | collective-permute-start | bytes 344072 | tf_op jit(solution)/shard_map/ppermute | solution.py:102
  8.1 5.9 %collective-permute-start.1 = (bf16[448,128]{1,0:T(8,128)(2,1)S(1)}, bf16[448,128]{1,0:T(8,128)(2,1)S(1)}, u32[]{:S(2)}, u32[]{:S(2)}) collective-permute-start(bf16[448,128]{1,0:T(8,128)(2,1)S(1)} %collective-permute-done.refs_0_), channel_id=1, source_target_pairs={{0,4},{4,8},{8,12},{12,14},{14,10},{10,6},{6,2},{2,0},{1,5},{5,9},... | collective-permute-start | bytes 344072 | tf_op jit(solution)/shard_map/ppermute | solution.py:103
  8.2 5.8 %collective-permute-start.3 = (bf16[448,128]{1,0:T(8,128)(2,1)S(1)}, bf16[448,128]{1,0:T(8,128)(2,1)S(1)}, u32[]{:S(2)}, u32[]{:S(2)}) collective-permute-start(bf16[448,128]{1,0:T(8,128)(2,1)S(1)} %collective-permute-done.2.refs_1_), channel_id=1, source_target_pairs={{4,0},{8,4},{12,8},{14,12},{10,14},{6,10},{2,6},{0,2},{5,1},{9,5},... | collective-permute-start | bytes 344072 | tf_op jit(solution)/shard_map/ppermute | solution.py:104
  10.1 5.9 %collective-permute-start.7 = (bf16[448,128]{1,0:T(8,128)(2,1)S(1)}, bf16[448,128]{1,0:T(8,128)(2,1)S(1)}, u32[]{:S(2)}, u32[]{:S(2)}) collective-permute-start(bf16[448,128]{1,0:T(8,128)(2,1)S(1)} %broadcast_select_fusion.2), channel_id=1, source_target_pairs={{4,6},{5,7},{8,10},{9,11},{10,8},{11,9},{6,4},{7,5},{0,1},{1,0},{1... | collective-permute-start | bytes 344072 | tf_op jit(solution)/shard_map/ppermute | solution.py:106
  14.0 4.8 %collective-permute-start.5 = (bf16[448,128]{1,0:T(8,128)(2,1)S(1)}, bf16[448,128]{1,0:T(8,128)(2,1)S(1)}, u32[]{:S(2)}, u32[]{:S(2)}) collective-permute-start(bf16[448,128]{1,0:T(8,128)(2,1)S(1)} %collective-permute-done.1.refs_2_), channel_id=1, source_target_pairs={{0,4},{4,8},{8,12},{12,14},{14,10},{10,6},{6,2},{2,0},{1,5},{5,9},... | collective-permute-start | bytes 344072 | tf_op jit(solution)/shard_map/ppermute | solution.py:111
  15.1 4.8 %collective-permute-start.6 = (bf16[448,128]{1,0:T(8,128)(2,1)S(1)}, bf16[448,128]{1,0:T(8,128)(2,1)S(1)}, u32[]{:S(2)}, u32[]{:S(2)}) collective-permute-start(bf16[448,128]{1,0:T(8,128)(2,1)S(1)} %collective-permute-done.3.refs_3_), channel_id=1, source_target_pairs={{4,0},{8,4},{12,8},{14,12},{10,14},{6,10},{2,6},{0,2},{5,1},{9,5},... | collective-permute-start | bytes 344072 | tf_op jit(solution)/shard_map/ppermute | solution.py:112
  16.0 12.0 %copy-start.1 = (s32[8,4]{0,1:T(4,128)S(1)}, s32[8,4]{0,1:T(4,128)}, u32[]{:S(2)}) copy-start(s32[8,4]{0,1:T(4,128)} %param.9) | copy-start | bytes 388
  20.4 5.0 %collective-permute-start.10 = (bf16[128,512]{1,0:T(8,128)(2,1)S(1)}, bf16[128,512]{1,0:T(8,128)(2,1)S(1)}, u32[]{:S(2)}, u32[]{:S(2)}) collective-permute-start(bf16[128,512]{1,0:T(8,128)(2,1)S(1)} %shard_map.56.refs_0_), channel_id=1, source_target_pairs={{4,0},{8,4},{12,8},{14,12},{10,14},{6,10},{2,6},{0,2},{5,1},{9,5},... | collective-permute-start | bytes 393224 | tf_op jit(solution)/shard_map/ppermute | solution.py:101
  21.4 5.6 %collective-permute-start.8 = (bf16[128,512]{1,0:T(8,128)(2,1)S(1)}, bf16[128,512]{1,0:T(8,128)(2,1)S(1)}, u32[]{:S(2)}, u32[]{:S(2)}) collective-permute-start(bf16[128,512]{1,0:T(8,128)(2,1)S(1)} %shard_map.56.refs_0_), channel_id=1, source_target_pairs={{0,4},{4,8},{8,12},{12,14},{14,10},{10,6},{6,2},{2,0},{1,5},{5,9},... | collective-permute-start | bytes 393224 | tf_op jit(solution)/shard_map/ppermute | solution.py:100
  22.5 5.1 %collective-permute-start.13 = (bf16[128,512]{1,0:T(8,128)(2,1)S(1)}, bf16[128,512]{1,0:T(8,128)(2,1)S(1)}, u32[]{:S(2)}, u32[]{:S(2)}) collective-permute-start(bf16[128,512]{1,0:T(8,128)(2,1)S(1)} %shard_map.56.refs_0_), channel_id=1, source_target_pairs={{0,1},{1,0},{2,3},{3,2},{4,5},{5,4},{6,7},{7,6},{8,9},{9,8},{10,11... | collective-permute-start | bytes 393224 | tf_op jit(solution)/shard_map/ppermute | solution.py:334
  22.5 9.0 %collective-permute-start.12 = (bf16[128,512]{1,0:T(8,128)(2,1)S(1)}, bf16[128,512]{1,0:T(8,128)(2,1)S(1)}, u32[]{:S(2)}, u32[]{:S(2)}) collective-permute-start(bf16[128,512]{1,0:T(8,128)(2,1)S(1)} %shard_map.56.refs_0_), channel_id=1, source_target_pairs={{0,14},{12,2},{14,0},{2,12},{4,6},{8,10},{10,8},{6,4},{1,15},{13,3... | collective-permute-start | bytes 393224 | tf_op jit(solution)/shard_map/ppermute | solution.py:102
  25.4 8.0 %collective-permute-start.11 = (bf16[128,512]{1,0:T(8,128)(2,1)S(1)}, bf16[128,512]{1,0:T(8,128)(2,1)S(1)}, u32[]{:S(2)}, u32[]{:S(2)}) collective-permute-start(bf16[128,512]{1,0:T(8,128)(2,1)S(1)} %collective-permute-done.10.refs_2_), channel_id=1, source_target_pairs={{4,0},{8,4},{12,8},{14,12},{10,14},{6,10},{2,6},{0,2},{5,1},{9,5},... | collective-permute-start | bytes 393224 | tf_op jit(solution)/shard_map/ppermute | solution.py:104
  27.0 7.0 %collective-permute-start.9 = (bf16[128,512]{1,0:T(8,128)(2,1)S(1)}, bf16[128,512]{1,0:T(8,128)(2,1)S(1)}, u32[]{:S(2)}, u32[]{:S(2)}) collective-permute-start(bf16[128,512]{1,0:T(8,128)(2,1)S(1)} %collective-permute-done.8.refs_1_), channel_id=1, source_target_pairs={{0,4},{4,8},{8,12},{12,14},{14,10},{10,6},{6,2},{2,0},{1,5},{5,9},... | collective-permute-start | bytes 393224 | tf_op jit(solution)/shard_map/ppermute | solution.py:103
  27.5 6.6 %collective-permute-start.14 = (bf16[128,512]{1,0:T(8,128)(2,1)S(1)}, bf16[128,512]{1,0:T(8,128)(2,1)S(1)}, u32[]{:S(2)}, u32[]{:S(2)}) collective-permute-start(bf16[128,512]{1,0:T(8,128)(2,1)S(1)} %broadcast_select_fusion.1), channel_id=1, source_target_pairs={{4,6},{5,7},{8,10},{9,11},{10,8},{11,9},{6,4},{7,5},{0,1},{1,0},{1... | collective-permute-start | bytes 393224 | tf_op jit(solution)/shard_map/ppermute | solution.py:106
  27.6 7.0 %collective-permute-start.15 = (bf16[128,512]{1,0:T(8,128)(2,1)S(1)}, bf16[128,512]{1,0:T(8,128)(2,1)S(1)}, u32[]{:S(2)}, u32[]{:S(2)}) collective-permute-start(bf16[128,512]{1,0:T(8,128)(2,1)S(1)} %collective-permute-done.8.refs_1_), channel_id=1, source_target_pairs={{0,1},{1,0},{2,3},{3,2},{4,5},{5,4},{6,7},{7,6},{8,9},{9,8},{10,11... | collective-permute-start | bytes 393224 | tf_op jit(solution)/shard_map/ppermute | solution.py:337
  31.5 4.8 %collective-permute-start.16 = (bf16[128,512]{1,0:T(8,128)(2,1)S(1)}, bf16[128,512]{1,0:T(8,128)(2,1)S(1)}, u32[]{:S(2)}, u32[]{:S(2)}) collective-permute-start(bf16[128,512]{1,0:T(8,128)(2,1)S(1)} %collective-permute-done.10.refs_2_), channel_id=1, source_target_pairs={{0,1},{1,0},{2,3},{3,2},{4,5},{5,4},{6,7},{7,6},{8,9},{9,8},{10,11... | collective-permute-start | bytes 393224 | tf_op jit(solution)/shard_map/ppermute | solution.py:337
  34.1 2.4 %collective-permute-start.17 = (bf16[128,512]{1,0:T(8,128)(2,1)S(1)}, bf16[128,512]{1,0:T(8,128)(2,1)S(1)}, u32[]{:S(2)}, u32[]{:S(2)}) collective-permute-start(bf16[128,512]{1,0:T(8,128)(2,1)S(1)} %collective-permute-done.9.refs_3_), channel_id=1, source_target_pairs={{0,1},{1,0},{2,3},{3,2},{4,5},{5,4},{6,7},{7,6},{8,9},{9,8},{10,11... | collective-permute-start | bytes 393224 | tf_op jit(solution)/shard_map/ppermute | solution.py:337
  34.1 5.9 %collective-permute-start.19 = (bf16[128,512]{1,0:T(8,128)(2,1)S(1)}, bf16[128,512]{1,0:T(8,128)(2,1)S(1)}, u32[]{:S(2)}, u32[]{:S(2)}) collective-permute-start(bf16[128,512]{1,0:T(8,128)(2,1)S(1)} %collective-permute-done.9.refs_3_), channel_id=1, source_target_pairs={{0,4},{4,8},{8,12},{12,14},{14,10},{10,6},{6,2},{2,0},{1,5},{5,9},... | collective-permute-start | bytes 393224 | tf_op jit(solution)/shard_map/ppermute | solution.py:111
  34.1 2.4 %collective-permute-start.18 = (bf16[128,512]{1,0:T(8,128)(2,1)S(1)}, bf16[128,512]{1,0:T(8,128)(2,1)S(1)}, u32[]{:S(2)}, u32[]{:S(2)}) collective-permute-start(bf16[128,512]{1,0:T(8,128)(2,1)S(1)} %collective-permute-done.11.refs_4_), channel_id=1, source_target_pairs={{0,1},{1,0},{2,3},{3,2},{4,5},{5,4},{6,7},{7,6},{8,9},{9,8},{10,11... | collective-permute-start | bytes 393224 | tf_op jit(solution)/shard_map/ppermute | solution.py:337
  34.6 5.5 %collective-permute-start.20 = (bf16[128,512]{1,0:T(8,128)(2,1)S(1)}, bf16[128,512]{1,0:T(8,128)(2,1)S(1)}, u32[]{:S(2)}, u32[]{:S(2)}) collective-permute-start(bf16[128,512]{1,0:T(8,128)(2,1)S(1)} %collective-permute-done.11.refs_4_), channel_id=1, source_target_pairs={{4,0},{8,4},{12,8},{14,12},{10,14},{6,10},{2,6},{0,2},{5,1},{9,5},... | collective-permute-start | bytes 393224 | tf_op jit(solution)/shard_map/ppermute | solution.py:112
  36.4 4.2 %collective-permute-start.23 = (bf16[128,512]{1,0:T(8,128)(2,1)S(1)}, bf16[128,512]{1,0:T(8,128)(2,1)S(1)}, u32[]{:S(2)}, u32[]{:S(2)}) collective-permute-start(bf16[128,512]{1,0:T(8,128)(2,1)S(1)} %broadcast_select_fusion.refs_3_), channel_id=1, source_target_pairs={{0,1},{1,0},{2,3},{3,2},{4,5},{5,4},{6,7},{7,6},{8,9},{9,8},{10,11... | collective-permute-start | bytes 393224 | tf_op jit(solution)/shard_map/ppermute | solution.py:337
  40.1 1.3 %collective-permute-start.21 = (bf16[128,512]{1,0:T(8,128)(2,1)S(1)}, bf16[128,512]{1,0:T(8,128)(2,1)S(1)}, u32[]{:S(2)}, u32[]{:S(2)}) collective-permute-start(bf16[128,512]{1,0:T(8,128)(2,1)S(1)} %collective-permute-done.19.refs_1_), channel_id=1, source_target_pairs={{0,1},{1,0},{2,3},{3,2},{4,5},{5,4},{6,7},{7,6},{8,9},{9,8},{10,11... | collective-permute-start | bytes 393224 | tf_op jit(solution)/shard_map/ppermute | solution.py:337
  40.1 1.5 %collective-permute-start.22 = (bf16[128,512]{1,0:T(8,128)(2,1)S(1)}, bf16[128,512]{1,0:T(8,128)(2,1)S(1)}, u32[]{:S(2)}, u32[]{:S(2)}) collective-permute-start(bf16[128,512]{1,0:T(8,128)(2,1)S(1)} %collective-permute-done.20.refs_2_), channel_id=1, source_target_pairs={{0,1},{1,0},{2,3},{3,2},{4,5},{5,4},{6,7},{7,6},{8,9},{9,8},{10,11... | collective-permute-start | bytes 393224 | tf_op jit(solution)/shard_map/ppermute | solution.py:337

commit v16 on v15

--- a/solution.py
+++ b/solution.py
@@ -348,8 +348,9 @@
         out, *late = ring.gather(acts, beside_second, beside_third)
         ahead, behind, corner, middle = late
         far = jnp.where(on_corner(n), corner, middle)
-        out, ahead, behind = lax.optimization_barrier((out, ahead, behind))
-        return add_tiles(out, (3, n - 3, n // 2), (ahead, behind, far))[1]
+        out, ahead = lax.optimization_barrier((out, ahead))
+        out = add_tiles(out, (3, n // 2), (ahead, far))
+        return add_tiles(out, (n - 3,), (behind,))[1]
     acts = encode_gathered(residual, enc_weight, enc_bias, threshold)
     acts_twin = lax.ppermute(acts, "tok", swap)
     slices = lax.all_to_all(acts.reshape(n, tok_rows // n, width), "lat", 0, 0)

time: 42.4 us -> 42.3 us (level); the launches traced: 42.7 us -> 41.7 us
  Pallas kernels: 6.2 us -> 4.62 us
  waiting for transfers between devices: 14.1 us -> 14.8 us
    pallas_call x3 -> x4, Pallas kernels: 3.64 us -> 2.06 us  [tiles_of(): pl.pallas_call(functools.partial(tiles_kernel, tok_scale, n, hops, first)...]
    ppermute x2, waiting for transfers between devices: 2.8 us -> 3.91 us  [gather(): ahead_3 = lax.ppermute(ahead_2, 'lat', self.forward)]
  transfers between devices with their start and end apart: 24 -> 24, of which waited for: 12 -> 11; matrix products, arithmetic and copies ran while one was open for 0% -> 0% of each run, Pallas kernels for 11% -> 9%
where the time goes in v16:
time: 42.3 us; the launch traced here: 41.7 us
  starting transfers between devices  22.1 us (52%)
  waiting for transfers between devices  14.8 us (35%)
  Pallas kernels  4.62 us (11%)
    ppermute x2, starting transfers between devices, gather(): corner = lax.ppermute(x, 'lat', self.across)  7.48 us
    ppermute x2, waiting for transfers between devices, gather(): corner = lax.ppermute(x, 'lat', self.across)  4.74 us
    ppermute x2, starting transfers between devices, gather(): ahead = lax.ppermute(x, 'lat', self.forward)  4.19 us
    ppermute x2, waiting for transfers between devices, gather(): ahead_3 = lax.ppermute(ahead_2, 'lat', self.forward)  3.91 us
    ppermute x2, starting transfers between devices, gather(): behind_2 = lax.ppermute(behind, 'lat', self.backward)  3.51 us
    ppermute x2, starting transfers between devices, gather(): behind_3 = lax.ppermute(behind_2, 'lat', self.backward)  2.66 us
    pallas_call x1, Pallas kernels, beside_third(): pl.pallas_call(functools.partial(first_step, hops, later), out_shape=(jax...  2.07 us
    pallas_call x4, Pallas kernels, tiles_of(): pl.pallas_call(functools.partial(tiles_kernel, tok_scale, n, hops, first)...  2.06 us
  transfers between devices with their start and end apart: 24, of which 11 were waited for; matrix products, arithmetic and copies ran while one was open for 0% of the time, Pallas kernels for 9%

profile of v16, /device:TPU:0, one launch (start us, length us, event | category | flops | bytes accessed | tf_op | source)
XLA Modules:
  0.0 41.7 jit_solution(11475931898489655243)
XLA Ops:
  0.0 3.1 %collective-permute-start = (bf16[448,128]{1,0:T(8,128)(2,1)}, bf16[448,128]{1,0:T(8,128)(2,1)S(1)}, u32[]{:S(2)}, u32[]{:S(2)}) collective-permute-start(bf16[448,128]{1,0:T(8,128)(2,1)} %bitcast.5), channel_id=1, source_target_pairs={{0,4},{4,8},{8,12},{12,14},{14,10},{10,6},{6,2},{2,0},{1,5},{5,9},... | collective-permute-start | bytes 344072 | tf_op jit(solution)/shard_map/ppermute | solution.py:100
  3.1 0.0 collective-permute-start.2
  3.1 5.0 %collective-permute-start.4 = (bf16[448,128]{1,0:T(8,128)(2,1)}, bf16[448,128]{1,0:T(8,128)(2,1)S(1)}, u32[]{:S(2)}, u32[]{:S(2)}) collective-permute-start(bf16[448,128]{1,0:T(8,128)(2,1)} %bitcast.7), channel_id=1, source_target_pairs={{0,14},{12,2},{14,0},{2,12},{4,6},{8,10},{10,8},{6,4},{1,15},{13,3... | collective-permute-start | bytes 344072 | tf_op jit(solution)/shard_map/ppermute | solution.py:102
  8.1 0.0 collective-permute-done.refs_0_
  8.1 0.1 collective-permute-start.1
  8.2 1.9 %collective-permute-start.3 = (bf16[448,128]{1,0:T(8,128)(2,1)S(1)}, bf16[448,128]{1,0:T(8,128)(2,1)S(1)}, u32[]{:S(2)}, u32[]{:S(2)}) collective-permute-start(bf16[448,128]{1,0:T(8,128)(2,1)S(1)} %collective-permute-done.2.refs_1_), channel_id=1, source_target_pairs={{4,0},{8,4},{12,8},{14,12},{10,14},{6,10},{2,6},{0,2},{5,1},{9,5},... | collective-permute-start | bytes 344072 | tf_op jit(solution)/shard_map/ppermute | solution.py:104
  10.1 0.1 collective-permute-start.7
  10.2 2.7 %collective-permute-done.4.x_corner = bf16[448,128]{1,0:T(8,128)(2,1)S(1)} collective-permute-done((bf16[448,128]{1,0:T(8,128)(2,1)}, bf16[448,128]{1,0:T(8,128)(2,1)S(1)}, u32[]{:S(2)}, u32[]{:S(2)}) %collective-permute-start.4) | collective-permute-done | bytes 114720 | tf_op jit(solution)/shard_map/ppermute | solution.py:102
  12.9 1.1 %collective-permute-done.1.refs_2_ = bf16[448,128]{1,0:T(8,128)(2,1)S(1)} collective-permute-done((bf16[448,128]{1,0:T(8,128)(2,1)S(1)}, bf16[448,128]{1,0:T(8,128)(2,1)S(1)}, u32[]{:S(2)}, u32[]{:S(2)}) %collective-permute-start.1) | collective-permute-done | bytes 114720 | tf_op jit(solution)/shard_map/ppermute | solution.py:103
  14.0 0.0 collective-permute-done.3.refs_3_
  14.0 1.1 %collective-permute-start.5 = (bf16[448,128]{1,0:T(8,128)(2,1)S(1)}, bf16[448,128]{1,0:T(8,128)(2,1)S(1)}, u32[]{:S(2)}, u32[]{:S(2)}) collective-permute-start(bf16[448,128]{1,0:T(8,128)(2,1)S(1)} %collective-permute-done.1.refs_2_), channel_id=1, source_target_pairs={{0,4},{4,8},{8,12},{12,14},{14,10},{10,6},{6,2},{2,0},{1,5},{5,9},... | collective-permute-start | bytes 344072 | tf_op jit(solution)/shard_map/ppermute | solution.py:111
  15.1 0.9 %collective-permute-start.6 = (bf16[448,128]{1,0:T(8,128)(2,1)S(1)}, bf16[448,128]{1,0:T(8,128)(2,1)S(1)}, u32[]{:S(2)}, u32[]{:S(2)}) collective-permute-start(bf16[448,128]{1,0:T(8,128)(2,1)S(1)} %collective-permute-done.3.refs_3_), channel_id=1, source_target_pairs={{4,0},{8,4},{12,8},{14,12},{10,14},{6,10},{2,6},{0,2},{5,1},{9,5},... | collective-permute-start | bytes 344072 | tf_op jit(solution)/shard_map/ppermute | solution.py:112
  16.0 2.1 %shard_map.55 = (f32[128,512]{1,0:T(8,128)S(1)}, bf16[4,448,512]{2,1,0:T(8,128)(2,1)S(1)}) custom-call(bf16[448,128]{1,0:T(8,128)(2,1)S(1)} %collective-permute-done.refs_0_, bf16[448,128]{1,0:T(8,128)(2,1)S(1)} %collective-permute-done.2.refs_1_, bf16[448,128]{1,0:T(8,128)(2,1)S(1)} %collective-permute-done.1.refs_2_, ...), custom_call_target="tpu_custom_call" | custom-call | flops 234881024 | bytes 2818048 | tf_op jit(solution)/shard_map/pallas_call | solution.py:128
  18.1 0.7 %collective-permute-done.5.x_f = bf16[448,128]{1,0:T(8,128)(2,1)S(1)} collective-permute-done((bf16[448,128]{1,0:T(8,128)(2,1)S(1)}, bf16[448,128]{1,0:T(8,128)(2,1)S(1)}, u32[]{:S(2)}, u32[]{:S(2)}) %collective-permute-start.5) | collective-permute-done | bytes 114720 | tf_op jit(solution)/shard_map/ppermute | solution.py:111
  18.8 1.1 %collective-permute-done.6.x_b = bf16[448,128]{1,0:T(8,128)(2,1)S(1)} collective-permute-done((bf16[448,128]{1,0:T(8,128)(2,1)S(1)}, bf16[448,128]{1,0:T(8,128)(2,1)S(1)}, u32[]{:S(2)}, u32[]{:S(2)}) %collective-permute-start.6) | collective-permute-done | bytes 114720 | tf_op jit(solution)/shard_map/ppermute | solution.py:112
  19.9 0.5 %shard_map.56.refs_0_ = bf16[128,512]{1,0:T(8,128)(2,1)S(1)} custom-call(bf16[448,128]{1,0:T(8,128)(2,1)S(1)} %bitcast.8, bf16[448,128]{1,0:T(8,128)(2,1)S(1)} %collective-permute-done.5.x_f, bf16[448,128]{1,0:T(8,128)(2,1)S(1)} %collective-permute-done.6.x_b, bf16[448,128]{1,0:T(8,128)(2,1)S(1)} %collective-permute-done.4.x_corner, ...), custom_call_target="tpu_custom_call" | custom-call | flops 234881024 | bytes 2818048 | tf_op jit(solution)/shard_map/pallas_call | solution.py:143
  20.4 1.0 %collective-permute-start.10 = (bf16[128,512]{1,0:T(8,128)(2,1)S(1)}, bf16[128,512]{1,0:T(8,128)(2,1)S(1)}, u32[]{:S(2)}, u32[]{:S(2)}) collective-permute-start(bf16[128,512]{1,0:T(8,128)(2,1)S(1)} %shard_map.56.refs_0_), channel_id=1, source_target_pairs={{4,0},{8,4},{12,8},{14,12},{10,14},{6,10},{2,6},{0,2},{5,1},{9,5},... | collective-permute-start | bytes 393224 | tf_op jit(solution)/shard_map/ppermute | solution.py:101
  21.4 1.1 %collective-permute-start.8 = (bf16[128,512]{1,0:T(8,128)(2,1)S(1)}, bf16[128,512]{1,0:T(8,128)(2,1)S(1)}, u32[]{:S(2)}, u32[]{:S(2)}) collective-permute-start(bf16[128,512]{1,0:T(8,128)(2,1)S(1)} %shard_map.56.refs_0_), channel_id=1, source_target_pairs={{0,4},{4,8},{8,12},{12,14},{14,10},{10,6},{6,2},{2,0},{1,5},{5,9},... | collective-permute-start | bytes 393224 | tf_op jit(solution)/shard_map/ppermute | solution.py:100
  22.5 0.0 collective-permute-start.13
  22.5 2.5 %collective-permute-start.12 = (bf16[128,512]{1,0:T(8,128)(2,1)S(1)}, bf16[128,512]{1,0:T(8,128)(2,1)S(1)}, u32[]{:S(2)}, u32[]{:S(2)}) collective-permute-start(bf16[128,512]{1,0:T(8,128)(2,1)S(1)} %shard_map.56.refs_0_), channel_id=1, source_target_pairs={{0,14},{12,2},{14,0},{2,12},{4,6},{8,10},{10,8},{6,4},{1,15},{13,3... | collective-permute-start | bytes 393224 | tf_op jit(solution)/shard_map/ppermute | solution.py:102
  25.0 0.4 %collective-permute-done.10.refs_2_ = bf16[128,512]{1,0:T(8,128)(2,1)S(1)} collective-permute-done((bf16[128,512]{1,0:T(8,128)(2,1)S(1)}, bf16[128,512]{1,0:T(8,128)(2,1)S(1)}, u32[]{:S(2)}, u32[]{:S(2)}) %collective-permute-start.10) | collective-permute-done | bytes 131104 | tf_op jit(solution)/shard_map/ppermute | solution.py:101
  25.4 1.6 %collective-permute-start.11 = (bf16[128,512]{1,0:T(8,128)(2,1)S(1)}, bf16[128,512]{1,0:T(8,128)(2,1)S(1)}, u32[]{:S(2)}, u32[]{:S(2)}) collective-permute-start(bf16[128,512]{1,0:T(8,128)(2,1)S(1)} %collective-permute-done.10.refs_2_), channel_id=1, source_target_pairs={{4,0},{8,4},{12,8},{14,12},{10,14},{6,10},{2,6},{0,2},{5,1},{9,5},... | collective-permute-start | bytes 393224 | tf_op jit(solution)/shard_map/ppermute | solution.py:104
  27.0 0.4 %collective-permute-start.9 = (bf16[128,512]{1,0:T(8,128)(2,1)S(1)}, bf16[128,512]{1,0:T(8,128)(2,1)S(1)}, u32[]{:S(2)}, u32[]{:S(2)}) collective-permute-start(bf16[128,512]{1,0:T(8,128)(2,1)S(1)} %collective-permute-done.8.refs_1_), channel_id=1, source_target_pairs={{0,4},{4,8},{8,12},{12,14},{14,10},{10,6},{6,2},{2,0},{1,5},{5,9},... | collective-permute-start | bytes 393224 | tf_op jit(solution)/shard_map/ppermute | solution.py:103
  27.5 0.1 collective-permute-start.14
  27.6 0.5 %collective-permute-start.15 = (bf16[128,512]{1,0:T(8,128)(2,1)S(1)}, bf16[128,512]{1,0:T(8,128)(2,1)S(1)}, u32[]{:S(2)}, u32[]{:S(2)}) collective-permute-start(bf16[128,512]{1,0:T(8,128)(2,1)S(1)} %collective-permute-done.8.refs_1_), channel_id=1, source_target_pairs={{0,1},{1,0},{2,3},{3,2},{4,5},{5,4},{6,7},{7,6},{8,9},{9,8},{10,11... | collective-permute-start | bytes 393224 | tf_op jit(solution)/shard_map/ppermute | solution.py:337
  28.1 1.4 %shard_map.57 = (bf16[256,256]{1,0:T(8,128)(2,1)S(1)}, bf16[1,4,256,512]{3,2,1,0:T(8,128)(2,1)}) custom-call(s32[4,8]{1,0:T(4,128)S(1)} %bitcast.9, bf16[128,512]{1,0:T(8,128)(2,1)S(1)} %shard_map.56.refs_0_, bf16[128,512]{1,0:T(8,128)(2,1)S(1)} %collective-permute-done.13.refs_1_), custom_call_target="tpu_custom_call" | custom-call | tf_op jit(solution)/shard_map/pallas_call | solution.py:302
  29.5 2.1 %collective-permute-done.12 = bf16[128,512]{1,0:T(8,128)(2,1)S(1)} collective-permute-done((bf16[128,512]{1,0:T(8,128)(2,1)S(1)}, bf16[128,512]{1,0:T(8,128)(2,1)S(1)}, u32[]{:S(2)}, u32[]{:S(2)}) %collective-permute-start.12) | collective-permute-done | bytes 131104 | tf_op jit(solution)/shard_map/ppermute | solution.py:102
  31.5 1.9 %collective-permute-done.11.refs_4_ = bf16[128,512]{1,0:T(8,128)(2,1)S(1)} collective-permute-done((bf16[128,512]{1,0:T(8,128)(2,1)S(1)}, bf16[128,512]{1,0:T(8,128)(2,1)S(1)}, u32[]{:S(2)}, u32[]{:S(2)}) %collective-permute-start.11) | collective-permute-done | bytes 131104 | tf_op jit(solution)/shard_map/ppermute | solution.py:104
  33.4 0.6 %collective-permute-done.9.refs_3_ = bf16[128,512]{1,0:T(8,128)(2,1)S(1)} collective-permute-done((bf16[128,512]{1,0:T(8,128)(2,1)S(1)}, bf16[128,512]{1,0:T(8,128)(2,1)S(1)}, u32[]{:S(2)}, u32[]{:S(2)}) %collective-permute-start.9) | collective-permute-done | bytes 131104 | tf_op jit(solution)/shard_map/ppermute | solution.py:103
  34.1 0.0 collective-permute-start.17
  34.1 0.0 collective-permute-start.19
  34.1 0.0 collective-permute-done.14
  34.1 0.5 %collective-permute-start.18 = (bf16[128,512]{1,0:T(8,128)(2,1)S(1)}, bf16[128,512]{1,0:T(8,128)(2,1)S(1)}, u32[]{:S(2)}, u32[]{:S(2)}) collective-permute-start(bf16[128,512]{1,0:T(8,128)(2,1)S(1)} %collective-permute-done.11.refs_4_), channel_id=1, source_target_pairs={{0,1},{1,0},{2,3},{3,2},{4,5},{5,4},{6,7},{7,6},{8,9},{9,8},{10,11... | collective-permute-start | bytes 393224 | tf_op jit(solution)/shard_map/ppermute | solution.py:337
  34.6 0.0 collective-permute-done.15.refs_5_
  34.6 1.7 %collective-permute-start.20 = (bf16[128,512]{1,0:T(8,128)(2,1)S(1)}, bf16[128,512]{1,0:T(8,128)(2,1)S(1)}, u32[]{:S(2)}, u32[]{:S(2)}) collective-permute-start(bf16[128,512]{1,0:T(8,128)(2,1)S(1)} %collective-permute-done.11.refs_4_), channel_id=1, source_target_pairs={{4,0},{8,4},{12,8},{14,12},{10,14},{6,10},{2,6},{0,2},{5,1},{9,5},... | collective-permute-start | bytes 393224 | tf_op jit(solution)/shard_map/ppermute | solution.py:112
  36.3 0.0 collective-permute-done.16.refs_6_
  36.4 0.1 collective-permute-start.23
  36.4 0.0 collective-permute-done.17.refs_7_
  36.4 0.0 collective-permute-done.18.refs_8_
  36.5 0.3 shard_map.58.refs_5_
  36.7 3.2 %collective-permute-done.19.refs_1_ = bf16[128,512]{1,0:T(8,128)(2,1)S(1)} collective-permute-done((bf16[128,512]{1,0:T(8,128)(2,1)S(1)}, bf16[128,512]{1,0:T(8,128)(2,1)S(1)}, u32[]{:S(2)}, u32[]{:S(2)}) %collective-permute-start.19) | collective-permute-done | bytes 131104 | tf_op jit(solution)/shard_map/ppermute | solution.py:111
  40.0 0.0 collective-permute-start.22
  40.0 0.1 collective-permute-done.20.refs_1_
  40.1 0.4 %collective-permute-start.21 = (bf16[128,512]{1,0:T(8,128)(2,1)S(1)}, bf16[128,512]{1,0:T(8,128)(2,1)S(1)}, u32[]{:S(2)}, u32[]{:S(2)}) collective-permute-start(bf16[128,512]{1,0:T(8,128)(2,1)S(1)} %collective-permute-done.20.refs_1_), channel_id=1, source_target_pairs={{0,1},{1,0},{2,3},{3,2},{4,5},{5,4},{6,7},{7,6},{8,9},{9,8},{10,11... | collective-permute-start | bytes 393224 | tf_op jit(solution)/shard_map/ppermute | solution.py:337
  40.5 0.0 collective-permute-done.23.refs_4_
  40.5 0.8 %collective-permute-done.22.refs_3_ = bf16[128,512]{1,0:T(8,128)(2,1)S(1)} collective-permute-done((bf16[128,512]{1,0:T(8,128)(2,1)S(1)}, bf16[128,512]{1,0:T(8,128)(2,1)S(1)}, u32[]{:S(2)}, u32[]{:S(2)}) %collective-permute-start.22) | collective-permute-done | bytes 131104 | tf_op jit(solution)/shard_map/ppermute | solution.py:337
  41.3 0.2 shard_map.59.refs_3_
  41.6 0.2 shard_map.60
  (17 shorter events, 0.1 us)
Async XLA Ops:
  0.0 19.9 %copy-start = (bf16[128,448]{0,1:T(8,128)(2,1)S(1)}, bf16[128,448]{0,1:T(8,128)(2,1)}, u32[]{:S(2)}) copy-start(bf16[128,448]{0,1:T(8,128)(2,1)} %param.5) | copy-start | bytes 344068
  0.0 19.9 %copy-start.2 = (f32[512]{0:T(512)S(1)}, f32[512]{0:T(512)}, u32[]{:S(2)}) copy-start(f32[512]{0:T(512)} %param.7) | copy-start | bytes 6148
  0.0 19.9 %copy-start.3 = (f32[512]{0:T(512)S(1)}, f32[512]{0:T(512)}, u32[]{:S(2)}) copy-start(f32[512]{0:T(512)} %param.8) | copy-start | bytes 6148
  0.0 8.1 %collective-permute-start = (bf16[448,128]{1,0:T(8,128)(2,1)}, bf16[448,128]{1,0:T(8,128)(2,1)S(1)}, u32[]{:S(2)}, u32[]{:S(2)}) collective-permute-start(bf16[448,128]{1,0:T(8,128)(2,1)} %bitcast.5), channel_id=1, source_target_pairs={{0,4},{4,8},{8,12},{12,14},{14,10},{10,6},{6,2},{2,0},{1,5},{5,9},... | collective-permute-start | bytes 344072 | tf_op jit(solution)/shard_map/ppermute | solution.py:100
  3.1 5.1 %collective-permute-start.2 = (bf16[448,128]{1,0:T(8,128)(2,1)}, bf16[448,128]{1,0:T(8,128)(2,1)S(1)}, u32[]{:S(2)}, u32[]{:S(2)}) collective-permute-start(bf16[448,128]{1,0:T(8,128)(2,1)} %bitcast.6), channel_id=1, source_target_pairs={{4,0},{8,4},{12,8},{14,12},{10,14},{6,10},{2,6},{0,2},{5,1},{9,5},... | collective-permute-start | bytes 344072 | tf_op jit(solution)/shard_map/ppermute | solution.py:101
  3.1 9.8 %collective-permute-start.4 = (bf16[448,128]{1,0:T(8,128)(2,1)}, bf16[448,128]{1,0:T(8,128)(2,1)S(1)}, u32[]{:S(2)}, u32[]{:S(2)}) collective-permute-start(bf16[448,128]{1,0:T(8,128)(2,1)} %bitcast.7), channel_id=1, source_target_pairs={{0,14},{12,2},{14,0},{2,12},{4,6},{8,10},{10,8},{6,4},{1,15},{13,3... | collective-permute-start | bytes 344072 | tf_op jit(solution)/shard_map/ppermute | solution.py:102
  8.1 5.9 %collective-permute-start.1 = (bf16[448,128]{1,0:T(8,128)(2,1)S(1)}, bf16[448,128]{1,0:T(8,128)(2,1)S(1)}, u32[]{:S(2)}, u32[]{:S(2)}) collective-permute-start(bf16[448,128]{1,0:T(8,128)(2,1)S(1)} %collective-permute-done.refs_0_), channel_id=1, source_target_pairs={{0,4},{4,8},{8,12},{12,14},{14,10},{10,6},{6,2},{2,0},{1,5},{5,9},... | collective-permute-start | bytes 344072 | tf_op jit(solution)/shard_map/ppermute | solution.py:103
  8.2 5.8 %collective-permute-start.3 = (bf16[448,128]{1,0:T(8,128)(2,1)S(1)}, bf16[448,128]{1,0:T(8,128)(2,1)S(1)}, u32[]{:S(2)}, u32[]{:S(2)}) collective-permute-start(bf16[448,128]{1,0:T(8,128)(2,1)S(1)} %collective-permute-done.2.refs_1_), channel_id=1, source_target_pairs={{4,0},{8,4},{12,8},{14,12},{10,14},{6,10},{2,6},{0,2},{5,1},{9,5},... | collective-permute-start | bytes 344072 | tf_op jit(solution)/shard_map/ppermute | solution.py:104
  10.1 5.9 %collective-permute-start.7 = (bf16[448,128]{1,0:T(8,128)(2,1)S(1)}, bf16[448,128]{1,0:T(8,128)(2,1)S(1)}, u32[]{:S(2)}, u32[]{:S(2)}) collective-permute-start(bf16[448,128]{1,0:T(8,128)(2,1)S(1)} %broadcast_select_fusion.2), channel_id=1, source_target_pairs={{4,6},{5,7},{8,10},{9,11},{10,8},{11,9},{6,4},{7,5},{0,1},{1,0},{1... | collective-permute-start | bytes 344072 | tf_op jit(solution)/shard_map/ppermute | solution.py:106
  14.0 4.8 %collective-permute-start.5 = (bf16[448,128]{1,0:T(8,128)(2,1)S(1)}, bf16[448,128]{1,0:T(8,128)(2,1)S(1)}, u32[]{:S(2)}, u32[]{:S(2)}) collective-permute-start(bf16[448,128]{1,0:T(8,128)(2,1)S(1)} %collective-permute-done.1.refs_2_), channel_id=1, source_target_pairs={{0,4},{4,8},{8,12},{12,14},{14,10},{10,6},{6,2},{2,0},{1,5},{5,9},... | collective-permute-start | bytes 344072 | tf_op jit(solution)/shard_map/ppermute | solution.py:111
  15.1 4.8 %collective-permute-start.6 = (bf16[448,128]{1,0:T(8,128)(2,1)S(1)}, bf16[448,128]{1,0:T(8,128)(2,1)S(1)}, u32[]{:S(2)}, u32[]{:S(2)}) collective-permute-start(bf16[448,128]{1,0:T(8,128)(2,1)S(1)} %collective-permute-done.3.refs_3_), channel_id=1, source_target_pairs={{4,0},{8,4},{12,8},{14,12},{10,14},{6,10},{2,6},{0,2},{5,1},{9,5},... | collective-permute-start | bytes 344072 | tf_op jit(solution)/shard_map/ppermute | solution.py:112
  16.0 12.0 %copy-start.1 = (s32[8,4]{0,1:T(4,128)S(1)}, s32[8,4]{0,1:T(4,128)}, u32[]{:S(2)}) copy-start(s32[8,4]{0,1:T(4,128)} %param.9) | copy-start | bytes 388
  20.4 5.0 %collective-permute-start.10 = (bf16[128,512]{1,0:T(8,128)(2,1)S(1)}, bf16[128,512]{1,0:T(8,128)(2,1)S(1)}, u32[]{:S(2)}, u32[]{:S(2)}) collective-permute-start(bf16[128,512]{1,0:T(8,128)(2,1)S(1)} %shard_map.56.refs_0_), channel_id=1, source_target_pairs={{4,0},{8,4},{12,8},{14,12},{10,14},{6,10},{2,6},{0,2},{5,1},{9,5},... | collective-permute-start | bytes 393224 | tf_op jit(solution)/shard_map/ppermute | solution.py:101
  21.4 5.6 %collective-permute-start.8 = (bf16[128,512]{1,0:T(8,128)(2,1)S(1)}, bf16[128,512]{1,0:T(8,128)(2,1)S(1)}, u32[]{:S(2)}, u32[]{:S(2)}) collective-permute-start(bf16[128,512]{1,0:T(8,128)(2,1)S(1)} %shard_map.56.refs_0_), channel_id=1, source_target_pairs={{0,4},{4,8},{8,12},{12,14},{14,10},{10,6},{6,2},{2,0},{1,5},{5,9},... | collective-permute-start | bytes 393224 | tf_op jit(solution)/shard_map/ppermute | solution.py:100
  22.5 5.1 %collective-permute-start.13 = (bf16[128,512]{1,0:T(8,128)(2,1)S(1)}, bf16[128,512]{1,0:T(8,128)(2,1)S(1)}, u32[]{:S(2)}, u32[]{:S(2)}) collective-permute-start(bf16[128,512]{1,0:T(8,128)(2,1)S(1)} %shard_map.56.refs_0_), channel_id=1, source_target_pairs={{0,1},{1,0},{2,3},{3,2},{4,5},{5,4},{6,7},{7,6},{8,9},{9,8},{10,11... | collective-permute-start | bytes 393224 | tf_op jit(solution)/shard_map/ppermute | solution.py:334
  22.5 9.0 %collective-permute-start.12 = (bf16[128,512]{1,0:T(8,128)(2,1)S(1)}, bf16[128,512]{1,0:T(8,128)(2,1)S(1)}, u32[]{:S(2)}, u32[]{:S(2)}) collective-permute-start(bf16[128,512]{1,0:T(8,128)(2,1)S(1)} %shard_map.56.refs_0_), channel_id=1, source_target_pairs={{0,14},{12,2},{14,0},{2,12},{4,6},{8,10},{10,8},{6,4},{1,15},{13,3... | collective-permute-start | bytes 393224 | tf_op jit(solution)/shard_map/ppermute | solution.py:102
  25.4 8.0 %collective-permute-start.11 = (bf16[128,512]{1,0:T(8,128)(2,1)S(1)}, bf16[128,512]{1,0:T(8,128)(2,1)S(1)}, u32[]{:S(2)}, u32[]{:S(2)}) collective-permute-start(bf16[128,512]{1,0:T(8,128)(2,1)S(1)} %collective-permute-done.10.refs_2_), channel_id=1, source_target_pairs={{4,0},{8,4},{12,8},{14,12},{10,14},{6,10},{2,6},{0,2},{5,1},{9,5},... | collective-permute-start | bytes 393224 | tf_op jit(solution)/shard_map/ppermute | solution.py:104
  27.0 7.0 %collective-permute-start.9 = (bf16[128,512]{1,0:T(8,128)(2,1)S(1)}, bf16[128,512]{1,0:T(8,128)(2,1)S(1)}, u32[]{:S(2)}, u32[]{:S(2)}) collective-permute-start(bf16[128,512]{1,0:T(8,128)(2,1)S(1)} %collective-permute-done.8.refs_1_), channel_id=1, source_target_pairs={{0,4},{4,8},{8,12},{12,14},{14,10},{10,6},{6,2},{2,0},{1,5},{5,9},... | collective-permute-start | bytes 393224 | tf_op jit(solution)/shard_map/ppermute | solution.py:103
  27.5 6.6 %collective-permute-start.14 = (bf16[128,512]{1,0:T(8,128)(2,1)S(1)}, bf16[128,512]{1,0:T(8,128)(2,1)S(1)}, u32[]{:S(2)}, u32[]{:S(2)}) collective-permute-start(bf16[128,512]{1,0:T(8,128)(2,1)S(1)} %broadcast_select_fusion.1), channel_id=1, source_target_pairs={{4,6},{5,7},{8,10},{9,11},{10,8},{11,9},{6,4},{7,5},{0,1},{1,0},{1... | collective-permute-start | bytes 393224 | tf_op jit(solution)/shard_map/ppermute | solution.py:106
  27.6 7.0 %collective-permute-start.15 = (bf16[128,512]{1,0:T(8,128)(2,1)S(1)}, bf16[128,512]{1,0:T(8,128)(2,1)S(1)}, u32[]{:S(2)}, u32[]{:S(2)}) collective-permute-start(bf16[128,512]{1,0:T(8,128)(2,1)S(1)} %collective-permute-done.8.refs_1_), channel_id=1, source_target_pairs={{0,1},{1,0},{2,3},{3,2},{4,5},{5,4},{6,7},{7,6},{8,9},{9,8},{10,11... | collective-permute-start | bytes 393224 | tf_op jit(solution)/shard_map/ppermute | solution.py:337
  31.5 4.8 %collective-permute-start.16 = (bf16[128,512]{1,0:T(8,128)(2,1)S(1)}, bf16[128,512]{1,0:T(8,128)(2,1)S(1)}, u32[]{:S(2)}, u32[]{:S(2)}) collective-permute-start(bf16[128,512]{1,0:T(8,128)(2,1)S(1)} %collective-permute-done.10.refs_2_), channel_id=1, source_target_pairs={{0,1},{1,0},{2,3},{3,2},{4,5},{5,4},{6,7},{7,6},{8,9},{9,8},{10,11... | collective-permute-start | bytes 393224 | tf_op jit(solution)/shard_map/ppermute | solution.py:337
  34.1 2.4 %collective-permute-start.17 = (bf16[128,512]{1,0:T(8,128)(2,1)S(1)}, bf16[128,512]{1,0:T(8,128)(2,1)S(1)}, u32[]{:S(2)}, u32[]{:S(2)}) collective-permute-start(bf16[128,512]{1,0:T(8,128)(2,1)S(1)} %collective-permute-done.9.refs_3_), channel_id=1, source_target_pairs={{0,1},{1,0},{2,3},{3,2},{4,5},{5,4},{6,7},{7,6},{8,9},{9,8},{10,11... | collective-permute-start | bytes 393224 | tf_op jit(solution)/shard_map/ppermute | solution.py:337
  34.1 5.9 %collective-permute-start.19 = (bf16[128,512]{1,0:T(8,128)(2,1)S(1)}, bf16[128,512]{1,0:T(8,128)(2,1)S(1)}, u32[]{:S(2)}, u32[]{:S(2)}) collective-permute-start(bf16[128,512]{1,0:T(8,128)(2,1)S(1)} %collective-permute-done.9.refs_3_), channel_id=1, source_target_pairs={{0,4},{4,8},{8,12},{12,14},{14,10},{10,6},{6,2},{2,0},{1,5},{5,9},... | collective-permute-start | bytes 393224 | tf_op jit(solution)/shard_map/ppermute | solution.py:111
  34.1 2.4 %collective-permute-start.18 = (bf16[128,512]{1,0:T(8,128)(2,1)S(1)}, bf16[128,512]{1,0:T(8,128)(2,1)S(1)}, u32[]{:S(2)}, u32[]{:S(2)}) collective-permute-start(bf16[128,512]{1,0:T(8,128)(2,1)S(1)} %collective-permute-done.11.refs_4_), channel_id=1, source_target_pairs={{0,1},{1,0},{2,3},{3,2},{4,5},{5,4},{6,7},{7,6},{8,9},{9,8},{10,11... | collective-permute-start | bytes 393224 | tf_op jit(solution)/shard_map/ppermute | solution.py:337
  34.6 5.5 %collective-permute-start.20 = (bf16[128,512]{1,0:T(8,128)(2,1)S(1)}, bf16[128,512]{1,0:T(8,128)(2,1)S(1)}, u32[]{:S(2)}, u32[]{:S(2)}) collective-permute-start(bf16[128,512]{1,0:T(8,128)(2,1)S(1)} %collective-permute-done.11.refs_4_), channel_id=1, source_target_pairs={{4,0},{8,4},{12,8},{14,12},{10,14},{6,10},{2,6},{0,2},{5,1},{9,5},... | collective-permute-start | bytes 393224 | tf_op jit(solution)/shard_map/ppermute | solution.py:112
  36.4 4.1 %collective-permute-start.23 = (bf16[128,512]{1,0:T(8,128)(2,1)S(1)}, bf16[128,512]{1,0:T(8,128)(2,1)S(1)}, u32[]{:S(2)}, u32[]{:S(2)}) collective-permute-start(bf16[128,512]{1,0:T(8,128)(2,1)S(1)} %broadcast_select_fusion.refs_2_), channel_id=1, source_target_pairs={{0,1},{1,0},{2,3},{3,2},{4,5},{5,4},{6,7},{7,6},{8,9},{9,8},{10,11... | collective-permute-start | bytes 393224 | tf_op jit(solution)/shard_map/ppermute | solution.py:337
  40.0 1.3 %collective-permute-start.22 = (bf16[128,512]{1,0:T(8,128)(2,1)S(1)}, bf16[128,512]{1,0:T(8,128)(2,1)S(1)}, u32[]{:S(2)}, u32[]{:S(2)}) collective-permute-start(bf16[128,512]{1,0:T(8,128)(2,1)S(1)} %collective-permute-done.19.refs_1_), channel_id=1, source_target_pairs={{0,1},{1,0},{2,3},{3,2},{4,5},{5,4},{6,7},{7,6},{8,9},{9,8},{10,11... | collective-permute-start | bytes 393224 | tf_op jit(solution)/shard_map/ppermute | solution.py:337
  40.1 1.5 %collective-permute-start.21 = (bf16[128,512]{1,0:T(8,128)(2,1)S(1)}, bf16[128,512]{1,0:T(8,128)(2,1)S(1)}, u32[]{:S(2)}, u32[]{:S(2)}) collective-permute-start(bf16[128,512]{1,0:T(8,128)(2,1)S(1)} %collective-permute-done.20.refs_1_), channel_id=1, source_target_pairs={{0,1},{1,0},{2,3},{3,2},{4,5},{5,4},{6,7},{7,6},{8,9},{9,8},{10,11... | collective-permute-start | bytes 393224 | tf_op jit(solution)/shard_map/ppermute | solution.py:337

commit v17 on v16

--- a/solution.py
+++ b/solution.py
@@ -348,8 +348,9 @@
         out, *late = ring.gather(acts, beside_second, beside_third)
         ahead, behind, corner, middle = late
         far = jnp.where(on_corner(n), corner, middle)
+        out = add_tiles(out, (n // 2,), (far,))
         out, ahead = lax.optimization_barrier((out, ahead))
-        out = add_tiles(out, (3, n // 2), (ahead, far))
+        out = add_tiles(out, (3,), (ahead,))
         return add_tiles(out, (n - 3,), (behind,))[1]
     acts = encode_gathered(residual, enc_weight, enc_bias, threshold)
     acts_twin = lax.ppermute(acts, "tok", swap)

time: 42.3 us -> 44.2 us (1.045)
  waiting for transfers between devices: 14.8 us -> 16.5 us
    ppermute x2, starting transfers between devices: 1.11 us -> 3.26 us  [gather(): ahead_3 = lax.ppermute(ahead_2, 'lat', self.forward)]
    ppermute x2, waiting for transfers between devices: 1.18 us -> 3.21 us  [gather(): behind_3 = lax.ppermute(behind_2, 'lat', self.backward)]
    ppermute x2, starting transfers between devices: 2.66 us -> 0.92 us  [gather(): behind_3 = lax.ppermute(behind_2, 'lat', self.backward)]
    ppermute x2, waiting for transfers between devices: 4.74 us -> 3.23 us  [gather(): corner = lax.ppermute(x, 'lat', self.across)]
    ppermute x2, starting transfers between devices: 0.55 us -> 2.02 us  [gather(): ahead_2 = lax.ppermute(ahead, 'lat', self.forward)]
    ppermute x2, waiting for transfers between devices: 0.01 us -> 1.39 us  [gather(): ahead = lax.ppermute(x, 'lat', self.forward)]
    ppermute x2, starting transfers between devices: 3.51 us -> 2.42 us  [gather(): behind_2 = lax.ppermute(behind, 'lat', self.backward)]
    ppermute x2, starting transfers between devices: 0.98 us -> 0.06 us  [gather(): behind = lax.ppermute(x, 'lat', self.backward)]
where the time goes in v17:
time: 44.2 us; the launch traced here: 44 us
  starting transfers between devices  22.5 us (51%)
  waiting for transfers between devices  16.5 us (37%)
  Pallas kernels  4.78 us (11%)
    ppermute x2, starting transfers between devices, gather(): corner = lax.ppermute(x, 'lat', self.across)  7.54 us
    ppermute x2, starting transfers between devices, gather(): ahead = lax.ppermute(x, 'lat', self.forward)  5.1 us
    ppermute x2, waiting for transfers between devices, gather(): ahead_3 = lax.ppermute(ahead_2, 'lat', self.forward)  3.89 us
    ppermute x2, starting transfers between devices, gather(): ahead_3 = lax.ppermute(ahead_2, 'lat', self.forward)  3.26 us
    ppermute x2, waiting for transfers between devices, gather(): corner = lax.ppermute(x, 'lat', self.across)  3.23 us
    ppermute x2, waiting for transfers between devices, gather(): behind_3 = lax.ppermute(behind_2, 'lat', self.backward)  3.21 us
    ppermute x2, starting transfers between devices, gather(): behind_2 = lax.ppermute(behind, 'lat', self.backward)  2.42 us
    ppermute x2, waiting for transfers between devices, gather(): ahead_2 = lax.ppermute(ahead, 'lat', self.forward)  2.28 us
  transfers between devices with their start and end apart: 24, of which 11 were waited for; matrix products, arithmetic and copies ran while one was open for 0% of the time, Pallas kernels for 9%

profile of v17, /device:TPU:0, one launch (start us, length us, event | category | flops | bytes accessed | tf_op | source)
XLA Modules:
  0.0 44.0 jit_solution(15262239481992785537)
XLA Ops:
  0.0 3.1 %collective-permute-start = (bf16[448,128]{1,0:T(8,128)(2,1)}, bf16[448,128]{1,0:T(8,128)(2,1)S(1)}, u32[]{:S(2)}, u32[]{:S(2)}) collective-permute-start(bf16[448,128]{1,0:T(8,128)(2,1)} %bitcast.5), channel_id=1, source_target_pairs={{0,4},{4,8},{8,12},{12,14},{14,10},{10,6},{6,2},{2,0},{1,5},{5,9},... | collective-permute-start | bytes 344072 | tf_op jit(solution)/shard_map/ppermute | solution.py:100
  3.1 0.0 collective-permute-start.2
  3.1 5.0 %collective-permute-start.4 = (bf16[448,128]{1,0:T(8,128)(2,1)}, bf16[448,128]{1,0:T(8,128)(2,1)S(1)}, u32[]{:S(2)}, u32[]{:S(2)}) collective-permute-start(bf16[448,128]{1,0:T(8,128)(2,1)} %bitcast.7), channel_id=1, source_target_pairs={{0,14},{12,2},{14,0},{2,12},{4,6},{8,10},{10,8},{6,4},{1,15},{13,3... | collective-permute-start | bytes 344072 | tf_op jit(solution)/shard_map/ppermute | solution.py:102
  8.1 0.0 collective-permute-done.refs_0_
  8.1 0.1 collective-permute-start.1
  8.2 0.0 collective-permute-done.2.refs_1_
  8.2 1.9 %collective-permute-start.3 = (bf16[448,128]{1,0:T(8,128)(2,1)S(1)}, bf16[448,128]{1,0:T(8,128)(2,1)S(1)}, u32[]{:S(2)}, u32[]{:S(2)}) collective-permute-start(bf16[448,128]{1,0:T(8,128)(2,1)S(1)} %collective-permute-done.2.refs_1_), channel_id=1, source_target_pairs={{4,0},{8,4},{12,8},{14,12},{10,14},{6,10},{2,6},{0,2},{5,1},{9,5},... | collective-permute-start | bytes 344072 | tf_op jit(solution)/shard_map/ppermute | solution.py:104
  10.1 0.1 collective-permute-start.7
  10.2 2.7 %collective-permute-done.4.x_corner = bf16[448,128]{1,0:T(8,128)(2,1)S(1)} collective-permute-done((bf16[448,128]{1,0:T(8,128)(2,1)}, bf16[448,128]{1,0:T(8,128)(2,1)S(1)}, u32[]{:S(2)}, u32[]{:S(2)}) %collective-permute-start.4) | collective-permute-done | bytes 114720 | tf_op jit(solution)/shard_map/ppermute | solution.py:102
  12.9 1.1 %collective-permute-done.1.refs_2_ = bf16[448,128]{1,0:T(8,128)(2,1)S(1)} collective-permute-done((bf16[448,128]{1,0:T(8,128)(2,1)S(1)}, bf16[448,128]{1,0:T(8,128)(2,1)S(1)}, u32[]{:S(2)}, u32[]{:S(2)}) %collective-permute-start.1) | collective-permute-done | bytes 114720 | tf_op jit(solution)/shard_map/ppermute | solution.py:103
  14.0 0.0 collective-permute-done.3.refs_3_
  14.0 1.1 %collective-permute-start.5 = (bf16[448,128]{1,0:T(8,128)(2,1)S(1)}, bf16[448,128]{1,0:T(8,128)(2,1)S(1)}, u32[]{:S(2)}, u32[]{:S(2)}) collective-permute-start(bf16[448,128]{1,0:T(8,128)(2,1)S(1)} %collective-permute-done.1.refs_2_), channel_id=1, source_target_pairs={{0,4},{4,8},{8,12},{12,14},{14,10},{10,6},{6,2},{2,0},{1,5},{5,9},... | collective-permute-start | bytes 344072 | tf_op jit(solution)/shard_map/ppermute | solution.py:111
  15.1 0.9 %collective-permute-start.6 = (bf16[448,128]{1,0:T(8,128)(2,1)S(1)}, bf16[448,128]{1,0:T(8,128)(2,1)S(1)}, u32[]{:S(2)}, u32[]{:S(2)}) collective-permute-start(bf16[448,128]{1,0:T(8,128)(2,1)S(1)} %collective-permute-done.3.refs_3_), channel_id=1, source_target_pairs={{4,0},{8,4},{12,8},{14,12},{10,14},{6,10},{2,6},{0,2},{5,1},{9,5},... | collective-permute-start | bytes 344072 | tf_op jit(solution)/shard_map/ppermute | solution.py:112
  16.0 0.0 collective-permute-done.7.x_middle
  16.0 2.1 %shard_map.55 = (f32[128,512]{1,0:T(8,128)S(1)}, bf16[4,448,512]{2,1,0:T(8,128)(2,1)S(1)}) custom-call(bf16[448,128]{1,0:T(8,128)(2,1)S(1)} %collective-permute-done.refs_0_, bf16[448,128]{1,0:T(8,128)(2,1)S(1)} %collective-permute-done.2.refs_1_, bf16[448,128]{1,0:T(8,128)(2,1)S(1)} %collective-permute-done.1.refs_2_, ...), custom_call_target="tpu_custom_call" | custom-call | flops 234881024 | bytes 2818048 | tf_op jit(solution)/shard_map/pallas_call | solution.py:128
  18.1 0.7 %collective-permute-done.5.x_f = bf16[448,128]{1,0:T(8,128)(2,1)S(1)} collective-permute-done((bf16[448,128]{1,0:T(8,128)(2,1)S(1)}, bf16[448,128]{1,0:T(8,128)(2,1)S(1)}, u32[]{:S(2)}, u32[]{:S(2)}) %collective-permute-start.5) | collective-permute-done | bytes 114720 | tf_op jit(solution)/shard_map/ppermute | solution.py:111
  18.8 1.1 %collective-permute-done.6.x_b = bf16[448,128]{1,0:T(8,128)(2,1)S(1)} collective-permute-done((bf16[448,128]{1,0:T(8,128)(2,1)S(1)}, bf16[448,128]{1,0:T(8,128)(2,1)S(1)}, u32[]{:S(2)}, u32[]{:S(2)}) %collective-permute-start.6) | collective-permute-done | bytes 114720 | tf_op jit(solution)/shard_map/ppermute | solution.py:112
  19.9 0.5 %shard_map.56.refs_0_ = bf16[128,512]{1,0:T(8,128)(2,1)S(1)} custom-call(bf16[448,128]{1,0:T(8,128)(2,1)S(1)} %bitcast.8, bf16[448,128]{1,0:T(8,128)(2,1)S(1)} %collective-permute-done.5.x_f, bf16[448,128]{1,0:T(8,128)(2,1)S(1)} %collective-permute-done.6.x_b, bf16[448,128]{1,0:T(8,128)(2,1)S(1)} %collective-permute-done.4.x_corner, ...), custom_call_target="tpu_custom_call" | custom-call | flops 234881024 | bytes 2818048 | tf_op jit(solution)/shard_map/pallas_call | solution.py:143
  20.4 2.0 %collective-permute-start.8 = (bf16[128,512]{1,0:T(8,128)(2,1)S(1)}, bf16[128,512]{1,0:T(8,128)(2,1)S(1)}, u32[]{:S(2)}, u32[]{:S(2)}) collective-permute-start(bf16[128,512]{1,0:T(8,128)(2,1)S(1)} %shard_map.56.refs_0_), channel_id=1, source_target_pairs={{0,4},{4,8},{8,12},{12,14},{14,10},{10,6},{6,2},{2,0},{1,5},{5,9},... | collective-permute-start | bytes 393224 | tf_op jit(solution)/shard_map/ppermute | solution.py:100
  22.4 0.1 collective-permute-start.10
  22.5 2.6 %collective-permute-start.12 = (bf16[128,512]{1,0:T(8,128)(2,1)S(1)}, bf16[128,512]{1,0:T(8,128)(2,1)S(1)}, u32[]{:S(2)}, u32[]{:S(2)}) collective-permute-start(bf16[128,512]{1,0:T(8,128)(2,1)S(1)} %shard_map.56.refs_0_), channel_id=1, source_target_pairs={{0,14},{12,2},{14,0},{2,12},{4,6},{8,10},{10,8},{6,4},{1,15},{13,3... | collective-permute-start | bytes 393224 | tf_op jit(solution)/shard_map/ppermute | solution.py:102
  25.1 1.4 %collective-permute-done.8.refs_1_ = bf16[128,512]{1,0:T(8,128)(2,1)S(1)} collective-permute-done((bf16[128,512]{1,0:T(8,128)(2,1)S(1)}, bf16[128,512]{1,0:T(8,128)(2,1)S(1)}, u32[]{:S(2)}, u32[]{:S(2)}) %collective-permute-start.8) | collective-permute-done | bytes 131104 | tf_op jit(solution)/shard_map/ppermute | solution.py:100
  26.4 1.9 %collective-permute-start.9 = (bf16[128,512]{1,0:T(8,128)(2,1)S(1)}, bf16[128,512]{1,0:T(8,128)(2,1)S(1)}, u32[]{:S(2)}, u32[]{:S(2)}) collective-permute-start(bf16[128,512]{1,0:T(8,128)(2,1)S(1)} %collective-permute-done.8.refs_1_), channel_id=1, source_target_pairs={{0,4},{4,8},{8,12},{12,14},{14,10},{10,6},{6,2},{2,0},{1,5},{5,9},... | collective-permute-start | bytes 393224 | tf_op jit(solution)/shard_map/ppermute | solution.py:103
  28.4 0.5 %collective-permute-start.11 = (bf16[128,512]{1,0:T(8,128)(2,1)S(1)}, bf16[128,512]{1,0:T(8,128)(2,1)S(1)}, u32[]{:S(2)}, u32[]{:S(2)}) collective-permute-start(bf16[128,512]{1,0:T(8,128)(2,1)S(1)} %collective-permute-done.10.refs_2_), channel_id=1, source_target_pairs={{4,0},{8,4},{12,8},{14,12},{10,14},{6,10},{2,6},{0,2},{5,1},{9,5},... | collective-permute-start | bytes 393224 | tf_op jit(solution)/shard_map/ppermute | solution.py:104
  28.9 0.1 collective-permute-start.14
  29.0 0.0 collective-permute-done.13.refs_1_
  29.0 0.5 %collective-permute-start.16 = (bf16[128,512]{1,0:T(8,128)(2,1)S(1)}, bf16[128,512]{1,0:T(8,128)(2,1)S(1)}, u32[]{:S(2)}, u32[]{:S(2)}) collective-permute-start(bf16[128,512]{1,0:T(8,128)(2,1)S(1)} %collective-permute-done.8.refs_1_), channel_id=1, source_target_pairs={{0,1},{1,0},{2,3},{3,2},{4,5},{5,4},{6,7},{7,6},{8,9},{9,8},{10,11... | collective-permute-start | bytes 393224 | tf_op jit(solution)/shard_map/ppermute | solution.py:337
  29.5 1.4 %shard_map.57 = (bf16[256,256]{1,0:T(8,128)(2,1)S(1)}, bf16[1,4,256,512]{3,2,1,0:T(8,128)(2,1)}) custom-call(s32[4,8]{1,0:T(4,128)S(1)} %bitcast.9, bf16[128,512]{1,0:T(8,128)(2,1)S(1)} %shard_map.56.refs_0_, bf16[128,512]{1,0:T(8,128)(2,1)S(1)} %collective-permute-done.13.refs_1_), custom_call_target="tpu_custom_call" | custom-call | tf_op jit(solution)/shard_map/pallas_call | solution.py:302
  30.9 0.6 %collective-permute-done.12 = bf16[128,512]{1,0:T(8,128)(2,1)S(1)} collective-permute-done((bf16[128,512]{1,0:T(8,128)(2,1)S(1)}, bf16[128,512]{1,0:T(8,128)(2,1)S(1)}, u32[]{:S(2)}, u32[]{:S(2)}) %collective-permute-start.12) | collective-permute-done | bytes 131104 | tf_op jit(solution)/shard_map/ppermute | solution.py:102
  31.4 1.2 %collective-permute-done.9.refs_3_ = bf16[128,512]{1,0:T(8,128)(2,1)S(1)} collective-permute-done((bf16[128,512]{1,0:T(8,128)(2,1)S(1)}, bf16[128,512]{1,0:T(8,128)(2,1)S(1)}, u32[]{:S(2)}, u32[]{:S(2)}) %collective-permute-start.9) | collective-permute-done | bytes 131104 | tf_op jit(solution)/shard_map/ppermute | solution.py:103
  32.6 1.3 %collective-permute-done.11.refs_4_ = bf16[128,512]{1,0:T(8,128)(2,1)S(1)} collective-permute-done((bf16[128,512]{1,0:T(8,128)(2,1)S(1)}, bf16[128,512]{1,0:T(8,128)(2,1)S(1)}, u32[]{:S(2)}, u32[]{:S(2)}) %collective-permute-start.11) | collective-permute-done | bytes 131104 | tf_op jit(solution)/shard_map/ppermute | solution.py:104
  33.9 0.5 %collective-permute-start.19 = (bf16[128,512]{1,0:T(8,128)(2,1)S(1)}, bf16[128,512]{1,0:T(8,128)(2,1)S(1)}, u32[]{:S(2)}, u32[]{:S(2)}) collective-permute-start(bf16[128,512]{1,0:T(8,128)(2,1)S(1)} %collective-permute-done.11.refs_4_), channel_id=1, source_target_pairs={{0,1},{1,0},{2,3},{3,2},{4,5},{5,4},{6,7},{7,6},{8,9},{9,8},{10,11... | collective-permute-start | bytes 393224 | tf_op jit(solution)/shard_map/ppermute | solution.py:337
  34.4 0.1 collective-permute-start.15
  34.5 0.0 collective-permute-done.16.refs_5_
  34.5 2.2 %collective-permute-start.20 = (bf16[128,512]{1,0:T(8,128)(2,1)S(1)}, bf16[128,512]{1,0:T(8,128)(2,1)S(1)}, u32[]{:S(2)}, u32[]{:S(2)}) collective-permute-start(bf16[128,512]{1,0:T(8,128)(2,1)S(1)} %collective-permute-done.9.refs_3_), channel_id=1, source_target_pairs={{0,4},{4,8},{8,12},{12,14},{14,10},{10,6},{6,2},{2,0},{1,5},{5,9},... | collective-permute-start | bytes 393224 | tf_op jit(solution)/shard_map/ppermute | solution.py:111
  36.7 0.0 collective-permute-done.17.refs_6_
  36.7 0.0 collective-permute-done.19.refs_8_
  36.7 0.3 shard_map.58.refs_3_
  37.0 0.0 collective-permute-done.15.refs_2_
  37.0 0.2 shard_map.59.refs_3_
  37.2 3.2 %collective-permute-done.20.refs_1_ = bf16[128,512]{1,0:T(8,128)(2,1)S(1)} collective-permute-done((bf16[128,512]{1,0:T(8,128)(2,1)S(1)}, bf16[128,512]{1,0:T(8,128)(2,1)S(1)}, u32[]{:S(2)}, u32[]{:S(2)}) %collective-permute-start.20) | collective-permute-done | bytes 131104 | tf_op jit(solution)/shard_map/ppermute | solution.py:111
  40.4 0.0 collective-permute-start.23
  40.4 2.1 %collective-permute-done.21.refs_1_ = bf16[128,512]{1,0:T(8,128)(2,1)S(1)} collective-permute-done((bf16[128,512]{1,0:T(8,128)(2,1)S(1)}, bf16[128,512]{1,0:T(8,128)(2,1)S(1)}, u32[]{:S(2)}, u32[]{:S(2)}) %collective-permute-start.21) | collective-permute-done | bytes 131104 | tf_op jit(solution)/shard_map/ppermute | solution.py:112
  42.5 0.0 collective-permute-start.22
  42.5 0.0 collective-permute-done.23.refs_2_
  42.5 0.2 shard_map.60.refs_3_
  42.7 1.2 %collective-permute-done.22.refs_2_ = bf16[128,512]{1,0:T(8,128)(2,1)S(1)} collective-permute-done((bf16[128,512]{1,0:T(8,128)(2,1)S(1)}, bf16[128,512]{1,0:T(8,128)(2,1)S(1)}, u32[]{:S(2)}, u32[]{:S(2)}) %collective-permute-start.22) | collective-permute-done | bytes 131104 | tf_op jit(solution)/shard_map/ppermute | solution.py:337
  43.9 0.2 shard_map.61
  (18 shorter events, 0.1 us)
Async XLA Ops:
  0.0 19.9 %copy-start = (bf16[128,448]{0,1:T(8,128)(2,1)S(1)}, bf16[128,448]{0,1:T(8,128)(2,1)}, u32[]{:S(2)}) copy-start(bf16[128,448]{0,1:T(8,128)(2,1)} %param.5) | copy-start | bytes 344068
  0.0 19.9 %copy-start.2 = (f32[512]{0:T(512)S(1)}, f32[512]{0:T(512)}, u32[]{:S(2)}) copy-start(f32[512]{0:T(512)} %param.7) | copy-start | bytes 6148
  0.0 19.9 %copy-start.3 = (f32[512]{0:T(512)S(1)}, f32[512]{0:T(512)}, u32[]{:S(2)}) copy-start(f32[512]{0:T(512)} %param.8) | copy-start | bytes 6148
  0.0 8.1 %collective-permute-start = (bf16[448,128]{1,0:T(8,128)(2,1)}, bf16[448,128]{1,0:T(8,128)(2,1)S(1)}, u32[]{:S(2)}, u32[]{:S(2)}) collective-permute-start(bf16[448,128]{1,0:T(8,128)(2,1)} %bitcast.5), channel_id=1, source_target_pairs={{0,4},{4,8},{8,12},{12,14},{14,10},{10,6},{6,2},{2,0},{1,5},{5,9},... | collective-permute-start | bytes 344072 | tf_op jit(solution)/shard_map/ppermute | solution.py:100
  3.1 5.1 %collective-permute-start.2 = (bf16[448,128]{1,0:T(8,128)(2,1)}, bf16[448,128]{1,0:T(8,128)(2,1)S(1)}, u32[]{:S(2)}, u32[]{:S(2)}) collective-permute-start(bf16[448,128]{1,0:T(8,128)(2,1)} %bitcast.6), channel_id=1, source_target_pairs={{4,0},{8,4},{12,8},{14,12},{10,14},{6,10},{2,6},{0,2},{5,1},{9,5},... | collective-permute-start | bytes 344072 | tf_op jit(solution)/shard_map/ppermute | solution.py:101
  3.1 9.8 %collective-permute-start.4 = (bf16[448,128]{1,0:T(8,128)(2,1)}, bf16[448,128]{1,0:T(8,128)(2,1)S(1)}, u32[]{:S(2)}, u32[]{:S(2)}) collective-permute-start(bf16[448,128]{1,0:T(8,128)(2,1)} %bitcast.7), channel_id=1, source_target_pairs={{0,14},{12,2},{14,0},{2,12},{4,6},{8,10},{10,8},{6,4},{1,15},{13,3... | collective-permute-start | bytes 344072 | tf_op jit(solution)/shard_map/ppermute | solution.py:102
  8.1 5.9 %collective-permute-start.1 = (bf16[448,128]{1,0:T(8,128)(2,1)S(1)}, bf16[448,128]{1,0:T(8,128)(2,1)S(1)}, u32[]{:S(2)}, u32[]{:S(2)}) collective-permute-start(bf16[448,128]{1,0:T(8,128)(2,1)S(1)} %collective-permute-done.refs_0_), channel_id=1, source_target_pairs={{0,4},{4,8},{8,12},{12,14},{14,10},{10,6},{6,2},{2,0},{1,5},{5,9},... | collective-permute-start | bytes 344072 | tf_op jit(solution)/shard_map/ppermute | solution.py:103
  8.2 5.8 %collective-permute-start.3 = (bf16[448,128]{1,0:T(8,128)(2,1)S(1)}, bf16[448,128]{1,0:T(8,128)(2,1)S(1)}, u32[]{:S(2)}, u32[]{:S(2)}) collective-permute-start(bf16[448,128]{1,0:T(8,128)(2,1)S(1)} %collective-permute-done.2.refs_1_), channel_id=1, source_target_pairs={{4,0},{8,4},{12,8},{14,12},{10,14},{6,10},{2,6},{0,2},{5,1},{9,5},... | collective-permute-start | bytes 344072 | tf_op jit(solution)/shard_map/ppermute | solution.py:104
  10.1 5.9 %collective-permute-start.7 = (bf16[448,128]{1,0:T(8,128)(2,1)S(1)}, bf16[448,128]{1,0:T(8,128)(2,1)S(1)}, u32[]{:S(2)}, u32[]{:S(2)}) collective-permute-start(bf16[448,128]{1,0:T(8,128)(2,1)S(1)} %broadcast_select_fusion.2), channel_id=1, source_target_pairs={{4,6},{5,7},{8,10},{9,11},{10,8},{11,9},{6,4},{7,5},{0,1},{1,0},{1... | collective-permute-start | bytes 344072 | tf_op jit(solution)/shard_map/ppermute | solution.py:106
  14.0 4.8 %collective-permute-start.5 = (bf16[448,128]{1,0:T(8,128)(2,1)S(1)}, bf16[448,128]{1,0:T(8,128)(2,1)S(1)}, u32[]{:S(2)}, u32[]{:S(2)}) collective-permute-start(bf16[448,128]{1,0:T(8,128)(2,1)S(1)} %collective-permute-done.1.refs_2_), channel_id=1, source_target_pairs={{0,4},{4,8},{8,12},{12,14},{14,10},{10,6},{6,2},{2,0},{1,5},{5,9},... | collective-permute-start | bytes 344072 | tf_op jit(solution)/shard_map/ppermute | solution.py:111
  15.1 4.8 %collective-permute-start.6 = (bf16[448,128]{1,0:T(8,128)(2,1)S(1)}, bf16[448,128]{1,0:T(8,128)(2,1)S(1)}, u32[]{:S(2)}, u32[]{:S(2)}) collective-permute-start(bf16[448,128]{1,0:T(8,128)(2,1)S(1)} %collective-permute-done.3.refs_3_), channel_id=1, source_target_pairs={{4,0},{8,4},{12,8},{14,12},{10,14},{6,10},{2,6},{0,2},{5,1},{9,5},... | collective-permute-start | bytes 344072 | tf_op jit(solution)/shard_map/ppermute | solution.py:112
  16.0 13.4 %copy-start.1 = (s32[8,4]{0,1:T(4,128)S(1)}, s32[8,4]{0,1:T(4,128)}, u32[]{:S(2)}) copy-start(s32[8,4]{0,1:T(4,128)} %param.9) | copy-start | bytes 388
  20.4 6.0 %collective-permute-start.8 = (bf16[128,512]{1,0:T(8,128)(2,1)S(1)}, bf16[128,512]{1,0:T(8,128)(2,1)S(1)}, u32[]{:S(2)}, u32[]{:S(2)}) collective-permute-start(bf16[128,512]{1,0:T(8,128)(2,1)S(1)} %shard_map.56.refs_0_), channel_id=1, source_target_pairs={{0,4},{4,8},{8,12},{12,14},{14,10},{10,6},{6,2},{2,0},{1,5},{5,9},... | collective-permute-start | bytes 393224 | tf_op jit(solution)/shard_map/ppermute | solution.py:100
  22.4 5.9 %collective-permute-start.10 = (bf16[128,512]{1,0:T(8,128)(2,1)S(1)}, bf16[128,512]{1,0:T(8,128)(2,1)S(1)}, u32[]{:S(2)}, u32[]{:S(2)}) collective-permute-start(bf16[128,512]{1,0:T(8,128)(2,1)S(1)} %shard_map.56.refs_0_), channel_id=1, source_target_pairs={{4,0},{8,4},{12,8},{14,12},{10,14},{6,10},{2,6},{0,2},{5,1},{9,5},... | collective-permute-start | bytes 393224 | tf_op jit(solution)/shard_map/ppermute | solution.py:101
  22.5 8.9 %collective-permute-start.12 = (bf16[128,512]{1,0:T(8,128)(2,1)S(1)}, bf16[128,512]{1,0:T(8,128)(2,1)S(1)}, u32[]{:S(2)}, u32[]{:S(2)}) collective-permute-start(bf16[128,512]{1,0:T(8,128)(2,1)S(1)} %shard_map.56.refs_0_), channel_id=1, source_target_pairs={{0,14},{12,2},{14,0},{2,12},{4,6},{8,10},{10,8},{6,4},{1,15},{13,3... | collective-permute-start | bytes 393224 | tf_op jit(solution)/shard_map/ppermute | solution.py:102
  25.1 3.9 %collective-permute-start.13 = (bf16[128,512]{1,0:T(8,128)(2,1)S(1)}, bf16[128,512]{1,0:T(8,128)(2,1)S(1)}, u32[]{:S(2)}, u32[]{:S(2)}) collective-permute-start(bf16[128,512]{1,0:T(8,128)(2,1)S(1)} %shard_map.56.refs_0_), channel_id=1, source_target_pairs={{0,1},{1,0},{2,3},{3,2},{4,5},{5,4},{6,7},{7,6},{8,9},{9,8},{10,11... | collective-permute-start | bytes 393224 | tf_op jit(solution)/shard_map/ppermute | solution.py:334
  26.4 6.1 %collective-permute-start.9 = (bf16[128,512]{1,0:T(8,128)(2,1)S(1)}, bf16[128,512]{1,0:T(8,128)(2,1)S(1)}, u32[]{:S(2)}, u32[]{:S(2)}) collective-permute-start(bf16[128,512]{1,0:T(8,128)(2,1)S(1)} %collective-permute-done.8.refs_1_), channel_id=1, source_target_pairs={{0,4},{4,8},{8,12},{12,14},{14,10},{10,6},{6,2},{2,0},{1,5},{5,9},... | collective-permute-start | bytes 393224 | tf_op jit(solution)/shard_map/ppermute | solution.py:103
  28.4 5.5 %collective-permute-start.11 = (bf16[128,512]{1,0:T(8,128)(2,1)S(1)}, bf16[128,512]{1,0:T(8,128)(2,1)S(1)}, u32[]{:S(2)}, u32[]{:S(2)}) collective-permute-start(bf16[128,512]{1,0:T(8,128)(2,1)S(1)} %collective-permute-done.10.refs_2_), channel_id=1, source_target_pairs={{4,0},{8,4},{12,8},{14,12},{10,14},{6,10},{2,6},{0,2},{5,1},{9,5},... | collective-permute-start | bytes 393224 | tf_op jit(solution)/shard_map/ppermute | solution.py:104
  28.9 5.0 %collective-permute-start.14 = (bf16[128,512]{1,0:T(8,128)(2,1)S(1)}, bf16[128,512]{1,0:T(8,128)(2,1)S(1)}, u32[]{:S(2)}, u32[]{:S(2)}) collective-permute-start(bf16[128,512]{1,0:T(8,128)(2,1)S(1)} %broadcast_select_fusion.1), channel_id=1, source_target_pairs={{4,6},{5,7},{8,10},{9,11},{10,8},{11,9},{6,4},{7,5},{0,1},{1,0},{1... | collective-permute-start | bytes 393224 | tf_op jit(solution)/shard_map/ppermute | solution.py:106
  29.0 5.5 %collective-permute-start.16 = (bf16[128,512]{1,0:T(8,128)(2,1)S(1)}, bf16[128,512]{1,0:T(8,128)(2,1)S(1)}, u32[]{:S(2)}, u32[]{:S(2)}) collective-permute-start(bf16[128,512]{1,0:T(8,128)(2,1)S(1)} %collective-permute-done.8.refs_1_), channel_id=1, source_target_pairs={{0,1},{1,0},{2,3},{3,2},{4,5},{5,4},{6,7},{7,6},{8,9},{9,8},{10,11... | collective-permute-start | bytes 393224 | tf_op jit(solution)/shard_map/ppermute | solution.py:337
  31.4 5.2 %collective-permute-start.17 = (bf16[128,512]{1,0:T(8,128)(2,1)S(1)}, bf16[128,512]{1,0:T(8,128)(2,1)S(1)}, u32[]{:S(2)}, u32[]{:S(2)}) collective-permute-start(bf16[128,512]{1,0:T(8,128)(2,1)S(1)} %collective-permute-done.10.refs_2_), channel_id=1, source_target_pairs={{0,1},{1,0},{2,3},{3,2},{4,5},{5,4},{6,7},{7,6},{8,9},{9,8},{10,11... | collective-permute-start | bytes 393224 | tf_op jit(solution)/shard_map/ppermute | solution.py:337
  33.9 2.8 %collective-permute-start.18 = (bf16[128,512]{1,0:T(8,128)(2,1)S(1)}, bf16[128,512]{1,0:T(8,128)(2,1)S(1)}, u32[]{:S(2)}, u32[]{:S(2)}) collective-permute-start(bf16[128,512]{1,0:T(8,128)(2,1)S(1)} %collective-permute-done.9.refs_3_), channel_id=1, source_target_pairs={{0,1},{1,0},{2,3},{3,2},{4,5},{5,4},{6,7},{7,6},{8,9},{9,8},{10,11... | collective-permute-start | bytes 393224 | tf_op jit(solution)/shard_map/ppermute | solution.py:337
  33.9 2.8 %collective-permute-start.19 = (bf16[128,512]{1,0:T(8,128)(2,1)S(1)}, bf16[128,512]{1,0:T(8,128)(2,1)S(1)}, u32[]{:S(2)}, u32[]{:S(2)}) collective-permute-start(bf16[128,512]{1,0:T(8,128)(2,1)S(1)} %collective-permute-done.11.refs_4_), channel_id=1, source_target_pairs={{0,1},{1,0},{2,3},{3,2},{4,5},{5,4},{6,7},{7,6},{8,9},{9,8},{10,11... | collective-permute-start | bytes 393224 | tf_op jit(solution)/shard_map/ppermute | solution.py:337
  34.4 2.6 %collective-permute-start.15 = (bf16[128,512]{1,0:T(8,128)(2,1)S(1)}, bf16[128,512]{1,0:T(8,128)(2,1)S(1)}, u32[]{:S(2)}, u32[]{:S(2)}) collective-permute-start(bf16[128,512]{1,0:T(8,128)(2,1)S(1)} %broadcast_select_fusion.refs_1_), channel_id=1, source_target_pairs={{0,1},{1,0},{2,3},{3,2},{4,5},{5,4},{6,7},{7,6},{8,9},{9,8},{10,11... | collective-permute-start | bytes 393224 | tf_op jit(solution)/shard_map/ppermute | solution.py:337
  34.5 5.9 %collective-permute-start.20 = (bf16[128,512]{1,0:T(8,128)(2,1)S(1)}, bf16[128,512]{1,0:T(8,128)(2,1)S(1)}, u32[]{:S(2)}, u32[]{:S(2)}) collective-permute-start(bf16[128,512]{1,0:T(8,128)(2,1)S(1)} %collective-permute-done.9.refs_3_), channel_id=1, source_target_pairs={{0,4},{4,8},{8,12},{12,14},{14,10},{10,6},{6,2},{2,0},{1,5},{5,9},... | collective-permute-start | bytes 393224 | tf_op jit(solution)/shard_map/ppermute | solution.py:111
  36.7 5.8 %collective-permute-start.21 = (bf16[128,512]{1,0:T(8,128)(2,1)S(1)}, bf16[128,512]{1,0:T(8,128)(2,1)S(1)}, u32[]{:S(2)}, u32[]{:S(2)}) collective-permute-start(bf16[128,512]{1,0:T(8,128)(2,1)S(1)} %collective-permute-done.11.refs_4_), channel_id=1, source_target_pairs={{4,0},{8,4},{12,8},{14,12},{10,14},{6,10},{2,6},{0,2},{5,1},{9,5},... | collective-permute-start | bytes 393224 | tf_op jit(solution)/shard_map/ppermute | solution.py:112
  40.4 2.1 %collective-permute-start.23 = (bf16[128,512]{1,0:T(8,128)(2,1)S(1)}, bf16[128,512]{1,0:T(8,128)(2,1)S(1)}, u32[]{:S(2)}, u32[]{:S(2)}) collective-permute-start(bf16[128,512]{1,0:T(8,128)(2,1)S(1)} %collective-permute-done.20.refs_1_), channel_id=1, source_target_pairs={{0,1},{1,0},{2,3},{3,2},{4,5},{5,4},{6,7},{7,6},{8,9},{9,8},{10,11... | collective-permute-start | bytes 393224 | tf_op jit(solution)/shard_map/ppermute | solution.py:337
  42.5 1.3 %collective-permute-start.22 = (bf16[128,512]{1,0:T(8,128)(2,1)S(1)}, bf16[128,512]{1,0:T(8,128)(2,1)S(1)}, u32[]{:S(2)}, u32[]{:S(2)}) collective-permute-start(bf16[128,512]{1,0:T(8,128)(2,1)S(1)} %collective-permute-done.21.refs_1_), channel_id=1, source_target_pairs={{0,1},{1,0},{2,3},{3,2},{4,5},{5,4},{6,7},{7,6},{8,9},{9,8},{10,11... | collective-permute-start | bytes 393224 | tf_op jit(solution)/shard_map/ppermute | solution.py:337

commit v18 on v16

--- a/solution.py
+++ b/solution.py
@@ -348,7 +348,6 @@
         out, *late = ring.gather(acts, beside_second, beside_third)
         ahead, behind, corner, middle = late
         far = jnp.where(on_corner(n), corner, middle)
-        out, ahead = lax.optimization_barrier((out, ahead))
         out = add_tiles(out, (3, n // 2), (ahead, far))
         return add_tiles(out, (n - 3,), (behind,))[1]
     acts = encode_gathered(residual, enc_weight, enc_bias, threshold)

time: 42.3 us -> 43 us (1.017)
  the two profiles are of different devices: /device:TPU:0 before, /device:TPU:3 now
where the time goes in v18:
time: 43 us; the launch traced here: 42.5 us
  starting transfers between devices  26.2 us (61%)
  waiting for transfers between devices  9.73 us (23%)
  Pallas kernels  6.37 us (15%)
    ppermute x2, starting transfers between devices, gather(): corner = lax.ppermute(x, 'lat', self.across)  6.62 us
    ppermute x7, starting transfers between devices, add_tiles(): twins = [lax.ppermute(block, 'tok', swap) for block in blocks]  4.4 us
    pallas_call x4, Pallas kernels, tiles_of(): pl.pallas_call(functools.partial(tiles_kernel, tok_scale, n, hops, first)...  3.81 us
    ppermute x1, starting transfers between devices, body(): acts_twin = lax.ppermute(acts, 'tok', swap)  3.23 us
    ppermute x2, starting transfers between devices, gather(): lax.ppermute(jnp.where(odd, behind, ahead), ('lat', 'tok'), self.beside)  3.05 us
    ppermute x2, waiting for transfers between devices, gather(): ahead_3 = lax.ppermute(ahead_2, 'lat', self.forward)  2.82 us
    ppermute x2, starting transfers between devices, gather(): ahead_2 = lax.ppermute(ahead, 'lat', self.forward)  2.67 us
    ppermute x2, waiting for transfers between devices, gather(): behind_2 = lax.ppermute(behind, 'lat', self.backward)  2.6 us
  transfers between devices with their start and end apart: 24, of which 9 were waited for; matrix products, arithmetic and copies ran while one was open for 0% of the time, Pallas kernels for 11%

profile of v18, /device:TPU:3, one launch (start us, length us, event | category | flops | bytes accessed | tf_op | source)
XLA Modules:
  0.0 42.5 jit_solution(2203192887630235947)
XLA Ops:
  0.0 0.1 collective-permute-start
  0.1 1.5 %collective-permute-start.2 = (bf16[448,128]{1,0:T(8,128)(2,1)}, bf16[448,128]{1,0:T(8,128)(2,1)S(1)}, u32[]{:S(2)}, u32[]{:S(2)}) collective-permute-start(bf16[448,128]{1,0:T(8,128)(2,1)} %bitcast.6), channel_id=1, source_target_pairs={{4,0},{8,4},{12,8},{14,12},{10,14},{6,10},{2,6},{0,2},{5,1},{9,5},... | collective-permute-start | bytes 344072 | tf_op jit(solution)/shard_map/ppermute | solution.py:101
  1.5 3.3 %collective-permute-start.4 = (bf16[448,128]{1,0:T(8,128)(2,1)}, bf16[448,128]{1,0:T(8,128)(2,1)S(1)}, u32[]{:S(2)}, u32[]{:S(2)}) collective-permute-start(bf16[448,128]{1,0:T(8,128)(2,1)} %bitcast.7), channel_id=1, source_target_pairs={{0,14},{12,2},{14,0},{2,12},{4,6},{8,10},{10,8},{6,4},{1,15},{13,3... | collective-permute-start | bytes 344072 | tf_op jit(solution)/shard_map/ppermute | solution.py:102
  4.8 0.0 collective-permute-done.refs_0_
  4.8 1.2 %collective-permute-start.1 = (bf16[448,128]{1,0:T(8,128)(2,1)S(1)}, bf16[448,128]{1,0:T(8,128)(2,1)S(1)}, u32[]{:S(2)}, u32[]{:S(2)}) collective-permute-start(bf16[448,128]{1,0:T(8,128)(2,1)S(1)} %collective-permute-done.refs_0_), channel_id=1, source_target_pairs={{0,4},{4,8},{8,12},{12,14},{14,10},{10,6},{6,2},{2,0},{1,5},{5,9},... | collective-permute-start | bytes 344072 | tf_op jit(solution)/shard_map/ppermute | solution.py:103
  6.0 0.0 collective-permute-done.2.refs_1_
  6.0 0.3 collective-permute-start.3
  6.3 2.1 %collective-permute-start.7 = (bf16[448,128]{1,0:T(8,128)(2,1)S(1)}, bf16[448,128]{1,0:T(8,128)(2,1)S(1)}, u32[]{:S(2)}, u32[]{:S(2)}) collective-permute-start(bf16[448,128]{1,0:T(8,128)(2,1)S(1)} %broadcast_select_fusion.2), channel_id=1, source_target_pairs={{4,6},{5,7},{8,10},{9,11},{10,8},{11,9},{6,4},{7,5},{0,1},{1,0},{1... | collective-permute-start | bytes 344072 | tf_op jit(solution)/shard_map/ppermute | solution.py:106
  8.5 1.0 %collective-permute-done.4.x_corner = bf16[448,128]{1,0:T(8,128)(2,1)S(1)} collective-permute-done((bf16[448,128]{1,0:T(8,128)(2,1)}, bf16[448,128]{1,0:T(8,128)(2,1)S(1)}, u32[]{:S(2)}, u32[]{:S(2)}) %collective-permute-start.4) | collective-permute-done | bytes 114720 | tf_op jit(solution)/shard_map/ppermute | solution.py:102
  9.4 1.6 %collective-permute-done.1.refs_2_ = bf16[448,128]{1,0:T(8,128)(2,1)S(1)} collective-permute-done((bf16[448,128]{1,0:T(8,128)(2,1)S(1)}, bf16[448,128]{1,0:T(8,128)(2,1)S(1)}, u32[]{:S(2)}, u32[]{:S(2)}) %collective-permute-start.1) | collective-permute-done | bytes 114720 | tf_op jit(solution)/shard_map/ppermute | solution.py:103
  11.0 0.5 %collective-permute-done.3.refs_3_ = bf16[448,128]{1,0:T(8,128)(2,1)S(1)} collective-permute-done((bf16[448,128]{1,0:T(8,128)(2,1)S(1)}, bf16[448,128]{1,0:T(8,128)(2,1)S(1)}, u32[]{:S(2)}, u32[]{:S(2)}) %collective-permute-start.3) | collective-permute-done | bytes 114720 | tf_op jit(solution)/shard_map/ppermute | solution.py:104
  11.6 0.7 %collective-permute-start.5 = (bf16[448,128]{1,0:T(8,128)(2,1)S(1)}, bf16[448,128]{1,0:T(8,128)(2,1)S(1)}, u32[]{:S(2)}, u32[]{:S(2)}) collective-permute-start(bf16[448,128]{1,0:T(8,128)(2,1)S(1)} %collective-permute-done.1.refs_2_), channel_id=1, source_target_pairs={{0,4},{4,8},{8,12},{12,14},{14,10},{10,6},{6,2},{2,0},{1,5},{5,9},... | collective-permute-start | bytes 344072 | tf_op jit(solution)/shard_map/ppermute | solution.py:111
  12.2 0.8 %collective-permute-start.6 = (bf16[448,128]{1,0:T(8,128)(2,1)S(1)}, bf16[448,128]{1,0:T(8,128)(2,1)S(1)}, u32[]{:S(2)}, u32[]{:S(2)}) collective-permute-start(bf16[448,128]{1,0:T(8,128)(2,1)S(1)} %collective-permute-done.3.refs_3_), channel_id=1, source_target_pairs={{4,0},{8,4},{12,8},{14,12},{10,14},{6,10},{2,6},{0,2},{5,1},{9,5},... | collective-permute-start | bytes 344072 | tf_op jit(solution)/shard_map/ppermute | solution.py:112
  13.1 2.1 %shard_map.55 = (f32[128,512]{1,0:T(8,128)S(1)}, bf16[4,448,512]{2,1,0:T(8,128)(2,1)S(1)}) custom-call(bf16[448,128]{1,0:T(8,128)(2,1)S(1)} %collective-permute-done.refs_0_, bf16[448,128]{1,0:T(8,128)(2,1)S(1)} %collective-permute-done.2.refs_1_, bf16[448,128]{1,0:T(8,128)(2,1)S(1)} %collective-permute-done.1.refs_2_, ...), custom_call_target="tpu_custom_call" | custom-call | flops 234881024 | bytes 2818048 | tf_op jit(solution)/shard_map/pallas_call | solution.py:128
  15.1 0.1 collective-permute-done.5.x_f
  15.2 0.7 %collective-permute-done.6.x_b = bf16[448,128]{1,0:T(8,128)(2,1)S(1)} collective-permute-done((bf16[448,128]{1,0:T(8,128)(2,1)S(1)}, bf16[448,128]{1,0:T(8,128)(2,1)S(1)}, u32[]{:S(2)}, u32[]{:S(2)}) %collective-permute-start.6) | collective-permute-done | bytes 114720 | tf_op jit(solution)/shard_map/ppermute | solution.py:112
  15.9 0.5 %shard_map.56.refs_0_ = bf16[128,512]{1,0:T(8,128)(2,1)S(1)} custom-call(bf16[448,128]{1,0:T(8,128)(2,1)S(1)} %bitcast.8, bf16[448,128]{1,0:T(8,128)(2,1)S(1)} %collective-permute-done.5.x_f, bf16[448,128]{1,0:T(8,128)(2,1)S(1)} %collective-permute-done.6.x_b, bf16[448,128]{1,0:T(8,128)(2,1)S(1)} %collective-permute-done.4.x_corner, ...), custom_call_target="tpu_custom_call" | custom-call | flops 234881024 | bytes 2818048 | tf_op jit(solution)/shard_map/pallas_call | solution.py:143
  16.4 1.1 %collective-permute-start.10 = (bf16[128,512]{1,0:T(8,128)(2,1)S(1)}, bf16[128,512]{1,0:T(8,128)(2,1)S(1)}, u32[]{:S(2)}, u32[]{:S(2)}) collective-permute-start(bf16[128,512]{1,0:T(8,128)(2,1)S(1)} %shard_map.56.refs_0_), channel_id=1, source_target_pairs={{4,0},{8,4},{12,8},{14,12},{10,14},{6,10},{2,6},{0,2},{5,1},{9,5},... | collective-permute-start | bytes 393224 | tf_op jit(solution)/shard_map/ppermute | solution.py:101
  17.5 0.4 collective-permute-start.8
  17.9 3.2 %collective-permute-start.13 = (bf16[128,512]{1,0:T(8,128)(2,1)S(1)}, bf16[128,512]{1,0:T(8,128)(2,1)S(1)}, u32[]{:S(2)}, u32[]{:S(2)}) collective-permute-start(bf16[128,512]{1,0:T(8,128)(2,1)S(1)} %shard_map.56.refs_0_), channel_id=1, source_target_pairs={{0,1},{1,0},{2,3},{3,2},{4,5},{5,4},{6,7},{7,6},{8,9},{9,8},{10,11... | collective-permute-start | bytes 393224 | tf_op jit(solution)/shard_map/ppermute | solution.py:334
  21.2 3.3 %collective-permute-start.12 = (bf16[128,512]{1,0:T(8,128)(2,1)S(1)}, bf16[128,512]{1,0:T(8,128)(2,1)S(1)}, u32[]{:S(2)}, u32[]{:S(2)}) collective-permute-start(bf16[128,512]{1,0:T(8,128)(2,1)S(1)} %shard_map.56.refs_0_), channel_id=1, source_target_pairs={{0,14},{12,2},{14,0},{2,12},{4,6},{8,10},{10,8},{6,4},{1,15},{13,3... | collective-permute-start | bytes 393224 | tf_op jit(solution)/shard_map/ppermute | solution.py:102
  24.5 0.0 collective-permute-done.10.refs_2_
  24.5 0.0 collective-permute-start.11
  24.5 0.0 collective-permute-done.8.refs_1_
  24.5 1.5 %collective-permute-start.9 = (bf16[128,512]{1,0:T(8,128)(2,1)S(1)}, bf16[128,512]{1,0:T(8,128)(2,1)S(1)}, u32[]{:S(2)}, u32[]{:S(2)}) collective-permute-start(bf16[128,512]{1,0:T(8,128)(2,1)S(1)} %collective-permute-done.8.refs_1_), channel_id=1, source_target_pairs={{0,4},{4,8},{8,12},{12,14},{14,10},{10,6},{6,2},{2,0},{1,5},{5,9},... | collective-permute-start | bytes 393224 | tf_op jit(solution)/shard_map/ppermute | solution.py:103
  26.0 0.9 %collective-permute-start.14 = (bf16[128,512]{1,0:T(8,128)(2,1)S(1)}, bf16[128,512]{1,0:T(8,128)(2,1)S(1)}, u32[]{:S(2)}, u32[]{:S(2)}) collective-permute-start(bf16[128,512]{1,0:T(8,128)(2,1)S(1)} %broadcast_select_fusion.1), channel_id=1, source_target_pairs={{4,6},{5,7},{8,10},{9,11},{10,8},{11,9},{6,4},{7,5},{0,1},{1,0},{1... | collective-permute-start | bytes 393224 | tf_op jit(solution)/shard_map/ppermute | solution.py:106
  26.9 0.1 collective-permute-start.20
  27.0 1.1 %shard_map.57 = (bf16[256,256]{1,0:T(8,128)(2,1)S(1)}, bf16[1,4,256,512]{3,2,1,0:T(8,128)(2,1)}) custom-call(s32[4,8]{1,0:T(4,128)S(1)} %bitcast.9, bf16[128,512]{1,0:T(8,128)(2,1)S(1)} %shard_map.56.refs_0_, bf16[128,512]{1,0:T(8,128)(2,1)S(1)} %collective-permute-done.13.refs_1_), custom_call_target="tpu_custom_call" | custom-call | tf_op jit(solution)/shard_map/pallas_call | solution.py:302
  28.1 1.0 %collective-permute-done.12 = bf16[128,512]{1,0:T(8,128)(2,1)S(1)} collective-permute-done((bf16[128,512]{1,0:T(8,128)(2,1)S(1)}, bf16[128,512]{1,0:T(8,128)(2,1)S(1)}, u32[]{:S(2)}, u32[]{:S(2)}) %collective-permute-start.12) | collective-permute-done | bytes 131104 | tf_op jit(solution)/shard_map/ppermute | solution.py:102
  29.1 1.2 %collective-permute-start.21 = (bf16[128,512]{1,0:T(8,128)(2,1)S(1)}, bf16[128,512]{1,0:T(8,128)(2,1)S(1)}, u32[]{:S(2)}, u32[]{:S(2)}) collective-permute-start(bf16[128,512]{1,0:T(8,128)(2,1)S(1)} %collective-permute-done.10.refs_2_), channel_id=1, source_target_pairs={{0,1},{1,0},{2,3},{3,2},{4,5},{5,4},{6,7},{7,6},{8,9},{9,8},{10,11... | collective-permute-start | bytes 393224 | tf_op jit(solution)/shard_map/ppermute | solution.py:337
  30.2 2.1 %collective-permute-done.11.refs_4_ = bf16[128,512]{1,0:T(8,128)(2,1)S(1)} collective-permute-done((bf16[128,512]{1,0:T(8,128)(2,1)S(1)}, bf16[128,512]{1,0:T(8,128)(2,1)S(1)}, u32[]{:S(2)}, u32[]{:S(2)}) %collective-permute-start.11) | collective-permute-done | bytes 131104 | tf_op jit(solution)/shard_map/ppermute | solution.py:104
  32.3 0.5 %collective-permute-start.22 = (bf16[128,512]{1,0:T(8,128)(2,1)S(1)}, bf16[128,512]{1,0:T(8,128)(2,1)S(1)}, u32[]{:S(2)}, u32[]{:S(2)}) collective-permute-start(bf16[128,512]{1,0:T(8,128)(2,1)S(1)} %collective-permute-done.9.refs_3_), channel_id=1, source_target_pairs={{0,1},{1,0},{2,3},{3,2},{4,5},{5,4},{6,7},{7,6},{8,9},{9,8},{10,11... | collective-permute-start | bytes 393224 | tf_op jit(solution)/shard_map/ppermute | solution.py:337
  32.8 0.8 %collective-permute-start.17 = (bf16[128,512]{1,0:T(8,128)(2,1)S(1)}, bf16[128,512]{1,0:T(8,128)(2,1)S(1)}, u32[]{:S(2)}, u32[]{:S(2)}) collective-permute-start(bf16[128,512]{1,0:T(8,128)(2,1)S(1)} %collective-permute-done.9.refs_3_), channel_id=1, source_target_pairs={{0,4},{4,8},{8,12},{12,14},{14,10},{10,6},{6,2},{2,0},{1,5},{5,9},... | collective-permute-start | bytes 393224 | tf_op jit(solution)/shard_map/ppermute | solution.py:111
  33.5 0.0 collective-permute-done.14
  33.5 0.3 collective-permute-start.23
  33.8 0.0 collective-permute-done.20.refs_5_
  33.9 0.7 %collective-permute-start.15 = (bf16[128,512]{1,0:T(8,128)(2,1)S(1)}, bf16[128,512]{1,0:T(8,128)(2,1)S(1)}, u32[]{:S(2)}, u32[]{:S(2)}) collective-permute-start(bf16[128,512]{1,0:T(8,128)(2,1)S(1)} %collective-permute-done.11.refs_4_), channel_id=1, source_target_pairs={{4,0},{8,4},{12,8},{14,12},{10,14},{6,10},{2,6},{0,2},{5,1},{9,5},... | collective-permute-start | bytes 393224 | tf_op jit(solution)/shard_map/ppermute | solution.py:112
  34.6 0.5 %collective-permute-start.19 = (bf16[128,512]{1,0:T(8,128)(2,1)S(1)}, bf16[128,512]{1,0:T(8,128)(2,1)S(1)}, u32[]{:S(2)}, u32[]{:S(2)}) collective-permute-start(bf16[128,512]{1,0:T(8,128)(2,1)S(1)} %broadcast_select_fusion.refs_2_), channel_id=1, source_target_pairs={{0,1},{1,0},{2,3},{3,2},{4,5},{5,4},{6,7},{7,6},{8,9},{9,8},{10,11... | collective-permute-start | bytes 393224 | tf_op jit(solution)/shard_map/ppermute | solution.py:337
  35.1 2.7 %collective-permute-done.17.refs_1_ = bf16[128,512]{1,0:T(8,128)(2,1)S(1)} collective-permute-done((bf16[128,512]{1,0:T(8,128)(2,1)S(1)}, bf16[128,512]{1,0:T(8,128)(2,1)S(1)}, u32[]{:S(2)}, u32[]{:S(2)}) %collective-permute-start.17) | collective-permute-done | bytes 131104 | tf_op jit(solution)/shard_map/ppermute | solution.py:111
  37.9 0.8 %collective-permute-start.18 = (bf16[128,512]{1,0:T(8,128)(2,1)S(1)}, bf16[128,512]{1,0:T(8,128)(2,1)S(1)}, u32[]{:S(2)}, u32[]{:S(2)}) collective-permute-start(bf16[128,512]{1,0:T(8,128)(2,1)S(1)} %collective-permute-done.17.refs_1_), channel_id=1, source_target_pairs={{0,1},{1,0},{2,3},{3,2},{4,5},{5,4},{6,7},{7,6},{8,9},{9,8},{10,11... | collective-permute-start | bytes 393224 | tf_op jit(solution)/shard_map/ppermute | solution.py:337
  38.7 0.1 collective-permute-done.15.refs_1_
  38.7 1.0 %collective-permute-start.16 = (bf16[128,512]{1,0:T(8,128)(2,1)S(1)}, bf16[128,512]{1,0:T(8,128)(2,1)S(1)}, u32[]{:S(2)}, u32[]{:S(2)}) collective-permute-start(bf16[128,512]{1,0:T(8,128)(2,1)S(1)} %collective-permute-done.15.refs_1_), channel_id=1, source_target_pairs={{0,1},{1,0},{2,3},{3,2},{4,5},{5,4},{6,7},{7,6},{8,9},{9,8},{10,11... | collective-permute-start | bytes 393224 | tf_op jit(solution)/shard_map/ppermute | solution.py:337
  39.8 0.0 collective-permute-done.22.refs_7_
  39.8 0.0 collective-permute-done.23.refs_8_
  39.8 1.4 %shard_map.58.refs_5_ = bf16[1,4,256,512]{3,2,1,0:T(8,128)(2,1)} custom-call(s32[4,8]{1,0:T(4,128)S(1)} %bitcast.10, bf16[256,256]{1,0:T(8,128)(2,1)S(1)} %get-tuple-element.29.refs_0_, bf16[128,512]{1,0:T(8,128)(2,1)S(1)} %collective-permute-done.8.refs_1_, bf16[128,512]{1,0:T(8,128)(2,1)S(1)} %collective-permute-done.10.refs_2_, ...), custom_call_target="tpu_custom_call", output_to_operand_aliasing={{}: (10, {})} | custom-call | flops 268435456 | bytes 2097152 | tf_op jit(solution)/shard_map/pallas_call | solution.py:302
  41.2 0.0 collective-permute-done.18.refs_3_
  41.2 0.2 shard_map.59.refs_3_
  41.4 1.1 %shard_map.60 = bf16[1,4,256,512]{3,2,1,0:T(8,128)(2,1)} custom-call(s32[4,8]{1,0:T(4,128)S(1)} %bitcast.12, bf16[256,256]{1,0:T(8,128)(2,1)S(1)} %get-tuple-element.29.refs_0_, bf16[128,512]{1,0:T(8,128)(2,1)S(1)} %collective-permute-done.15.refs_1_, bf16[128,512]{1,0:T(8,128)(2,1)S(1)} %collective-permute-done.16.refs_2_, ...), custom_call_target="tpu_custom_call", output_to_operand_aliasing={{}: (4, {})} | custom-call | flops 67108864 | bytes 524288 | tf_op jit(solution)/shard_map/pallas_call | solution.py:302
  (17 shorter events, 0.1 us)
Async XLA Ops:
  0.0 15.9 %copy-start = (bf16[128,448]{0,1:T(8,128)(2,1)S(1)}, bf16[128,448]{0,1:T(8,128)(2,1)}, u32[]{:S(2)}) copy-start(bf16[128,448]{0,1:T(8,128)(2,1)} %param.5) | copy-start | bytes 344068
  0.0 15.9 %copy-start.2 = (f32[512]{0:T(512)S(1)}, f32[512]{0:T(512)}, u32[]{:S(2)}) copy-start(f32[512]{0:T(512)} %param.7) | copy-start | bytes 6148
  0.0 15.9 %copy-start.3 = (f32[512]{0:T(512)S(1)}, f32[512]{0:T(512)}, u32[]{:S(2)}) copy-start(f32[512]{0:T(512)} %param.8) | copy-start | bytes 6148
  0.0 4.8 %collective-permute-start = (bf16[448,128]{1,0:T(8,128)(2,1)}, bf16[448,128]{1,0:T(8,128)(2,1)S(1)}, u32[]{:S(2)}, u32[]{:S(2)}) collective-permute-start(bf16[448,128]{1,0:T(8,128)(2,1)} %bitcast.5), channel_id=1, source_target_pairs={{0,4},{4,8},{8,12},{12,14},{14,10},{10,6},{6,2},{2,0},{1,5},{5,9},... | collective-permute-start | bytes 344072 | tf_op jit(solution)/shard_map/ppermute | solution.py:100
  0.1 6.0 %collective-permute-start.2 = (bf16[448,128]{1,0:T(8,128)(2,1)}, bf16[448,128]{1,0:T(8,128)(2,1)S(1)}, u32[]{:S(2)}, u32[]{:S(2)}) collective-permute-start(bf16[448,128]{1,0:T(8,128)(2,1)} %bitcast.6), channel_id=1, source_target_pairs={{4,0},{8,4},{12,8},{14,12},{10,14},{6,10},{2,6},{0,2},{5,1},{9,5},... | collective-permute-start | bytes 344072 | tf_op jit(solution)/shard_map/ppermute | solution.py:101
  1.5 7.9 %collective-permute-start.4 = (bf16[448,128]{1,0:T(8,128)(2,1)}, bf16[448,128]{1,0:T(8,128)(2,1)S(1)}, u32[]{:S(2)}, u32[]{:S(2)}) collective-permute-start(bf16[448,128]{1,0:T(8,128)(2,1)} %bitcast.7), channel_id=1, source_target_pairs={{0,14},{12,2},{14,0},{2,12},{4,6},{8,10},{10,8},{6,4},{1,15},{13,3... | collective-permute-start | bytes 344072 | tf_op jit(solution)/shard_map/ppermute | solution.py:102
  4.8 6.2 %collective-permute-start.1 = (bf16[448,128]{1,0:T(8,128)(2,1)S(1)}, bf16[448,128]{1,0:T(8,128)(2,1)S(1)}, u32[]{:S(2)}, u32[]{:S(2)}) collective-permute-start(bf16[448,128]{1,0:T(8,128)(2,1)S(1)} %collective-permute-done.refs_0_), channel_id=1, source_target_pairs={{0,4},{4,8},{8,12},{12,14},{14,10},{10,6},{6,2},{2,0},{1,5},{5,9},... | collective-permute-start | bytes 344072 | tf_op jit(solution)/shard_map/ppermute | solution.py:103
  6.0 5.5 %collective-permute-start.3 = (bf16[448,128]{1,0:T(8,128)(2,1)S(1)}, bf16[448,128]{1,0:T(8,128)(2,1)S(1)}, u32[]{:S(2)}, u32[]{:S(2)}) collective-permute-start(bf16[448,128]{1,0:T(8,128)(2,1)S(1)} %collective-permute-done.2.refs_1_), channel_id=1, source_target_pairs={{4,0},{8,4},{12,8},{14,12},{10,14},{6,10},{2,6},{0,2},{5,1},{9,5},... | collective-permute-start | bytes 344072 | tf_op jit(solution)/shard_map/ppermute | solution.py:104
  6.3 6.7 %collective-permute-start.7 = (bf16[448,128]{1,0:T(8,128)(2,1)S(1)}, bf16[448,128]{1,0:T(8,128)(2,1)S(1)}, u32[]{:S(2)}, u32[]{:S(2)}) collective-permute-start(bf16[448,128]{1,0:T(8,128)(2,1)S(1)} %broadcast_select_fusion.2), channel_id=1, source_target_pairs={{4,6},{5,7},{8,10},{9,11},{10,8},{11,9},{6,4},{7,5},{0,1},{1,0},{1... | collective-permute-start | bytes 344072 | tf_op jit(solution)/shard_map/ppermute | solution.py:106
  11.6 3.6 %collective-permute-start.5 = (bf16[448,128]{1,0:T(8,128)(2,1)S(1)}, bf16[448,128]{1,0:T(8,128)(2,1)S(1)}, u32[]{:S(2)}, u32[]{:S(2)}) collective-permute-start(bf16[448,128]{1,0:T(8,128)(2,1)S(1)} %collective-permute-done.1.refs_2_), channel_id=1, source_target_pairs={{0,4},{4,8},{8,12},{12,14},{14,10},{10,6},{6,2},{2,0},{1,5},{5,9},... | collective-permute-start | bytes 344072 | tf_op jit(solution)/shard_map/ppermute | solution.py:111
  12.2 3.6 %collective-permute-start.6 = (bf16[448,128]{1,0:T(8,128)(2,1)S(1)}, bf16[448,128]{1,0:T(8,128)(2,1)S(1)}, u32[]{:S(2)}, u32[]{:S(2)}) collective-permute-start(bf16[448,128]{1,0:T(8,128)(2,1)S(1)} %collective-permute-done.3.refs_3_), channel_id=1, source_target_pairs={{4,0},{8,4},{12,8},{14,12},{10,14},{6,10},{2,6},{0,2},{5,1},{9,5},... | collective-permute-start | bytes 344072 | tf_op jit(solution)/shard_map/ppermute | solution.py:112
  13.1 13.9 %copy-start.1 = (s32[8,4]{0,1:T(4,128)S(1)}, s32[8,4]{0,1:T(4,128)}, u32[]{:S(2)}) copy-start(s32[8,4]{0,1:T(4,128)} %param.9) | copy-start | bytes 388
  16.4 8.1 %collective-permute-start.10 = (bf16[128,512]{1,0:T(8,128)(2,1)S(1)}, bf16[128,512]{1,0:T(8,128)(2,1)S(1)}, u32[]{:S(2)}, u32[]{:S(2)}) collective-permute-start(bf16[128,512]{1,0:T(8,128)(2,1)S(1)} %shard_map.56.refs_0_), channel_id=1, source_target_pairs={{4,0},{8,4},{12,8},{14,12},{10,14},{6,10},{2,6},{0,2},{5,1},{9,5},... | collective-permute-start | bytes 393224 | tf_op jit(solution)/shard_map/ppermute | solution.py:101
  17.5 6.9 %collective-permute-start.8 = (bf16[128,512]{1,0:T(8,128)(2,1)S(1)}, bf16[128,512]{1,0:T(8,128)(2,1)S(1)}, u32[]{:S(2)}, u32[]{:S(2)}) collective-permute-start(bf16[128,512]{1,0:T(8,128)(2,1)S(1)} %shard_map.56.refs_0_), channel_id=1, source_target_pairs={{0,4},{4,8},{8,12},{12,14},{14,10},{10,6},{6,2},{2,0},{1,5},{5,9},... | collective-permute-start | bytes 393224 | tf_op jit(solution)/shard_map/ppermute | solution.py:100
  17.9 9.0 %collective-permute-start.13 = (bf16[128,512]{1,0:T(8,128)(2,1)S(1)}, bf16[128,512]{1,0:T(8,128)(2,1)S(1)}, u32[]{:S(2)}, u32[]{:S(2)}) collective-permute-start(bf16[128,512]{1,0:T(8,128)(2,1)S(1)} %shard_map.56.refs_0_), channel_id=1, source_target_pairs={{0,1},{1,0},{2,3},{3,2},{4,5},{5,4},{6,7},{7,6},{8,9},{9,8},{10,11... | collective-permute-start | bytes 393224 | tf_op jit(solution)/shard_map/ppermute | solution.py:334
  21.2 7.9 %collective-permute-start.12 = (bf16[128,512]{1,0:T(8,128)(2,1)S(1)}, bf16[128,512]{1,0:T(8,128)(2,1)S(1)}, u32[]{:S(2)}, u32[]{:S(2)}) collective-permute-start(bf16[128,512]{1,0:T(8,128)(2,1)S(1)} %shard_map.56.refs_0_), channel_id=1, source_target_pairs={{0,14},{12,2},{14,0},{2,12},{4,6},{8,10},{10,8},{6,4},{1,15},{13,3... | collective-permute-start | bytes 393224 | tf_op jit(solution)/shard_map/ppermute | solution.py:102
  24.5 7.8 %collective-permute-start.11 = (bf16[128,512]{1,0:T(8,128)(2,1)S(1)}, bf16[128,512]{1,0:T(8,128)(2,1)S(1)}, u32[]{:S(2)}, u32[]{:S(2)}) collective-permute-start(bf16[128,512]{1,0:T(8,128)(2,1)S(1)} %collective-permute-done.10.refs_2_), channel_id=1, source_target_pairs={{4,0},{8,4},{12,8},{14,12},{10,14},{6,10},{2,6},{0,2},{5,1},{9,5},... | collective-permute-start | bytes 393224 | tf_op jit(solution)/shard_map/ppermute | solution.py:104
  24.5 7.8 %collective-permute-start.9 = (bf16[128,512]{1,0:T(8,128)(2,1)S(1)}, bf16[128,512]{1,0:T(8,128)(2,1)S(1)}, u32[]{:S(2)}, u32[]{:S(2)}) collective-permute-start(bf16[128,512]{1,0:T(8,128)(2,1)S(1)} %collective-permute-done.8.refs_1_), channel_id=1, source_target_pairs={{0,4},{4,8},{8,12},{12,14},{14,10},{10,6},{6,2},{2,0},{1,5},{5,9},... | collective-permute-start | bytes 393224 | tf_op jit(solution)/shard_map/ppermute | solution.py:103
  26.0 7.6 %collective-permute-start.14 = (bf16[128,512]{1,0:T(8,128)(2,1)S(1)}, bf16[128,512]{1,0:T(8,128)(2,1)S(1)}, u32[]{:S(2)}, u32[]{:S(2)}) collective-permute-start(bf16[128,512]{1,0:T(8,128)(2,1)S(1)} %broadcast_select_fusion.1), channel_id=1, source_target_pairs={{4,6},{5,7},{8,10},{9,11},{10,8},{11,9},{6,4},{7,5},{0,1},{1,0},{1... | collective-permute-start | bytes 393224 | tf_op jit(solution)/shard_map/ppermute | solution.py:106
  26.9 7.0 %collective-permute-start.20 = (bf16[128,512]{1,0:T(8,128)(2,1)S(1)}, bf16[128,512]{1,0:T(8,128)(2,1)S(1)}, u32[]{:S(2)}, u32[]{:S(2)}) collective-permute-start(bf16[128,512]{1,0:T(8,128)(2,1)S(1)} %collective-permute-done.8.refs_1_), channel_id=1, source_target_pairs={{0,1},{1,0},{2,3},{3,2},{4,5},{5,4},{6,7},{7,6},{8,9},{9,8},{10,11... | collective-permute-start | bytes 393224 | tf_op jit(solution)/shard_map/ppermute | solution.py:337
  29.1 5.5 %collective-permute-start.21 = (bf16[128,512]{1,0:T(8,128)(2,1)S(1)}, bf16[128,512]{1,0:T(8,128)(2,1)S(1)}, u32[]{:S(2)}, u32[]{:S(2)}) collective-permute-start(bf16[128,512]{1,0:T(8,128)(2,1)S(1)} %collective-permute-done.10.refs_2_), channel_id=1, source_target_pairs={{0,1},{1,0},{2,3},{3,2},{4,5},{5,4},{6,7},{7,6},{8,9},{9,8},{10,11... | collective-permute-start | bytes 393224 | tf_op jit(solution)/shard_map/ppermute | solution.py:337
  32.3 7.5 %collective-permute-start.22 = (bf16[128,512]{1,0:T(8,128)(2,1)S(1)}, bf16[128,512]{1,0:T(8,128)(2,1)S(1)}, u32[]{:S(2)}, u32[]{:S(2)}) collective-permute-start(bf16[128,512]{1,0:T(8,128)(2,1)S(1)} %collective-permute-done.9.refs_3_), channel_id=1, source_target_pairs={{0,1},{1,0},{2,3},{3,2},{4,5},{5,4},{6,7},{7,6},{8,9},{9,8},{10,11... | collective-permute-start | bytes 393224 | tf_op jit(solution)/shard_map/ppermute | solution.py:337
  32.8 5.1 %collective-permute-start.17 = (bf16[128,512]{1,0:T(8,128)(2,1)S(1)}, bf16[128,512]{1,0:T(8,128)(2,1)S(1)}, u32[]{:S(2)}, u32[]{:S(2)}) collective-permute-start(bf16[128,512]{1,0:T(8,128)(2,1)S(1)} %collective-permute-done.9.refs_3_), channel_id=1, source_target_pairs={{0,4},{4,8},{8,12},{12,14},{14,10},{10,6},{6,2},{2,0},{1,5},{5,9},... | collective-permute-start | bytes 393224 | tf_op jit(solution)/shard_map/ppermute | solution.py:111
  33.5 6.2 %collective-permute-start.23 = (bf16[128,512]{1,0:T(8,128)(2,1)S(1)}, bf16[128,512]{1,0:T(8,128)(2,1)S(1)}, u32[]{:S(2)}, u32[]{:S(2)}) collective-permute-start(bf16[128,512]{1,0:T(8,128)(2,1)S(1)} %collective-permute-done.11.refs_4_), channel_id=1, source_target_pairs={{0,1},{1,0},{2,3},{3,2},{4,5},{5,4},{6,7},{7,6},{8,9},{9,8},{10,11... | collective-permute-start | bytes 393224 | tf_op jit(solution)/shard_map/ppermute | solution.py:337
  33.9 4.9 %collective-permute-start.15 = (bf16[128,512]{1,0:T(8,128)(2,1)S(1)}, bf16[128,512]{1,0:T(8,128)(2,1)S(1)}, u32[]{:S(2)}, u32[]{:S(2)}) collective-permute-start(bf16[128,512]{1,0:T(8,128)(2,1)S(1)} %collective-permute-done.11.refs_4_), channel_id=1, source_target_pairs={{4,0},{8,4},{12,8},{14,12},{10,14},{6,10},{2,6},{0,2},{5,1},{9,5},... | collective-permute-start | bytes 393224 | tf_op jit(solution)/shard_map/ppermute | solution.py:112
  34.6 6.6 %collective-permute-start.19 = (bf16[128,512]{1,0:T(8,128)(2,1)S(1)}, bf16[128,512]{1,0:T(8,128)(2,1)S(1)}, u32[]{:S(2)}, u32[]{:S(2)}) collective-permute-start(bf16[128,512]{1,0:T(8,128)(2,1)S(1)} %broadcast_select_fusion.refs_2_), channel_id=1, source_target_pairs={{0,1},{1,0},{2,3},{3,2},{4,5},{5,4},{6,7},{7,6},{8,9},{9,8},{10,11... | collective-permute-start | bytes 393224 | tf_op jit(solution)/shard_map/ppermute | solution.py:337
  37.9 3.3 %collective-permute-start.18 = (bf16[128,512]{1,0:T(8,128)(2,1)S(1)}, bf16[128,512]{1,0:T(8,128)(2,1)S(1)}, u32[]{:S(2)}, u32[]{:S(2)}) collective-permute-start(bf16[128,512]{1,0:T(8,128)(2,1)S(1)} %collective-permute-done.17.refs_1_), channel_id=1, source_target_pairs={{0,1},{1,0},{2,3},{3,2},{4,5},{5,4},{6,7},{7,6},{8,9},{9,8},{10,11... | collective-permute-start | bytes 393224 | tf_op jit(solution)/shard_map/ppermute | solution.py:337
  38.7 2.7 %collective-permute-start.16 = (bf16[128,512]{1,0:T(8,128)(2,1)S(1)}, bf16[128,512]{1,0:T(8,128)(2,1)S(1)}, u32[]{:S(2)}, u32[]{:S(2)}) collective-permute-start(bf16[128,512]{1,0:T(8,128)(2,1)S(1)} %collective-permute-done.15.refs_1_), channel_id=1, source_target_pairs={{0,1},{1,0},{2,3},{3,2},{4,5},{5,4},{6,7},{7,6},{8,9},{9,8},{10,11... | collective-permute-start | bytes 393224 | tf_op jit(solution)/shard_map/ppermute | solution.py:337

commit v19 on v16

--- a/solution.py
+++ b/solution.py
@@ -237,7 +237,7 @@
     blocks, twins = refs[:count], refs[count : 2 * count]
     out, tiles, sems = refs[-3:]
     rows, width = tiles.shape[1:]
-    half = rows // 2
+    half = rows
     slots = partners.shape[0]
     if is_first:
         columns = pl.ds(pl.multiple_of(lax.axis_index("tok") * rows, rows), rows)
@@ -248,7 +248,7 @@
 
     def send(place, slot, when, pair):
         both = []
-        for i in range(2):
+        for i in range(1):
             part = pl.ds(i * half, half)
             sem = sems.at[len(copies), i]
             both.append(
@@ -260,7 +260,7 @@
         def _():
             if pair is not None:
                 right = jnp.concatenate([pair[0][...], pair[1][...]], axis=0)
-            for i in range(2):
+            for i in range(1):
                 part = pl.ds(i * half, half)
                 if pair is not None:
                     tile = jnp.dot(left[part, :], right, preferred_element_type=jnp.float32)

time: 42.3 us -> 41.9 us (level)
  Pallas kernels: 4.62 us -> 5.46 us
  waiting for transfers between devices: 14.8 us -> 14 us
    ppermute x2, waiting for transfers between devices: 3.91 us -> 3 us  [gather(): ahead_3 = lax.ppermute(ahead_2, 'lat', self.forward)]
    pallas_call x4, Pallas kernels: 2.06 us -> 2.9 us  [tiles_of(): pl.pallas_call(functools.partial(tiles_kernel, tok_scale, n, hops, first)...]
  transfers between devices with their start and end apart: 24 -> 24, of which waited for: 11 -> 11; matrix products, arithmetic and copies ran while one was open for 0% -> 0% of each run, Pallas kernels for 9% -> 11%
where the time goes in v19:
time: 41.9 us; the launch traced here: 41.7 us
  starting transfers between devices  22.1 us (53%)
  waiting for transfers between devices  14 us (33%)
  Pallas kernels  5.46 us (13%)
    ppermute x2, starting transfers between devices, gather(): corner = lax.ppermute(x, 'lat', self.across)  7.48 us
    ppermute x2, waiting for transfers between devices, gather(): corner = lax.ppermute(x, 'lat', self.across)  4.82 us
    ppermute x2, starting transfers between devices, gather(): ahead = lax.ppermute(x, 'lat', self.forward)  4.19 us
    ppermute x2, starting transfers between devices, gather(): behind_2 = lax.ppermute(behind, 'lat', self.backward)  3.51 us
    ppermute x2, waiting for transfers between devices, gather(): ahead_3 = lax.ppermute(ahead_2, 'lat', self.forward)  3 us
    pallas_call x4, Pallas kernels, tiles_of(): pl.pallas_call(functools.partial(tiles_kernel, tok_scale, n, hops, first)...  2.9 us
    ppermute x2, starting transfers between devices, gather(): behind_3 = lax.ppermute(behind_2, 'lat', self.backward)  2.66 us
    pallas_call x1, Pallas kernels, beside_third(): pl.pallas_call(functools.partial(first_step, hops, later), out_shape=(jax...  2.07 us
  transfers between devices with their start and end apart: 24, of which 11 were waited for; matrix products, arithmetic and copies ran while one was open for 0% of the time, Pallas kernels for 11%

profile of v19, /device:TPU:0, one launch (start us, length us, event | category | flops | bytes accessed | tf_op | source)
XLA Modules:
  0.0 41.7 jit_solution(13851985364238245324)
XLA Ops:
  0.0 3.1 %collective-permute-start = (bf16[448,128]{1,0:T(8,128)(2,1)}, bf16[448,128]{1,0:T(8,128)(2,1)S(1)}, u32[]{:S(2)}, u32[]{:S(2)}) collective-permute-start(bf16[448,128]{1,0:T(8,128)(2,1)} %bitcast.5), channel_id=1, source_target_pairs={{0,4},{4,8},{8,12},{12,14},{14,10},{10,6},{6,2},{2,0},{1,5},{5,9},... | collective-permute-start | bytes 344072 | tf_op jit(solution)/shard_map/ppermute | solution.py:100
  3.1 0.0 collective-permute-start.2
  3.1 5.0 %collective-permute-start.4 = (bf16[448,128]{1,0:T(8,128)(2,1)}, bf16[448,128]{1,0:T(8,128)(2,1)S(1)}, u32[]{:S(2)}, u32[]{:S(2)}) collective-permute-start(bf16[448,128]{1,0:T(8,128)(2,1)} %bitcast.7), channel_id=1, source_target_pairs={{0,14},{12,2},{14,0},{2,12},{4,6},{8,10},{10,8},{6,4},{1,15},{13,3... | collective-permute-start | bytes 344072 | tf_op jit(solution)/shard_map/ppermute | solution.py:102
  8.1 0.0 collective-permute-done.refs_0_
  8.1 0.1 collective-permute-start.1
  8.2 1.9 %collective-permute-start.3 = (bf16[448,128]{1,0:T(8,128)(2,1)S(1)}, bf16[448,128]{1,0:T(8,128)(2,1)S(1)}, u32[]{:S(2)}, u32[]{:S(2)}) collective-permute-start(bf16[448,128]{1,0:T(8,128)(2,1)S(1)} %collective-permute-done.2.refs_1_), channel_id=1, source_target_pairs={{4,0},{8,4},{12,8},{14,12},{10,14},{6,10},{2,6},{0,2},{5,1},{9,5},... | collective-permute-start | bytes 344072 | tf_op jit(solution)/shard_map/ppermute | solution.py:104
  10.1 0.1 collective-permute-start.7
  10.2 2.7 %collective-permute-done.4.x_corner = bf16[448,128]{1,0:T(8,128)(2,1)S(1)} collective-permute-done((bf16[448,128]{1,0:T(8,128)(2,1)}, bf16[448,128]{1,0:T(8,128)(2,1)S(1)}, u32[]{:S(2)}, u32[]{:S(2)}) %collective-permute-start.4) | collective-permute-done | bytes 114720 | tf_op jit(solution)/shard_map/ppermute | solution.py:102
  12.9 1.1 %collective-permute-done.1.refs_2_ = bf16[448,128]{1,0:T(8,128)(2,1)S(1)} collective-permute-done((bf16[448,128]{1,0:T(8,128)(2,1)S(1)}, bf16[448,128]{1,0:T(8,128)(2,1)S(1)}, u32[]{:S(2)}, u32[]{:S(2)}) %collective-permute-start.1) | collective-permute-done | bytes 114720 | tf_op jit(solution)/shard_map/ppermute | solution.py:103
  14.0 0.0 collective-permute-done.3.refs_3_
  14.0 1.1 %collective-permute-start.5 = (bf16[448,128]{1,0:T(8,128)(2,1)S(1)}, bf16[448,128]{1,0:T(8,128)(2,1)S(1)}, u32[]{:S(2)}, u32[]{:S(2)}) collective-permute-start(bf16[448,128]{1,0:T(8,128)(2,1)S(1)} %collective-permute-done.1.refs_2_), channel_id=1, source_target_pairs={{0,4},{4,8},{8,12},{12,14},{14,10},{10,6},{6,2},{2,0},{1,5},{5,9},... | collective-permute-start | bytes 344072 | tf_op jit(solution)/shard_map/ppermute | solution.py:111
  15.1 0.9 %collective-permute-start.6 = (bf16[448,128]{1,0:T(8,128)(2,1)S(1)}, bf16[448,128]{1,0:T(8,128)(2,1)S(1)}, u32[]{:S(2)}, u32[]{:S(2)}) collective-permute-start(bf16[448,128]{1,0:T(8,128)(2,1)S(1)} %collective-permute-done.3.refs_3_), channel_id=1, source_target_pairs={{4,0},{8,4},{12,8},{14,12},{10,14},{6,10},{2,6},{0,2},{5,1},{9,5},... | collective-permute-start | bytes 344072 | tf_op jit(solution)/shard_map/ppermute | solution.py:112
  16.0 0.0 collective-permute-done.7.x_middle
  16.0 2.1 %shard_map.55 = (f32[128,512]{1,0:T(8,128)S(1)}, bf16[4,448,512]{2,1,0:T(8,128)(2,1)S(1)}) custom-call(bf16[448,128]{1,0:T(8,128)(2,1)S(1)} %collective-permute-done.refs_0_, bf16[448,128]{1,0:T(8,128)(2,1)S(1)} %collective-permute-done.2.refs_1_, bf16[448,128]{1,0:T(8,128)(2,1)S(1)} %collective-permute-done.1.refs_2_, ...), custom_call_target="tpu_custom_call" | custom-call | flops 234881024 | bytes 2818048 | tf_op jit(solution)/shard_map/pallas_call | solution.py:128
  18.1 0.7 %collective-permute-done.5.x_f = bf16[448,128]{1,0:T(8,128)(2,1)S(1)} collective-permute-done((bf16[448,128]{1,0:T(8,128)(2,1)S(1)}, bf16[448,128]{1,0:T(8,128)(2,1)S(1)}, u32[]{:S(2)}, u32[]{:S(2)}) %collective-permute-start.5) | collective-permute-done | bytes 114720 | tf_op jit(solution)/shard_map/ppermute | solution.py:111
  18.8 1.1 %collective-permute-done.6.x_b = bf16[448,128]{1,0:T(8,128)(2,1)S(1)} collective-permute-done((bf16[448,128]{1,0:T(8,128)(2,1)S(1)}, bf16[448,128]{1,0:T(8,128)(2,1)S(1)}, u32[]{:S(2)}, u32[]{:S(2)}) %collective-permute-start.6) | collective-permute-done | bytes 114720 | tf_op jit(solution)/shard_map/ppermute | solution.py:112
  19.9 0.5 %shard_map.56.refs_0_ = bf16[128,512]{1,0:T(8,128)(2,1)S(1)} custom-call(bf16[448,128]{1,0:T(8,128)(2,1)S(1)} %bitcast.8, bf16[448,128]{1,0:T(8,128)(2,1)S(1)} %collective-permute-done.5.x_f, bf16[448,128]{1,0:T(8,128)(2,1)S(1)} %collective-permute-done.6.x_b, bf16[448,128]{1,0:T(8,128)(2,1)S(1)} %collective-permute-done.4.x_corner, ...), custom_call_target="tpu_custom_call" | custom-call | flops 234881024 | bytes 2818048 | tf_op jit(solution)/shard_map/pallas_call | solution.py:143
  20.4 1.0 %collective-permute-start.10 = (bf16[128,512]{1,0:T(8,128)(2,1)S(1)}, bf16[128,512]{1,0:T(8,128)(2,1)S(1)}, u32[]{:S(2)}, u32[]{:S(2)}) collective-permute-start(bf16[128,512]{1,0:T(8,128)(2,1)S(1)} %shard_map.56.refs_0_), channel_id=1, source_target_pairs={{4,0},{8,4},{12,8},{14,12},{10,14},{6,10},{2,6},{0,2},{5,1},{9,5},... | collective-permute-start | bytes 393224 | tf_op jit(solution)/shard_map/ppermute | solution.py:101
  21.4 1.1 %collective-permute-start.8 = (bf16[128,512]{1,0:T(8,128)(2,1)S(1)}, bf16[128,512]{1,0:T(8,128)(2,1)S(1)}, u32[]{:S(2)}, u32[]{:S(2)}) collective-permute-start(bf16[128,512]{1,0:T(8,128)(2,1)S(1)} %shard_map.56.refs_0_), channel_id=1, source_target_pairs={{0,4},{4,8},{8,12},{12,14},{14,10},{10,6},{6,2},{2,0},{1,5},{5,9},... | collective-permute-start | bytes 393224 | tf_op jit(solution)/shard_map/ppermute | solution.py:100
  22.5 2.5 %collective-permute-start.12 = (bf16[128,512]{1,0:T(8,128)(2,1)S(1)}, bf16[128,512]{1,0:T(8,128)(2,1)S(1)}, u32[]{:S(2)}, u32[]{:S(2)}) collective-permute-start(bf16[128,512]{1,0:T(8,128)(2,1)S(1)} %shard_map.56.refs_0_), channel_id=1, source_target_pairs={{0,14},{12,2},{14,0},{2,12},{4,6},{8,10},{10,8},{6,4},{1,15},{13,3... | collective-permute-start | bytes 393224 | tf_op jit(solution)/shard_map/ppermute | solution.py:102
  25.0 0.4 %collective-permute-done.10.refs_2_ = bf16[128,512]{1,0:T(8,128)(2,1)S(1)} collective-permute-done((bf16[128,512]{1,0:T(8,128)(2,1)S(1)}, bf16[128,512]{1,0:T(8,128)(2,1)S(1)}, u32[]{:S(2)}, u32[]{:S(2)}) %collective-permute-start.10) | collective-permute-done | bytes 131104 | tf_op jit(solution)/shard_map/ppermute | solution.py:101
  25.4 1.6 %collective-permute-start.11 = (bf16[128,512]{1,0:T(8,128)(2,1)S(1)}, bf16[128,512]{1,0:T(8,128)(2,1)S(1)}, u32[]{:S(2)}, u32[]{:S(2)}) collective-permute-start(bf16[128,512]{1,0:T(8,128)(2,1)S(1)} %collective-permute-done.10.refs_2_), channel_id=1, source_target_pairs={{4,0},{8,4},{12,8},{14,12},{10,14},{6,10},{2,6},{0,2},{5,1},{9,5},... | collective-permute-start | bytes 393224 | tf_op jit(solution)/shard_map/ppermute | solution.py:104
  27.0 0.4 %collective-permute-start.9 = (bf16[128,512]{1,0:T(8,128)(2,1)S(1)}, bf16[128,512]{1,0:T(8,128)(2,1)S(1)}, u32[]{:S(2)}, u32[]{:S(2)}) collective-permute-start(bf16[128,512]{1,0:T(8,128)(2,1)S(1)} %collective-permute-done.8.refs_1_), channel_id=1, source_target_pairs={{0,4},{4,8},{8,12},{12,14},{14,10},{10,6},{6,2},{2,0},{1,5},{5,9},... | collective-permute-start | bytes 393224 | tf_op jit(solution)/shard_map/ppermute | solution.py:103
  27.5 0.1 collective-permute-start.14
  27.6 0.0 collective-permute-done.13.refs_1_
  27.6 0.5 %collective-permute-start.15 = (bf16[128,512]{1,0:T(8,128)(2,1)S(1)}, bf16[128,512]{1,0:T(8,128)(2,1)S(1)}, u32[]{:S(2)}, u32[]{:S(2)}) collective-permute-start(bf16[128,512]{1,0:T(8,128)(2,1)S(1)} %collective-permute-done.8.refs_1_), channel_id=1, source_target_pairs={{0,1},{1,0},{2,3},{3,2},{4,5},{5,4},{6,7},{7,6},{8,9},{9,8},{10,11... | collective-permute-start | bytes 393224 | tf_op jit(solution)/shard_map/ppermute | solution.py:337
  28.1 1.3 %shard_map.57 = (bf16[256,256]{1,0:T(8,128)(2,1)S(1)}, bf16[1,4,256,512]{3,2,1,0:T(8,128)(2,1)}) custom-call(s32[4,8]{1,0:T(4,128)S(1)} %bitcast.9, bf16[128,512]{1,0:T(8,128)(2,1)S(1)} %shard_map.56.refs_0_, bf16[128,512]{1,0:T(8,128)(2,1)S(1)} %collective-permute-done.13.refs_1_), custom_call_target="tpu_custom_call" | custom-call | tf_op jit(solution)/shard_map/pallas_call | solution.py:302
  29.4 2.2 %collective-permute-done.12 = bf16[128,512]{1,0:T(8,128)(2,1)S(1)} collective-permute-done((bf16[128,512]{1,0:T(8,128)(2,1)S(1)}, bf16[128,512]{1,0:T(8,128)(2,1)S(1)}, u32[]{:S(2)}, u32[]{:S(2)}) %collective-permute-start.12) | collective-permute-done | bytes 131104 | tf_op jit(solution)/shard_map/ppermute | solution.py:102
  31.5 0.0 collective-permute-start.16
  31.5 1.9 %collective-permute-done.11.refs_4_ = bf16[128,512]{1,0:T(8,128)(2,1)S(1)} collective-permute-done((bf16[128,512]{1,0:T(8,128)(2,1)S(1)}, bf16[128,512]{1,0:T(8,128)(2,1)S(1)}, u32[]{:S(2)}, u32[]{:S(2)}) %collective-permute-start.11) | collective-permute-done | bytes 131104 | tf_op jit(solution)/shard_map/ppermute | solution.py:104
  33.4 0.6 %collective-permute-done.9.refs_3_ = bf16[128,512]{1,0:T(8,128)(2,1)S(1)} collective-permute-done((bf16[128,512]{1,0:T(8,128)(2,1)S(1)}, bf16[128,512]{1,0:T(8,128)(2,1)S(1)}, u32[]{:S(2)}, u32[]{:S(2)}) %collective-permute-start.9) | collective-permute-done | bytes 131104 | tf_op jit(solution)/shard_map/ppermute | solution.py:103
  34.1 0.0 collective-permute-start.17
  34.1 0.0 collective-permute-start.19
  34.1 0.0 collective-permute-done.14
  34.1 0.5 %collective-permute-start.18 = (bf16[128,512]{1,0:T(8,128)(2,1)S(1)}, bf16[128,512]{1,0:T(8,128)(2,1)S(1)}, u32[]{:S(2)}, u32[]{:S(2)}) collective-permute-start(bf16[128,512]{1,0:T(8,128)(2,1)S(1)} %collective-permute-done.11.refs_4_), channel_id=1, source_target_pairs={{0,1},{1,0},{2,3},{3,2},{4,5},{5,4},{6,7},{7,6},{8,9},{9,8},{10,11... | collective-permute-start | bytes 393224 | tf_op jit(solution)/shard_map/ppermute | solution.py:337
  34.6 0.0 collective-permute-done.15.refs_5_
  34.6 1.7 %collective-permute-start.20 = (bf16[128,512]{1,0:T(8,128)(2,1)S(1)}, bf16[128,512]{1,0:T(8,128)(2,1)S(1)}, u32[]{:S(2)}, u32[]{:S(2)}) collective-permute-start(bf16[128,512]{1,0:T(8,128)(2,1)S(1)} %collective-permute-done.11.refs_4_), channel_id=1, source_target_pairs={{4,0},{8,4},{12,8},{14,12},{10,14},{6,10},{2,6},{0,2},{5,1},{9,5},... | collective-permute-start | bytes 393224 | tf_op jit(solution)/shard_map/ppermute | solution.py:112
  36.3 0.0 collective-permute-done.16.refs_6_
  36.4 0.1 collective-permute-start.23
  36.4 0.0 collective-permute-done.18.refs_8_
  36.5 1.2 %shard_map.58.refs_5_ = bf16[1,4,256,512]{3,2,1,0:T(8,128)(2,1)} custom-call(s32[4,8]{1,0:T(4,128)S(1)} %bitcast.10, bf16[256,256]{1,0:T(8,128)(2,1)S(1)} %get-tuple-element.36.refs_0_, bf16[128,512]{1,0:T(8,128)(2,1)S(1)} %collective-permute-done.8.refs_1_, bf16[128,512]{1,0:T(8,128)(2,1)S(1)} %collective-permute-done.10.refs_2_, ...), custom_call_target="tpu_custom_call", output_to_operand_aliasing={{}: (10, {})} | custom-call | flops 268435456 | bytes 2097152 | tf_op jit(solution)/shard_map/pallas_call | solution.py:302
  37.7 2.3 %collective-permute-done.19.refs_1_ = bf16[128,512]{1,0:T(8,128)(2,1)S(1)} collective-permute-done((bf16[128,512]{1,0:T(8,128)(2,1)S(1)}, bf16[128,512]{1,0:T(8,128)(2,1)S(1)}, u32[]{:S(2)}, u32[]{:S(2)}) %collective-permute-start.19) | collective-permute-done | bytes 131104 | tf_op jit(solution)/shard_map/ppermute | solution.py:111
  40.0 0.1 collective-permute-done.20.refs_1_
  40.1 0.4 %collective-permute-start.21 = (bf16[128,512]{1,0:T(8,128)(2,1)S(1)}, bf16[128,512]{1,0:T(8,128)(2,1)S(1)}, u32[]{:S(2)}, u32[]{:S(2)}) collective-permute-start(bf16[128,512]{1,0:T(8,128)(2,1)S(1)} %collective-permute-done.20.refs_1_), channel_id=1, source_target_pairs={{0,1},{1,0},{2,3},{3,2},{4,5},{5,4},{6,7},{7,6},{8,9},{9,8},{10,11... | collective-permute-start | bytes 393224 | tf_op jit(solution)/shard_map/ppermute | solution.py:337
  40.5 0.8 %collective-permute-done.22.refs_3_ = bf16[128,512]{1,0:T(8,128)(2,1)S(1)} collective-permute-done((bf16[128,512]{1,0:T(8,128)(2,1)S(1)}, bf16[128,512]{1,0:T(8,128)(2,1)S(1)}, u32[]{:S(2)}, u32[]{:S(2)}) %collective-permute-start.22) | collective-permute-done | bytes 131104 | tf_op jit(solution)/shard_map/ppermute | solution.py:337
  41.3 0.2 shard_map.59.refs_3_
  41.5 0.0 collective-permute-done.21.refs_2_
  41.6 0.2 shard_map.60
  (17 shorter events, 0.1 us)
Async XLA Ops:
  0.0 19.9 %copy-start = (bf16[128,448]{0,1:T(8,128)(2,1)S(1)}, bf16[128,448]{0,1:T(8,128)(2,1)}, u32[]{:S(2)}) copy-start(bf16[128,448]{0,1:T(8,128)(2,1)} %param.5) | copy-start | bytes 344068
  0.0 19.9 %copy-start.2 = (f32[512]{0:T(512)S(1)}, f32[512]{0:T(512)}, u32[]{:S(2)}) copy-start(f32[512]{0:T(512)} %param.7) | copy-start | bytes 6148
  0.0 19.9 %copy-start.3 = (f32[512]{0:T(512)S(1)}, f32[512]{0:T(512)}, u32[]{:S(2)}) copy-start(f32[512]{0:T(512)} %param.8) | copy-start | bytes 6148
  0.0 8.1 %collective-permute-start = (bf16[448,128]{1,0:T(8,128)(2,1)}, bf16[448,128]{1,0:T(8,128)(2,1)S(1)}, u32[]{:S(2)}, u32[]{:S(2)}) collective-permute-start(bf16[448,128]{1,0:T(8,128)(2,1)} %bitcast.5), channel_id=1, source_target_pairs={{0,4},{4,8},{8,12},{12,14},{14,10},{10,6},{6,2},{2,0},{1,5},{5,9},... | collective-permute-start | bytes 344072 | tf_op jit(solution)/shard_map/ppermute | solution.py:100
  3.1 5.1 %collective-permute-start.2 = (bf16[448,128]{1,0:T(8,128)(2,1)}, bf16[448,128]{1,0:T(8,128)(2,1)S(1)}, u32[]{:S(2)}, u32[]{:S(2)}) collective-permute-start(bf16[448,128]{1,0:T(8,128)(2,1)} %bitcast.6), channel_id=1, source_target_pairs={{4,0},{8,4},{12,8},{14,12},{10,14},{6,10},{2,6},{0,2},{5,1},{9,5},... | collective-permute-start | bytes 344072 | tf_op jit(solution)/shard_map/ppermute | solution.py:101
  3.1 9.8 %collective-permute-start.4 = (bf16[448,128]{1,0:T(8,128)(2,1)}, bf16[448,128]{1,0:T(8,128)(2,1)S(1)}, u32[]{:S(2)}, u32[]{:S(2)}) collective-permute-start(bf16[448,128]{1,0:T(8,128)(2,1)} %bitcast.7), channel_id=1, source_target_pairs={{0,14},{12,2},{14,0},{2,12},{4,6},{8,10},{10,8},{6,4},{1,15},{13,3... | collective-permute-start | bytes 344072 | tf_op jit(solution)/shard_map/ppermute | solution.py:102
  8.1 5.9 %collective-permute-start.1 = (bf16[448,128]{1,0:T(8,128)(2,1)S(1)}, bf16[448,128]{1,0:T(8,128)(2,1)S(1)}, u32[]{:S(2)}, u32[]{:S(2)}) collective-permute-start(bf16[448,128]{1,0:T(8,128)(2,1)S(1)} %collective-permute-done.refs_0_), channel_id=1, source_target_pairs={{0,4},{4,8},{8,12},{12,14},{14,10},{10,6},{6,2},{2,0},{1,5},{5,9},... | collective-permute-start | bytes 344072 | tf_op jit(solution)/shard_map/ppermute | solution.py:103
  8.2 5.8 %collective-permute-start.3 = (bf16[448,128]{1,0:T(8,128)(2,1)S(1)}, bf16[448,128]{1,0:T(8,128)(2,1)S(1)}, u32[]{:S(2)}, u32[]{:S(2)}) collective-permute-start(bf16[448,128]{1,0:T(8,128)(2,1)S(1)} %collective-permute-done.2.refs_1_), channel_id=1, source_target_pairs={{4,0},{8,4},{12,8},{14,12},{10,14},{6,10},{2,6},{0,2},{5,1},{9,5},... | collective-permute-start | bytes 344072 | tf_op jit(solution)/shard_map/ppermute | solution.py:104
  10.1 5.9 %collective-permute-start.7 = (bf16[448,128]{1,0:T(8,128)(2,1)S(1)}, bf16[448,128]{1,0:T(8,128)(2,1)S(1)}, u32[]{:S(2)}, u32[]{:S(2)}) collective-permute-start(bf16[448,128]{1,0:T(8,128)(2,1)S(1)} %broadcast_select_fusion.2), channel_id=1, source_target_pairs={{4,6},{5,7},{8,10},{9,11},{10,8},{11,9},{6,4},{7,5},{0,1},{1,0},{1... | collective-permute-start | bytes 344072 | tf_op jit(solution)/shard_map/ppermute | solution.py:106
  14.0 4.8 %collective-permute-start.5 = (bf16[448,128]{1,0:T(8,128)(2,1)S(1)}, bf16[448,128]{1,0:T(8,128)(2,1)S(1)}, u32[]{:S(2)}, u32[]{:S(2)}) collective-permute-start(bf16[448,128]{1,0:T(8,128)(2,1)S(1)} %collective-permute-done.1.refs_2_), channel_id=1, source_target_pairs={{0,4},{4,8},{8,12},{12,14},{14,10},{10,6},{6,2},{2,0},{1,5},{5,9},... | collective-permute-start | bytes 344072 | tf_op jit(solution)/shard_map/ppermute | solution.py:111
  15.1 4.8 %collective-permute-start.6 = (bf16[448,128]{1,0:T(8,128)(2,1)S(1)}, bf16[448,128]{1,0:T(8,128)(2,1)S(1)}, u32[]{:S(2)}, u32[]{:S(2)}) collective-permute-start(bf16[448,128]{1,0:T(8,128)(2,1)S(1)} %collective-permute-done.3.refs_3_), channel_id=1, source_target_pairs={{4,0},{8,4},{12,8},{14,12},{10,14},{6,10},{2,6},{0,2},{5,1},{9,5},... | collective-permute-start | bytes 344072 | tf_op jit(solution)/shard_map/ppermute | solution.py:112
  16.0 12.0 %copy-start.1 = (s32[8,4]{0,1:T(4,128)S(1)}, s32[8,4]{0,1:T(4,128)}, u32[]{:S(2)}) copy-start(s32[8,4]{0,1:T(4,128)} %param.9) | copy-start | bytes 388
  20.4 5.0 %collective-permute-start.10 = (bf16[128,512]{1,0:T(8,128)(2,1)S(1)}, bf16[128,512]{1,0:T(8,128)(2,1)S(1)}, u32[]{:S(2)}, u32[]{:S(2)}) collective-permute-start(bf16[128,512]{1,0:T(8,128)(2,1)S(1)} %shard_map.56.refs_0_), channel_id=1, source_target_pairs={{4,0},{8,4},{12,8},{14,12},{10,14},{6,10},{2,6},{0,2},{5,1},{9,5},... | collective-permute-start | bytes 393224 | tf_op jit(solution)/shard_map/ppermute | solution.py:101
  21.4 5.6 %collective-permute-start.8 = (bf16[128,512]{1,0:T(8,128)(2,1)S(1)}, bf16[128,512]{1,0:T(8,128)(2,1)S(1)}, u32[]{:S(2)}, u32[]{:S(2)}) collective-permute-start(bf16[128,512]{1,0:T(8,128)(2,1)S(1)} %shard_map.56.refs_0_), channel_id=1, source_target_pairs={{0,4},{4,8},{8,12},{12,14},{14,10},{10,6},{6,2},{2,0},{1,5},{5,9},... | collective-permute-start | bytes 393224 | tf_op jit(solution)/shard_map/ppermute | solution.py:100
  22.5 5.1 %collective-permute-start.13 = (bf16[128,512]{1,0:T(8,128)(2,1)S(1)}, bf16[128,512]{1,0:T(8,128)(2,1)S(1)}, u32[]{:S(2)}, u32[]{:S(2)}) collective-permute-start(bf16[128,512]{1,0:T(8,128)(2,1)S(1)} %shard_map.56.refs_0_), channel_id=1, source_target_pairs={{0,1},{1,0},{2,3},{3,2},{4,5},{5,4},{6,7},{7,6},{8,9},{9,8},{10,11... | collective-permute-start | bytes 393224 | tf_op jit(solution)/shard_map/ppermute | solution.py:334
  22.5 9.0 %collective-permute-start.12 = (bf16[128,512]{1,0:T(8,128)(2,1)S(1)}, bf16[128,512]{1,0:T(8,128)(2,1)S(1)}, u32[]{:S(2)}, u32[]{:S(2)}) collective-permute-start(bf16[128,512]{1,0:T(8,128)(2,1)S(1)} %shard_map.56.refs_0_), channel_id=1, source_target_pairs={{0,14},{12,2},{14,0},{2,12},{4,6},{8,10},{10,8},{6,4},{1,15},{13,3... | collective-permute-start | bytes 393224 | tf_op jit(solution)/shard_map/ppermute | solution.py:102
  25.4 8.0 %collective-permute-start.11 = (bf16[128,512]{1,0:T(8,128)(2,1)S(1)}, bf16[128,512]{1,0:T(8,128)(2,1)S(1)}, u32[]{:S(2)}, u32[]{:S(2)}) collective-permute-start(bf16[128,512]{1,0:T(8,128)(2,1)S(1)} %collective-permute-done.10.refs_2_), channel_id=1, source_target_pairs={{4,0},{8,4},{12,8},{14,12},{10,14},{6,10},{2,6},{0,2},{5,1},{9,5},... | collective-permute-start | bytes 393224 | tf_op jit(solution)/shard_map/ppermute | solution.py:104
  27.0 7.0 %collective-permute-start.9 = (bf16[128,512]{1,0:T(8,128)(2,1)S(1)}, bf16[128,512]{1,0:T(8,128)(2,1)S(1)}, u32[]{:S(2)}, u32[]{:S(2)}) collective-permute-start(bf16[128,512]{1,0:T(8,128)(2,1)S(1)} %collective-permute-done.8.refs_1_), channel_id=1, source_target_pairs={{0,4},{4,8},{8,12},{12,14},{14,10},{10,6},{6,2},{2,0},{1,5},{5,9},... | collective-permute-start | bytes 393224 | tf_op jit(solution)/shard_map/ppermute | solution.py:103
  27.5 6.6 %collective-permute-start.14 = (bf16[128,512]{1,0:T(8,128)(2,1)S(1)}, bf16[128,512]{1,0:T(8,128)(2,1)S(1)}, u32[]{:S(2)}, u32[]{:S(2)}) collective-permute-start(bf16[128,512]{1,0:T(8,128)(2,1)S(1)} %broadcast_select_fusion.1), channel_id=1, source_target_pairs={{4,6},{5,7},{8,10},{9,11},{10,8},{11,9},{6,4},{7,5},{0,1},{1,0},{1... | collective-permute-start | bytes 393224 | tf_op jit(solution)/shard_map/ppermute | solution.py:106
  27.6 7.0 %collective-permute-start.15 = (bf16[128,512]{1,0:T(8,128)(2,1)S(1)}, bf16[128,512]{1,0:T(8,128)(2,1)S(1)}, u32[]{:S(2)}, u32[]{:S(2)}) collective-permute-start(bf16[128,512]{1,0:T(8,128)(2,1)S(1)} %collective-permute-done.8.refs_1_), channel_id=1, source_target_pairs={{0,1},{1,0},{2,3},{3,2},{4,5},{5,4},{6,7},{7,6},{8,9},{9,8},{10,11... | collective-permute-start | bytes 393224 | tf_op jit(solution)/shard_map/ppermute | solution.py:337
  31.5 4.8 %collective-permute-start.16 = (bf16[128,512]{1,0:T(8,128)(2,1)S(1)}, bf16[128,512]{1,0:T(8,128)(2,1)S(1)}, u32[]{:S(2)}, u32[]{:S(2)}) collective-permute-start(bf16[128,512]{1,0:T(8,128)(2,1)S(1)} %collective-permute-done.10.refs_2_), channel_id=1, source_target_pairs={{0,1},{1,0},{2,3},{3,2},{4,5},{5,4},{6,7},{7,6},{8,9},{9,8},{10,11... | collective-permute-start | bytes 393224 | tf_op jit(solution)/shard_map/ppermute | solution.py:337
  34.1 2.4 %collective-permute-start.17 = (bf16[128,512]{1,0:T(8,128)(2,1)S(1)}, bf16[128,512]{1,0:T(8,128)(2,1)S(1)}, u32[]{:S(2)}, u32[]{:S(2)}) collective-permute-start(bf16[128,512]{1,0:T(8,128)(2,1)S(1)} %collective-permute-done.9.refs_3_), channel_id=1, source_target_pairs={{0,1},{1,0},{2,3},{3,2},{4,5},{5,4},{6,7},{7,6},{8,9},{9,8},{10,11... | collective-permute-start | bytes 393224 | tf_op jit(solution)/shard_map/ppermute | solution.py:337
  34.1 5.9 %collective-permute-start.19 = (bf16[128,512]{1,0:T(8,128)(2,1)S(1)}, bf16[128,512]{1,0:T(8,128)(2,1)S(1)}, u32[]{:S(2)}, u32[]{:S(2)}) collective-permute-start(bf16[128,512]{1,0:T(8,128)(2,1)S(1)} %collective-permute-done.9.refs_3_), channel_id=1, source_target_pairs={{0,4},{4,8},{8,12},{12,14},{14,10},{10,6},{6,2},{2,0},{1,5},{5,9},... | collective-permute-start | bytes 393224 | tf_op jit(solution)/shard_map/ppermute | solution.py:111
  34.1 2.4 %collective-permute-start.18 = (bf16[128,512]{1,0:T(8,128)(2,1)S(1)}, bf16[128,512]{1,0:T(8,128)(2,1)S(1)}, u32[]{:S(2)}, u32[]{:S(2)}) collective-permute-start(bf16[128,512]{1,0:T(8,128)(2,1)S(1)} %collective-permute-done.11.refs_4_), channel_id=1, source_target_pairs={{0,1},{1,0},{2,3},{3,2},{4,5},{5,4},{6,7},{7,6},{8,9},{9,8},{10,11... | collective-permute-start | bytes 393224 | tf_op jit(solution)/shard_map/ppermute | solution.py:337
  34.6 5.5 %collective-permute-start.20 = (bf16[128,512]{1,0:T(8,128)(2,1)S(1)}, bf16[128,512]{1,0:T(8,128)(2,1)S(1)}, u32[]{:S(2)}, u32[]{:S(2)}) collective-permute-start(bf16[128,512]{1,0:T(8,128)(2,1)S(1)} %collective-permute-done.11.refs_4_), channel_id=1, source_target_pairs={{4,0},{8,4},{12,8},{14,12},{10,14},{6,10},{2,6},{0,2},{5,1},{9,5},... | collective-permute-start | bytes 393224 | tf_op jit(solution)/shard_map/ppermute | solution.py:112
  36.4 4.1 %collective-permute-start.23 = (bf16[128,512]{1,0:T(8,128)(2,1)S(1)}, bf16[128,512]{1,0:T(8,128)(2,1)S(1)}, u32[]{:S(2)}, u32[]{:S(2)}) collective-permute-start(bf16[128,512]{1,0:T(8,128)(2,1)S(1)} %broadcast_select_fusion.refs_2_), channel_id=1, source_target_pairs={{0,1},{1,0},{2,3},{3,2},{4,5},{5,4},{6,7},{7,6},{8,9},{9,8},{10,11... | collective-permute-start | bytes 393224 | tf_op jit(solution)/shard_map/ppermute | solution.py:337
  40.0 1.3 %collective-permute-start.22 = (bf16[128,512]{1,0:T(8,128)(2,1)S(1)}, bf16[128,512]{1,0:T(8,128)(2,1)S(1)}, u32[]{:S(2)}, u32[]{:S(2)}) collective-permute-start(bf16[128,512]{1,0:T(8,128)(2,1)S(1)} %collective-permute-done.19.refs_1_), channel_id=1, source_target_pairs={{0,1},{1,0},{2,3},{3,2},{4,5},{5,4},{6,7},{7,6},{8,9},{9,8},{10,11... | collective-permute-start | bytes 393224 | tf_op jit(solution)/shard_map/ppermute | solution.py:337
  40.1 1.5 %collective-permute-start.21 = (bf16[128,512]{1,0:T(8,128)(2,1)S(1)}, bf16[128,512]{1,0:T(8,128)(2,1)S(1)}, u32[]{:S(2)}, u32[]{:S(2)}) collective-permute-start(bf16[128,512]{1,0:T(8,128)(2,1)S(1)} %collective-permute-done.20.refs_1_), channel_id=1, source_target_pairs={{0,1},{1,0},{2,3},{3,2},{4,5},{5,4},{6,7},{7,6},{8,9},{9,8},{10,11... | collective-permute-start | bytes 393224 | tf_op jit(solution)/shard_map/ppermute | solution.py:337
